TPU v7x, 32 devices: a whole 2x2x4 slice. The times are simulated.
32 devices in a mesh: wide: 8 (over y, x, core), narrow: 4 (over z).
Axes of the slice: x: 2, y: 2, z: 4, core: 2. Of those that a mesh axis runs over, the one named last changes fastest.
Arguments:
- tokens: bfloat16 [64, 512, 768], P(('wide', 'narrow')), may hold values from -6 to 6
- segments: int32 [64, 512], P(('wide', 'narrow')), may hold values from 0 to 3, never falling along the last dimension, each value on 1 to 256 neighbouring positions
- exit_layer: int32 [64], P(('wide', 'narrow')), may hold values from 0 to 1, as said below
- attn_in: bfloat16 [2, 768, 2304], replicated, may hold values from -0.21875 to 0.21875
- qv_bias: bfloat16 [2, 1536], replicated, may hold values from -3 to 3
- attn_out: bfloat16 [2, 768, 768], replicated, may hold values from -0.875 to 0.875
- out_bias: bfloat16 [2, 768], replicated, may hold values from -2 to 2
- ln_gain: bfloat16 [2, 1536], replicated, may hold values from 0.25 to 1.75
- ln_bias: bfloat16 [2, 1536], replicated, may hold values from -2 to 2
- ff_in: bfloat16 [2, 768, 3072], replicated, may hold values from -0.21875 to 0.21875
- ff_in_bias: bfloat16 [2, 3072], replicated, may hold values from -3 to 3
- ff_out: bfloat16 [2, 3072, 768], replicated, may hold values from -0.109375 to 0.109375
- ff_out_bias: bfloat16 [2, 768], replicated, may hold values from -2 to 2
- stu_proj: bfloat16 [2, 768, 128], replicated, may hold values from -0.21875 to 0.21875
- stu_bias: bfloat16 [2, 128], replicated, may hold values from -3 to 3
- pool_query: bfloat16 [2, 128], replicated, may hold values from -5 to 5
- stu_dense: bfloat16 [2, 128, 128], replicated, may hold values from -1 to 1
- stu_dense_bias: bfloat16 [2, 128], replicated, may hold values from -2 to 2
- stu_cls: bfloat16 [2, 128, 14], replicated, may hold values from -1 to 1
- stu_cls_bias: bfloat16 [2, 14], replicated, may hold values from -3 to 3
- out_cot: bfloat16 [64, 512, 768], P(('wide', 'narrow')), may hold values from -6 to 6
- logit_cot: bfloat16 [64, 2, 14], P(('wide', 'narrow')), may hold values from -6 to 6
Outputs:
- activations: bfloat16 [64, 512, 768], P(('wide', 'narrow'))
- logits: bfloat16 [64, 2, 14], P(('wide', 'narrow'))
- grad_tokens: bfloat16 [64, 512, 768], P(('wide', 'narrow'))
- grad_attn_in: float32 [2, 768, 2304], P(None, 'narrow')
- grad_qv_bias: float32 [2, 1536], P(None, 'narrow')
- grad_attn_out: float32 [2, 768, 768], P(None, 'narrow')
- grad_out_bias: float32 [2, 768], P(None, 'narrow')
- grad_ln_gain: float32 [2, 1536], P(None, 'narrow')
- grad_ln_bias: float32 [2, 1536], P(None, 'narrow')
- grad_ff_in: float32 [2, 768, 3072], P(None, 'narrow')
- grad_ff_in_bias: float32 [2, 3072], P(None, 'narrow')
- grad_ff_out: float32 [2, 3072, 768], P(None, 'narrow')
- grad_ff_out_bias: float32 [2, 768], P(None, 'narrow')
- grad_stu_proj: float32 [2, 768, 128], P(None, 'narrow')
- grad_stu_bias: float32 [2, 128], P(None, 'narrow')
- grad_pool_query: float32 [2, 128], P(None, 'narrow')
- grad_stu_dense: float32 [2, 128, 128], P(None, 'narrow')
- grad_stu_dense_bias: float32 [2, 128], P(None, 'narrow')
- grad_stu_cls: float32 [2, 128, 14], P(None, 'narrow')
- grad_stu_cls_bias: float32 [2, 14], replicated
Inputs may be any that keep to these rules, and one draw needn't show every extreme that they name: `exit_layer`: exactly half of the rows of each aligned block of 4 × 2 rows have exit layer 1, and in each such block all 2 rows of one device do.
All inputs are finite; a program needn't handle non-finite values.
Results may differ from a plain program's by a relative error of at most 0.022.
Values may be sent and summed in bfloat16 or wider, within the bound.
No kernel may reach another device: no remote copies, remote signals or barrier semaphores. Data moves between devices by JAX's collectives and lax.ppermute only.
A program may use at most 320 MiB of HBM per device.

v0:
```python
from functools import partial

import jax
import jax.numpy as jnp
from jax import lax
from jax.sharding import PartitionSpec as P

HEADS = 12
STU_HEADS = 2


eps_norm = 1e-12
highest = lax.Precision.HIGHEST


def as_sent(value):
    return jax.tree.map(lambda a: a.astype(jnp.bfloat16) if a.dtype == jnp.float32 else a, value)


def norm(values, gain_vec, shift_vec):
    mean_val = jnp.mean(values, -1, keepdims=True)
    centered = values - mean_val
    variance = jnp.mean(centered * centered, -1, keepdims=True)
    return centered * lax.rsqrt(variance + eps_norm) * gain_vec + shift_vec


def student_head(proj_rows, pool_query, dense, dense_bias, classes_w, classes_bias):
    row_count, seq_len, stu_width = proj_rows.shape
    head_width = stu_width // STU_HEADS
    head_split = proj_rows.reshape(row_count, seq_len, STU_HEADS, head_width)
    queries = pool_query.reshape(STU_HEADS, head_width)
    pool_scores = jnp.sum(head_split * queries, -1) * head_width ** (-0.5)
    weights = jax.nn.softmax(pool_scores, axis=1)
    pooled = jnp.sum(weights[..., None] * head_split, 1).reshape(row_count, stu_width)
    dense_out = jnp.tanh(jnp.dot(pooled, dense, precision=highest) + dense_bias)
    return jnp.dot(dense_out, classes_w, precision=highest) + classes_bias


def masked_scores(query_rows, key_rows, seg_row):
    score_scale = query_rows.shape[-1] ** (-0.5)
    scores = (
        jnp.einsum("qhd,khd->hqk", query_rows, key_rows, preferred_element_type=jnp.float32)
        * score_scale
    )
    same_doc = seg_row[:, None] == seg_row[None, :]
    return (jnp.where(same_doc[None], scores, -1e30), score_scale)


def attend_row(parts):
    query_rows, key_rows, value_rows, seg_row = parts
    scores, score_scale = masked_scores(query_rows, key_rows, seg_row)
    row_max = jnp.max(scores, -1, keepdims=True)
    exp_terms = jnp.exp(scores - row_max)
    row_total = jnp.sum(exp_terms, -1, keepdims=True)
    prob_rows = (exp_terms / row_total).astype(jnp.bfloat16)
    mix_out = jnp.einsum("hqk,khd->qhd", prob_rows, value_rows, preferred_element_type=jnp.float32)
    return (mix_out.astype(jnp.bfloat16), (row_max + jnp.log(row_total))[..., 0])


def attend_back(parts):
    query_rows, key_rows, value_rows, seg_row, logsum, grad_mix = parts
    scores, score_scale = masked_scores(query_rows, key_rows, seg_row)
    prob_rows = jnp.exp(scores - logsum[..., None])
    grad_prob = jnp.einsum("qhd,khd->hqk", grad_mix, value_rows, preferred_element_type=jnp.float32)
    grad_value = jnp.einsum(
        "hqk,qhd->khd", prob_rows.astype(jnp.bfloat16), grad_mix, preferred_element_type=jnp.float32
    )
    row_delta = jnp.sum(prob_rows * grad_prob, -1, keepdims=True)
    grad_score = (prob_rows * (grad_prob - row_delta)).astype(jnp.bfloat16)
    grad_query = (
        jnp.einsum("hqk,khd->qhd", grad_score, key_rows, preferred_element_type=jnp.float32)
        * score_scale
    )
    grad_key = (
        jnp.einsum("hqk,qhd->khd", grad_score, query_rows, preferred_element_type=jnp.float32)
        * score_scale
    )
    return jnp.stack([grad_query, grad_key, grad_value], 1).astype(jnp.bfloat16)


def layer_forward(layer_in, seg_rows, weights):
    (
        attn_in,
        qv_bias,
        attn_out,
        out_bias,
        gain_vec,
        shift_vec,
        ff_in,
        ff_in_bias,
        ff_out,
        ff_out_bias,
    ) = weights
    row_count, seq_len, model_width = layer_in.shape
    gain_vec = gain_vec.astype(jnp.float32)
    shift_vec = shift_vec.astype(jnp.float32)
    flat_in = layer_in.reshape(row_count * seq_len, model_width)
    zero_bias = jnp.zeros((model_width,), jnp.float32)
    full_bias = jnp.concatenate(
        [
            qv_bias[:model_width].astype(jnp.float32),
            zero_bias,
            qv_bias[model_width:].astype(jnp.float32),
        ]
    )
    qkv_rows = (jnp.dot(flat_in, attn_in, preferred_element_type=jnp.float32) + full_bias).astype(
        jnp.bfloat16
    )
    qkv_rows = qkv_rows.reshape(row_count, seq_len, 3, HEADS, model_width // HEADS)
    mix_out, logsum = lax.map(
        attend_row, (qkv_rows[:, :, 0], qkv_rows[:, :, 1], qkv_rows[:, :, 2], seg_rows)
    )
    mix_out = mix_out.reshape(row_count * seq_len, model_width)
    residual = (
        flat_in.astype(jnp.float32)
        + jnp.dot(mix_out, attn_out, preferred_element_type=jnp.float32)
        + out_bias.astype(jnp.float32)
    )
    first_norm = norm(residual, gain_vec[:model_width], shift_vec[:model_width])
    ff_inner = jnp.dot(
        first_norm.astype(jnp.bfloat16), ff_in, preferred_element_type=jnp.float32
    ) + ff_in_bias.astype(jnp.float32)
    active = jax.nn.gelu(ff_inner, approximate=False).astype(jnp.bfloat16)
    residual_two = (
        first_norm
        + jnp.dot(active, ff_out, preferred_element_type=jnp.float32)
        + ff_out_bias.astype(jnp.float32)
    )
    layer_out = norm(residual_two, gain_vec[model_width:], shift_vec[model_width:]).astype(
        jnp.bfloat16
    )
    saved = (flat_in, qkv_rows, logsum, mix_out, residual, first_norm, ff_inner, residual_two)
    return (layer_out.reshape(row_count, seq_len, model_width), saved)


def layer_backward(saved, seg_rows, weights, grad_out):
    (
        attn_in,
        qv_bias,
        attn_out,
        out_bias,
        gain_vec,
        shift_vec,
        ff_in,
        ff_in_bias,
        ff_out,
        ff_out_bias,
    ) = weights
    flat_in, qkv_rows, logsum, mix_out, residual, first_norm, ff_inner, residual_two = saved
    row_count, seq_len = (qkv_rows.shape[0], qkv_rows.shape[1])
    model_width = flat_in.shape[1]
    gain_vec = gain_vec.astype(jnp.float32)
    shift_vec = shift_vec.astype(jnp.float32)
    grad_flat = grad_out.reshape(-1, model_width)
    _, norm_two_back = jax.vjp(norm, residual_two, gain_vec[model_width:], shift_vec[model_width:])
    d_resid_two, d_gain_two, d_shift_two = norm_two_back(grad_flat)
    d_second = d_resid_two.astype(jnp.bfloat16)
    d_ff_out_bias = jnp.sum(d_second, 0, dtype=jnp.float32)
    active = jax.nn.gelu(ff_inner, approximate=False).astype(jnp.bfloat16)
    d_ff_out = jnp.einsum("tf,td->fd", active, d_second, preferred_element_type=jnp.float32)
    d_active = jnp.einsum("td,fd->tf", d_second, ff_out, preferred_element_type=jnp.float32)
    _, gelu_back = jax.vjp(partial(jax.nn.gelu, approximate=False), ff_inner)
    d_inner = gelu_back(d_active)[0].astype(jnp.bfloat16)
    d_ff_in_bias = jnp.sum(d_inner, 0, dtype=jnp.float32)
    d_ff_in = jnp.einsum(
        "td,tf->df", first_norm.astype(jnp.bfloat16), d_inner, preferred_element_type=jnp.float32
    )
    d_first = (
        jnp.einsum("tf,df->td", d_inner, ff_in, preferred_element_type=jnp.float32) + d_resid_two
    )
    _, norm_one_back = jax.vjp(norm, residual, gain_vec[:model_width], shift_vec[:model_width])
    d_resid, d_gain_one, d_shift_one = norm_one_back(d_first)
    d_branch = d_resid.astype(jnp.bfloat16)
    d_out_bias = jnp.sum(d_branch, 0, dtype=jnp.float32)
    d_attn_out = jnp.einsum("td,te->de", mix_out, d_branch, preferred_element_type=jnp.float32)
    d_mix = jnp.einsum("te,de->td", d_branch, attn_out, preferred_element_type=jnp.float32).astype(
        jnp.bfloat16
    )
    d_mix = d_mix.reshape(row_count, seq_len, HEADS, model_width // HEADS)
    d_qkv = lax.map(
        attend_back,
        (qkv_rows[:, :, 0], qkv_rows[:, :, 1], qkv_rows[:, :, 2], seg_rows, logsum, d_mix),
    )
    d_qkv = d_qkv.reshape(row_count * seq_len, 3 * model_width)
    col_sums = jnp.sum(d_qkv, 0, dtype=jnp.float32)
    d_qv_bias = jnp.concatenate([col_sums[:model_width], col_sums[2 * model_width :]])
    d_attn_in = jnp.einsum("td,te->de", flat_in, d_qkv, preferred_element_type=jnp.float32)
    d_layer_in = (
        jnp.einsum("te,de->td", d_qkv, attn_in, preferred_element_type=jnp.float32) + d_resid
    )
    gradients = (
        d_attn_in,
        d_qv_bias,
        d_attn_out,
        d_out_bias,
        jnp.concatenate([d_gain_one, d_gain_two]),
        jnp.concatenate([d_shift_one, d_shift_two]),
        d_ff_in,
        d_ff_in_bias,
        d_ff_out,
        d_ff_out_bias,
    )
    return (d_layer_in.reshape(grad_out.shape), gradients)


def student_forward(hidden, weights):
    proj, proj_bias, pool_query, dense, dense_bias, classes_w, classes_bias = weights
    proj_rows = jnp.einsum(
        "rld,ds->rls", hidden, proj, preferred_element_type=jnp.float32
    ) + proj_bias.astype(jnp.float32)
    return jax.vjp(
        student_head,
        proj_rows,
        pool_query.astype(jnp.float32),
        dense.astype(jnp.float32),
        dense_bias.astype(jnp.float32),
        classes_w.astype(jnp.float32),
        classes_bias.astype(jnp.float32),
    )


def student_backward(hidden, weights, back_fn, grad_logits, group_size):
    proj = weights[0]
    d_proj_rows, d_query, d_dense, d_dense_bias, d_classes, d_classes_bias = back_fn(grad_logits)
    d_proj_rows = d_proj_rows.astype(jnp.bfloat16)
    d_proj = jnp.einsum("rld,rls->ds", hidden, d_proj_rows, preferred_element_type=jnp.float32)
    d_proj_bias = jnp.sum(d_proj_rows, (0, 1), dtype=jnp.float32)
    d_hidden = jnp.einsum("rls,ds->rld", d_proj_rows, proj, preferred_element_type=jnp.float32)
    spread_bias = jnp.broadcast_to(d_classes_bias[None], (group_size, d_classes_bias.shape[0]))
    return (d_hidden, (d_proj, d_proj_bias, d_query, d_dense, d_dense_bias, d_classes, spread_bias))


def reduce_layer(gradients):
    shares = jax.tree.map(
        lambda part: part.astype(jnp.float32),
        lax.psum_scatter(as_sent(gradients), "narrow", scatter_dimension=0, tiled=True),
    )
    return jax.tree.map(lambda part: part.astype(jnp.float32), lax.psum(as_sent(shares), "wide"))


def shards(
    tokens,
    segments,
    exit_layer,
    attn_in,
    qv_bias,
    attn_out,
    out_bias,
    ln_gain,
    ln_bias,
    ff_in,
    ff_in_bias,
    ff_out,
    ff_out_bias,
    stu_proj,
    stu_bias,
    pool_query,
    stu_dense,
    stu_dense_bias,
    stu_cls,
    stu_cls_bias,
    out_cot,
    logit_cot,
):
    layer_weights = (
        attn_in,
        qv_bias,
        attn_out,
        out_bias,
        ln_gain,
        ln_bias,
        ff_in,
        ff_in_bias,
        ff_out,
        ff_out_bias,
    )
    head_weights = (
        stu_proj,
        stu_bias,
        pool_query,
        stu_dense,
        stu_dense_bias,
        stu_cls,
        stu_cls_bias,
    )
    layer_zero = tuple((item[0] for item in layer_weights))
    layer_one = tuple((item[1] for item in layer_weights))
    head_zero = tuple((item[0] for item in head_weights))
    head_one = tuple((item[1] for item in head_weights))
    row_count = tokens.shape[0]
    group_size = lax.axis_size("narrow")
    narrow_index = lax.axis_index("narrow")
    capacity = row_count // 2
    hidden_zero, saved_zero = layer_forward(tokens, segments, layer_zero)
    logits_zero, back_zero = student_forward(hidden_zero, head_zero)
    all_exits = lax.all_gather(exit_layer, "narrow", axis=0, tiled=True)
    alive_all = (all_exits == 1).astype(jnp.int32)
    alive_rows = lax.dynamic_slice_in_dim(alive_all, narrow_index * row_count, row_count)
    alive_float = alive_rows.astype(jnp.float32)
    alive_dev = alive_all.reshape(group_size, row_count)
    local_rank = jnp.cumsum(alive_dev, 1) - 1
    kept_count = jnp.minimum(jnp.sum(alive_dev, 1), capacity)
    room = capacity - kept_count
    room_end = jnp.cumsum(room)
    room_start = room_end - room
    surplus = (alive_dev == 1) & (local_rank >= capacity)
    surplus_rank = (jnp.cumsum(surplus.reshape(-1).astype(jnp.int32)) - 1).reshape(
        group_size, row_count
    )
    target_dev = jnp.sum((room_end[None, None, :] <= surplus_rank[..., None]).astype(jnp.int32), -1)
    device_ids = jnp.arange(group_size, dtype=jnp.int32)
    slot_ids = jnp.arange(capacity, dtype=jnp.int32)
    target_hot = target_dev[..., None] == device_ids[None, None, :]
    offset = jnp.sum(jnp.where(target_hot, (kept_count - room_start)[None, None, :], 0), -1)
    target_slot = offset + surplus_rank
    send_all = (
        surplus[..., None, None]
        & target_hot[..., None]
        & (target_slot[..., None, None] == slot_ids)
    )
    kept_all = (alive_dev == 1)[..., None] & (local_rank[..., None] == slot_ids)
    send_mine = lax.dynamic_index_in_dim(send_all, narrow_index, 0, keepdims=False)
    kept_mine = lax.dynamic_index_in_dim(kept_all, narrow_index, 0, keepdims=False)
    arrive_map = jnp.sum(
        lax.dynamic_index_in_dim(send_all, narrow_index, 2, keepdims=False).astype(jnp.int32), 1
    )
    send_map = send_mine.astype(jnp.bfloat16)
    kept_map = kept_mine.astype(jnp.bfloat16)
    arrive_float = arrive_map.astype(jnp.bfloat16)

    def to_slots(values):
        return jnp.einsum(
            "ips,i...->ps...", send_map, values, preferred_element_type=jnp.float32
        ).astype(jnp.bfloat16)

    def keep_slots(values):
        return jnp.einsum("is,i...->s...", kept_map, values, preferred_element_type=jnp.float32)

    own_rows = (hidden_zero, segments.astype(jnp.bfloat16), out_cot, logit_cot[:, 1])
    outgoing = tuple((to_slots(item) for item in own_rows))
    received = jax.tree.map(
        lambda part, own: part.astype(own.dtype),
        lax.all_to_all(as_sent(outgoing), "narrow", split_axis=0, concat_axis=0, tiled=True),
        outgoing,
    )
    work_in, work_seg, work_cot, work_logit_cot = tuple(
        (
            (jnp.sum(item, 0, dtype=jnp.float32) + keep_slots(local)).astype(jnp.bfloat16)
            for item, local in zip(received, own_rows)
        )
    )
    work_seg = work_seg.astype(jnp.int32)
    hidden_one, saved_one = layer_forward(work_in, work_seg, layer_one)
    logits_one, back_one = student_forward(hidden_one, head_one)
    d_hidden_one, grads_head_one = student_backward(
        hidden_one, head_one, back_one, work_logit_cot.astype(jnp.float32), group_size
    )
    d_input_one, grads_one = layer_backward(
        saved_one, work_seg, layer_one, d_hidden_one + work_cot.astype(jnp.float32)
    )
    results = (hidden_one, logits_one.astype(jnp.bfloat16), d_input_one.astype(jnp.bfloat16))

    def spread(values):
        shaped = arrive_float.reshape(arrive_float.shape + (1,) * (values.ndim - 1))
        return shaped * values[None]

    returned = lax.all_to_all(
        as_sent(tuple((spread(item) for item in results))),
        "narrow",
        split_axis=0,
        concat_axis=0,
        tiled=True,
    )

    def from_slots(values, local):
        moved_back = jnp.einsum(
            "ips,ps...->i...", send_map, values, preferred_element_type=jnp.float32
        )
        stayed = jnp.einsum("is,s...->i...", kept_map, local, preferred_element_type=jnp.float32)
        return moved_back + stayed

    hidden_own = from_slots(returned[0], results[0]).astype(jnp.bfloat16)
    logits_own = from_slots(returned[1], results[1]).astype(jnp.bfloat16)
    d_input_own = from_slots(returned[2], results[2])
    alive_col = alive_float[:, None, None]
    activations = jnp.where(alive_col > 0, hidden_own, hidden_zero)
    logit_pair = jnp.stack([logits_zero.astype(jnp.bfloat16), logits_own], 1)
    layer_grads_one = grads_one + grads_head_one
    summed_one = reduce_layer(layer_grads_one)
    d_hidden_zero, grads_head_zero = student_backward(
        hidden_zero, head_zero, back_zero, logit_cot[:, 0].astype(jnp.float32), group_size
    )
    grad_zero = d_hidden_zero + out_cot.astype(jnp.float32) * (1.0 - alive_col) + d_input_own
    d_tokens, grads_zero = layer_backward(saved_zero, segments, layer_zero, grad_zero)
    layer_grads_zero = grads_zero + grads_head_zero
    summed_zero = reduce_layer(layer_grads_zero)
    totals = tuple(
        (
            jnp.stack([first_item, second_item])
            for first_item, second_item in zip(summed_zero, summed_one)
        )
    )
    bias_total = totals[16].reshape(2, totals[16].shape[-1])
    return (
        (activations, logit_pair, d_tokens.astype(jnp.bfloat16))
        + tuple(totals[:16])
        + (bias_total,)
    )


def solution(mesh):
    return jax.shard_map(
        shards,
        mesh=mesh,
        in_specs=(
            P(("wide", "narrow"), None, None),
            P(("wide", "narrow"), None),
            P(("wide", "narrow")),
            P(),
            P(),
            P(),
            P(),
            P(),
            P(),
            P(),
            P(),
            P(),
            P(),
            P(),
            P(),
            P(),
            P(),
            P(),
            P(),
            P(),
            P(("wide", "narrow"), None, None),
            P(("wide", "narrow"), None, None),
        ),
        out_specs=(
            P(("wide", "narrow"), None, None),
            P(("wide", "narrow"), None, None),
            P(("wide", "narrow"), None, None),
            P(None, "narrow", None),
            P(None, "narrow"),
            P(None, "narrow", None),
            P(None, "narrow"),
            P(None, "narrow"),
            P(None, "narrow"),
            P(None, "narrow", None),
            P(None, "narrow"),
            P(None, "narrow", None),
            P(None, "narrow"),
            P(None, "narrow", None),
            P(None, "narrow"),
            P(None, "narrow"),
            P(None, "narrow", None),
            P(None, "narrow"),
            P(None, "narrow", None),
            P(),
        ),
        check_vma=False,
    )
```

profile of v0, /device:TPU:0, one launch (start us, length us, event | category | flops | bytes accessed | tf_op | source)
XLA Modules:
  0.0 1345.9 jit_solution(16108194021904016656)
XLA Ops:
  10.1 9.9 all-reduce
  38.3 8.5 add_convert_fusion.1
  46.8 6.6 copy.223
  53.4 8.8 reshape.1287
  62.2 5.4 slice_bitcast_fusion
  69.7 21.0 %while.4 = (s32[]{:T(128)}, bf16[2,512,12,64]{1,3,2,0:T(8,128)(2,1)}, f32[2,12,512]{2,1,0:T(8,128)S(1)}, bf16[2,512,12,64]{1,3,2,0:T(8,128)(2,1)}, s32[2,512]{1,...) while((s32[]{:T(128)}, ...), condition=%wide.region_10.11_spmd, body=%wide.region_7.10_spmd.sunk | while | flops 843704320 | bytes 42172516 | solution.py:110
  74.8 5.5 fusion.343
  85.2 5.5 fusion.343
  99.4 36.9 %multiply_convert_fusion.4 = (bf16[1024,3072]{1,0:T(8,128)(2,1)S(1)}, f32[1024,3072]{1,0:T(8,128)}, f32[1024,3072]{1,0:T(8,128)}) fusion(f32[3072]{0:T(1024)S(1)} %bitcast.626, bf16[2,768,3072]{2,1,0:T(8,128)(2,1)} %param.35, f32[1024,768]{1,0:T(8,128)S(1)} %get-tuple-element.501, f32[768]{0:T(1024)S(1)} %get-tuple-element.537, ...), kind=kOutput, calls=%fused_computation.72 | convolution fusion | flops 5043388416 | bytes 39348224 | tf_op jit(solution)/shard_map/dot_general | solution.py:120
  136.5 5.4 fusion.263
  146.1 5.0 all-to-all-start.1
  180.5 48.7 %all-to-all-done = bf16[4,1,512,768]{3,2,1,0:T(8,128)(2,1)} async-done(((bf16[4,1,512,768]{3,2,1,0:T(8,128)(2,1)}), bf16[4,1,512,768]{3,2,1,0:T(8,128)(2,1)}, u32[]{:S(2)}, u32[]{:S(2)}) %all-to-all-start) | async-done | bytes 3145760 | tf_op jit(solution)/shard_map/all_to_all | solution.py:343
  229.2 4.9 all-to-all-start.5
  237.8 5.4 fusion.87
  257.8 21.3 %multiply_convert_fusion.5 = (bf16[512,3072]{1,0:T(8,128)(2,1)S(1)}, f32[512,3072]{1,0:T(8,128)}, f32[512,3072]{1,0:T(8,128)}) fusion(f32[3072]{0:T(1024)S(1)} %bitcast.628, bf16[2,768,3072]{2,1,0:T(8,128)(2,1)} %param.35, f32[512,768]{1,0:T(8,128)S(1)} %get-tuple-element.508, f32[768]{0:T(1024)S(1)} %get-tuple-element.330, ...), kind=kOutput, calls=%fused_computation.95 | convolution fusion | flops 2521694208 | bytes 22042624 | tf_op jit(solution)/shard_map/dot_general | solution.py:120
  287.3 17.0 %all-to-all-done.5 = bf16[4,1,512,768]{3,2,1,0:T(8,128)(2,1)} async-done(((bf16[4,1,512,768]{3,2,1,0:T(8,128)(2,1)}), bf16[4,1,512,768]{3,2,1,0:T(8,128)(2,1)}, u32[]{:S(2)}, u32[]{:S(2)}) %all-to-all-start.5) | async-done | bytes 3145760 | tf_op jit(solution)/shard_map/all_to_all | solution.py:343
  309.9 8.5 fusion.270
  328.7 7.8 fusion.126
  336.5 9.8 multiply_reduce_fusion.1
  346.3 7.0 multiply_convert_fusion.3
  364.5 4.8 all-to-all-start.6
  397.2 5.5 convolution_convert_fusion.4
  402.8 37.6 %all-to-all-done.6 = bf16[4,1,512,768]{3,2,1,0:T(8,128)(2,1)} async-done(((bf16[4,1,512,768]{3,2,1,0:T(8,128)(2,1)}), bf16[4,1,512,768]{3,2,1,0:T(8,128)(2,1)}, u32[]{:S(2)}, u32[]{:S(2)}) %all-to-all-start.6) | async-done | bytes 3145760 | tf_op jit(solution)/shard_map/all_to_all | solution.py:367
  440.4 9.4 fusion.269
  457.0 19.1 %fusion.271 = (bf16[3072]{0:T(1024)(128)(2,1)}, bf16[1024,3072]{1,0:T(8,128)(2,1)}) fusion(f32[1024,3072]{1,0:T(8,128)} %get-tuple-element.458, bf16[1024,768]{1,0:T(8,128)(2,1)} %get-tuple-element.430, bf16[2,3072,768]{2,1,0:T(8,128)(2,1)} %param.37, f32[1024,3072]{1,0:T(8,128)} %get-tuple-element.502, f32[3072]{0:T(1024)S(1)} %bitcast.627), kind=kOutput, calls=%fused_computation.503 | convolution fusion | flops 4882166784 | bytes 37767168 | tf_op jit(solution)/shard_map/td,fd->tf/dot_general | solution.py:161
  476.1 10.8 multiply_reduce_fusion.2
  502.2 54.4 %while.5 = (s32[]{:T(128)}, bf16[2,512,3,12,64]{1,4,3,2,0:T(8,128)(2,1)}, bf16[2,512,12,64]{1,3,2,0:T(8,128)(2,1)S(1)}, s32[2,512]{1,0:T(2,128)S(1)}, bf16[2,512...) while((s32[]{:T(128)}, ...), condition=%wide.region_48.49_spmd, body=%wide.region_46.48_spmd.sunk | while | flops 2069751808 | bytes 156958992 | solution.py:180
  508.6 6.8 multiply_reduce_fusion.22
  515.5 7.0 multiply_convert_fusion.9
  535.5 6.8 multiply_reduce_fusion.22
  542.4 7.1 multiply_convert_fusion.9
  556.6 9.5 copy.258
  587.7 6.4 convolution_convert_fusion.3
  595.2 6.7 convolution_convert_fusion.2
  604.4 9.8 convolution_convert_fusion.1
  615.6 9.7 convolution_convert_fusion
  626.3 8.4 all_to_all.35
  634.8 4.8 all-to-all-start.2
  650.0 109.1 %all-reduce.23 = (bf16[1536]{0:T(1024)(128)(2,1)S(1)}, bf16[1536]{0:T(1024)(128)(2,1)S(1)}, bf16[768]{0:T(1024)(128)(2,1)S(1)}, bf16[768]{0:T(1024)(128)(2,1)S(1...) all-reduce(bf16[1536]{0:T(1024)(128)(2,1)S(1)} %pad_maximum_fusion., ...), channel_id=5, replica_groups=mesh['wide'=8,'narrow'=4] {'narrow'}, use_global_device_ids=true, to_apply=%region_57.58.clone | all-reduce | flops 19312 | bytes 77248
  778.1 83.2 %reduce-scatter.29.cloned.1.call-done = bf16[192,3072]{1,0:T(8,128)(2,1)} async-done(((bf16[768,3072]{1,0:T(8,128)(2,1)}), bf16[192,3072]{1,0:T(8,128)(2,1)}) %reduce-scatter.29.cloned.1.call-update) | async-done | bytes 1179664 | tf_op jit(solution)/shard_map/reduce_scatter | solution.py:236
  861.3 88.0 %reduce-scatter.33.cloned.1.call-done = bf16[768,768]{1,0:T(8,128)(2,1)} async-done(((bf16[3072,768]{1,0:T(8,128)(2,1)}), bf16[768,768]{1,0:T(8,128)(2,1)}) %reduce-scatter.33.cloned.1.call-update) | async-done | bytes 1179664 | tf_op jit(solution)/shard_map/reduce_scatter | solution.py:236
  949.2 88.1 %reduce-scatter.27.cloned.1.call-done = bf16[192,3072]{1,0:T(8,128)(2,1)} async-done(((bf16[768,3072]{1,0:T(8,128)(2,1)}), bf16[192,3072]{1,0:T(8,128)(2,1)}) %reduce-scatter.27.cloned.1.call-update) | async-done | bytes 1179664 | tf_op jit(solution)/shard_map/reduce_scatter | solution.py:236
  1037.4 88.0 %reduce-scatter.31.cloned.1.call-done = bf16[768,768]{1,0:T(8,128)(2,1)} async-done(((bf16[3072,768]{1,0:T(8,128)(2,1)}), bf16[768,768]{1,0:T(8,128)(2,1)}) %reduce-scatter.31.cloned.1.call-update) | async-done | bytes 1179664 | tf_op jit(solution)/shard_map/reduce_scatter | solution.py:236
  1127.2 5.8 broadcast_select_fusion
  1135.5 8.7 add_convert_fusion.3
  1144.2 52.2 %all-reduce.27.cloned.1.call-done = (bf16[1,384]{1,0:T(2,128)(2,1)}, bf16[1,384]{1,0:T(2,128)(2,1)}, bf16[1,192]{1,0:T(2,128)(2,1)}, bf16[1,192]{1,0:T(2,128)(2,...) async-done(((bf16[1,384]{1,0:T(2,128)(2,1)}, ...) | async-done | bytes 126152 | tf_op jit(solution)/shard_map/psum | solution.py:238
  1213.0 109.6 %all-reduce.29.cloned.1.call-done = (bf16[1,192,2304]{1,2,0:T(8,128)(2,1)}, bf16[1,192,2304]{1,2,0:T(8,128)(2,1)}, bf16[1,192,768]{2,1,0:T(8,128)(2,1)}, bf16[1,...) async-done(((bf16[1,192,2304]{1,2,0:T(8,128)(2,1)}, ...) | async-done | bytes 7077904 | tf_op jit(solution)/shard_map/psum | solution.py:238
  1327.0 5.8 copy.265
  (770 shorter events, 288.1 us)
Async XLA Ops:
  26.7 119.4 %all-to-all-start.4 = ((bf16[4,1,14]{2,1,0:T(2,128)(2,1)}), bf16[4,1,14]{2,1,0:T(2,128)(2,1)}, u32[]{:S(2)}, u32[]{:S(2)}) async-start(bf16[4,1,14]{2,1,0:T(2,128)(2,1)} %copy.244), calls=%async_computation.4 | async-start | bytes 4096 | tf_op jit(solution)/shard_map/all_to_all | solution.py:343
  34.0 65.4 %copy-start.102 = (f32[1,3072]{1,0:T(1,128)}, f32[1,3072]{1,0:T(1,128)S(1)}, u32[]{:S(2)}) copy-start(f32[1,3072]{1,0:T(1,128)S(1)} %get-tuple-element.473) | copy-start | bytes 36868
  95.5 41.0 %slice-start.5 = ((s8[9437184]{0:T(1024)(128)(4,1)}), s8[4194304]{0:T(1024)(128)(4,1)S(1)}, s32[]{:S(2)}) async-start(s8[9437184]{0:T(1024)(128)(4,1)} %bitcast.635), calls=%async_computation.42 | async-start | bytes 8388608
  97.2 39.2 %copy-start.16 = (f32[1024,768]{1,0:T(8,128)}, f32[1024,768]{1,0:T(8,128)S(1)}, u32[]{:S(2)}) copy-start(f32[1024,768]{1,0:T(8,128)S(1)} %get-tuple-element.501) | copy-start | bytes 9437188
  97.2 39.2 %copy-start.75 = (f32[1024]{0:T(1024)}, f32[1024]{0:T(1024)S(1)}, u32[]{:S(2)}) copy-start(f32[1024]{0:T(1024)S(1)} %broadcast_multiply_fusion.3) | copy-start | bytes 12292
  97.8 38.6 %copy-start.78 = (f32[1024]{0:T(1024)}, f32[1024]{0:T(1024)S(1)}, u32[]{:S(2)}) copy-start(f32[1024]{0:T(1024)S(1)} %multiply_reduce_fusion.6) | copy-start | bytes 12292
  97.8 38.6 %copy-start.91 = (f32[1024]{0:T(1024)}, f32[1024]{0:T(1024)S(1)}, u32[]{:S(2)}) copy-start(f32[1024]{0:T(1024)S(1)} %fusion.198) | copy-start | bytes 12292
  98.8 37.6 %copy-start.130 = (f32[768]{0:T(1024)}, f32[768]{0:T(1024)S(1)}, u32[]{:S(2)}) copy-start(f32[768]{0:T(1024)S(1)} %get-tuple-element.537) | copy-start | bytes 9220
  98.8 180.3 %copy-start.132 = (f32[768]{0:T(1024)}, f32[768]{0:T(1024)S(1)}, u32[]{:S(2)}) copy-start(f32[768]{0:T(1024)S(1)} %get-tuple-element.330) | copy-start | bytes 9220
  99.4 37.0 %copy-start.87 = (f32[768]{0:T(1024)}, f32[768]{0:T(1024)S(1)}, u32[]{:S(2)}) copy-start(f32[768]{0:T(1024)S(1)} %get-tuple-element.336) | copy-start | bytes 9220
  99.4 43.1 %copy-start.70 = (f32[768]{0:T(1024)}, f32[768]{0:T(1024)S(1)}, u32[]{:S(2)}) copy-start(f32[768]{0:T(1024)S(1)} %get-tuple-element.335) | copy-start | bytes 9220
  99.4 37.0 %slice-start.6 = ((s8[9437184]{0:T(1024)(128)(4,1)}), s8[4194304]{0:T(1024)(128)(4,1)S(1)}, s32[]{:S(2)}) async-start(s8[9437184]{0:T(1024)(128)(4,1)} %bitcast.635), calls=%async_computation.43 | async-start | bytes 8388608
  99.4 37.0 %slice-start.7 = ((s8[9437184]{0:T(1024)(128)(4,1)}), s8[1048576]{0:T(1024)(128)(4,1)S(1)}, s32[]{:S(2)}) async-start(s8[9437184]{0:T(1024)(128)(4,1)} %bitcast.635), calls=%async_computation.44 | async-start | bytes 2097152
  144.2 28.9 %copy-start.13 = (bf16[1024,768]{1,0:T(8,128)(2,1)}, bf16[1024,768]{1,0:T(8,128)(2,1)S(1)}, u32[]{:S(2)}) copy-start(bf16[1024,768]{1,0:T(8,128)(2,1)S(1)} %add_convert_fusion.5) | copy-start | bytes 4718596
  146.1 10.6 all-to-all-start.1
  156.7 72.5 %all-to-all-start = ((bf16[4,1,512,768]{3,2,1,0:T(8,128)(2,1)}), bf16[4,1,512,768]{3,2,1,0:T(8,128)(2,1)}, u32[]{:S(2)}, u32[]{:S(2)}) async-start(bf16[4,1,512,768]{3,2,1,0:T(8,128)(2,1)} %copy.229), calls=%async_computation | async-start | bytes 6291456 | tf_op jit(solution)/shard_map/all_to_all | solution.py:343
  168.1 118.5 %copy-start.108 = (f32[2,64]{1,0:T(2,128)}, f32[2,64]{1,0:T(2,128)S(1)}, u32[]{:S(2)}) copy-start(f32[2,64]{1,0:T(2,128)S(1)} %reshape.1319) | copy-start | bytes 1540
  171.7 150.3 %copy-start.99 = (f32[768]{0:T(1024)}, f32[768]{0:T(1024)S(1)}, u32[]{:S(2)}) copy-start(f32[768]{0:T(1024)S(1)} %get-tuple-element.328) | copy-start | bytes 9220
  172.4 112.5 %copy-start.126 = (bf16[1,128,14]{1,0,2:T(2,128)(2,1)}, bf16[1,128,14]{1,0,2:T(2,128)(2,1)S(1)}, u32[]{:S(2)}) copy-start(bf16[1,128,14]{1,0,2:T(2,128)(2,1)S(1)} %get-tuple-element.477) | copy-start | bytes 10756
  180.2 104.7 %copy-start.183 = (bf16[14]{0:T(256)(128)(2,1)}, bf16[14]{0:T(256)(128)(2,1)S(1)}, u32[]{:S(2)}) copy-start(bf16[14]{0:T(256)(128)(2,1)S(1)} %get-tuple-element.536) | copy-start | bytes 88
  229.2 75.1 %all-to-all-start.5 = ((bf16[4,1,512,768]{3,2,1,0:T(8,128)(2,1)}), bf16[4,1,512,768]{3,2,1,0:T(8,128)(2,1)}, u32[]{:S(2)}, u32[]{:S(2)}) async-start(bf16[4,1,512,768]{3,2,1,0:T(8,128)(2,1)} %copy.246), calls=%async_computation.5 | async-start | bytes 6291456 | tf_op jit(solution)/shard_map/all_to_all | solution.py:343
  257.4 64.7 %copy-start.85 = (f32[512]{0:T(512)}, f32[512]{0:T(512)S(1)}, u32[]{:S(2)}) copy-start(f32[512]{0:T(512)S(1)} %broadcast_multiply_fusion.6) | copy-start | bytes 6148
  257.7 64.4 %copy-start.117 = (f32[512]{0:T(512)}, f32[512]{0:T(512)S(1)}, u32[]{:S(2)}) copy-start(f32[512]{0:T(512)S(1)} %fusion.212) | copy-start | bytes 6148
  364.5 25.2 %copy-start.14 = (bf16[1024,768]{1,0:T(8,128)(2,1)S(1)}, bf16[1024,768]{1,0:T(8,128)(2,1)}, u32[]{:S(2)}) copy-start(bf16[1024,768]{1,0:T(8,128)(2,1)} %copy-done.13) | copy-start | bytes 4718596
  364.5 75.8 %all-to-all-start.6 = ((bf16[4,1,512,768]{3,2,1,0:T(8,128)(2,1)}), bf16[4,1,512,768]{3,2,1,0:T(8,128)(2,1)}, u32[]{:S(2)}, u32[]{:S(2)}) async-start(bf16[4,1,512,768]{3,2,1,0:T(8,128)(2,1)} %get-tuple-element.494), calls=%async_computation.6 | async-start | bytes 6291456 | tf_op jit(solution)/shard_map/all_to_all | solution.py:367
  369.4 273.9 %reduce-scatter.47.cloned.1.call-start = ((), (), s32[]{:S(2)}) async-start(), calls=%async_computation.33 | async-start | bytes 40960
  370.2 24.3 %copy-start.54 = (f32[2,512,2]{1,2,0:T(2,128)}, f32[2,512,2]{1,2,0:T(2,128)S(1)}, u32[]{:S(2)}) copy-start(f32[2,512,2]{1,2,0:T(2,128)S(1)} %broadcast_divide_fusion) | copy-start | bytes 24580
  375.3 269.9 %reduce-scatter.49.cloned.1.call-start = ((), (), s32[]{:S(2)}) async-start(), calls=%async_computation.34 | async-start | bytes 40960
  380.1 392.9 %reduce-scatter.39.cloned.1.call-start = ((), (), s32[]{:S(2)}) async-start(), calls=%async_computation.29 | async-start | bytes 40960 | tf_op jit(solution)/shard_map/reduce_scatter | solution.py:236
  381.7 391.2 %reduce-scatter.35.cloned.1.call-start = ((), (), s32[]{:S(2)}) async-start(), calls=%async_computation.27 | async-start | bytes 245760 | tf_op jit(solution)/shard_map/reduce_scatter | solution.py:236
  391.1 381.8 %reduce-scatter.41.cloned.1.call-start = ((), (), s32[]{:S(2)}) async-start(), calls=%async_computation.30 | async-start | bytes 40960 | tf_op jit(solution)/shard_map/reduce_scatter | solution.py:236
  396.0 377.0 %reduce-scatter.37.cloned.1.call-start = ((), (), s32[]{:S(2)}) async-start(), calls=%async_computation.28 | async-start | bytes 245760 | tf_op jit(solution)/shard_map/reduce_scatter | solution.py:236
  397.2 376.3 %reduce-scatter.45.cloned.1.call-start = ((), (), s32[]{:S(2)}) async-start(), calls=%async_computation.32 | async-start | bytes 4423680
  402.8 37.6 %copy-start.28 = (f32[2,512,768]{2,1,0:T(8,128)S(1)}, f32[2,512,768]{2,1,0:T(8,128)}, u32[]{:S(2)}) copy-start(f32[2,512,768]{2,1,0:T(8,128)} %fusion.176) | copy-start | bytes 9437188
  402.8 37.6 %copy-start.165 = (f32[2]{0:T(128)S(1)}, f32[2]{0:T(128)}, u32[]{:S(2)}) copy-start(f32[2]{0:T(128)} %get-tuple-element.449) | copy-start | bytes 28
  402.8 37.6 %copy-start.181 = (pred[1,2,4,1]{2,1,3,0:T(4,128)(4,1)S(1)}, pred[1,2,4,1]{2,1,3,0:T(4,128)(4,1)}, u32[]{:S(2)}) copy-start(pred[1,2,4,1]{2,1,3,0:T(4,128)(4,1)} %copy-done.179) | copy-start | bytes 28
  402.8 373.0 %reduce-scatter.43.cloned.1.call-start = ((), (), s32[]{:S(2)}) async-start(), calls=%async_computation.31 | async-start | bytes 4423680
  580.3 197.7 %reduce-scatter.25.cloned.1.call-start = ((), (), s32[]{:S(2)}) async-start(), calls=%async_computation.22 | async-start | bytes 1474560 | tf_op jit(solution)/shard_map/reduce_scatter | solution.py:236
  583.5 194.6 %reduce-scatter.23.cloned.1.call-start = ((), (), s32[]{:S(2)}) async-start(), calls=%async_computation.21 | async-start | bytes 1474560 | tf_op jit(solution)/shard_map/reduce_scatter | solution.py:236
  587.6 273.7 %reduce-scatter.29.cloned.1.call-start = ((), (), s32[]{:S(2)}) async-start(), calls=%async_computation.24 | async-start | bytes 5898240 | tf_op jit(solution)/shard_map/reduce_scatter | solution.py:236
  594.1 355.1 %reduce-scatter.33.cloned.1.call-start = ((), (), s32[]{:S(2)}) async-start(), calls=%async_computation.26 | async-start | bytes 5898240 | tf_op jit(solution)/shard_map/reduce_scatter | solution.py:236
  602.0 435.4 %reduce-scatter.27.cloned.1.call-start = ((), (), s32[]{:S(2)}) async-start(), calls=%async_computation.23 | async-start | bytes 5898240 | tf_op jit(solution)/shard_map/reduce_scatter | solution.py:236
  614.3 511.1 %reduce-scatter.31.cloned.1.call-start = ((), (), s32[]{:S(2)}) async-start(), calls=%async_computation.25 | async-start | bytes 5898240 | tf_op jit(solution)/shard_map/reduce_scatter | solution.py:236
  634.8 491.1 %all-to-all-start.2 = ((bf16[4,1,512,768]{3,2,1,0:T(8,128)(2,1)}), bf16[4,1,512,768]{3,2,1,0:T(8,128)(2,1)}, u32[]{:S(2)}, u32[]{:S(2)}) async-start(bf16[4,1,512,768]{3,2,1,0:T(8,128)(2,1)} %get-tuple-element.495), calls=%async_computation.2 | async-start | bytes 6291456 | tf_op jit(solution)/shard_map/all_to_all | solution.py:367
  639.8 133.5 %copy-start.166 = (f32[2]{0:T(128)S(1)}, f32[2]{0:T(128)}, u32[]{:S(2)}) copy-start(f32[2]{0:T(128)} %get-tuple-element.449) | copy-start | bytes 28
  639.9 133.5 %copy-start.182 = (pred[1,2,4,1]{2,1,3,0:T(4,128)(4,1)S(1)}, pred[1,2,4,1]{2,1,3,0:T(4,128)(4,1)}, u32[]{:S(2)}) copy-start(pred[1,2,4,1]{2,1,3,0:T(4,128)(4,1)} %copy-done.179) | copy-start | bytes 28
  639.9 556.6 %all-reduce.27.cloned.1.call-start = ((), (), s32[]{:S(2)}) async-start(), calls=%async_computation.35 | async-start | bytes 292864 | tf_op jit(solution)/shard_map/psum | solution.py:238
  773.0 549.6 %all-reduce.29.cloned.1.call-start = ((), (), s32[]{:S(2)}) async-start(), calls=%async_computation.36 | async-start | bytes 15335424 | tf_op jit(solution)/shard_map/psum | solution.py:238
  (186 other events, 1103.7 us)
Sparse Core Ops, SparseCore 0:
  375.5 21.6 reduce-scatter.46
  399.5 47.6 reduce-scatter.48
  449.5 17.2 reduce-scatter.38
  469.0 17.4 reduce-scatter.34
  489.2 17.0 reduce-scatter.40
  509.1 17.4 reduce-scatter.36
  529.5 64.5 reduce-scatter.44
  596.5 92.7 reduce-scatter.42
  692.1 49.5 reduce-scatter.24
  743.9 31.0 reduce-scatter.22
  777.3 83.9 reduce-scatter.28
  863.4 85.7 reduce-scatter.32
  951.5 85.7 reduce-scatter.26
  1039.5 85.7 reduce-scatter.30
  1133.2 63.1 all-reduce.26
  1201.0 121.5 all-reduce.28
where the time goes:
time: 1350 us
  waiting for transfers between devices  613 us (45%)
  matrix products  308 us (23%)
  local copies, waits for them, and re-layouts  138 us (10%)
  blocking collectives  127 us (9%)
  other arithmetic  109 us (8%)
  starting transfers between devices  29.5 us (2%)
  between operations  20.2 us (1%)
    reduce_scatter x10, waiting for transfers between devices, reduce_layer(): lax.psum_scatter(as_sent(gradients), 'narrow', scatter_dimension=0, tiled...  347 us
    psum x2, waiting for transfers between devices, reduce_layer(): lax.psum(as_sent(shares), 'wide')  162 us
    unnamed x2, blocking collectives  119 us
    all_to_all x4, waiting for transfers between devices, shards(): lax.all_to_all(as_sent(outgoing), 'narrow', split_axis=0, concat_axis=0,...  66.6 us
    dot_general x2, matrix products, layer_forward(): jnp.dot(first_norm.astype(jnp.bfloat16), ff_in, preferred_element_type=jn...  58.2 us
    unnamed x430, local copies, waits for them, and re-layouts  56.8 us
    all_to_all x2, waiting for transfers between devices, shards(): lax.all_to_all(as_sent(tuple((spread(item) for item in results))), 'narro...  37.6 us
    dot_general x2, matrix products, layer_backward(): jnp.einsum('td,fd->tf', d_second, ff_out, preferred_element_type=jnp.floa...  27.6 us
  transfers between devices with their start and end apart: 22, of which 10 were waited for; matrix products, arithmetic and copies ran while one was open for 33% of the time, Pallas kernels for 0%

commit v1 on v0

v1 whole, which is shorter than its diff:
```python
from functools import partial

import jax
import jax.numpy as jnp
import numpy as np
from jax import lax
from jax.experimental import pallas as pl
from jax.experimental.pallas import tpu as pltpu
from jax.sharding import PartitionSpec as P

HEADS = 12
HEAD = 64
STU_HEADS = 2
LANES = 128
CHUNK = 128
REACH = 256
EPS = 1e-12
MASKED = -1e30
HIGH = lax.Precision.HIGHEST
F32 = jnp.float32
BF16 = jnp.bfloat16
LIMIT = 52 * 1024 * 1024

NN = (((1,), (0,)), ((), ()))
NT = (((1,), (1,)), ((), ()))
TN = (((0,), (0,)), ((), ()))


def mm(left, right, dims=NN):
    return lax.dot_general(left, right, dims, preferred_element_type=F32)


def mm_high(left, right, dims=NN):
    return lax.dot_general(left, right, dims, precision=HIGH, preferred_element_type=F32)


def vec(ref, layer, start, size):
    return ref[...].astype(F32)[layer : layer + 1, start : start + size]


def gelu_pair(value):
    dist = jnp.abs(value) * (0.5**0.5)
    den = 1.0 + 0.3275911 * dist
    part = pl.reciprocal(den, approx=True)
    part = part * (2.0 - den * part)
    series = 0.5 * 1.061405429
    for term in (-1.453152027, 1.421413741, -0.284496736, 0.254829592):
        series = series * part + 0.5 * term
    bell = jnp.exp(-(dist * dist))
    tail = series * part * bell
    below = jnp.where(value >= 0, 1.0 - tail, tail)
    return value * below, below + value * bell * ((2.0 * np.pi) ** -0.5)


def row_norm(value):
    mean = jnp.mean(value, -1, keepdims=True)
    centered = value - mean
    spread = lax.rsqrt(jnp.mean(centered * centered, -1, keepdims=True) + EPS)
    return centered * spread, spread


def norm_back(grad, hat, spread, gain):
    scaled = grad * gain
    low = jnp.mean(scaled, -1, keepdims=True)
    high = jnp.mean(scaled * hat, -1, keepdims=True)
    return spread * (scaled - low - hat * high)


def window(place, length):
    start = max(0, (place - REACH + 1) // CHUNK * CHUNK)
    stop = min(length, -(-(place + CHUNK + REACH - 1) // CHUNK) * CHUNK)
    return start, stop


def fill_bias(seg_ref, row, bias_ref):
    length = bias_ref.shape[0]
    seg_row = seg_ref[pl.ds(row, 1), :].astype(F32)
    seg_cols = jnp.broadcast_to(seg_row, (LANES, length)).T
    for start in range(0, length, LANES):
        same = seg_cols == seg_row[:, start : start + LANES]
        bias_ref[:, start : start + LANES] = jnp.where(same, 0.0, MASKED)


ANY = pl.BlockSpec(memory_space=pl.ANY)
WHOLE = pl.BlockSpec(memory_space=pltpu.VMEM)
SCALAR = pl.BlockSpec(memory_space=pltpu.SMEM)


def low(*shape):
    return jax.ShapeDtypeStruct(shape, BF16)


def full(*shape):
    return jax.ShapeDtypeStruct(shape, F32)


def vm(like):
    return pltpu.VMEM(like.shape, like.dtype)


def call(kernel, name, outs, out_specs, inputs, in_specs, scratch, after, flops, moved):
    count, extra = len(inputs), len(after)

    def body(*refs):
        kernel(*refs[:count], *refs[count + extra :])

    return pl.pallas_call(
        body,
        out_shape=outs,
        in_specs=list(in_specs) + [ANY] * extra,
        out_specs=out_specs,
        scratch_shapes=scratch,
        compiler_params=pltpu.CompilerParams(vmem_limit_bytes=LIMIT),
        cost_estimate=pl.CostEstimate(flops=flops, bytes_accessed=moved, transcendentals=0),
        name=name,
    )(*inputs, *after)


def copier(sems):
    def copy(src, dst, number):
        made = pltpu.make_async_copy(src, dst, sems.at[number])
        made.start()
        return made

    return copy


def chunks(length):
    return [slice(place, place + CHUNK) for place in range(0, length, CHUNK)]


def forward_attention_kernel(
    layer,
    scale,
    row_ref,
    x_hbm,
    seg_ref,
    w_in_hbm,
    w_out_hbm,
    qv_ref,
    out_b_ref,
    gain_ref,
    shift_ref,
    qkv_hbm,
    lse_ref,
    mixed_hbm,
    hat_hbm,
    first_hbm,
    full_hbm,
    spread_ref,
    x_ref,
    w_in,
    w_out,
    qkv,
    mixed,
    hat,
    first,
    full,
    bias,
    terms_ref,
    sems,
):
    row = row_ref[0]
    length, width = x_ref.shape
    copy = copier(sems)
    get_x = copy(x_hbm.at[row], x_ref, 0)
    get_in = copy(w_in_hbm.at[layer], w_in, 1)
    get_out = copy(w_out_hbm.at[layer], w_out, 2)
    fill_bias(seg_ref, row, bias)
    terms_ref[...] = jnp.zeros_like(terms_ref)
    lse_ref[...] = jnp.zeros_like(lse_ref)
    get_x.wait()
    get_in.wait()

    x = x_ref[...]
    qkv[:, :width] = (
        (mm(x, w_in[:, :width]) + vec(qv_ref, layer, 0, width)).astype(BF16).astype(F32) * scale
    ).astype(BF16)
    qkv[:, width : 2 * width] = mm(x, w_in[:, width : 2 * width]).astype(BF16)
    qkv[:, 2 * width :] = (
        mm(x, w_in[:, 2 * width :]) + vec(qv_ref, layer, width, width)
    ).astype(BF16)
    put_qkv = copy(qkv, qkv_hbm, 3)

    low_half = lax.broadcasted_iota(jnp.int32, (length, LANES), 1) < HEAD
    low_rows = lax.broadcasted_iota(jnp.int32, (LANES, length), 0) < HEAD

    def pair(number, carry):
        at = pl.multiple_of(number * LANES, LANES)
        queries = qkv[:, pl.ds(at, LANES)]
        keys = qkv[:, pl.ds(at + width, LANES)]
        values_t = qkv[:, pl.ds(at + 2 * width, LANES)].T
        outs = []
        for sub in range(2):
            mine = jnp.where(low_half == (sub == 0), keys, jnp.zeros_like(keys))
            scores = mm(mine, queries, NT)
            tops = []
            for cols in chunks(length):
                start, stop = window(cols.start, length)
                part = scores[start:stop, cols] + bias[start:stop, cols]
                top = jnp.max(part, 0, keepdims=True)
                terms_ref[sub, start:stop, cols] = jnp.exp(part - top).astype(BF16)
                tops.append(top)
            mine_t = jnp.where(low_rows == (sub == 0), values_t, jnp.ones_like(values_t))
            product = mm(mine_t, terms_ref[sub])
            beside = HEAD * (1 - sub)
            total = product[beside : beside + 1, :]
            lse_ref[pl.ds(2 * number + sub, 1), :] = jnp.concatenate(tops, 1) + jnp.log(total)
            outs.append(product * (1.0 / total))
        mixed[:, pl.ds(at, LANES)] = jnp.where(low_rows, outs[0], outs[1]).T.astype(BF16)
        return carry

    lax.fori_loop(0, HEADS * HEAD // LANES, pair, 0)
    put_mixed = copy(mixed, mixed_hbm, 4)

    get_out.wait()
    gain, shift = vec(gain_ref, layer, 0, width), vec(shift_ref, layer, 0, width)
    out_b = vec(out_b_ref, layer, 0, width)
    branch = mm(mixed[...], w_out[...])
    for rows in chunks(length):
        normed, spread = row_norm(x_ref[rows, :].astype(F32) + branch[rows] + out_b)
        hat[rows, :] = normed.astype(BF16)
        normed = normed * gain + shift
        full[rows, :] = normed
        first[rows, :] = normed.astype(BF16)
        spread_ref[rows, :] = jnp.broadcast_to(spread, (CHUNK, LANES))
    puts = (copy(hat, hat_hbm, 5), copy(first, first_hbm, 6), copy(full, full_hbm, 7))
    for made in (put_qkv, put_mixed) + puts:
        made.wait()


def forward_attention(layer, row, x, seg, weights, after=()):
    w_in, qv, w_out, out_b, gain, shift = weights[:6]
    length, width = x.shape[-2], x.shape[-1]
    outs = (
        low(length, 3 * width),
        full(16, length),
        low(length, width),
        low(length, width),
        low(length, width),
        full(length, width),
        full(length, LANES),
    )
    return call(
        partial(forward_attention_kernel, layer, HEAD**-0.5),
        f"forward_attention{layer}",
        outs,
        (ANY, WHOLE) + (ANY,) * 4 + (WHOLE,),
        (row, x, seg, w_in, w_out, qv, out_b, gain, shift),
        [SCALAR, ANY, WHOLE, ANY, ANY] + [WHOLE] * 4,
        [
            pltpu.VMEM((length, width), BF16),
            pltpu.VMEM(w_in.shape[1:], BF16),
            pltpu.VMEM(w_out.shape[1:], BF16),
            vm(outs[0]),
            vm(outs[2]),
            vm(outs[3]),
            vm(outs[4]),
            vm(outs[5]),
            pltpu.VMEM((length, length), F32),
            pltpu.VMEM((2, length, length), BF16),
            pltpu.SemaphoreType.DMA((8,)),
        ],
        after,
        14 * 10**9,
        16 * 10**6,
    )


def forward_ff_kernel(
    layer,
    row_ref,
    first_hbm,
    full_hbm,
    cot_ref,
    w_fi_hbm,
    w_fo_hbm,
    gain_ref,
    shift_ref,
    fi_b_ref,
    fo_b_ref,
    proj_ref,
    proj_b_ref,
    query_ref,
    dense_ref,
    dense_b_ref,
    cls_ref,
    cls_b_ref,
    slope_hbm,
    active_hbm,
    hat_hbm,
    h_hbm,
    spread_ref,
    d_upper_ref,
    logit_ref,
    small_ref,
    first,
    full,
    w_fi,
    w_fo,
    slope,
    active,
    hat,
    h,
    even,
    odd,
    sems,
):
    length, width = first.shape
    ff = w_fi.shape[1]
    copy = copier(sems)
    get_first = copy(first_hbm, first, 0)
    get_fi = copy(w_fi_hbm.at[layer], w_fi, 1)
    get_full = copy(full_hbm, full, 2)
    get_fo = copy(w_fo_hbm.at[layer], w_fo, 3)
    get_first.wait()
    get_fi.wait()
    part = even.shape[1]

    def multiply(at, into):
        into[...] = mm(first[...], w_fi[:, pl.ds(at, part)])

    def bend(at, source):
        bias_part = fi_b_ref[:, pl.ds(at, part)].astype(F32)[layer : layer + 1]
        for rows in chunks(length):
            out, grad = gelu_pair(source[rows, :] + bias_part)
            active[rows, pl.ds(at, part)] = out.astype(BF16)
            slope[rows, pl.ds(at, part)] = grad.astype(BF16)

    multiply(0, even)
    steps = ff // part // 2

    def inner(number, carry):
        at = pl.multiple_of(number * (2 * part), 2 * part)
        multiply(at + part, odd)
        bend(at, even)
        later = pl.multiple_of(jnp.minimum(at + 2 * part, ff - part), part)
        multiply(later, even)
        bend(at + part, odd)
        return carry

    lax.fori_loop(0, steps, inner, 0)
    put_slope = copy(slope, slope_hbm, 4)
    put_active = copy(active, active_hbm, 5)

    get_fo.wait()
    get_full.wait()
    gain, shift = vec(gain_ref, layer, width, width), vec(shift_ref, layer, width, width)
    fo_b = vec(fo_b_ref, layer, 0, width)
    second = mm(active[...], w_fo[...])
    for rows in chunks(length):
        normed, spread = row_norm(full[rows, :] + second[rows] + fo_b)
        hat[rows, :] = normed.astype(BF16)
        h[rows, :] = (normed * gain + shift).astype(BF16)
        spread_ref[rows, :] = jnp.broadcast_to(spread, (CHUNK, LANES))
    put_hat = copy(hat, hat_hbm, 6)
    put_h = copy(h, h_hbm, 7)

    stu_width = proj_ref.shape[2]
    stu_scale = (stu_width // STU_HEADS) ** -0.5
    hidden = h[...]
    upper = mm(hidden, proj_ref[layer]) + vec(proj_b_ref, layer, 0, stu_width)
    query = vec(query_ref, layer, 0, stu_width)
    lane_full = lax.broadcasted_iota(jnp.int32, (length, stu_width), 1)
    left = lane_full < stu_width // STU_HEADS

    def both(value):
        zero = jnp.zeros_like(value)
        return (
            jnp.sum(jnp.where(left, value, zero), -1, keepdims=True),
            jnp.sum(jnp.where(left, zero, value), -1, keepdims=True),
        )

    weights = []
    for score in both(upper * query):
        score = score * stu_scale
        terms = jnp.exp(score - jnp.max(score, 0, keepdims=True))
        weights.append(terms / jnp.sum(terms, 0, keepdims=True))
    weight = jnp.where(left, weights[0], weights[1])
    pooled = jnp.sum(weight * upper, 0, keepdims=True)
    dense = dense_ref[layer].astype(F32)
    cls = cls_ref[layer].astype(F32)
    eight = (8, stu_width)
    z = jnp.tanh(
        mm_high(jnp.broadcast_to(pooled, eight), dense) + vec(dense_b_ref, layer, 0, stu_width)
    )
    logit_ref[...] = mm_high(z, cls) + vec(cls_b_ref, layer, 0, LANES)
    cot = cot_ref[pl.ds(row_ref[0], 1), :]
    d_pre = mm_high(jnp.broadcast_to(cot, (8, LANES)), cls, NT) * (1.0 - z * z)
    d_pooled = mm_high(d_pre, dense, NT)[:1]
    d_pre = d_pre[:1]

    def column(value):
        return jnp.broadcast_to(value, (value.shape[1], value.shape[1])).T

    d_scores = []
    for weight_col, d_weight in zip(weights, both(upper * d_pooled)):
        mean = jnp.sum(weight_col * d_weight, 0, keepdims=True)
        d_scores.append(weight_col * (d_weight - mean) * stu_scale)
    d_score = jnp.where(left, d_scores[0], d_scores[1])
    d_upper = (weight * d_pooled + d_score * query).astype(BF16)
    d_upper_ref[...] = d_upper
    small_ref[:width, :] = mm(hidden, d_upper, TN)
    small_ref[width : width + stu_width, :] = column(pooled) * d_pre
    small_ref[width + stu_width : width + 2 * stu_width, :] = column(z[:1]) * cot
    base = width + 2 * stu_width
    small_ref[base : base + 1, :] = jnp.sum(d_upper.astype(F32), 0, keepdims=True)
    small_ref[base + 1 : base + 2, :] = jnp.sum(d_score * upper, 0, keepdims=True)
    small_ref[base + 2 : base + 3, :] = d_pre
    small_ref[base + 3 : base + 4, :] = cot
    small_ref[base + 4 :, :] = jnp.zeros((4, LANES), F32)

    for made in (put_slope, put_active, put_hat, put_h):
        made.wait()


def forward_ff(layer, row, first, first_full, cot, weights, after=()):
    gain, shift, w_fi, fi_b, w_fo, fo_b = weights[4:10]
    length, width = first.shape
    ff = w_fi.shape[2]
    stu = weights[10].shape[2]
    outs = (
        low(length, ff),
        low(length, ff),
        low(length, width),
        low(length, width),
        full(length, LANES),
        low(length, stu),
        full(8, LANES),
        full(width + 2 * stu + 8, LANES),
    )
    return call(
        partial(forward_ff_kernel, layer),
        f"forward_ff{layer}",
        outs,
        (ANY,) * 4 + (WHOLE,) * 4,
        (row, first, first_full, cot, w_fi, w_fo, gain, shift, fi_b, fo_b) + tuple(weights[10:]),
        [SCALAR, ANY, ANY, WHOLE, ANY, ANY] + [WHOLE] * 11,
        [
            pltpu.VMEM((length, width), BF16),
            pltpu.VMEM((length, width), F32),
            pltpu.VMEM(w_fi.shape[1:], BF16),
            pltpu.VMEM(w_fo.shape[1:], BF16),
            vm(outs[0]),
            vm(outs[1]),
            vm(outs[2]),
            vm(outs[3]),
            pltpu.VMEM((length, 512), F32),
            pltpu.VMEM((length, 512), F32),
            pltpu.SemaphoreType.DMA((8,)),
        ],
        after,
        18 * 10**9,
        20 * 10**6,
    )


def backward_ff_kernel(
    layer,
    grad_ref,
    d_upper_ref,
    spread1_ref,
    spread2_ref,
    proj_ref,
    gain_ref,
    w_fi_hbm,
    w_fo_hbm,
    hat1_hbm,
    slope_hbm,
    hat2_hbm,
    second_hbm,
    inner_hbm,
    branch_hbm,
    resid_hbm,
    sums_ref,
    w_fi,
    w_fo,
    hat1,
    slope,
    hat2,
    second,
    inner,
    branch,
    d_resid,
    sems,
):
    length, width = grad_ref.shape
    ff = w_fi.shape[1]
    copy = copier(sems)
    get_hat2 = copy(hat2_hbm, hat2, 0)
    get_fo = copy(w_fo_hbm.at[layer], w_fo, 1)
    get_slope = copy(slope_hbm, slope, 2)
    get_fi = copy(w_fi_hbm.at[layer], w_fi, 3)
    get_hat1 = copy(hat1_hbm, hat1, 4)
    sums_ref[...] = jnp.zeros_like(sums_ref)
    get_hat2.wait()
    gain1, gain2 = vec(gain_ref, layer, 0, width), vec(gain_ref, layer, width, width)
    total = lambda value: jnp.sum(value.astype(F32), 0, keepdims=True)

    def through_norm(grads, hat_ref, spread_ref, gain, out_ref):
        d_gain = jnp.zeros((1, width), F32)
        d_shift = jnp.zeros((1, width), F32)
        d_bias = jnp.zeros((1, width), F32)
        for rows in chunks(length):
            grad = grads(rows)
            hat = hat_ref[rows, :].astype(F32)
            d_gain += total(grad * hat)
            d_shift += total(grad)
            moved = norm_back(grad, hat, spread_ref[rows, 0:1], gain)
            d_resid[rows, :] = moved
            out_ref[rows, :] = moved.astype(BF16)
            d_bias += total(moved.astype(BF16))
        return d_gain, d_shift, d_bias

    from_student = mm(d_upper_ref[...], proj_ref[layer], NT)
    d_gain, d_shift, d_bias = through_norm(
        lambda rows: grad_ref[rows, :].astype(F32) + from_student[rows],
        hat2,
        spread2_ref,
        gain2,
        second,
    )
    sums_ref[1:2, 3 * width : 4 * width] = d_gain
    sums_ref[2:3, width : 2 * width] = d_shift
    sums_ref[2:3, 3 * width : 4 * width] = d_bias
    put_second = copy(second, second_hbm, 5)

    get_fo.wait()
    get_slope.wait()
    part = 512

    def ff_part(number, carry):
        at = pl.multiple_of(number * part, part)
        column = jnp.zeros((1, part), F32)
        d_active = mm(second[...], w_fo[pl.ds(at, part), :], NT)
        for rows in chunks(length):
            d_inner = (d_active[rows] * slope[rows, pl.ds(at, part)].astype(F32)).astype(BF16)
            inner[rows, pl.ds(at, part)] = d_inner
            column += total(d_inner)
        sums_ref[0:1, pl.ds(at, part)] = column
        return carry

    lax.fori_loop(0, ff // part, ff_part, 0)
    put_inner = copy(inner, inner_hbm, 6)

    get_fi.wait()
    get_hat1.wait()
    d_first = mm(inner[...], w_fi[...], NT)
    d_gain, d_shift, d_bias = through_norm(
        lambda rows: d_resid[rows, :] + d_first[rows], hat1, spread1_ref, gain1, branch
    )
    sums_ref[1:2, 2 * width : 3 * width] = d_gain
    sums_ref[2:3, :width] = d_shift
    sums_ref[2:3, 2 * width : 3 * width] = d_bias
    for made in (
        put_second,
        put_inner,
        copy(branch, branch_hbm, 7),
        copy(d_resid, resid_hbm, 8),
    ):
        made.wait()


def backward_ff(layer, grad, saved1, saved2, weights, after=()):
    _, _, _, hat1, _, _, spread1 = saved1
    slope, _, hat2, _, spread2, d_upper, _, _ = saved2
    gain, _, w_fi, _, w_fo, _ = weights[4:10]
    length, width = grad.shape
    ff = w_fi.shape[2]
    outs = (
        low(length, width),
        low(length, ff),
        low(length, width),
        full(length, width),
        full(8, ff),
    )
    return call(
        partial(backward_ff_kernel, layer),
        f"backward_ff{layer}",
        outs,
        (ANY,) * 4 + (WHOLE,),
        (grad, d_upper, spread1, spread2, weights[10], gain, w_fi, w_fo, hat1, slope, hat2),
        [WHOLE] * 6 + [ANY] * 5,
        [
            pltpu.VMEM(w_fi.shape[1:], BF16),
            pltpu.VMEM(w_fo.shape[1:], BF16),
            vm(hat1),
            vm(slope),
            vm(hat2),
            vm(outs[0]),
            vm(outs[1]),
            vm(outs[2]),
            vm(outs[3]),
            pltpu.SemaphoreType.DMA((9,)),
        ],
        after,
        16 * 10**9,
        22 * 10**6,
    )


def backward_attention_kernel(
    layer,
    scale,
    row_ref,
    seg_ref,
    lse_ref,
    w_in_hbm,
    w_out_hbm,
    qkv_hbm,
    mixed_hbm,
    branch_hbm,
    resid_hbm,
    d_qkv_hbm,
    d_x_ref,
    sums_ref,
    w_in,
    w_out,
    qkv,
    mixed,
    branch,
    d_resid,
    d_qkv,
    d_mix,
    bias,
    delta_ref,
    probs_ref,
    ds_ref,
    sems,
):
    length, width = branch.shape
    copy = copier(sems)
    get_branch = copy(branch_hbm, branch, 0)
    get_out = copy(w_out_hbm.at[layer], w_out, 1)
    get_mixed = copy(mixed_hbm, mixed, 2)
    get_qkv = copy(qkv_hbm, qkv, 3)
    get_in = copy(w_in_hbm.at[layer], w_in, 4)
    get_resid = copy(resid_hbm, d_resid, 5)
    fill_bias(seg_ref, row_ref[0], bias)
    probs_ref[...] = jnp.zeros_like(probs_ref)
    ds_ref[...] = jnp.zeros_like(ds_ref)
    sums_ref[...] = jnp.zeros_like(sums_ref)
    total = lambda value: jnp.sum(value.astype(F32), 0, keepdims=True)
    head_of = lax.broadcasted_iota(jnp.int32, (16, width), 1) // HEAD
    ones = (head_of == lax.broadcasted_iota(jnp.int32, (16, width), 0)).astype(F32).astype(BF16)
    get_branch.wait()
    get_out.wait()
    d_mix[...] = mm(branch[...], w_out[...], NT).astype(BF16)
    get_mixed.wait()
    product = d_mix[...].astype(F32) * mixed[...].astype(F32)
    high = product.astype(BF16)
    rest = (product - high.astype(F32)).astype(BF16)
    delta_ref[...] = mm(ones, high, NT) + mm(ones, rest, NT)

    get_qkv.wait()
    low_half = lax.broadcasted_iota(jnp.int32, (length, LANES), 1) < HEAD
    low_rows = lax.broadcasted_iota(jnp.int32, (LANES, length), 0) < HEAD

    def pair(number, carry):
        at = pl.multiple_of(number * LANES, LANES)
        cols = pl.ds(at, LANES)
        key_cols = pl.ds(at + width, LANES)
        value_cols = pl.ds(at + 2 * width, LANES)
        queries, keys, values, mix = qkv[:, cols], qkv[:, key_cols], qkv[:, value_cols], d_mix[:, cols]
        keys_t = keys.T
        d_query = jnp.zeros((LANES, length), F32)
        d_keys, d_values = [], []
        zero = jnp.zeros_like(keys)
        for sub in range(2):
            head = 2 * number + sub
            lse = lse_ref[pl.ds(head, 1), :]
            delta = delta_ref[pl.ds(head, 1), :]
            mine = low_half == (sub == 0)
            scores = mm(jnp.where(mine, keys, zero), queries, NT)
            d_probs = mm(jnp.where(mine, values, zero), mix, NT)
            for rows in chunks(length):
                start, stop = window(rows.start, length)
                probs = jnp.exp(
                    scores[rows, start:stop] + bias[rows, start:stop] - lse[:, start:stop]
                )
                probs_ref[sub, rows, start:stop] = probs.astype(BF16)
                ds_ref[sub, rows, start:stop] = (
                    probs * (d_probs[rows, start:stop] - delta[:, start:stop])
                ).astype(BF16)
            d_values.append(mm(probs_ref[sub], mix))
            d_keys.append(mm(ds_ref[sub], queries))
            mine_t = jnp.where(low_rows == (sub == 0), keys_t, jnp.zeros_like(keys_t))
            d_query += mm(mine_t, ds_ref[sub])
        dq = (d_query.T * scale).astype(BF16)
        d_qkv[:, cols] = dq
        sums_ref[1:2, cols] = total(dq)
        d_qkv[:, key_cols] = jnp.where(low_half, d_keys[0], d_keys[1]).astype(BF16)
        dv = jnp.where(low_half, d_values[0], d_values[1]).astype(BF16)
        d_qkv[:, value_cols] = dv
        sums_ref[1:2, key_cols] = total(dv)
        return carry

    lax.fori_loop(0, HEADS * HEAD // LANES, pair, 0)
    put_qkv = copy(d_qkv, d_qkv_hbm, 6)
    get_in.wait()
    get_resid.wait()
    d_x = mm(d_qkv[...], w_in[...], NT)
    for rows in chunks(length):
        d_x_ref[rows, :] = (d_resid[rows, :] + d_x[rows]).astype(BF16)
    put_qkv.wait()


def backward_attention(layer, row, seg, saved1, branch, d_resid, weights, after=()):
    qkv, lse, mixed = saved1[:3]
    w_in, _, w_out = weights[:3]
    ff = weights[6].shape[2]
    length, width = mixed.shape
    outs = (low(length, 3 * width), low(length, width), full(8, ff))
    return call(
        partial(backward_attention_kernel, layer, HEAD**-0.5),
        f"backward_attention{layer}",
        outs,
        (ANY, WHOLE, WHOLE),
        (row, seg, lse, w_in, w_out, qkv, mixed, branch, d_resid),
        [SCALAR, WHOLE, WHOLE] + [ANY] * 6,
        [
            pltpu.VMEM(w_in.shape[1:], BF16),
            pltpu.VMEM(w_out.shape[1:], BF16),
            vm(qkv),
            vm(mixed),
            vm(branch),
            vm(d_resid),
            vm(outs[0]),
            vm(outs[1]),
            pltpu.VMEM((length, length), F32),
            pltpu.VMEM((16, length), F32),
            pltpu.VMEM((2, length, length), BF16),
            pltpu.VMEM((2, length, length), BF16),
            pltpu.SemaphoreType.DMA((7,)),
        ],
        after,
        20 * 10**9,
        16 * 10**6,
    )


def pick_cols_kernel(half_ref, *refs, rows, recv):
    lefts, rights = refs[:rows], refs[rows : 2 * rows]
    out_ref, turned = refs[-2], refs[-1]
    length = lefts[0].shape[0]

    @pl.when(pl.program_id(0) == 0)
    def _():
        for number, left in enumerate(lefts):
            turned[:, number * length : (number + 1) * length] = left[...].T

    found = None
    for number, right in enumerate(rights):
        part = mm(turned[:, number * length : (number + 1) * length], right[...])
        found = part if found is None else found + part
    found = found.reshape(out_ref.shape)
    if recv:
        found = found + refs[2 * rows][...].astype(F32)
    out_ref[...] = found.astype(BF16)


def weight_grad_cols(half, lefts, rights, narrow, recv=None, after=()):
    rows = len(lefts)
    length, width = lefts[0].shape
    cols = rights[0].shape[1] // 2
    tile = next((size for size in (512, 384) if cols % size == 0), cols)
    steps = cols // tile
    out_block = pl.BlockSpec((narrow, width // narrow, tile), lambda j, half: (0, 0, j))
    return pl.pallas_call(
        partial(pick_cols_kernel, rows=rows, recv=recv is not None),
        out_shape=jax.ShapeDtypeStruct((narrow, width // narrow, cols), BF16),
        grid_spec=pltpu.PrefetchScalarGridSpec(
            num_scalar_prefetch=1,
            grid=(steps,),
            in_specs=[pl.BlockSpec((length, width), lambda j, half: (0, 0))] * rows
            + [pl.BlockSpec((length, tile), lambda j, half: (0, half[0] * steps + j))] * rows
            + [out_block] * (recv is not None)
            + [ANY] * len(after),
            out_specs=out_block,
            scratch_shapes=[pltpu.VMEM((width, rows * length), BF16)],
        ),
        compiler_params=pltpu.CompilerParams(vmem_limit_bytes=LIMIT),
        cost_estimate=pl.CostEstimate(
            flops=2 * rows * length * width * cols,
            bytes_accessed=2 * (rows * length * (width + cols) + width * cols),
            transcendentals=0,
        ),
        name="weight_grad_cols",
    )(half, *lefts, *rights, *(() if recv is None else (recv,)), *after)


def pick_rows_kernel(half_ref, *refs, rows, recv):
    lefts, rights = refs[:rows], refs[rows : 2 * rows]
    out_ref = refs[-1]
    unit = out_ref.shape[1]
    width = rights[0].shape[1]
    found = None
    for left, right in zip(lefts, rights):
        part = mm(left[...], right[...], TN)
        found = part if found is None else found + part
    for block in range(out_ref.shape[2] // width):
        cols = slice(block * width, (block + 1) * width)
        part = found[block * unit : (block + 1) * unit]
        if recv:
            part = part + refs[2 * rows][0, :, cols].astype(F32)
        out_ref[0, :, cols] = part.astype(BF16)


def weight_grad_rows(half, lefts, rights, narrow, recv=None, after=()):
    rows = len(lefts)
    length, deep = lefts[0].shape
    width = rights[0].shape[1]
    unit = width // narrow
    part = deep // narrow // 2
    cols = part // unit * width
    out_block = pl.BlockSpec((1, unit, cols), lambda j, half: (j, 0, 0))
    return pl.pallas_call(
        partial(pick_rows_kernel, rows=rows, recv=recv is not None),
        out_shape=jax.ShapeDtypeStruct((narrow, unit, cols), BF16),
        grid_spec=pltpu.PrefetchScalarGridSpec(
            num_scalar_prefetch=1,
            grid=(narrow,),
            in_specs=[pl.BlockSpec((length, part), lambda j, half: (0, 2 * j + half[0]))] * rows
            + [pl.BlockSpec((length, width), lambda j, half: (0, 0))] * rows
            + [out_block] * (recv is not None)
            + [ANY] * len(after),
            out_specs=out_block,
        ),
        compiler_params=pltpu.CompilerParams(vmem_limit_bytes=LIMIT),
        cost_estimate=pl.CostEstimate(
            flops=rows * length * deep * width,
            bytes_accessed=rows * length * (deep + 2 * width) + deep * width,
            transcendentals=0,
        ),
        name="weight_grad_rows",
    )(half, *lefts, *rights, *(() if recv is None else (recv,)), *after)


def swap(value, bit):
    size = lax.axis_size("wide")
    return lax.ppermute(value, "wide", [(i, i ^ bit) for i in range(size)])


def tie(values, on):
    return lax.optimization_barrier((values, on))[0]


def add_low(left, right):
    return (left.astype(F32) + right.astype(F32)).astype(BF16)


def halves(value, side, axis):
    half = value.shape[axis] // 2
    keep = lax.dynamic_slice_in_dim(value, side * half, half, axis)
    give = lax.dynamic_slice_in_dim(value, (1 - side) * half, half, axis)
    return keep, give


def wide_bits():
    return [1 << i for i in range((lax.axis_size("wide") - 1).bit_length())]


def bit_order(turn):
    rest = wide_bits()[1:]
    return rest[::-1] if turn else rest


class Halving:
    def __init__(self, groups):
        self.place = lax.axis_index("wide")
        self.bits = list(zip(*(bit_order(turn) for turn in range(2))))
        self.groups = groups
        self.flying = None

    def step(self, on=None):
        if self.flying is not None:
            if on is not None:
                self.flying = [(keep, tie(recv, on)) for keep, recv in self.flying]
            self.groups = [[add_low(keep, recv)] for keep, recv in self.flying]
            self.flying = None
        if not self.bits:
            return [group[0] for group in self.groups]
        flying, gives = [], []
        for bit, group in zip(self.bits.pop(0), self.groups):
            split = [halves(part, (self.place // bit) % 2, 1) for part in group]
            keep = jnp.concatenate([pair[0] for pair in split], -1)
            give = jnp.concatenate([pair[1] for pair in split], -1)
            gives.append(give)
            flying.append((keep, swap(give, bit)))
        self.flying = flying
        return gives

    def finish(self, on=None):
        mine = self.step(on)
        while self.flying is not None:
            mine = self.step()
        return jnp.concatenate(mine, -1)


def narrow_sum_swaps(mine):
    size = lax.axis_size("narrow")
    place = lax.axis_index("narrow")
    cur = mine.reshape((2,) * (size.bit_length() - 1) + mine.shape[1:])
    depth = size.bit_length() - 1
    for level in range(depth):
        bit = 1 << level
        axis = depth - 1 - level
        keep, give = halves(cur, (place // bit) % 2, axis)
        cur = add_low(
            keep, lax.ppermute(give, "narrow", [(i, i ^ bit) for i in range(size)])
        )
    return cur.reshape(mine.shape[1:])


def wide_gather_swaps(mine):
    place = lax.axis_index("wide")
    cur = mine[None]
    for bit in wide_bits()[::-1]:
        other = swap(cur, bit)
        upper = (place // bit) % 2 == 1
        cur = jnp.stack([jnp.where(upper, other, cur), jnp.where(upper, cur, other)])
        cur = cur.reshape((-1,) + mine.shape)
    return cur


def narrow_sum(mine):
    return lax.psum_scatter(mine, "narrow", scatter_dimension=0, tiled=True)[0]


def small_pack(small, sums, narrow):
    stu = small.shape[1]
    width = small.shape[0] - 2 * stu - 8
    deep = sums.shape[1]
    unit = width // narrow
    proj = small[:width].reshape(narrow, unit, stu)
    split = small[width : width + 2 * stu].reshape(2, narrow, stu // narrow, stu)
    own = small[width + 2 * stu :]
    vectors = [
        sums[1, : 2 * width],
        sums[2, 2 * width : 3 * width],
        sums[1, 2 * width :],
        sums[2, : 2 * width],
        sums[0],
        sums[2, 3 * width :],
    ]
    vectors = [value.reshape(narrow, -1) for value in vectors]
    vectors += [own[i].reshape(narrow, -1) for i in range(3)]
    vectors += [jnp.broadcast_to(own[3], (narrow, stu))]
    rows = [
        jnp.pad(value, ((0, 0), (0, -value.shape[1] % LANES))).reshape(narrow, -1, LANES)
        for value in vectors
    ]
    rest = jnp.concatenate([split[0], split[1]] + rows, 1)
    rest = jnp.pad(rest, ((0, 0), (0, unit - rest.shape[1]), (0, 0)))
    return jnp.stack([proj, rest]).astype(BF16)


def place_kernel(layer, orders, turned, aliased, ff_ref, at_ref, *refs):
    outs, small = refs[aliased : aliased + 4], refs[aliased + 4]
    ai, ao, fi, fo, sems = refs[aliased + 5 :]
    unit, deep = fi.shape
    width = ao.shape[1]
    total, rows, _ = ff_ref.shape
    count = (total - 1).bit_length()
    half_in, half_out = ai.shape[1] // 2, width // 2
    cut = at_ref.shape[2] // 2
    rest = half_in - cut
    blocks = fo.shape[0] // unit // 2

    def put(number, src):
        made = pltpu.make_async_copy(src, outs[number].at[layer], sems.at[number])
        made.start()
        return made

    def starts(place):
        found = []
        for order in orders:
            at = 0
            for bit in order:
                at = 2 * at + (place // bit) % 2
            found.append(at * rows)
        return found

    for place in range(total):
        core = place % 2
        x_at, y_at = starts(place)
        get = lambda start, size: ff_ref[place, :, start : start + size].astype(F32)
        fi[x_at : x_at + rows, core * deep // 2 : (core + 1) * deep // 2] = get(0, deep // 2)
        for block in range(blocks):
            at = (core * blocks + block) * unit + y_at
            fo[at : at + rows, :] = get(deep // 2 + block * width, width)
        ao[y_at : y_at + rows, core * half_out : (core + 1) * half_out] = get(deep, half_out)
    puts = [put(2, fi), put(3, fo), put(1, ao)]
    for place in range(total):
        core = place % 2
        x_at, y_at = starts(place)
        held = place
        if turned:
            held = sum(((place >> i) & 1) << (count - 1 - i) for i in range(count))
        get = lambda start, size: at_ref[held, :, start : start + size].astype(F32)
        start = core * half_in
        ai[x_at : x_at + rows, start : start + cut] = get(0, cut)
        ai[y_at : y_at + rows, start + cut : start + half_in] = get(cut, rest)
        small[y_at : y_at + rows, core * LANES : (core + 1) * LANES] = get(cut + rest, LANES)
    puts.append(put(0, ai))
    for made in puts:
        made.wait()


def place_layer(layer, ff, at, turned, shapes, previous=()):
    unit = shapes[0].shape[1]
    held = len(previous)
    return pl.pallas_call(
        partial(place_kernel, layer, [bit_order(turn) for turn in range(2)], turned, held),
        out_shape=tuple(shapes) + (full(unit, 2 * LANES),),
        in_specs=[WHOLE, WHOLE] + [ANY] * held,
        out_specs=(ANY,) * 4 + (WHOLE,),
        scratch_shapes=[pltpu.VMEM(shape.shape[1:], F32) for shape in shapes]
        + [pltpu.SemaphoreType.DMA((4,))],
        input_output_aliases={2 + i: i for i in range(held)},
        compiler_params=pltpu.CompilerParams(vmem_limit_bytes=LIMIT),
        cost_estimate=pl.CostEstimate(flops=10**6, bytes_accessed=11 * 10**6, transcendentals=0),
        name=f"place_layer{layer}",
    )(ff, at, *previous)


def place_small_kernel(first_ref, second_ref, proj_ref, dense_ref, cls_ref, *vec_refs):
    for layer, ref in enumerate((first_ref, second_ref)):
        stu = dense_ref.shape[1]
        proj_ref[layer] = ref[:, :LANES]
        dense_ref[layer] = ref[:stu, LANES:]
        cls_ref[layer] = ref[stu : 2 * stu, LANES : LANES + cls_ref.shape[2]]
        row = 2 * stu
        for out in vec_refs:
            size = out.shape[1]
            for start in range(0, size, LANES):
                part = min(LANES, size - start)
                out[layer : layer + 1, start : start + part] = ref[
                    row : row + 1, LANES : LANES + part
                ]
                row += 1


def place_small(first, second, width, deep, classes, narrow):
    sizes = [2 * width, width, 2 * width, 2 * width, deep, width, LANES, LANES, LANES]
    stu = LANES // narrow
    outs = (
        full(2, width // narrow, LANES),
        full(2, stu, LANES),
        full(2, stu, classes),
    ) + tuple(full(2, size // narrow) for size in sizes)
    return pl.pallas_call(
        place_small_kernel,
        out_shape=outs + (full(2, classes),),
        in_specs=[WHOLE, WHOLE],
        out_specs=(WHOLE,) * 13,
        name="place_small",
    )(first, second)


def route_kernel(me_ref, *refs):
    around, out_ref, held = refs[:-2], refs[-2], refs[-1]
    me, size = me_ref[0], len(around)
    for step, ref in enumerate(around):
        held[lax.rem(me + (size - step), size)] = ref[0]
    counts = [held[i] for i in range(size)]
    flow, before = [], []
    total = jnp.int32(0)
    for value in counts:
        before.append(total)
        total = total + value - 1
        flow.append(total)
    right1 = [(f >= 1) & (c >= 1) for f, c in zip(flow, counts)]
    left1 = [(f <= -1) & (c >= 1) for f, c in zip(before, counts)]
    right2 = [(f >= 1) & ((f >= 2) | (c == 0)) for f, c in zip(flow, counts)]
    left2 = [(f <= -1) & ((f <= -2) | (c == 0)) for f, c in zip(before, counts)]

    def at(values, shift):
        found = jnp.int32(0)
        for i, value in enumerate(values):
            found = jnp.where(me + shift == i, value.astype(jnp.int32), found)
        return found

    count = at(counts, 0)
    from_left2, from_right2 = at(right2, -1), at(left2, 1)
    sent_right, sent_left = at(right1, 0), at(left1, 0)
    results = (
        at(right1, -1),
        from_left2,
        from_left2 | from_right2,
        (count == 2).astype(jnp.int32),
        ((count == 1) & (sent_right + sent_left == 0)).astype(jnp.int32),
        at(right2, 0),
        sent_left,
        (sent_right & at(right2, 1)) | (sent_left & at(left2, -1)),
        (count >= 1).astype(jnp.int32),
        (count >= 2).astype(jnp.int32),
    )
    for i, value in enumerate(results):
        out_ref[i] = value
    for i in range(len(results), out_ref.shape[0]):
        out_ref[i] = 0


def route(me, around):
    return pl.pallas_call(
        route_kernel,
        out_shape=jax.ShapeDtypeStruct((16,), jnp.int32),
        in_specs=[SCALAR] * (1 + len(around)),
        out_specs=SCALAR,
        scratch_shapes=[pltpu.SMEM((len(around),), jnp.int32)],
        name="route",
    )(me, *around)


def shards(
    tokens,
    segments,
    exit_layer,
    attn_in,
    qv_bias,
    attn_out,
    out_bias,
    ln_gain,
    ln_bias,
    ff_in,
    ff_in_bias,
    ff_out,
    ff_out_bias,
    stu_proj,
    stu_bias,
    pool_query,
    stu_dense,
    stu_dense_bias,
    stu_cls,
    stu_cls_bias,
    out_cot,
    logit_cot,
):
    row_count, length, width = tokens.shape
    classes = stu_cls.shape[-1]
    blank = LANES - classes
    narrow = lax.axis_size("narrow")
    me = lax.axis_index("narrow")
    core = lax.axis_index("wide") % 2
    weights = (
        attn_in,
        qv_bias,
        attn_out,
        out_bias,
        ln_gain,
        ln_bias,
        ff_in,
        ff_in_bias,
        ff_out,
        ff_out_bias,
        stu_proj,
        stu_bias,
        pool_query,
        stu_dense,
        stu_dense_bias,
        jnp.pad(stu_cls, ((0, 0), (0, 0), (0, blank))),
        jnp.pad(stu_cls_bias, ((0, 0), (0, blank))),
    )
    wide_cot = jnp.pad(logit_cot.astype(F32), ((0, 0), (0, 0), (0, blank)))

    alive = exit_layer == 1
    mine = jnp.sum(alive.astype(jnp.int32)).reshape(1)
    around = [mine] + [
        lax.ppermute(mine, "narrow", [(i, (i + step) % narrow) for i in range(narrow)])
        for step in range(1, narrow)
    ]
    flags = route(me.reshape(1), around)
    from_left1, from_left2, use_two, use_b, use_a, on_right, sent_left, is_far, a_alive, b_alive = (
        flags[i] == 1 for i in range(10)
    )
    row_a = jnp.where(alive[0], 0, jnp.where(alive[1], 1, 0)).astype(jnp.int32)
    row_b = 1 - row_a

    even = me % 2 == 0
    inner = [(i, i ^ 1) for i in range(narrow)]
    outer = []
    for i in range(lax.axis_size("wide") * narrow):
        place, line = i // narrow, i % narrow
        other = ((line + 1) ^ 1) - 1
        inside = 0 <= other < narrow
        outer.append((i, place * narrow + other if inside else (place ^ 1) * narrow + line))

    def shift(value):
        return (
            lax.ppermute(value, "narrow", inner),
            lax.ppermute(value, ("wide", "narrow"), outer),
        )

    def pick(pair, is_left):
        return jnp.where(is_left == even, pair[1], pair[0])

    def out_one(pair):
        return pick(pair, from_left1)

    def out_two(pair, one, own_a, own_b):
        two = pick(pair, from_left2)
        return jnp.where(use_b, own_b, jnp.where(use_a, own_a, jnp.where(use_two, two, one)))

    def back_one(pair):
        return pick(pair, ~on_right)

    def back_two(value, pair, pair2):
        return jnp.where(
            use_a, value, jnp.where(is_far, pick(pair2, sent_left), pick(pair, sent_left))
        )

    def row_of(value, row):
        return lax.dynamic_index_in_dim(value, row, 0, False)

    def cot_pack(row):
        tail = jnp.zeros((16, width), BF16)
        tail = tail.at[0, :length].set(row_of(segments, row).astype(BF16))
        tail = tail.at[1, :classes].set(row_of(logit_cot[:, 1], row))
        return jnp.concatenate([row_of(out_cot, row), tail], 0)

    index = lambda row: row.reshape(1)
    first_row = jnp.zeros((1,), jnp.int32)
    own, other = index(core), index(1 - core)
    ia, ib = index(row_a), index(row_b)
    early_cot = wide_cot[:, 0]

    pack_a, pack_b = cot_pack(row_a), cot_pack(row_b)
    pair = shift(pack_a)
    a1 = forward_attention(0, ia, tokens, segments, weights, (pack_a,))
    pack_one = out_one(tie(pair, a1[4]))
    pair = shift(pack_one)
    a2 = forward_ff(0, ia, a1[4], a1[5], early_cot, weights, (pack_one,))
    work_pack = out_two(tie(pair, a2[3]), pack_one, pack_a, pack_b)
    pair = shift(a2[3])
    b1 = forward_attention(0, ib, tokens, segments, weights, (a2[3], work_pack))
    one = out_one(tie(pair, b1[4]))
    pair = shift(one)
    b2 = forward_ff(0, ib, b1[4], b1[5], early_cot, weights, (one,))
    work_in = out_two(tie(pair, b2[3]), one, a2[3], b2[3])
    work_seg = work_pack[length : length + 1, :length].astype(jnp.int32)
    work_cot = work_pack[length + 1 : length + 2, :LANES].astype(F32)

    w1 = forward_attention(1, first_row, work_in[None], work_seg, weights)
    w2 = forward_ff(1, first_row, w1[4], w1[5], work_cot, weights)
    sent_h = jnp.concatenate(
        [w2[3], jnp.pad(w2[6], ((0, 8), (0, width - LANES))).astype(BF16)], 0
    )
    pair_h = shift(sent_h)
    w3 = backward_ff(1, work_pack[:length], w1, w2, weights, (sent_h,))

    def ff_jobs(saved1, saved2, back):
        first = [s[4] for s in saved1]
        mixed = [s[2] for s in saved1]
        active = [s[1] for s in saved2]
        second, inner, branch = ([b[i] for b in back] for i in range(3))
        return (
            (weight_grad_cols, first, inner),
            (weight_grad_rows, active, second),
            (weight_grad_cols, mixed, branch),
        )

    def give_half(jobs, after=()):
        return [job(other, lefts, rights, narrow, None, after) for job, lefts, rights in jobs]

    def own_half(jobs, sent, after=()):
        return [
            job(own, lefts, rights, narrow, swap(value, 1), after)
            for (job, lefts, rights), value in zip(jobs, sent)
        ]

    def ff_halving(parts):
        return Halving([[parts[0]], [parts[1], parts[2]]])

    def attn_halving(part, small):
        keep, give = halves(small, core, 0)
        small = add_low(keep, swap(give, 1))[0]
        cut = (part.shape[-1] + LANES) // 2
        return Halving([[part[..., :cut]], [part[..., cut:], small]])

    jobs = ff_jobs([w1], [w2], [w3])
    forth_h = back_one(tie(pair_h, w3[2]))
    pair_h2 = shift(forth_h)
    sent = give_half(jobs, (forth_h,))
    w4 = backward_attention(1, first_row, work_seg, w1, w3[2], w3[3], weights, tuple(sent))
    pair_x = shift(w4[1])
    parts = own_half(jobs, sent, (w4[1],))
    ff1 = ff_halving(parts)
    flying = ff1.step()
    jobs1 = ((weight_grad_cols, [work_in], [w4[0]]),)
    sent1 = give_half(jobs1, tuple(flying))
    forth_x = back_one(tie(pair_x, sent1[0]))
    pair_x2 = shift(forth_x)
    far_h = back_two(sent_h, pair_h, tie(pair_h2, w4[1]))

    base_b = jnp.where(b_alive, w4[1], row_of(out_cot, row_b))
    b3 = backward_ff(0, base_b, b1, b2, weights, (*sent1, forth_x, far_h))
    far_x = back_two(w4[1], pair_x, tie(pair_x2, b3[2]))
    part1 = own_half(jobs1, sent1, (b3[0],))[0]
    at1 = attn_halving(part1, small_pack(w2[7], w3[4] + w4[2], narrow))
    flying = at1.step() + ff1.step(b3[2])
    base_a = jnp.where(a_alive, far_x, row_of(out_cot, row_a))
    a3 = backward_ff(0, base_a, a1, a2, weights, tuple(flying))
    mine_ff1 = ff1.finish(a3[2])
    flying = at1.step(a3[2])
    jobs = ff_jobs([a1, b1], [a2, b2], [a3, b3])
    sent = give_half(jobs, (mine_ff1, *flying))
    sum_ff1 = narrow_sum(mine_ff1)
    ff0 = ff_halving(own_half(jobs, sent))
    flying = ff0.step()
    mine_at1 = at1.finish(flying[0])
    b4 = backward_attention(
        0, ib, segments, b1, b3[2], b3[3], weights, (*flying, sum_ff1, mine_at1)
    )
    every = lambda value: lax.all_gather(value, "wide", axis=0, tiled=False)
    sum_at1 = narrow_sum(mine_at1)
    all_ff1 = every(sum_ff1)
    a4 = backward_attention(
        0, ia, segments, a1, a3[2], a3[3], weights, (b4[1],)
    )
    flying = ff0.step(a4[1])
    jobs0 = (
        (
            weight_grad_cols,
            [row_of(tokens, row_a), row_of(tokens, row_b)],
            [a4[0], b4[0]],
        ),
    )
    sent0 = give_half(jobs0, tuple(flying))
    part0 = own_half(jobs0, sent0, (all_ff1, sum_at1))[0]
    at0 = attn_halving(
        part0, small_pack(a2[7] + b2[7], a3[4] + b3[4] + a4[2] + b4[2], narrow)
    )
    flying = at0.step()
    sum_ff0 = narrow_sum(ff0.finish(flying[0]))
    all_at0 = wide_gather_swaps(narrow_sum_swaps(at0.finish()))

    deep = ff_in.shape[2]
    shapes = [
        full(2, width // narrow, 3 * width),
        full(2, width // narrow, width),
        full(2, width // narrow, deep),
        full(2, deep // narrow, width),
    ]
    *large, small1 = place_layer(1, all_ff1, wide_gather_swaps(tie(sum_at1, part0)), True, shapes)
    *large, small0 = place_layer(0, every(sum_ff0), all_at0, True, shapes, large)
    (d_proj, d_dense, d_cls, d_qv, d_out_b, d_gain, d_shift, d_fi_b, d_fo_b, *rest) = place_small(
        small0, small1, width, deep, classes, narrow
    )
    d_stu_b, d_query, d_dense_b, d_cls_b = rest
    totals = (
        large[0],
        d_qv,
        large[1],
        d_out_b,
        d_gain,
        d_shift,
        large[2],
        d_fi_b,
        large[3],
        d_fo_b,
        d_proj,
        d_stu_b,
        d_query,
        d_dense,
        d_dense_b,
        d_cls,
        d_cls_b,
    )

    in_order = lambda for_a, for_b: jnp.where(
        row_a == 0, jnp.stack([for_a, for_b]), jnp.stack([for_b, for_a])
    )
    act_a = jnp.where(a_alive, far_h[:length], a2[3])
    act_b = jnp.where(b_alive, w2[3], b2[3])
    logit_a = jnp.where(a_alive, far_h[length, :classes], jnp.zeros((classes,), BF16))
    logit_b = jnp.where(b_alive, w2[6][0, :classes].astype(BF16), jnp.zeros((classes,), BF16))
    early = in_order(a2[6][0, :classes], b2[6][0, :classes]).astype(BF16)
    logits = jnp.stack([early, in_order(logit_a, logit_b)], 1)
    return (in_order(act_a, act_b), logits, in_order(a4[1], b4[1])) + totals


def solution(mesh):
    rows = ("wide", "narrow")
    return jax.shard_map(
        shards,
        mesh=mesh,
        in_specs=(P(rows, None, None), P(rows, None), P(rows))
        + (P(),) * 17
        + (P(rows, None, None), P(rows, None, None)),
        out_specs=(P(rows, None, None),) * 3
        + (
            P(None, "narrow", None),
            P(None, "narrow"),
            P(None, "narrow", None),
            P(None, "narrow"),
            P(None, "narrow"),
            P(None, "narrow"),
            P(None, "narrow", None),
            P(None, "narrow"),
            P(None, "narrow", None),
            P(None, "narrow"),
            P(None, "narrow", None),
            P(None, "narrow"),
            P(None, "narrow"),
            P(None, "narrow", None),
            P(None, "narrow"),
            P(None, "narrow", None),
            P(),
        ),
        check_vma=False,
    )
```

time: 1350 us -> 532 us (0.39)
  waiting for transfers between devices: 613 us -> 69.4 us
  matrix products: 308 us -> 0 us
  Pallas kernels: 0 us -> 276 us
  blocking collectives: 127 us -> 0 us
  local copies, waits for them, and re-layouts: 138 us -> 49.7 us
  other arithmetic: 109 us -> 55.4 us
  starting transfers between devices: 29.5 us -> 48.4 us
    reduce_scatter x10 -> x3, waiting for transfers between devices: 347 us -> 1.52 us  [narrow_sum(): return lax.psum_scatter(mine, 'narrow', scatter_dimension=0, tiled=True)[0]]
    dot_general x71 -> x0, matrix products: 308 us -> none  [the longest x2 58.2 us: layer_forward(): jnp.dot(first_norm.astype(jnp.bfloat16), ff_in, preferred_element_type=jn...]
    pallas_call x0 -> x32, Pallas kernels: none -> 276 us  [the longest x12 185 us: call(): pl.pallas_call(body, out_shape=outs, in_specs=list(in_specs) + [ANY] * ex...]
    psum x2 -> x0, waiting for transfers between devices: 162 us -> none  [reduce_layer(): lax.psum(as_sent(shares), 'wide')]
    unnamed x2 -> x0, blocking collectives: 119 us -> none
    all_to_all x6 -> x0, waiting for transfers between devices: 104 us -> none  [the longest x4 66.6 us: shards(): lax.all_to_all(as_sent(outgoing), 'narrow', split_axis=0, concat_axis=0,...]
    ppermute x0 -> x53, waiting for transfers between devices: none -> 61.2 us  [the longest x32 32.5 us: swap(): return lax.ppermute(value, 'wide', [(i, i ^ bit) for i in range(size)])]
    ppermute x0 -> x53, starting transfers between devices: none -> 47.9 us  [the longest x32 26.4 us: swap(): return lax.ppermute(value, 'wide', [(i, i ^ bit) for i in range(size)])]
  transfers between devices with their start and end apart: 22 -> 58, of which waited for: 10 -> 17; matrix products, arithmetic and copies ran while one was open for 33% -> 14% of each run, Pallas kernels for 0% -> 42%
where the time goes in v1:
time: 532 us; the launch traced here: 523 us
  Pallas kernels  276 us (52%)
  waiting for transfers between devices  69.4 us (13%)
  other arithmetic  55.4 us (10%)
  local copies, waits for them, and re-layouts  49.7 us (9%)
  starting transfers between devices  48.4 us (9%)
  between operations  24 us (5%)
    pallas_call x12, Pallas kernels, call(): pl.pallas_call(body, out_shape=outs, in_specs=list(in_specs) + [ANY] * ex...  185 us
    pallas_call x12, Pallas kernels, weight_grad_cols(): pl.pallas_call(partial(pick_cols_kernel, rows=rows, recv=recv is not None...  53.8 us
    ppermute x32, waiting for transfers between devices, swap(): return lax.ppermute(value, 'wide', [(i, i ^ bit) for i in range(size)])  32.5 us
    ppermute x32, starting transfers between devices, swap(): return lax.ppermute(value, 'wide', [(i, i ^ bit) for i in range(size)])  26.4 us
    pallas_call x4, Pallas kernels, weight_grad_rows(): pl.pallas_call(partial(pick_rows_kernel, rows=rows, recv=recv is not None...  22.4 us
    unnamed x217, local copies, waits for them, and re-layouts  17.7 us
    convert_element_type x19, other arithmetic, add_low(): return (left.astype(F32) + right.astype(F32)).astype(BF16)  16.5 us
    ppermute x2, waiting for transfers between devices, narrow_sum_swaps(): lax.ppermute(give, 'narrow', [(i, i ^ bit) for i in range(size)])  14.8 us
  transfers between devices with their start and end apart: 58, of which 17 were waited for; matrix products, arithmetic and copies ran while one was open for 14% of the time, Pallas kernels for 42%

profile of v1, /device:TPU:0, one launch (start us, length us, event | category | flops | bytes accessed | tf_op | source)
XLA Modules:
  0.0 523.0 jit_solution(7789303434966924423)
XLA Ops:
  14.8 3.0 collective-permute-start.3
  18.5 3.1 collective-permute-start
  21.6 2.4 collective-permute-start.2
  24.1 14.2 %forward_attention0.2 = (bf16[512,2304]{1,0:T(8,128)(2,1)}, f32[16,512]{1,0:T(8,128)S(1)}, bf16[512,768]{1,0:T(8,128)(2,1)S(1)}, bf16[512,768]{1,0:T(8,128)(2,1)...) custom-call(s32[1]{0:T(128)} %select_n.464.refs_0_, bf16[2,512,768]{2,1,0:T(8,128)(2,1)} %refs_1_.5, ...), custom_call_target="tpu_custom_call" | custom-call | flops 14000000000 | bytes 16000000 | tf_op jit(solution)/shard_map/forward_attention0/pallas_call | solution.py:107
  40.5 3.1 route.1
  51.4 18.1 %forward_ff0.2 = (bf16[512,3072]{1,0:T(8,128)(2,1)}, bf16[512,3072]{1,0:T(8,128)(2,1)}, bf16[512,768]{1,0:T(8,128)(2,1)}, bf16[512,768]{1,0:T(8,128)(2,1)}, f32[...) custom-call(s32[1]{0:T(128)} %select_n.464.refs_0_, ...), custom_call_target="tpu_custom_call" | custom-call | flops 17999998976 | bytes 20000000 | tf_op jit(solution)/shard_map/forward_ff0/pallas_call | solution.py:107
  71.9 2.6 maximum_select_fusion.2.refs_10_
  74.5 14.2 %forward_attention0.3 = (bf16[512,2304]{1,0:T(8,128)(2,1)}, f32[16,512]{1,0:T(8,128)S(1)}, bf16[512,768]{1,0:T(8,128)(2,1)S(1)}, bf16[512,768]{1,0:T(8,128)(2,1)...) custom-call(s32[1]{0:T(128)} %bitcast.6.refs_0_, bf16[2,512,768]{2,1,0:T(8,128)(2,1)} %refs_1_.5, ...), custom_call_target="tpu_custom_call" | custom-call | flops 14000000000 | bytes 16000000 | tf_op jit(solution)/shard_map/forward_attention0/pallas_call | solution.py:107
  93.0 17.7 %forward_ff0.3 = (bf16[512,3072]{1,0:T(8,128)(2,1)}, bf16[512,3072]{1,0:T(8,128)(2,1)}, bf16[512,768]{1,0:T(8,128)(2,1)}, bf16[512,768]{1,0:T(8,128)(2,1)}, f32[...) custom-call(s32[1]{0:T(128)} %bitcast.6.refs_0_, ...), custom_call_target="tpu_custom_call" | custom-call | flops 17999998976 | bytes 20000000 | tf_op jit(solution)/shard_map/forward_ff0/pallas_call | solution.py:107
  114.7 14.2 %forward_attention1.1 = (bf16[512,2304]{1,0:T(8,128)(2,1)}, f32[16,512]{1,0:T(8,128)S(1)}, bf16[512,768]{1,0:T(8,128)(2,1)S(1)}, bf16[512,768]{1,0:T(8,128)(2,1)...) custom-call(s32[1]{0:T(128)} %constant.324.clone.1.refs_0_, ...), custom_call_target="tpu_custom_call" | custom-call | flops 14000000000 | bytes 16000000 | tf_op jit(solution)/shard_map/forward_attention1/pallas_call | solution.py:107
  130.7 18.7 %forward_ff1.1 = (bf16[512,3072]{1,0:T(8,128)(2,1)}, bf16[512,3072]{1,0:T(8,128)(2,1)}, bf16[512,768]{1,0:T(8,128)(2,1)}, bf16[512,768]{1,0:T(8,128)(2,1)}, f32[...) custom-call(s32[1]{0:T(128)} %constant.324.clone.1.refs_0_, ...), custom_call_target="tpu_custom_call" | custom-call | flops 17999998976 | bytes 20000000 | tf_op jit(solution)/shard_map/forward_ff1/pallas_call | solution.py:107
  151.8 13.5 %backward_ff1.1 = (bf16[512,768]{1,0:T(8,128)(2,1)S(1)}, bf16[512,3072]{1,0:T(8,128)(2,1)}, bf16[512,768]{1,0:T(8,128)(2,1)}, f32[512,768]{1,0:T(8,128)}, f32[8,3072]{1,0:T(8,128)S(1)}) custom-call(bf16[512,768]{1,0:T(8,128)(2,1)} %slice.325.refs_0_, bf16[512,128]{1,0:T(8,128)(2,1)S(1)} %get-tuple-element.207.refs_1_, ...), custom_call_target="tpu_custom_call" | custom-call | flops 16000000000 | bytes 22000000 | tf_op jit(solution)/shard_map/backward_ff1/pallas_call | solution.py:107
  175.1 4.7 weight_grad_cols.12.refs_9_
  179.8 4.7 weight_grad_rows.4.refs_10_
  185.0 15.9 %backward_attention1.1 = (bf16[512,2304]{1,0:T(8,128)(2,1)}, bf16[512,768]{1,0:T(8,128)(2,1)S(1)}, f32[8,3072]{1,0:T(8,128)S(1)}) custom-call(s32[1]{0:T(128)} %constant.324.clone.1.refs_0_, s32[1,512]{1,0:T(1,128)S(1)} %slice_convert_fusion.refs_2_.refs_1_, f32[16,512]{1,0:T(8,128)S(1)} %get-tuple-element.216.refs_2_, bf16[2,768,2304]{2,1,0:T(8,128)(2,1)} %refs_3_.11, ...), custom_call_target="tpu_custom_call" | custom-call | flops 20000000000 | bytes 16000000 | tf_op jit(solution)/shard_map/backward_attention1/pallas_call | solution.py:107
  205.2 2.6 dynamic-slice_bitcast_fusion
  216.8 7.7 %collective-permute-done.13 = bf16[528,768]{1,0:T(8,128)(2,1)} collective-permute-done((bf16[528,768]{1,0:T(8,128)(2,1)S(1)}, bf16[528,768]{1,0:T(8,128)(2,1)}, u32[]{:S(2)}, u32[]{:S(2)}) %collective-permute-start.13) | collective-permute-done | bytes 811040 | tf_op jit(solution)/shard_map/ppermute | solution.py:1191
  224.5 2.9 select_select_fusion.refs_13_
  227.4 5.1 weight_grad_rows.5
  232.6 2.8 constant_dynamic-slice_fusion.19
  237.1 5.5 %weight_grad_cols.14 = bf16[4,192,1536]{2,1,0:T(8,128)(2,1)} custom-call(s32[1]{0:T(128)} %bitcast.27.half_ref, bf16[512,768]{1,0:T(8,128)(2,1)S(1)} %copy-done.13, bf16[512,3072]{1,0:T(8,128)(2,1)} %get-tuple-element.220.refs_1_, bf16[4,192,1536]{2,1,0:T(8,128)(2,1)} %collective-permute-done.17.refs_2_, bf16[512,768]{1,0:T(8,128)(2,1)S(1)} %copy-done.1), custom_call_target="tpu_custom_call" | custom-call | flops 1207959552 | bytes 4718592 | tf_op jit(solution)/shard_map/weight_grad_cols/pallas_call | solution.py:769
  245.5 4.5 weight_grad_cols.16.refs_11_
  251.1 2.7 collective-permute-start.20
  254.2 13.7 %backward_ff0.2 = (bf16[512,768]{1,0:T(8,128)(2,1)S(1)}, bf16[512,3072]{1,0:T(8,128)(2,1)}, bf16[512,768]{1,0:T(8,128)(2,1)}, f32[512,768]{1,0:T(8,128)}, f32[8,3072]{1,0:T(8,128)S(1)}) custom-call(bf16[512,768]{1,0:T(8,128)(2,1)} %broadcast_select_fusion.3.refs_0_, bf16[512,128]{1,0:T(8,128)(2,1)S(1)} %get-tuple-element.234.refs_1_, ...), custom_call_target="tpu_custom_call" | custom-call | flops 16000000000 | bytes 22000000 | tf_op jit(solution)/shard_map/backward_ff0/pallas_call | solution.py:107
  267.9 4.5 collective-permute-done.20
  273.5 2.7 select_select_fusion.1.refs_0_
  281.6 4.8 weight_grad_cols.17
  291.3 13.7 %backward_ff0.3 = (bf16[512,768]{1,0:T(8,128)(2,1)}, bf16[512,3072]{1,0:T(8,128)(2,1)}, bf16[512,768]{1,0:T(8,128)(2,1)}, f32[512,768]{1,0:T(8,128)}, f32[8,3072]{1,0:T(8,128)S(1)}) custom-call(bf16[512,768]{1,0:T(8,128)(2,1)} %select_select_fusion.1.refs_0_, bf16[512,128]{1,0:T(8,128)(2,1)S(1)} %copy-done.57, f32[512,128]{1,0:T(8,128)S(1)} %copy-done.53, ...), custom_call_target="tpu_custom_call" | custom-call | flops 16000000000 | bytes 22000000 | tf_op jit(solution)/shard_map/backward_ff0/pallas_call | solution.py:107
  312.0 6.4 %weight_grad_cols.18 = bf16[4,192,1536]{2,1,0:T(8,128)(2,1)} custom-call(s32[1]{0:T(128)} %bitcast.19.half_ref, bf16[512,768]{1,0:T(8,128)(2,1)S(1)} %copy-done.8, bf16[512,768]{1,0:T(8,128)(2,1)} %get-tuple-element.196.refs_1_, bf16[512,3072]{1,0:T(8,128)(2,1)} %get-tuple-element.261.refs_2_, bf16[512,3072]{1,0:T(8,128)(2,1)} %get-tuple-element.262.refs_3_, ...), custom_call_target="tpu_custom_call" | custom-call | flops 2415919104 | bytes 7077888 | tf_op jit(solution)/shard_map/weight_grad_cols/pallas_call | solution.py:769
  318.5 6.3 %weight_grad_rows.6 = bf16[4,192,1536]{2,1,0:T(8,128)(2,1)} custom-call(s32[1]{0:T(128)} %bitcast.19.half_ref, bf16[512,3072]{1,0:T(8,128)(2,1)} %get-tuple-element.267.refs_0_, bf16[512,3072]{1,0:T(8,128)(2,1)} %get-tuple-element.268.refs_1_, bf16[512,768]{1,0:T(8,128)(2,1)S(1)} %copy-done.10, bf16[512,768]{1,0:T(8,128)(2,1)} %copy-done.5, ...), custom_call_target="tpu_custom_call" | custom-call | flops 2415919104 | bytes 7077888 | tf_op jit(solution)/shard_map/weight_grad_rows/pallas_call | solution.py:817
  329.5 3.2 weight_grad_cols.20
  341.5 6.6 %weight_grad_cols.19 = bf16[4,192,1536]{2,1,0:T(8,128)(2,1)} custom-call(s32[1]{0:T(128)} %bitcast.27.half_ref, bf16[512,768]{1,0:T(8,128)(2,1)S(1)} %copy-done.8, bf16[512,768]{1,0:T(8,128)(2,1)S(1)} %copy-done.9, bf16[512,3072]{1,0:T(8,128)(2,1)} %get-tuple-element.261.refs_2_, bf16[512,3072]{1,0:T(8,128)(2,1)} %get-tuple-element.262.refs_3_, ...), custom_call_target="tpu_custom_call" | custom-call | flops 2415919104 | bytes 7077888 | tf_op jit(solution)/shard_map/weight_grad_cols/pallas_call | solution.py:769
  348.1 2.4 constant_dynamic-slice_fusion.13.refs_9_
  352.0 6.3 %weight_grad_rows.7 = bf16[4,192,1536]{2,1,0:T(8,128)(2,1)} custom-call(s32[1]{0:T(128)} %bitcast.27.half_ref, bf16[512,3072]{1,0:T(8,128)(2,1)} %get-tuple-element.267.refs_0_, bf16[512,3072]{1,0:T(8,128)(2,1)} %get-tuple-element.268.refs_1_, bf16[512,768]{1,0:T(8,128)(2,1)S(1)} %copy-done.10, bf16[512,768]{1,0:T(8,128)(2,1)S(1)} %copy-done.6, ...), custom_call_target="tpu_custom_call" | custom-call | flops 2415919104 | bytes 7077888 | tf_op jit(solution)/shard_map/weight_grad_rows/pallas_call | solution.py:817
  365.6 15.6 %backward_attention0.2 = (bf16[512,2304]{1,0:T(8,128)(2,1)}, bf16[512,768]{1,0:T(8,128)(2,1)S(1)}, f32[8,3072]{1,0:T(8,128)S(1)}) custom-call(s32[1]{0:T(128)} %bitcast.6.refs_0_, s32[2,512]{1,0:T(2,128)S(1)} %copy-done.32, f32[16,512]{1,0:T(8,128)S(1)} %copy-done.59, bf16[2,768,2304]{2,1,0:T(8,128)(2,1)} %refs_3_.11, bf16[2,768,768]{2,1,0:T(8,128)(2,1)} %refs_4_.23, ...), custom_call_target="tpu_custom_call" | custom-call | flops 20000000000 | bytes 16000000 | tf_op jit(solution)/shard_map/backward_attention0/pallas_call | solution.py:107
  382.2 15.7 %backward_attention0.3 = (bf16[512,2304]{1,0:T(8,128)(2,1)}, bf16[512,768]{1,0:T(8,128)(2,1)S(1)}, f32[8,3072]{1,0:T(8,128)S(1)}) custom-call(s32[1]{0:T(128)} %select_n.464.refs_0_, s32[2,512]{1,0:T(2,128)S(1)} %copy-done.32, f32[16,512]{1,0:T(8,128)S(1)} %copy-done.61, bf16[2,768,2304]{2,1,0:T(8,128)(2,1)} %refs_3_.11, bf16[2,768,768]{2,1,0:T(8,128)(2,1)} %refs_4_.23, ...), custom_call_target="tpu_custom_call" | custom-call | flops 20000000000 | bytes 16000000 | tf_op jit(solution)/shard_map/backward_attention0/pallas_call | solution.py:107
  403.2 6.4 %weight_grad_cols.22 = bf16[4,192,1152]{2,1,0:T(8,128)(2,1)} custom-call(s32[1]{0:T(128)} %bitcast.19.half_ref, bf16[512,768]{1,0:T(8,128)(2,1)} %get-tuple-element.391.refs_0_, bf16[512,768]{1,0:T(8,128)(2,1)} %get-tuple-element.390.refs_1_, bf16[512,2304]{1,0:T(8,128)(2,1)} %get-tuple-element.275.refs_2_, bf16[512,2304]{1,0:T(8,128)(2,1)} %get-tuple-element.276.refs_3_, ...), custom_call_target="tpu_custom_call" | custom-call | flops 1811939328 | bytes 5701632 | tf_op jit(solution)/shard_map/weight_grad_cols/pallas_call | solution.py:769
  418.1 6.1 %weight_grad_cols.23 = bf16[4,192,1152]{2,1,0:T(8,128)(2,1)} custom-call(s32[1]{0:T(128)} %bitcast.27.half_ref, bf16[512,768]{1,0:T(8,128)(2,1)S(1)} %copy-done.4, bf16[512,768]{1,0:T(8,128)(2,1)S(1)} %copy-done.3, bf16[512,2304]{1,0:T(8,128)(2,1)} %get-tuple-element.275.refs_2_, bf16[512,2304]{1,0:T(8,128)(2,1)} %get-tuple-element.276.refs_3_, ...), custom_call_target="tpu_custom_call" | custom-call | flops 1811939328 | bytes 5701632 | tf_op jit(solution)/shard_map/weight_grad_cols/pallas_call | solution.py:769
  431.3 3.9 collective-permute-done.39
  438.0 6.8 %collective-permute-done.40 = bf16[4,96,640]{2,1,0:T(8,128)(2,1)} collective-permute-done((bf16[4,96,640]{2,1,0:T(8,128)(2,1)}, bf16[4,96,640]{2,1,0:T(8,128)(2,1)}, u32[]{:S(2)}, u32[]{:S(2)}) %collective-permute-start.40) | collective-permute-done | bytes 491552 | tf_op jit(solution)/shard_map/ppermute | solution.py:841
  449.4 3.8 collective-permute-done.41
  459.4 10.2 %collective-permute-done.45 = bf16[2,1,48,1280]{3,2,1,0:T(8,128)(2,1)S(1)} collective-permute-done((bf16[2,1,48,1280]{3,2,1,0:T(8,128)(2,1)S(1)}, bf16[2,1,48,1280]{3,2,1,0:T(8,128)(2,1)S(1)}, u32[]{:S(2)}, u32[]{:S(2)}) %collective-permute-start.45) | collective-permute-done | bytes 245792 | tf_op jit(solution)/shard_map/ppermute | solution.py:910
  472.8 4.5 collective-permute-done.46
  483.8 7.6 %collective-permute-done.51 = bf16[2,48,1280]{2,1,0:T(8,128)(2,1)S(1)} collective-permute-done((bf16[2,48,1280]{2,1,0:T(8,128)(2,1)S(1)}, bf16[2,48,1280]{2,1,0:T(8,128)(2,1)S(1)}, u32[]{:S(2)}, u32[]{:S(2)}) %collective-permute-start.51) | collective-permute-done | bytes 245792 | tf_op jit(solution)/shard_map/ppermute | solution.py:841
  491.5 3.0 collective-permute-done.48
  494.9 5.0 place_layer1.1
  500.7 6.6 %all-gather.5.cloned.1.call-done.ff_ref = bf16[8,48,3456]{2,1,0:T(8,128)(2,1)} async-done(((bf16[1,48,3456]{2,1,0:T(8,128)(2,1)}), bf16[8,48,3456]{2,1,0:T(8,128)(2,1)}) %all-gather.5.cloned.1.call-update) | async-done | bytes 2654224 | tf_op jit(solution)/shard_map/all_gather | solution.py:1315
  507.3 4.9 place_layer0.1
  (494 shorter events, 144.5 us)
Async XLA Ops:
  7.2 356.4 %reduce-scatter.4.cloned.1.call-start = ((), (), s32[]{:S(2)}) async-start(), calls=%async_computation.3 | async-start | bytes 1658880 | tf_op jit(solution)/shard_map/reduce_scatter | solution.py:927
  14.8 34.4 %collective-permute-start.3 = (bf16[528,768]{1,0:T(8,128)(2,1)}, bf16[528,768]{1,0:T(8,128)(2,1)}, u32[]{:S(2)}, u32[]{:S(2)}) collective-permute-start(bf16[528,768]{1,0:T(8,128)(2,1)} %pad_maximum_fusion.6.refs_9_), channel_id=1, source_target_pairs={{0,1},{1,0},{2,3},{3,2},{4,5},{5,4},{6,7},{7,6},{8,9},{9,8},{10,11... | collective-permute-start | bytes 2433032 | tf_op jit(solution)/shard_map/ppermute | solution.py:1191
  17.8 31.4 %collective-permute-start.4 = (bf16[528,768]{1,0:T(8,128)(2,1)}, bf16[528,768]{1,0:T(8,128)(2,1)}, u32[]{:S(2)}, u32[]{:S(2)}) collective-permute-start(bf16[528,768]{1,0:T(8,128)(2,1)} %pad_maximum_fusion.6.refs_9_), channel_id=1, source_target_pairs={{0,4},{1,2},{2,1},{3,7},{4,0},{5,6},{6,5},{7,3},{8,12},{9,10},{10,... | collective-permute-start | bytes 2433032 | tf_op jit(solution)/shard_map/ppermute | solution.py:1192
  18.5 22.0 %collective-permute-start = (s32[1]{0:T(128)}, s32[1]{0:T(128)}, u32[]{:S(2)}, u32[]{:S(2)}) collective-permute-start(s32[1]{0:T(128)} %bitcast.2.refs_0_), channel_id=1, source_target_pairs={{0,1},{1,2},{2,3},{3,0},{4,5},{5,6},{6,7},{7,4},{8,9},{9,10},{10,1... | collective-permute-start | bytes 20 | tf_op jit(solution)/shard_map/ppermute | solution.py:1170
  21.6 18.9 %collective-permute-start.1 = (s32[1]{0:T(128)}, s32[1]{0:T(128)}, u32[]{:S(2)}, u32[]{:S(2)}) collective-permute-start(s32[1]{0:T(128)} %bitcast.2.refs_0_), channel_id=1, source_target_pairs={{0,2},{1,3},{2,0},{3,1},{4,6},{5,7},{6,4},{7,5},{8,10},{9,11},{10,... | collective-permute-start | bytes 20 | tf_op jit(solution)/shard_map/ppermute | solution.py:1170
  21.6 18.9 %collective-permute-start.2 = (s32[1]{0:T(128)}, s32[1]{0:T(128)}, u32[]{:S(2)}, u32[]{:S(2)}) collective-permute-start(s32[1]{0:T(128)} %bitcast.2.refs_0_), channel_id=1, source_target_pairs={{0,3},{1,0},{2,1},{3,2},{4,7},{5,4},{6,5},{7,6},{8,11},{9,8},{10,9... | collective-permute-start | bytes 20 | tf_op jit(solution)/shard_map/ppermute | solution.py:1170
  50.5 21.4 %collective-permute-start.5 = (bf16[528,768]{1,0:T(8,128)(2,1)S(1)}, bf16[528,768]{1,0:T(8,128)(2,1)S(1)}, u32[]{:S(2)}, u32[]{:S(2)}) collective-permute-start(bf16[528,768]{1,0:T(8,128)(2,1)S(1)} %broadcast_select_fusion.1.refs_17_), channel_id=1, source_target_pairs={{0,1},{1,0},{2,3},{3,2},{4,5},{5,4},{6,7},{7,6},{8,9},{9,8},{10,11... | collective-permute-start | bytes 2433032 | tf_op jit(solution)/shard_map/ppermute | solution.py:1191
  50.6 21.3 %collective-permute-start.6 = (bf16[528,768]{1,0:T(8,128)(2,1)S(1)}, bf16[528,768]{1,0:T(8,128)(2,1)S(1)}, u32[]{:S(2)}, u32[]{:S(2)}) collective-permute-start(bf16[528,768]{1,0:T(8,128)(2,1)S(1)} %broadcast_select_fusion.1.refs_17_), channel_id=1, source_target_pairs={{0,4},{1,2},{2,1},{3,7},{4,0},{5,6},{6,5},{7,3},{8,12},{9,10},{10,... | collective-permute-start | bytes 2433032 | tf_op jit(solution)/shard_map/ppermute | solution.py:1192
  69.5 20.1 %collective-permute-start.7 = (bf16[512,768]{1,0:T(8,128)(2,1)}, bf16[512,768]{1,0:T(8,128)(2,1)S(1)}, u32[]{:S(2)}, u32[]{:S(2)}) collective-permute-start(bf16[512,768]{1,0:T(8,128)(2,1)} %get-tuple-element.193.refs_9_), channel_id=1, source_target_pairs={{0,1},{1,0},{2,3},{3,2},{4,5},{5,4},{6,7},{7,6},{8,9},{9,8},{10,11... | collective-permute-start | bytes 2359304 | tf_op jit(solution)/shard_map/ppermute | solution.py:1191
  71.9 17.8 %collective-permute-start.8 = (bf16[512,768]{1,0:T(8,128)(2,1)}, bf16[512,768]{1,0:T(8,128)(2,1)S(1)}, u32[]{:S(2)}, u32[]{:S(2)}) collective-permute-start(bf16[512,768]{1,0:T(8,128)(2,1)} %get-tuple-element.193.refs_9_), channel_id=1, source_target_pairs={{0,4},{1,2},{2,1},{3,7},{4,0},{5,6},{6,5},{7,3},{8,12},{9,10},{10,... | collective-permute-start | bytes 2359304 | tf_op jit(solution)/shard_map/ppermute | solution.py:1192
  90.8 21.0 %collective-permute-start.10 = (bf16[512,768]{1,0:T(8,128)(2,1)}, bf16[512,768]{1,0:T(8,128)(2,1)S(1)}, u32[]{:S(2)}, u32[]{:S(2)}) collective-permute-start(bf16[512,768]{1,0:T(8,128)(2,1)} %broadcast_select_fusion.4.refs_17_), channel_id=1, source_target_pairs={{0,4},{1,2},{2,1},{3,7},{4,0},{5,6},{6,5},{7,3},{8,12},{9,10},{10,... | collective-permute-start | bytes 2359304 | tf_op jit(solution)/shard_map/ppermute | solution.py:1192
  91.3 20.5 %collective-permute-start.9 = (bf16[512,768]{1,0:T(8,128)(2,1)}, bf16[512,768]{1,0:T(8,128)(2,1)S(1)}, u32[]{:S(2)}, u32[]{:S(2)}) collective-permute-start(bf16[512,768]{1,0:T(8,128)(2,1)} %broadcast_select_fusion.4.refs_17_), channel_id=1, source_target_pairs={{0,1},{1,0},{2,3},{3,2},{4,5},{5,4},{6,7},{7,6},{8,9},{9,8},{10,11... | collective-permute-start | bytes 2359304 | tf_op jit(solution)/shard_map/ppermute | solution.py:1191
  151.4 18.6 %collective-permute-start.11 = (bf16[528,768]{1,0:T(8,128)(2,1)}, bf16[528,768]{1,0:T(8,128)(2,1)}, u32[]{:S(2)}, u32[]{:S(2)}) collective-permute-start(bf16[528,768]{1,0:T(8,128)(2,1)} %fusion.1.refs_11_), channel_id=1, source_target_pairs={{0,1},{1,0},{2,3},{3,2},{4,5},{5,4},{6,7},{7,6},{8,9},{9,8},{10,11... | collective-permute-start | bytes 2433032 | tf_op jit(solution)/shard_map/ppermute | solution.py:1191
  151.8 18.3 %collective-permute-start.12 = (bf16[528,768]{1,0:T(8,128)(2,1)}, bf16[528,768]{1,0:T(8,128)(2,1)}, u32[]{:S(2)}, u32[]{:S(2)}) collective-permute-start(bf16[528,768]{1,0:T(8,128)(2,1)} %fusion.1.refs_11_), channel_id=1, source_target_pairs={{0,4},{1,2},{2,1},{3,7},{4,0},{5,6},{6,5},{7,3},{8,12},{9,10},{10,... | collective-permute-start | bytes 2433032 | tf_op jit(solution)/shard_map/ppermute | solution.py:1192
  184.5 42.9 %collective-permute-start.18 = (bf16[4,192,1536]{2,1,0:T(8,128)(2,1)}, bf16[4,192,1536]{2,1,0:T(8,128)(2,1)}, u32[]{:S(2)}, u32[]{:S(2)}) collective-permute-start(bf16[4,192,1536]{2,1,0:T(8,128)(2,1)} %weight_grad_rows.4.refs_10_), channel_id=1, source_target_pairs={{0,4},{4,0},{8,12},{12,8},{16,20},{20,16},{24,28},{28,24},{1,5},{5... | collective-permute-start | bytes 7077896 | tf_op jit(solution)/shard_map/ppermute | solution.py:841
  184.5 52.6 %collective-permute-start.17 = (bf16[4,192,1536]{2,1,0:T(8,128)(2,1)}, bf16[4,192,1536]{2,1,0:T(8,128)(2,1)}, u32[]{:S(2)}, u32[]{:S(2)}) collective-permute-start(bf16[4,192,1536]{2,1,0:T(8,128)(2,1)} %weight_grad_cols.12.refs_9_), channel_id=1, source_target_pairs={{0,4},{4,0},{8,12},{12,8},{16,20},{20,16},{24,28},{28,24},{1,5},{5... | collective-permute-start | bytes 7077896 | tf_op jit(solution)/shard_map/ppermute | solution.py:841
  202.5 8.1 %collective-permute-start.23 = (bf16[1,4,192,128]{3,2,1,0:T(8,128)(2,1)}, bf16[1,4,192,128]{3,2,1,0:T(8,128)(2,1)}, u32[]{:S(2)}, u32[]{:S(2)}) collective-permute-start(bf16[1,4,192,128]{3,2,1,0:T(8,128)(2,1)} %fusion.5), channel_id=1, source_target_pairs={{0,4},{4,0},{8,12},{12,8},{16,20},{20,16},{24,28},{28,24},{1,5},{5... | collective-permute-start | bytes 589832 | tf_op jit(solution)/shard_map/ppermute | solution.py:841
  203.5 21.0 %collective-permute-start.13 = (bf16[528,768]{1,0:T(8,128)(2,1)S(1)}, bf16[528,768]{1,0:T(8,128)(2,1)}, u32[]{:S(2)}, u32[]{:S(2)}) collective-permute-start(bf16[528,768]{1,0:T(8,128)(2,1)S(1)} %copy-done.2), channel_id=1, source_target_pairs={{0,1},{1,0},{2,3},{3,2},{4,5},{5,4},{6,7},{7,6},{8,9},{9,8},{10,11... | collective-permute-start | bytes 2433032 | tf_op jit(solution)/shard_map/ppermute | solution.py:1191
  205.2 19.3 %collective-permute-start.14 = (bf16[528,768]{1,0:T(8,128)(2,1)S(1)}, bf16[528,768]{1,0:T(8,128)(2,1)}, u32[]{:S(2)}, u32[]{:S(2)}) collective-permute-start(bf16[528,768]{1,0:T(8,128)(2,1)S(1)} %copy-done.2), channel_id=1, source_target_pairs={{0,4},{1,2},{2,1},{3,7},{4,0},{5,6},{6,5},{7,3},{8,12},{9,10},{10,... | collective-permute-start | bytes 2433032 | tf_op jit(solution)/shard_map/ppermute | solution.py:1192
  215.0 35.1 %collective-permute-start.15 = (bf16[512,768]{1,0:T(8,128)(2,1)S(1)}, bf16[512,768]{1,0:T(8,128)(2,1)S(1)}, u32[]{:S(2)}, u32[]{:S(2)}) collective-permute-start(bf16[512,768]{1,0:T(8,128)(2,1)S(1)} %get-tuple-element.223.refs_3_), channel_id=1, source_target_pairs={{0,1},{1,0},{2,3},{3,2},{4,5},{5,4},{6,7},{7,6},{8,9},{9,8},{10,11... | collective-permute-start | bytes 2359304 | tf_op jit(solution)/shard_map/ppermute | solution.py:1191
  224.5 25.6 %collective-permute-start.16 = (bf16[512,768]{1,0:T(8,128)(2,1)S(1)}, bf16[512,768]{1,0:T(8,128)(2,1)S(1)}, u32[]{:S(2)}, u32[]{:S(2)}) collective-permute-start(bf16[512,768]{1,0:T(8,128)(2,1)S(1)} %copy-done.1), channel_id=1, source_target_pairs={{0,4},{1,2},{2,1},{3,7},{4,0},{5,6},{6,5},{7,3},{8,12},{9,10},{10,... | collective-permute-start | bytes 2359304 | tf_op jit(solution)/shard_map/ppermute | solution.py:1192
  235.5 43.6 %collective-permute-start.25 = (bf16[4,96,1920]{2,1,0:T(8,128)(2,1)S(1)}, bf16[4,96,1920]{2,1,0:T(8,128)(2,1)}, u32[]{:S(2)}, u32[]{:S(2)}) collective-permute-start(bf16[4,96,1920]{2,1,0:T(8,128)(2,1)S(1)} %pad_maximum_fusion.refs_3_), channel_id=1, source_target_pairs={{0,16},{4,20},{8,24},{12,28},{16,0},{20,4},{24,8},{28,12},{1,17},{... | collective-permute-start | bytes 4423688 | tf_op jit(solution)/shard_map/ppermute | solution.py:841
  244.0 32.2 %collective-permute-start.24 = (bf16[4,96,1536]{2,1,0:T(8,128)(2,1)S(1)}, bf16[4,96,1536]{2,1,0:T(8,128)(2,1)}, u32[]{:S(2)}, u32[]{:S(2)}) collective-permute-start(bf16[4,96,1536]{2,1,0:T(8,128)(2,1)S(1)} %constant_dynamic-slice_fusion.25.refs_2_), channel_id=1, source_target_pairs={{0,8},{4,12},{8,0},{12,4},{16,24},{20,28},{24,16},{28,20},{1,9},{5... | collective-permute-start | bytes 3538952 | tf_op jit(solution)/shard_map/ppermute | solution.py:841
  250.0 31.6 %collective-permute-start.22 = (bf16[4,192,1152]{2,1,0:T(8,128)(2,1)}, bf16[4,192,1152]{2,1,0:T(8,128)(2,1)}, u32[]{:S(2)}, u32[]{:S(2)}) collective-permute-start(bf16[4,192,1152]{2,1,0:T(8,128)(2,1)} %weight_grad_cols.16.refs_11_), channel_id=1, source_target_pairs={{0,4},{4,0},{8,12},{12,8},{16,20},{20,16},{24,28},{28,24},{1,5},{5... | collective-permute-start | bytes 5308424 | tf_op jit(solution)/shard_map/ppermute | solution.py:841
  251.1 21.2 %collective-permute-start.20 = (bf16[512,768]{1,0:T(8,128)(2,1)}, bf16[512,768]{1,0:T(8,128)(2,1)S(1)}, u32[]{:S(2)}, u32[]{:S(2)}) collective-permute-start(bf16[512,768]{1,0:T(8,128)(2,1)} %broadcast_select_fusion.2.refs_12_), channel_id=1, source_target_pairs={{0,1},{1,0},{2,3},{3,2},{4,5},{5,4},{6,7},{7,6},{8,9},{9,8},{10,11... | collective-permute-start | bytes 2359304 | tf_op jit(solution)/shard_map/ppermute | solution.py:1191
  253.8 18.5 %collective-permute-start.21 = (bf16[512,768]{1,0:T(8,128)(2,1)}, bf16[512,768]{1,0:T(8,128)(2,1)S(1)}, u32[]{:S(2)}, u32[]{:S(2)}) collective-permute-start(bf16[512,768]{1,0:T(8,128)(2,1)} %broadcast_select_fusion.2.refs_12_), channel_id=1, source_target_pairs={{0,4},{1,2},{2,1},{3,7},{4,0},{5,6},{6,5},{7,3},{8,12},{9,10},{10,... | collective-permute-start | bytes 2359304 | tf_op jit(solution)/shard_map/ppermute | solution.py:1192
  277.9 27.1 %collective-permute-start.26 = (bf16[4,48,1536]{2,1,0:T(8,128)(2,1)S(1)}, bf16[4,48,1536]{2,1,0:T(8,128)(2,1)S(1)}, u32[]{:S(2)}, u32[]{:S(2)}) collective-permute-start(bf16[4,48,1536]{2,1,0:T(8,128)(2,1)S(1)} %constant_dynamic-slice_fusion.20.refs_13_), channel_id=1, source_target_pairs={{0,16},{4,20},{8,24},{12,28},{16,0},{20,4},{24,8},{28,12},{1,17},{... | collective-permute-start | bytes 1769480 | tf_op jit(solution)/shard_map/ppermute | solution.py:841
  281.0 24.2 %collective-permute-start.27 = (bf16[4,48,1920]{2,1,0:T(8,128)(2,1)S(1)}, bf16[4,48,1920]{2,1,0:T(8,128)(2,1)S(1)}, u32[]{:S(2)}, u32[]{:S(2)}) collective-permute-start(bf16[4,48,1920]{2,1,0:T(8,128)(2,1)S(1)} %constant_dynamic-slice_fusion.17.refs_14_), channel_id=1, source_target_pairs={{0,8},{4,12},{8,0},{12,4},{16,24},{20,28},{24,16},{28,20},{1,9},{5... | collective-permute-start | bytes 2211848 | tf_op jit(solution)/shard_map/ppermute | solution.py:841
  289.0 17.9 %collective-permute-start.29 = (bf16[4,96,640]{2,1,0:T(8,128)(2,1)}, bf16[4,96,640]{2,1,0:T(8,128)(2,1)}, u32[]{:S(2)}, u32[]{:S(2)}) collective-permute-start(bf16[4,96,640]{2,1,0:T(8,128)(2,1)} %pad_maximum_fusion.7.refs_12_), channel_id=1, source_target_pairs={{0,16},{4,20},{8,24},{12,28},{16,0},{20,4},{24,8},{28,12},{1,17},{... | collective-permute-start | bytes 1474568 | tf_op jit(solution)/shard_map/ppermute | solution.py:841
  289.8 20.1 %collective-permute-start.28 = (bf16[4,96,640]{2,1,0:T(8,128)(2,1)S(1)}, bf16[4,96,640]{2,1,0:T(8,128)(2,1)}, u32[]{:S(2)}, u32[]{:S(2)}) collective-permute-start(bf16[4,96,640]{2,1,0:T(8,128)(2,1)S(1)} %constant_dynamic-slice_fusion.22.refs_11_), channel_id=1, source_target_pairs={{0,8},{4,12},{8,0},{12,4},{16,24},{20,28},{24,16},{28,20},{1,9},{5... | collective-permute-start | bytes 1474568 | tf_op jit(solution)/shard_map/ppermute | solution.py:841
  318.4 22.7 %collective-permute-start.30 = (bf16[4,192,1536]{2,1,0:T(8,128)(2,1)}, bf16[4,192,1536]{2,1,0:T(8,128)(2,1)}, u32[]{:S(2)}, u32[]{:S(2)}) collective-permute-start(bf16[4,192,1536]{2,1,0:T(8,128)(2,1)} %weight_grad_cols.18), channel_id=1, source_target_pairs={{0,4},{4,0},{8,12},{12,8},{16,20},{20,16},{24,28},{28,24},{1,5},{5... | collective-permute-start | bytes 7077896 | tf_op jit(solution)/shard_map/ppermute | solution.py:841
  324.8 27.2 %collective-permute-start.31 = (bf16[4,192,1536]{2,1,0:T(8,128)(2,1)}, bf16[4,192,1536]{2,1,0:T(8,128)(2,1)}, u32[]{:S(2)}, u32[]{:S(2)}) collective-permute-start(bf16[4,192,1536]{2,1,0:T(8,128)(2,1)} %weight_grad_rows.6), channel_id=1, source_target_pairs={{0,4},{4,0},{8,12},{12,8},{16,20},{20,16},{24,28},{28,24},{1,5},{5... | collective-permute-start | bytes 7077896 | tf_op jit(solution)/shard_map/ppermute | solution.py:841
  333.5 83.7 %reduce-scatter.6.cloned.1.call-start = ((), (), s32[]{:S(2)}) async-start(), calls=%async_computation.5 | async-start | bytes 614400 | tf_op jit(solution)/shard_map/reduce_scatter | solution.py:927
  336.3 15.7 %collective-permute-start.33 = (bf16[4,48,640]{2,1,0:T(8,128)(2,1)S(1)}, bf16[4,48,640]{2,1,0:T(8,128)(2,1)S(1)}, u32[]{:S(2)}, u32[]{:S(2)}) collective-permute-start(bf16[4,48,640]{2,1,0:T(8,128)(2,1)S(1)} %constant_dynamic-slice_fusion.16.refs_5_), channel_id=1, source_target_pairs={{0,16},{4,20},{8,24},{12,28},{16,0},{20,4},{24,8},{28,12},{1,17},{... | collective-permute-start | bytes 737288 | tf_op jit(solution)/shard_map/ppermute | solution.py:841
  337.3 14.7 %collective-permute-start.34 = (bf16[4,48,640]{2,1,0:T(8,128)(2,1)S(1)}, bf16[4,48,640]{2,1,0:T(8,128)(2,1)S(1)}, u32[]{:S(2)}, u32[]{:S(2)}) collective-permute-start(bf16[4,48,640]{2,1,0:T(8,128)(2,1)S(1)} %constant_dynamic-slice_fusion.14.refs_6_), channel_id=1, source_target_pairs={{0,8},{4,12},{8,0},{12,4},{16,24},{20,28},{24,16},{28,20},{1,9},{5... | collective-permute-start | bytes 737288 | tf_op jit(solution)/shard_map/ppermute | solution.py:841
  350.6 47.4 %collective-permute-start.35 = (bf16[4,96,1536]{2,1,0:T(8,128)(2,1)}, bf16[4,96,1536]{2,1,0:T(8,128)(2,1)}, u32[]{:S(2)}, u32[]{:S(2)}) collective-permute-start(bf16[4,96,1536]{2,1,0:T(8,128)(2,1)} %constant_dynamic-slice_fusion.13.refs_9_), channel_id=1, source_target_pairs={{0,8},{4,12},{8,0},{12,4},{16,24},{20,28},{24,16},{28,20},{1,9},{5... | collective-permute-start | bytes 3538952 | tf_op jit(solution)/shard_map/ppermute | solution.py:841
  361.4 38.6 %collective-permute-start.37 = (bf16[4,96,1920]{2,1,0:T(8,128)(2,1)}, bf16[4,96,1920]{2,1,0:T(8,128)(2,1)}, u32[]{:S(2)}, u32[]{:S(2)}) collective-permute-start(bf16[4,96,1920]{2,1,0:T(8,128)(2,1)} %pad_maximum_fusion.1.refs_10_), channel_id=1, source_target_pairs={{0,16},{4,20},{8,24},{12,28},{16,0},{20,4},{24,8},{28,12},{1,17},{... | collective-permute-start | bytes 4423688 | tf_op jit(solution)/shard_map/ppermute | solution.py:841
  363.5 53.7 %all-gather.3.cloned.1.call-start = ((), (), s32[]{:S(2)}) async-start(), calls=%async_computation.4 | async-start | bytes 2985984 | tf_op jit(solution)/shard_map/all_gather | solution.py:1315
  382.2 90.6 %reduce-scatter.8.cloned.1.call-start = ((), (), s32[]{:S(2)}) async-start(), calls=%async_computation.6 | async-start | bytes 1658880 | tf_op jit(solution)/shard_map/reduce_scatter | solution.py:927
  414.3 15.8 %collective-permute-start.36 = (bf16[4,48,1536]{2,1,0:T(8,128)(2,1)S(1)}, bf16[4,48,1536]{2,1,0:T(8,128)(2,1)}, u32[]{:S(2)}, u32[]{:S(2)}) collective-permute-start(bf16[4,48,1536]{2,1,0:T(8,128)(2,1)S(1)} %constant_dynamic-slice_fusion.10.refs_4_), channel_id=1, source_target_pairs={{0,16},{4,20},{8,24},{12,28},{16,0},{20,4},{24,8},{28,12},{1,17},{... | collective-permute-start | bytes 1769480 | tf_op jit(solution)/shard_map/ppermute | solution.py:841
  415.6 19.5 %collective-permute-start.39 = (bf16[4,48,1920]{2,1,0:T(8,128)(2,1)S(1)}, bf16[4,48,1920]{2,1,0:T(8,128)(2,1)}, u32[]{:S(2)}, u32[]{:S(2)}) collective-permute-start(bf16[4,48,1920]{2,1,0:T(8,128)(2,1)S(1)} %constant_dynamic-slice_fusion.7.refs_5_), channel_id=1, source_target_pairs={{0,8},{4,12},{8,0},{12,4},{16,24},{20,28},{24,16},{28,20},{1,9},{5... | collective-permute-start | bytes 2211848 | tf_op jit(solution)/shard_map/ppermute | solution.py:841
  426.4 18.5 %collective-permute-start.40 = (bf16[4,96,640]{2,1,0:T(8,128)(2,1)}, bf16[4,96,640]{2,1,0:T(8,128)(2,1)}, u32[]{:S(2)}, u32[]{:S(2)}) collective-permute-start(bf16[4,96,640]{2,1,0:T(8,128)(2,1)} %constant_dynamic-slice_fusion.6), channel_id=1, source_target_pairs={{0,8},{4,12},{8,0},{12,4},{16,24},{20,28},{24,16},{28,20},{1,9},{5... | collective-permute-start | bytes 1474568 | tf_op jit(solution)/shard_map/ppermute | solution.py:841
  428.1 18.7 %collective-permute-start.43 = (bf16[4,96,640]{2,1,0:T(8,128)(2,1)}, bf16[4,96,640]{2,1,0:T(8,128)(2,1)}, u32[]{:S(2)}, u32[]{:S(2)}) collective-permute-start(bf16[4,96,640]{2,1,0:T(8,128)(2,1)} %pad_maximum_fusion.9), channel_id=1, source_target_pairs={{0,16},{4,20},{8,24},{12,28},{16,0},{20,4},{24,8},{28,12},{1,17},{... | collective-permute-start | bytes 1474568 | tf_op jit(solution)/shard_map/ppermute | solution.py:841
  437.6 69.6 %all-gather.5.cloned.1.call-start = ((), (), s32[]{:S(2)}) async-start(), calls=%async_computation.7 | async-start | bytes 2985984 | tf_op jit(solution)/shard_map/all_gather | solution.py:1315
  455.1 14.5 %collective-permute-start.45 = (bf16[2,1,48,1280]{3,2,1,0:T(8,128)(2,1)S(1)}, bf16[2,1,48,1280]{3,2,1,0:T(8,128)(2,1)S(1)}, u32[]{:S(2)}, u32[]{:S(2)}) collective-permute-start(bf16[2,1,48,1280]{3,2,1,0:T(8,128)(2,1)S(1)} %constant_dynamic-slice_fusion.1), channel_id=1, source_target_pairs={{0,1},{1,0},{2,3},{3,2},{4,5},{5,4},{6,7},{7,6},{8,9},{9,8},{10,11... | collective-permute-start | bytes 737288 | tf_op jit(solution)/shard_map/ppermute | solution.py:910
  458.6 14.2 %collective-permute-start.50 = (bf16[1,48,1280]{2,1,0:T(8,128)(2,1)S(1)}, bf16[1,48,1280]{2,1,0:T(8,128)(2,1)S(1)}, u32[]{:S(2)}, u32[]{:S(2)}) collective-permute-start(bf16[1,48,1280]{2,1,0:T(8,128)(2,1)S(1)} %copy-done.25), channel_id=1, source_target_pairs={{0,16},{4,20},{8,24},{12,28},{16,0},{20,4},{24,8},{28,12},{1,17},{... | collective-permute-start | bytes 368648 | tf_op jit(solution)/shard_map/ppermute | solution.py:841
  478.8 12.5 %collective-permute-start.51 = (bf16[2,48,1280]{2,1,0:T(8,128)(2,1)S(1)}, bf16[2,48,1280]{2,1,0:T(8,128)(2,1)S(1)}, u32[]{:S(2)}, u32[]{:S(2)}) collective-permute-start(bf16[2,48,1280]{2,1,0:T(8,128)(2,1)S(1)} %maximum_bitcast_fusion.1), channel_id=1, source_target_pairs={{0,8},{4,12},{8,0},{12,4},{16,24},{20,28},{24,16},{28,20},{1,9},{5... | collective-permute-start | bytes 737288 | tf_op jit(solution)/shard_map/ppermute | solution.py:841
  482.4 12.1 %collective-permute-start.48 = (bf16[2,48,1280]{2,1,0:T(8,128)(2,1)S(1)}, bf16[2,48,1280]{2,1,0:T(8,128)(2,1)S(1)}, u32[]{:S(2)}, u32[]{:S(2)}) collective-permute-start(bf16[2,48,1280]{2,1,0:T(8,128)(2,1)S(1)} %maximum_bitcast_fusion), channel_id=1, source_target_pairs={{0,8},{4,12},{8,0},{12,4},{16,24},{20,28},{24,16},{28,20},{1,9},{5... | collective-permute-start | bytes 737288 | tf_op jit(solution)/shard_map/ppermute | solution.py:841
  (119 other events, 866.1 us)
Sparse Core Ops, SparseCore 0:
  333.6 29.7 reduce-scatter.3
  365.7 20.1 reduce-scatter.5
  388.0 28.5 all-gather.2
  437.8 34.9 reduce-scatter.7
  474.7 32.5 all-gather.4

commit v2 on v1

--- a/solution.py
+++ b/solution.py
@@ -16,10 +16,12 @@
 REACH = 256
 EPS = 1e-12
 MASKED = -1e30
+SEGMENTS = 4
 HIGH = lax.Precision.HIGHEST
 F32 = jnp.float32
 BF16 = jnp.bfloat16
 LIMIT = 52 * 1024 * 1024
+BRIEF = pl.CostEstimate(flops=10**6, bytes_accessed=10**5, transcendentals=0)
 
 NN = (((1,), (0,)), ((), ()))
 NT = (((1,), (1,)), ((), ()))
@@ -72,13 +74,14 @@
     return start, stop
 
 
-def fill_bias(seg_ref, row, bias_ref):
-    length = bias_ref.shape[0]
+def fill_codes(seg_ref, row, code_q, code_k):
+    length = code_q.shape[0]
     seg_row = seg_ref[pl.ds(row, 1), :].astype(F32)
     seg_cols = jnp.broadcast_to(seg_row, (LANES, length)).T
-    for start in range(0, length, LANES):
-        same = seg_cols == seg_row[:, start : start + LANES]
-        bias_ref[:, start : start + LANES] = jnp.where(same, 0.0, MASKED)
+    lane = lax.broadcasted_iota(jnp.int32, (length, LANES), 1) % HEAD
+    same = seg_cols == lane.astype(F32)
+    code_q[...] = jnp.where(same, 1.0, 0.0).astype(BF16)
+    code_k[...] = jnp.where(same | (lane >= SEGMENTS), 0.0, MASKED).astype(BF16)
 
 
 ANY = pl.BlockSpec(memory_space=pl.ANY)
@@ -156,17 +159,18 @@
     hat,
     first,
     full,
-    bias,
+    code_q,
+    code_k,
     terms_ref,
     sems,
 ):
     row = row_ref[0]
     length, width = x_ref.shape
     copy = copier(sems)
-    get_x = copy(x_hbm.at[row], x_ref, 0)
+    get_x = copy(x_hbm.at[row, pl.ds(0, length)], x_ref, 0)
     get_in = copy(w_in_hbm.at[layer], w_in, 1)
     get_out = copy(w_out_hbm.at[layer], w_out, 2)
-    fill_bias(seg_ref, row, bias)
+    fill_codes(seg_ref, row, code_q, code_k)
     terms_ref[...] = jnp.zeros_like(terms_ref)
     lse_ref[...] = jnp.zeros_like(lse_ref)
     get_x.wait()
@@ -192,12 +196,14 @@
         values_t = qkv[:, pl.ds(at + 2 * width, LANES)].T
         outs = []
         for sub in range(2):
-            mine = jnp.where(low_half == (sub == 0), keys, jnp.zeros_like(keys))
-            scores = mm(mine, queries, NT)
+            mine = low_half == (sub == 0)
+            scores = mm(
+                jnp.where(mine, keys, code_k[...]), jnp.where(mine, queries, code_q[...]), NT
+            )
             tops = []
             for cols in chunks(length):
                 start, stop = window(cols.start, length)
-                part = scores[start:stop, cols] + bias[start:stop, cols]
+                part = scores[start:stop, cols]
                 top = jnp.max(part, 0, keepdims=True)
                 terms_ref[sub, start:stop, cols] = jnp.exp(part - top).astype(BF16)
                 tops.append(top)
@@ -231,7 +237,7 @@
 
 def forward_attention(layer, row, x, seg, weights, after=()):
     w_in, qv, w_out, out_b, gain, shift = weights[:6]
-    length, width = x.shape[-2], x.shape[-1]
+    length, width = seg.shape[-1], x.shape[-1]
     outs = (
         low(length, 3 * width),
         full(16, length),
@@ -257,7 +263,8 @@
             vm(outs[3]),
             vm(outs[4]),
             vm(outs[5]),
-            pltpu.VMEM((length, length), F32),
+            pltpu.VMEM((length, LANES), BF16),
+            pltpu.VMEM((length, LANES), BF16),
             pltpu.VMEM((2, length, length), BF16),
             pltpu.SemaphoreType.DMA((8,)),
         ],
@@ -273,6 +280,8 @@
     first_hbm,
     full_hbm,
     cot_ref,
+    seg_ref,
+    later_ref,
     w_fi_hbm,
     w_fo_hbm,
     gain_ref,
@@ -292,7 +301,6 @@
     h_hbm,
     spread_ref,
     d_upper_ref,
-    logit_ref,
     small_ref,
     first,
     full,
@@ -310,12 +318,15 @@
     ff = w_fi.shape[1]
     copy = copier(sems)
     get_first = copy(first_hbm, first, 0)
-    get_fi = copy(w_fi_hbm.at[layer], w_fi, 1)
+    part = even.shape[1]
+    get_fi = [
+        copy(w_fi_hbm.at[layer, :, pl.ds(at, part)], w_fi.at[:, pl.ds(at, part)], 8 + at // part)
+        for at in range(0, ff, part)
+    ]
     get_full = copy(full_hbm, full, 2)
     get_fo = copy(w_fo_hbm.at[layer], w_fo, 3)
     get_first.wait()
-    get_fi.wait()
-    part = even.shape[1]
+    get_fi[0].wait()
 
     def multiply(at, into):
         into[...] = mm(first[...], w_fi[:, pl.ds(at, part)])
@@ -328,6 +339,8 @@
             slope[rows, pl.ds(at, part)] = grad.astype(BF16)
 
     multiply(0, even)
+    for made in get_fi[1:]:
+        made.wait()
     steps = ff // part // 2
 
     def inner(number, carry):
@@ -354,11 +367,10 @@
         h[rows, :] = (normed * gain + shift).astype(BF16)
         spread_ref[rows, :] = jnp.broadcast_to(spread, (CHUNK, LANES))
     put_hat = copy(hat, hat_hbm, 6)
-    put_h = copy(h, h_hbm, 7)
 
     stu_width = proj_ref.shape[2]
     stu_scale = (stu_width // STU_HEADS) ** -0.5
-    hidden = h[...]
+    hidden = h[:length, :]
     upper = mm(hidden, proj_ref[layer]) + vec(proj_b_ref, layer, 0, stu_width)
     query = vec(query_ref, layer, 0, stu_width)
     lane_full = lax.broadcasted_iota(jnp.int32, (length, stu_width), 1)
@@ -384,7 +396,17 @@
     z = jnp.tanh(
         mm_high(jnp.broadcast_to(pooled, eight), dense) + vec(dense_b_ref, layer, 0, stu_width)
     )
-    logit_ref[...] = mm_high(z, cls) + vec(cls_b_ref, layer, 0, LANES)
+    logits = mm_high(z, cls) + vec(cls_b_ref, layer, 0, LANES)
+    below = lax.broadcasted_iota(jnp.int32, (16, length), 0)
+    segments = jnp.broadcast_to(seg_ref[pl.ds(row_ref[0], 1), :].astype(F32), (16, length))
+    later = jnp.broadcast_to(later_ref[pl.ds(row_ref[0], 1), :], (16, LANES))
+    tail = jnp.where(below == 1, segments, 0.0)
+    narrow_tail = jnp.where(below[:, :LANES] == 2, later, tail[:, :LANES])
+    narrow_tail = jnp.where(below[:, :LANES] == 0, jnp.concatenate([logits, logits], 0), narrow_tail)
+    h[length:, :LANES] = narrow_tail.astype(BF16)
+    h[length:, LANES:length] = tail[:, LANES:].astype(BF16)
+    h[length:, length:] = jnp.zeros((16, width - length), BF16)
+    put_h = copy(h, h_hbm, 7)
     cot = cot_ref[pl.ds(row_ref[0], 1), :]
     d_pre = mm_high(jnp.broadcast_to(cot, (8, LANES)), cls, NT) * (1.0 - z * z)
     d_pooled = mm_high(d_pre, dense, NT)[:1]
@@ -414,7 +436,7 @@
         made.wait()
 
 
-def forward_ff(layer, row, first, first_full, cot, weights, after=()):
+def forward_ff(layer, row, first, first_full, cot, seg, later, weights, after=()):
     gain, shift, w_fi, fi_b, w_fo, fo_b = weights[4:10]
     length, width = first.shape
     ff = w_fi.shape[2]
@@ -423,19 +445,19 @@
         low(length, ff),
         low(length, ff),
         low(length, width),
-        low(length, width),
+        low(length + 16, width),
         full(length, LANES),
         low(length, stu),
-        full(8, LANES),
         full(width + 2 * stu + 8, LANES),
     )
     return call(
         partial(forward_ff_kernel, layer),
         f"forward_ff{layer}",
         outs,
-        (ANY,) * 4 + (WHOLE,) * 4,
-        (row, first, first_full, cot, w_fi, w_fo, gain, shift, fi_b, fo_b) + tuple(weights[10:]),
-        [SCALAR, ANY, ANY, WHOLE, ANY, ANY] + [WHOLE] * 11,
+        (ANY,) * 4 + (WHOLE,) * 3,
+        (row, first, first_full, cot, seg, later, w_fi, w_fo, gain, shift, fi_b, fo_b)
+        + tuple(weights[10:]),
+        [SCALAR, ANY, ANY, WHOLE, WHOLE, WHOLE, ANY, ANY] + [WHOLE] * 11,
         [
             pltpu.VMEM((length, width), BF16),
             pltpu.VMEM((length, width), F32),
@@ -447,7 +469,7 @@
             vm(outs[3]),
             pltpu.VMEM((length, 512), F32),
             pltpu.VMEM((length, 512), F32),
-            pltpu.SemaphoreType.DMA((8,)),
+            pltpu.SemaphoreType.DMA((8 + ff // 512,)),
         ],
         after,
         18 * 10**9,
@@ -563,7 +585,7 @@
 
 def backward_ff(layer, grad, saved1, saved2, weights, after=()):
     _, _, _, hat1, _, _, spread1 = saved1
-    slope, _, hat2, _, spread2, d_upper, _, _ = saved2
+    slope, _, hat2, _, spread2, d_upper, _ = saved2
     gain, _, w_fi, _, w_fo, _ = weights[4:10]
     length, width = grad.shape
     ff = w_fi.shape[2]
@@ -622,7 +644,8 @@
     d_resid,
     d_qkv,
     d_mix,
-    bias,
+    code_q,
+    code_k,
     delta_ref,
     probs_ref,
     ds_ref,
@@ -636,7 +659,7 @@
     get_qkv = copy(qkv_hbm, qkv, 3)
     get_in = copy(w_in_hbm.at[layer], w_in, 4)
     get_resid = copy(resid_hbm, d_resid, 5)
-    fill_bias(seg_ref, row_ref[0], bias)
+    fill_codes(seg_ref, row_ref[0], code_q, code_k)
     probs_ref[...] = jnp.zeros_like(probs_ref)
     ds_ref[...] = jnp.zeros_like(ds_ref)
     sums_ref[...] = jnp.zeros_like(sums_ref)
@@ -671,13 +694,13 @@
             lse = lse_ref[pl.ds(head, 1), :]
             delta = delta_ref[pl.ds(head, 1), :]
             mine = low_half == (sub == 0)
-            scores = mm(jnp.where(mine, keys, zero), queries, NT)
+            scores = mm(
+                jnp.where(mine, keys, code_k[...]), jnp.where(mine, queries, code_q[...]), NT
+            )
             d_probs = mm(jnp.where(mine, values, zero), mix, NT)
             for rows in chunks(length):
                 start, stop = window(rows.start, length)
-                probs = jnp.exp(
-                    scores[rows, start:stop] + bias[rows, start:stop] - lse[:, start:stop]
-                )
+                probs = jnp.exp(scores[rows, start:stop] - lse[:, start:stop])
                 probs_ref[sub, rows, start:stop] = probs.astype(BF16)
                 ds_ref[sub, rows, start:stop] = (
                     probs * (d_probs[rows, start:stop] - delta[:, start:stop])
@@ -727,7 +750,8 @@
             vm(d_resid),
             vm(outs[0]),
             vm(outs[1]),
-            pltpu.VMEM((length, length), F32),
+            pltpu.VMEM((length, LANES), BF16),
+            pltpu.VMEM((length, LANES), BF16),
             pltpu.VMEM((16, length), F32),
             pltpu.VMEM((2, length, length), BF16),
             pltpu.VMEM((2, length, length), BF16),
@@ -739,12 +763,13 @@
     )
 
 
-def pick_cols_kernel(half_ref, *refs, rows, recv):
+def grad_cols_kernel(half_ref, *refs, rows, steps):
     lefts, rights = refs[:rows], refs[rows : 2 * rows]
-    out_ref, turned = refs[-2], refs[-1]
+    other_ref, own_ref, turned = refs[-3:]
     length = lefts[0].shape[0]
-
-    @pl.when(pl.program_id(0) == 0)
+    step = pl.program_id(0)
+
+    @pl.when(step == 0)
     def _():
         for number, left in enumerate(lefts):
             turned[:, number * length : (number + 1) * length] = left[...].T
@@ -753,87 +778,108 @@
     for number, right in enumerate(rights):
         part = mm(turned[:, number * length : (number + 1) * length], right[...])
         found = part if found is None else found + part
-    found = found.reshape(out_ref.shape)
-    if recv:
-        found = found + refs[2 * rows][...].astype(F32)
-    out_ref[...] = found.astype(BF16)
-
-
-def weight_grad_cols(half, lefts, rights, narrow, recv=None, after=()):
+    found = found.reshape(own_ref.shape).astype(BF16)
+
+    @pl.when(step < steps)
+    def _():
+        other_ref[...] = found
+
+    @pl.when(step >= steps)
+    def _():
+        own_ref[...] = found
+
+
+def weight_grad_cols(half, lefts, rights, narrow, after=()):
     rows = len(lefts)
     length, width = lefts[0].shape
     cols = rights[0].shape[1] // 2
-    tile = next((size for size in (512, 384) if cols % size == 0), cols)
+    tile = next((size for size in (768, 384) if cols % size == 0), cols)
     steps = cols // tile
-    out_block = pl.BlockSpec((narrow, width // narrow, tile), lambda j, half: (0, 0, j))
+    shape = jax.ShapeDtypeStruct((narrow, width // narrow, cols), BF16)
+    block = (narrow, width // narrow, tile)
+
+    def right_at(j, half):
+        mine = jnp.where(j < steps, 1 - half[0], half[0])
+        return (0, mine * steps + jnp.where(j < steps, j, j - steps))
+
     return pl.pallas_call(
-        partial(pick_cols_kernel, rows=rows, recv=recv is not None),
-        out_shape=jax.ShapeDtypeStruct((narrow, width // narrow, cols), BF16),
+        partial(grad_cols_kernel, rows=rows, steps=steps),
+        out_shape=(shape, shape),
         grid_spec=pltpu.PrefetchScalarGridSpec(
             num_scalar_prefetch=1,
-            grid=(steps,),
+            grid=(2 * steps,),
             in_specs=[pl.BlockSpec((length, width), lambda j, half: (0, 0))] * rows
-            + [pl.BlockSpec((length, tile), lambda j, half: (0, half[0] * steps + j))] * rows
-            + [out_block] * (recv is not None)
+            + [pl.BlockSpec((length, tile), right_at)] * rows
             + [ANY] * len(after),
-            out_specs=out_block,
+            out_specs=(
+                pl.BlockSpec(block, lambda j, half: (0, 0, jnp.minimum(j, steps - 1))),
+                pl.BlockSpec(block, lambda j, half: (0, 0, jnp.maximum(j - steps, 0))),
+            ),
             scratch_shapes=[pltpu.VMEM((width, rows * length), BF16)],
         ),
         compiler_params=pltpu.CompilerParams(vmem_limit_bytes=LIMIT),
-        cost_estimate=pl.CostEstimate(
-            flops=2 * rows * length * width * cols,
-            bytes_accessed=2 * (rows * length * (width + cols) + width * cols),
-            transcendentals=0,
-        ),
+        cost_estimate=BRIEF,
         name="weight_grad_cols",
-    )(half, *lefts, *rights, *(() if recv is None else (recv,)), *after)
-
-
-def pick_rows_kernel(half_ref, *refs, rows, recv):
+    )(half, *lefts, *rights, *after)
+
+
+def grad_rows_kernel(half_ref, *refs, rows, narrow):
     lefts, rights = refs[:rows], refs[rows : 2 * rows]
-    out_ref = refs[-1]
-    unit = out_ref.shape[1]
+    other_ref, own_ref = refs[-2:]
+    unit = own_ref.shape[1]
     width = rights[0].shape[1]
     found = None
     for left, right in zip(lefts, rights):
         part = mm(left[...], right[...], TN)
         found = part if found is None else found + part
-    for block in range(out_ref.shape[2] // width):
-        cols = slice(block * width, (block + 1) * width)
-        part = found[block * unit : (block + 1) * unit]
-        if recv:
-            part = part + refs[2 * rows][0, :, cols].astype(F32)
-        out_ref[0, :, cols] = part.astype(BF16)
-
-
-def weight_grad_rows(half, lefts, rights, narrow, recv=None, after=()):
+    found = found.astype(BF16)
+
+    def write(ref):
+        for block in range(ref.shape[2] // width):
+            ref[0, :, block * width : (block + 1) * width] = found[
+                block * unit : (block + 1) * unit
+            ]
+
+    @pl.when(pl.program_id(0) < narrow)
+    def _():
+        write(other_ref)
+
+    @pl.when(pl.program_id(0) >= narrow)
+    def _():
+        write(own_ref)
+
+
+def weight_grad_rows(half, lefts, rights, narrow, after=()):
     rows = len(lefts)
     length, deep = lefts[0].shape
     width = rights[0].shape[1]
     unit = width // narrow
     part = deep // narrow // 2
     cols = part // unit * width
-    out_block = pl.BlockSpec((1, unit, cols), lambda j, half: (j, 0, 0))
+    shape = jax.ShapeDtypeStruct((narrow, unit, cols), BF16)
+
+    def left_at(j, half):
+        first = j < narrow
+        return (0, 2 * jnp.where(first, j, j - narrow) + jnp.where(first, 1 - half[0], half[0]))
+
     return pl.pallas_call(
-        partial(pick_rows_kernel, rows=rows, recv=recv is not None),
-        out_shape=jax.ShapeDtypeStruct((narrow, unit, cols), BF16),
+        partial(grad_rows_kernel, rows=rows, narrow=narrow),
+        out_shape=(shape, shape),
         grid_spec=pltpu.PrefetchScalarGridSpec(
             num_scalar_prefetch=1,
-            grid=(narrow,),
-            in_specs=[pl.BlockSpec((length, part), lambda j, half: (0, 2 * j + half[0]))] * rows
+            grid=(2 * narrow,),
+            in_specs=[pl.BlockSpec((length, part), left_at)] * rows
             + [pl.BlockSpec((length, width), lambda j, half: (0, 0))] * rows
-            + [out_block] * (recv is not None)
             + [ANY] * len(after),
-            out_specs=out_block,
+            out_specs=(
+                pl.BlockSpec((1, unit, cols), lambda j, half: (jnp.minimum(j, narrow - 1), 0, 0)),
+                pl.BlockSpec((1, unit, cols), lambda j, half: (jnp.maximum(j - narrow, 0), 0, 0)),
+            ),
         ),
         compiler_params=pltpu.CompilerParams(vmem_limit_bytes=LIMIT),
-        cost_estimate=pl.CostEstimate(
-            flops=rows * length * deep * width,
-            bytes_accessed=rows * length * (deep + 2 * width) + deep * width,
-            transcendentals=0,
-        ),
+        cost_estimate=BRIEF,
         name="weight_grad_rows",
-    )(half, *lefts, *rights, *(() if recv is None else (recv,)), *after)
+    )(half, *lefts, *rights, *after)
 
 
 def swap(value, bit):
@@ -897,7 +943,7 @@
         return jnp.concatenate(mine, -1)
 
 
-def narrow_sum_swaps(mine):
+def narrow_sum_swaps(mine, ons=(None, None)):
     size = lax.axis_size("narrow")
     place = lax.axis_index("narrow")
     cur = mine.reshape((2,) * (size.bit_length() - 1) + mine.shape[1:])
@@ -906,17 +952,18 @@
         bit = 1 << level
         axis = depth - 1 - level
         keep, give = halves(cur, (place // bit) % 2, axis)
-        cur = add_low(
-            keep, lax.ppermute(give, "narrow", [(i, i ^ bit) for i in range(size)])
-        )
+        recv = lax.ppermute(give, "narrow", [(i, i ^ bit) for i in range(size)])
+        if level < len(ons) and ons[level] is not None:
+            recv = tie(recv, ons[level])
+        cur = add_low(keep, recv)
     return cur.reshape(mine.shape[1:])
 
 
-def wide_gather_swaps(mine):
+def wide_gather_swaps(mine, got=None):
     place = lax.axis_index("wide")
     cur = mine[None]
-    for bit in wide_bits()[::-1]:
-        other = swap(cur, bit)
+    for number, bit in enumerate(wide_bits()[::-1]):
+        other = got[None] if number == 0 and got is not None else swap(cur, bit)
         upper = (place // bit) % 2 == 1
         cur = jnp.stack([jnp.where(upper, other, cur), jnp.where(upper, cur, other)])
         cur = cur.reshape((-1,) + mine.shape)
@@ -927,101 +974,158 @@
     return lax.psum_scatter(mine, "narrow", scatter_dimension=0, tiled=True)[0]
 
 
-def small_pack(small, sums, narrow):
-    stu = small.shape[1]
-    width = small.shape[0] - 2 * stu - 8
+def small_pack_kernel(smalls, *refs):
+    small_refs, sums_refs = refs[:smalls], refs[smalls:-4]
+    out_ref, small, sums, rest = refs[-4:]
+    _, narrow, unit, lanes = out_ref.shape
+    width = narrow * unit
+    stu = lanes
+    share = stu // narrow
     deep = sums.shape[1]
+    small[...] = sum(ref[...] for ref in small_refs)
+    sums[...] = sum(ref[...] for ref in sums_refs)
+    own = width + 2 * stu
+    vectors = [
+        (sums, 1, 0, 2 * width),
+        (sums, 2, 2 * width, width),
+        (sums, 1, 2 * width, 2 * width),
+        (sums, 2, 0, 2 * width),
+        (sums, 0, 0, deep),
+        (sums, 2, 3 * width, width),
+        (small, own, 0, stu),
+        (small, own + 1, 0, stu),
+        (small, own + 2, 0, stu),
+    ]
+    for place in range(narrow):
+        out_ref[0, place] = small[place * unit : (place + 1) * unit, :].astype(BF16)
+        rest[...] = jnp.zeros_like(rest)
+        for number in range(2):
+            start = width + number * stu + place * share
+            rest[number * share : (number + 1) * share, :] = small[start : start + share, :]
+        row = 2 * share
+        for ref, line, start, size in vectors:
+            size = size // narrow
+            value = ref[line : line + 1, :][:, start + place * size : start + (place + 1) * size]
+            for at in range(0, size, lanes):
+                part = min(lanes, size - at)
+                rest[row : row + 1, :part] = value[:, at : at + part]
+                row += 1
+        rest[row : row + 1, :] = small[own + 3 : own + 4, :]
+        out_ref[1, place] = rest[...].astype(BF16)
+
+
+def small_pack(smalls, sums, narrow):
+    stu = smalls[0].shape[1]
+    width = smalls[0].shape[0] - 2 * stu - 8
     unit = width // narrow
-    proj = small[:width].reshape(narrow, unit, stu)
-    split = small[width : width + 2 * stu].reshape(2, narrow, stu // narrow, stu)
-    own = small[width + 2 * stu :]
-    vectors = [
-        sums[1, : 2 * width],
-        sums[2, 2 * width : 3 * width],
-        sums[1, 2 * width :],
-        sums[2, : 2 * width],
-        sums[0],
-        sums[2, 3 * width :],
-    ]
-    vectors = [value.reshape(narrow, -1) for value in vectors]
-    vectors += [own[i].reshape(narrow, -1) for i in range(3)]
-    vectors += [jnp.broadcast_to(own[3], (narrow, stu))]
-    rows = [
-        jnp.pad(value, ((0, 0), (0, -value.shape[1] % LANES))).reshape(narrow, -1, LANES)
-        for value in vectors
-    ]
-    rest = jnp.concatenate([split[0], split[1]] + rows, 1)
-    rest = jnp.pad(rest, ((0, 0), (0, unit - rest.shape[1]), (0, 0)))
-    return jnp.stack([proj, rest]).astype(BF16)
-
-
-def place_kernel(layer, orders, turned, aliased, ff_ref, at_ref, *refs):
-    outs, small = refs[aliased : aliased + 4], refs[aliased + 4]
-    ai, ao, fi, fo, sems = refs[aliased + 5 :]
+    return pl.pallas_call(
+        partial(small_pack_kernel, len(smalls)),
+        out_shape=low(2, narrow, unit, stu),
+        in_specs=[WHOLE] * (len(smalls) + len(sums)),
+        out_specs=WHOLE,
+        scratch_shapes=[vm(smalls[0]), vm(sums[0]), pltpu.VMEM((unit, stu), F32)],
+        cost_estimate=BRIEF,
+        name="small_pack",
+    )(*smalls, *sums)
+
+
+def place_rows(orders, place, rows):
+    found = []
+    for order in orders:
+        at = 0
+        for bit in order:
+            at = 2 * at + (place // bit) % 2
+        found.append(at * rows)
+    return found
+
+
+def turn_bits(place, total):
+    count = (total - 1).bit_length()
+    return sum(((place >> i) & 1) << (count - 1 - i) for i in range(count))
+
+
+def place_ff_kernel(layer, orders, turned, held, got_ref, *refs):
+    outs = refs[held : held + 3]
+    fi, fo, ao, sems = refs[held + 3 :]
     unit, deep = fi.shape
     width = ao.shape[1]
-    total, rows, _ = ff_ref.shape
-    count = (total - 1).bit_length()
-    half_in, half_out = ai.shape[1] // 2, width // 2
-    cut = at_ref.shape[2] // 2
-    rest = half_in - cut
+    half = width // 2
+    total, rows, _ = got_ref.shape
     blocks = fo.shape[0] // unit // 2
-
-    def put(number, src):
-        made = pltpu.make_async_copy(src, outs[number].at[layer], sems.at[number])
-        made.start()
-        return made
-
-    def starts(place):
-        found = []
-        for order in orders:
-            at = 0
-            for bit in order:
-                at = 2 * at + (place // bit) % 2
-            found.append(at * rows)
-        return found
-
     for place in range(total):
         core = place % 2
-        x_at, y_at = starts(place)
-        get = lambda start, size: ff_ref[place, :, start : start + size].astype(F32)
+        x_at, y_at = place_rows(orders, place, rows)
+        at = turn_bits(place, total) if turned else place
+        get = lambda start, size, at=at: got_ref[at, :, start : start + size].astype(F32)
         fi[x_at : x_at + rows, core * deep // 2 : (core + 1) * deep // 2] = get(0, deep // 2)
         for block in range(blocks):
             at = (core * blocks + block) * unit + y_at
             fo[at : at + rows, :] = get(deep // 2 + block * width, width)
-        ao[y_at : y_at + rows, core * half_out : (core + 1) * half_out] = get(deep, half_out)
-    puts = [put(2, fi), put(3, fo), put(1, ao)]
+        ao[y_at : y_at + rows, core * half : (core + 1) * half] = get(deep, half)
+    puts = []
+    for number, (src, dst) in enumerate(zip((fi, fo, ao), outs)):
+        puts.append(pltpu.make_async_copy(src, dst.at[layer], sems.at[number]))
+        puts[-1].start()
+    for made in puts:
+        made.wait()
+
+
+def place_attn_kernel(layer, orders, held, got_ref, *refs):
+    out, small = refs[held], refs[held + 1]
+    ai, sem = refs[held + 2 :]
+    total, rows, cols = got_ref.shape
+    half = ai.shape[1] // 2
+    cut = cols // 2
+    rest = half - cut
     for place in range(total):
         core = place % 2
-        x_at, y_at = starts(place)
-        held = place
-        if turned:
-            held = sum(((place >> i) & 1) << (count - 1 - i) for i in range(count))
-        get = lambda start, size: at_ref[held, :, start : start + size].astype(F32)
-        start = core * half_in
+        x_at, y_at = place_rows(orders, place, rows)
+        at = turn_bits(place, total)
+        get = lambda start, size: got_ref[at, :, start : start + size].astype(F32)
+        start = core * half
         ai[x_at : x_at + rows, start : start + cut] = get(0, cut)
-        ai[y_at : y_at + rows, start + cut : start + half_in] = get(cut, rest)
+        ai[y_at : y_at + rows, start + cut : start + half] = get(cut, rest)
         small[y_at : y_at + rows, core * LANES : (core + 1) * LANES] = get(cut + rest, LANES)
-    puts.append(put(0, ai))
-    for made in puts:
-        made.wait()
-
-
-def place_layer(layer, ff, at, turned, shapes, previous=()):
-    unit = shapes[0].shape[1]
+    made = pltpu.make_async_copy(ai, out.at[layer], sem)
+    made.start()
+    made.wait()
+
+
+def place_ff(layer, got, turned, shapes, previous=()):
     held = len(previous)
     return pl.pallas_call(
-        partial(place_kernel, layer, [bit_order(turn) for turn in range(2)], turned, held),
-        out_shape=tuple(shapes) + (full(unit, 2 * LANES),),
-        in_specs=[WHOLE, WHOLE] + [ANY] * held,
-        out_specs=(ANY,) * 4 + (WHOLE,),
+        partial(place_ff_kernel, layer, [bit_order(turn) for turn in range(2)], turned, held),
+        out_shape=tuple(shapes),
+        in_specs=[WHOLE] + [ANY] * held,
+        out_specs=(ANY,) * 3,
         scratch_shapes=[pltpu.VMEM(shape.shape[1:], F32) for shape in shapes]
-        + [pltpu.SemaphoreType.DMA((4,))],
-        input_output_aliases={2 + i: i for i in range(held)},
+        + [pltpu.SemaphoreType.DMA((3,))],
+        input_output_aliases={1 + i: i for i in range(held)},
         compiler_params=pltpu.CompilerParams(vmem_limit_bytes=LIMIT),
-        cost_estimate=pl.CostEstimate(flops=10**6, bytes_accessed=11 * 10**6, transcendentals=0),
-        name=f"place_layer{layer}",
-    )(ff, at, *previous)
+        cost_estimate=pl.CostEstimate(flops=10**6, bytes_accessed=8 * 10**6, transcendentals=0),
+        name=f"place_ff{layer}",
+    )(got, *previous)
+
+
+def place_attn(layer, got, shape, previous=(), after=()):
+    held = len(previous)
+
+    def body(got_ref, *refs):
+        kept = refs[:held] + refs[held + len(after) :]
+        place_attn_kernel(layer, orders, held, got_ref, *kept)
+
+    orders = [bit_order(turn) for turn in range(2)]
+    return pl.pallas_call(
+        body,
+        out_shape=(shape, full(shape.shape[1], 2 * LANES)),
+        in_specs=[WHOLE] + [ANY] * (held + len(after)),
+        out_specs=(ANY, WHOLE),
+        scratch_shapes=[pltpu.VMEM(shape.shape[1:], F32), pltpu.SemaphoreType.DMA],
+        input_output_aliases={1 + i: i for i in range(held)},
+        compiler_params=pltpu.CompilerParams(vmem_limit_bytes=LIMIT),
+        cost_estimate=pl.CostEstimate(flops=10**6, bytes_accessed=3 * 10**6, transcendentals=0),
+        name=f"place_attn{layer}",
+    )(got, *previous, *after)
 
 
 def place_small_kernel(first_ref, second_ref, proj_ref, dense_ref, cls_ref, *vec_refs):
@@ -1165,7 +1269,17 @@
     wide_cot = jnp.pad(logit_cot.astype(F32), ((0, 0), (0, 0), (0, blank)))
 
     alive = exit_layer == 1
-    mine = jnp.sum(alive.astype(jnp.int32)).reshape(1)
+    row_a = jnp.where(alive[0], 0, jnp.where(alive[1], 1, 0)).astype(jnp.int32)
+    row_b = 1 - row_a
+
+    index = lambda row: row.reshape(1)
+    first_row = jnp.zeros((1,), jnp.int32)
+    own = index(core)
+    ia, ib = index(row_a), index(row_b)
+    early_cot, late_cot = wide_cot[:, 0], wide_cot[:, 1]
+    a1 = forward_attention(0, ia, tokens, segments, weights)
+
+    mine = tie(jnp.sum(alive.astype(jnp.int32)).reshape(1), a1[4])
     around = [mine] + [
         lax.ppermute(mine, "narrow", [(i, (i + step) % narrow) for i in range(narrow)])
         for step in range(1, narrow)
@@ -1174,8 +1288,6 @@
     from_left1, from_left2, use_two, use_b, use_a, on_right, sent_left, is_far, a_alive, b_alive = (
         flags[i] == 1 for i in range(10)
     )
-    row_a = jnp.where(alive[0], 0, jnp.where(alive[1], 1, 0)).astype(jnp.int32)
-    row_b = 1 - row_a
 
     even = me % 2 == 0
     inner = [(i, i ^ 1) for i in range(narrow)]
@@ -1213,41 +1325,28 @@
     def row_of(value, row):
         return lax.dynamic_index_in_dim(value, row, 0, False)
 
-    def cot_pack(row):
-        tail = jnp.zeros((16, width), BF16)
-        tail = tail.at[0, :length].set(row_of(segments, row).astype(BF16))
-        tail = tail.at[1, :classes].set(row_of(logit_cot[:, 1], row))
-        return jnp.concatenate([row_of(out_cot, row), tail], 0)
-
-    index = lambda row: row.reshape(1)
-    first_row = jnp.zeros((1,), jnp.int32)
-    own, other = index(core), index(1 - core)
-    ia, ib = index(row_a), index(row_b)
-    early_cot = wide_cot[:, 0]
-
-    pack_a, pack_b = cot_pack(row_a), cot_pack(row_b)
-    pair = shift(pack_a)
-    a1 = forward_attention(0, ia, tokens, segments, weights, (pack_a,))
-    pack_one = out_one(tie(pair, a1[4]))
-    pair = shift(pack_one)
-    a2 = forward_ff(0, ia, a1[4], a1[5], early_cot, weights, (pack_one,))
-    work_pack = out_two(tie(pair, a2[3]), pack_one, pack_a, pack_b)
+    cot_a, cot_b = row_of(out_cot, row_a), row_of(out_cot, row_b)
+    pair = shift(tie(cot_a, a1[4]))
+    a2 = forward_ff(0, ia, a1[4], a1[5], early_cot, segments, late_cot, weights, (cot_a,))
+    cot_one = out_one(tie(pair, a2[3]))
     pair = shift(a2[3])
-    b1 = forward_attention(0, ib, tokens, segments, weights, (a2[3], work_pack))
+    b1 = forward_attention(0, ib, tokens, segments, weights, (a2[3], cot_one))
     one = out_one(tie(pair, b1[4]))
     pair = shift(one)
-    b2 = forward_ff(0, ib, b1[4], b1[5], early_cot, weights, (one,))
+    b2 = forward_ff(0, ib, b1[4], b1[5], early_cot, segments, late_cot, weights, (one,))
     work_in = out_two(tie(pair, b2[3]), one, a2[3], b2[3])
-    work_seg = work_pack[length : length + 1, :length].astype(jnp.int32)
-    work_cot = work_pack[length + 1 : length + 2, :LANES].astype(F32)
-
+    work_seg = work_in[length + 1 : length + 2, :length].astype(jnp.int32)
+    work_late = work_in[length + 2 : length + 3, :LANES].astype(F32)
+
+    pair = shift(tie(cot_one, b2[3]))
     w1 = forward_attention(1, first_row, work_in[None], work_seg, weights)
-    w2 = forward_ff(1, first_row, w1[4], w1[5], work_cot, weights)
-    sent_h = jnp.concatenate(
-        [w2[3], jnp.pad(w2[6], ((0, 8), (0, width - LANES))).astype(BF16)], 0
-    )
+    work_cot = out_two(tie(pair, w1[4]), cot_one, cot_a, cot_b)
+    w2 = forward_ff(
+        1, first_row, w1[4], w1[5], work_late, work_seg, work_late, weights, (work_cot,)
+    )
+    sent_h = w2[3]
     pair_h = shift(sent_h)
-    w3 = backward_ff(1, work_pack[:length], w1, w2, weights, (sent_h,))
+    w3 = backward_ff(1, work_cot, w1, w2, weights, (sent_h,))
 
     def ff_jobs(saved1, saved2, back):
         first = [s[4] for s in saved1]
@@ -1260,14 +1359,14 @@
             (weight_grad_cols, mixed, branch),
         )
 
-    def give_half(jobs, after=()):
-        return [job(other, lefts, rights, narrow, None, after) for job, lefts, rights in jobs]
-
-    def own_half(jobs, sent, after=()):
-        return [
-            job(own, lefts, rights, narrow, swap(value, 1), after)
-            for (job, lefts, rights), value in zip(jobs, sent)
-        ]
+    def weight_grads(jobs, after=()):
+        return [job(own, lefts, rights, narrow, after) for job, lefts, rights in jobs]
+
+    def core_sum(pairs, on=None):
+        received = [swap(other, 1) for other, _ in pairs]
+        if on is not None:
+            received = tie(received, on)
+        return [add_low(mine, recv) for (_, mine), recv in zip(pairs, received)]
 
     def ff_halving(parts):
         return Halving([[parts[0]], [parts[1], parts[2]]])
@@ -1278,86 +1377,86 @@
         cut = (part.shape[-1] + LANES) // 2
         return Halving([[part[..., :cut]], [part[..., cut:], small]])
 
-    jobs = ff_jobs([w1], [w2], [w3])
-    forth_h = back_one(tie(pair_h, w3[2]))
+    halves1 = weight_grads(ff_jobs([w1], [w2], [w3]))
+    sent = tuple(pair[0] for pair in halves1)
+    w4 = backward_attention(1, first_row, work_seg, w1, w3[2], w3[3], weights, sent)
+    pair_x = shift(w4[1])
+    ff1 = ff_halving(core_sum(halves1))
+    flying = ff1.step()
+    half1 = weight_grads(((weight_grad_cols, [work_in[:length]], [w4[0]]),), tuple(flying))
+    small1 = small_pack([w2[6]], [w3[4], w4[2]], narrow)
+    forth_x = back_one(tie(pair_x, half1[0][0]))
+    pair_x2 = shift(forth_x)
+
+    base_b = jnp.where(b_alive, w4[1], row_of(out_cot, row_b))
+    b3 = backward_ff(0, base_b, b1, b2, weights, (half1[0][0], forth_x, small1))
+    far_x = back_two(w4[1], pair_x, tie(pair_x2, b3[2]))
+    forth_h = back_one(tie(pair_h, far_x))
     pair_h2 = shift(forth_h)
-    sent = give_half(jobs, (forth_h,))
-    w4 = backward_attention(1, first_row, work_seg, w1, w3[2], w3[3], weights, tuple(sent))
-    pair_x = shift(w4[1])
-    parts = own_half(jobs, sent, (w4[1],))
-    ff1 = ff_halving(parts)
-    flying = ff1.step()
-    jobs1 = ((weight_grad_cols, [work_in], [w4[0]]),)
-    sent1 = give_half(jobs1, tuple(flying))
-    forth_x = back_one(tie(pair_x, sent1[0]))
-    pair_x2 = shift(forth_x)
-    far_h = back_two(sent_h, pair_h, tie(pair_h2, w4[1]))
-
-    base_b = jnp.where(b_alive, w4[1], row_of(out_cot, row_b))
-    b3 = backward_ff(0, base_b, b1, b2, weights, (*sent1, forth_x, far_h))
-    far_x = back_two(w4[1], pair_x, tie(pair_x2, b3[2]))
-    part1 = own_half(jobs1, sent1, (b3[0],))[0]
-    at1 = attn_halving(part1, small_pack(w2[7], w3[4] + w4[2], narrow))
+    at1 = attn_halving(core_sum(half1)[0], small1)
     flying = at1.step() + ff1.step(b3[2])
     base_a = jnp.where(a_alive, far_x, row_of(out_cot, row_a))
-    a3 = backward_ff(0, base_a, a1, a2, weights, tuple(flying))
+    a3 = backward_ff(0, base_a, a1, a2, weights, (*flying, forth_h))
     mine_ff1 = ff1.finish(a3[2])
     flying = at1.step(a3[2])
-    jobs = ff_jobs([a1, b1], [a2, b2], [a3, b3])
-    sent = give_half(jobs, (mine_ff1, *flying))
-    sum_ff1 = narrow_sum(mine_ff1)
-    ff0 = ff_halving(own_half(jobs, sent))
+    halves0 = weight_grads(ff_jobs([a1, b1], [a2, b2], [a3, b3]), (mine_ff1, *flying))
+    ff0 = ff_halving(core_sum(halves0))
     flying = ff0.step()
-    mine_at1 = at1.finish(flying[0])
+    mine_at1 = at1.finish(halves0[-1][0])
+    far_h = back_two(sent_h, pair_h, tie(pair_h2, a3[2]))
     b4 = backward_attention(
-        0, ib, segments, b1, b3[2], b3[3], weights, (*flying, sum_ff1, mine_at1)
-    )
-    every = lambda value: lax.all_gather(value, "wide", axis=0, tiled=False)
+        0, ib, segments, b1, b3[2], b3[3], weights, (*flying, mine_at1, far_h)
+    )
     sum_at1 = narrow_sum(mine_at1)
-    all_ff1 = every(sum_ff1)
+    sum_ff1 = narrow_sum_swaps(mine_ff1, (halves0[1][0], b4[1]))
+    flying = ff0.step(b4[1])
     a4 = backward_attention(
-        0, ia, segments, a1, a3[2], a3[3], weights, (b4[1],)
-    )
-    flying = ff0.step(a4[1])
-    jobs0 = (
+        0, ia, segments, a1, a3[2], a3[3], weights, (b4[1], sum_at1, sum_ff1, *flying)
+    )
+    mine_ff0 = ff0.finish(a4[1])
+    sum_ff0 = narrow_sum(mine_ff0)
+    half0 = weight_grads(
         (
-            weight_grad_cols,
-            [row_of(tokens, row_a), row_of(tokens, row_b)],
-            [a4[0], b4[0]],
+            (
+                weight_grad_cols,
+                [row_of(tokens, row_a), row_of(tokens, row_b)],
+                [a4[0], b4[0]],
+            ),
         ),
-    )
-    sent0 = give_half(jobs0, tuple(flying))
-    part0 = own_half(jobs0, sent0, (all_ff1, sum_at1))[0]
-    at0 = attn_halving(
-        part0, small_pack(a2[7] + b2[7], a3[4] + b3[4] + a4[2] + b4[2], narrow)
-    )
+        (mine_ff0,),
+    )
+    small0 = small_pack([a2[6], b2[6]], [a3[4], b3[4], a4[2], b4[2]], narrow)
+    at0 = attn_halving(core_sum(half0)[0], small0)
     flying = at0.step()
-    sum_ff0 = narrow_sum(ff0.finish(flying[0]))
-    all_at0 = wide_gather_swaps(narrow_sum_swaps(at0.finish()))
+    all_ff1 = wide_gather_swaps(tie(sum_ff1, flying[0]))
+    got = swap(tie(sum_at1, flying), wide_bits()[-1])
+    all_at1 = wide_gather_swaps(sum_at1, got)
+    all_ff0 = lax.all_gather(tie(sum_ff0, got), "wide", axis=0, tiled=False)
+    all_at0 = wide_gather_swaps(narrow_sum_swaps(at0.finish(), (sum_ff0,)))
 
     deep = ff_in.shape[2]
-    shapes = [
-        full(2, width // narrow, 3 * width),
-        full(2, width // narrow, width),
-        full(2, width // narrow, deep),
-        full(2, deep // narrow, width),
-    ]
-    *large, small1 = place_layer(1, all_ff1, wide_gather_swaps(tie(sum_at1, part0)), True, shapes)
-    *large, small0 = place_layer(0, every(sum_ff0), all_at0, True, shapes, large)
+    unit = width // narrow
+    shapes = [full(2, unit, deep), full(2, deep // narrow, width), full(2, unit, width)]
+    attn_shape = full(2, unit, 3 * width)
+    placed = place_ff(1, all_ff1, True, shapes)
+    d_attn_in, small1 = place_attn(1, all_at1, attn_shape)
+    placed = place_ff(0, all_ff0, False, shapes, placed)
+    d_attn_in, small0 = place_attn(0, all_at0, attn_shape, (d_attn_in,), (placed[2],))
+    d_ff_in, d_ff_out, d_attn_out = placed
     (d_proj, d_dense, d_cls, d_qv, d_out_b, d_gain, d_shift, d_fi_b, d_fo_b, *rest) = place_small(
         small0, small1, width, deep, classes, narrow
     )
     d_stu_b, d_query, d_dense_b, d_cls_b = rest
     totals = (
-        large[0],
+        d_attn_in,
         d_qv,
-        large[1],
+        d_attn_out,
         d_out_b,
         d_gain,
         d_shift,
-        large[2],
+        d_ff_in,
         d_fi_b,
-        large[3],
+        d_ff_out,
         d_fo_b,
         d_proj,
         d_stu_b,
@@ -1371,12 +1470,13 @@
     in_order = lambda for_a, for_b: jnp.where(
         row_a == 0, jnp.stack([for_a, for_b]), jnp.stack([for_b, for_a])
     )
-    act_a = jnp.where(a_alive, far_h[:length], a2[3])
+    act_a = jnp.where(a_alive, far_h, a2[3])
     act_b = jnp.where(b_alive, w2[3], b2[3])
-    logit_a = jnp.where(a_alive, far_h[length, :classes], jnp.zeros((classes,), BF16))
-    logit_b = jnp.where(b_alive, w2[6][0, :classes].astype(BF16), jnp.zeros((classes,), BF16))
-    early = in_order(a2[6][0, :classes], b2[6][0, :classes]).astype(BF16)
-    logits = jnp.stack([early, in_order(logit_a, logit_b)], 1)
+    cut = lambda value: value[length, :classes]
+    logits = jnp.where(jnp.stack([a_alive, b_alive])[:, None], jnp.stack([cut(act_a), cut(act_b)]), 0)
+    early = in_order(cut(a2[3]), cut(b2[3]))
+    logits = jnp.stack([early, in_order(logits[0], logits[1])], 1).astype(BF16)
+    act_a, act_b = act_a[:length], act_b[:length]
     return (in_order(act_a, act_b), logits, in_order(a4[1], b4[1])) + totals
 
 

time: 532 us -> 526 us (0.989)
  local copies, waits for them, and re-layouts: 49.7 us -> 35.9 us
  waiting for transfers between devices: 69.4 us -> 81.7 us
  Pallas kernels: 276 us -> 264 us
  starting transfers between devices: 48.4 us -> 56.9 us
    ppermute x32 -> x35, waiting for transfers between devices: 32.5 us -> 52.6 us  [swap(): return lax.ppermute(value, 'wide', [(i, i ^ bit) for i in range(size)])]
    pallas_call x18 -> x14, Pallas kernels: 86.1 us -> 76.8 us  [the longest x6 41.8 us: weight_grad_cols(): pl.pallas_call(partial(grad_cols_kernel, rows=rows, steps=steps), out_sha...]
    convert_element_type x19 -> x27, other arithmetic: 16.5 us -> 24.6 us  [add_low(): return (left.astype(F32) + right.astype(F32)).astype(BF16)]
    slice x13 -> x2, local copies, waits for them, and re-layouts: 5.82 us -> 0.06 us  [the longest x1 0.05 us: shards(): work_in[:length]]
    unnamed x217 -> x215, local copies, waits for them, and re-layouts: 17.7 us -> 23.3 us
    ppermute x32 -> x35, starting transfers between devices: 26.4 us -> 29.3 us  [swap(): return lax.ppermute(value, 'wide', [(i, i ^ bit) for i in range(size)])]
    ppermute x2 -> x4, waiting for transfers between devices: 14.8 us -> 14.3 us  [narrow_sum_swaps(): recv = lax.ppermute(give, 'narrow', [(i, i ^ bit) for i in range(size)])]
  transfers between devices with their start and end apart: 58 -> 61, of which waited for: 17 -> 16; matrix products, arithmetic and copies ran while one was open for 14% -> 11% of each run, Pallas kernels for 42% -> 37%
where the time goes in v2:
time: 526 us; the launch traced here: 521 us
  Pallas kernels  264 us (50%)
  waiting for transfers between devices  81.7 us (16%)
  other arithmetic  58.1 us (11%)
  starting transfers between devices  56.9 us (11%)
  local copies, waits for them, and re-layouts  35.9 us (7%)
  between operations  23.8 us (5%)
    pallas_call x12, Pallas kernels, call(): pl.pallas_call(body, out_shape=outs, in_specs=list(in_specs) + [ANY] * ex...  183 us
    ppermute x35, waiting for transfers between devices, swap(): return lax.ppermute(value, 'wide', [(i, i ^ bit) for i in range(size)])  52.6 us
    pallas_call x6, Pallas kernels, weight_grad_cols(): pl.pallas_call(partial(grad_cols_kernel, rows=rows, steps=steps), out_sha...  41.8 us
    ppermute x35, starting transfers between devices, swap(): return lax.ppermute(value, 'wide', [(i, i ^ bit) for i in range(size)])  29.3 us
    convert_element_type x27, other arithmetic, add_low(): return (left.astype(F32) + right.astype(F32)).astype(BF16)  24.6 us
    unnamed x215, local copies, waits for them, and re-layouts  23.3 us
    pallas_call x2, Pallas kernels, weight_grad_rows(): pl.pallas_call(partial(grad_rows_kernel, rows=rows, narrow=narrow), out_s...  19.6 us
    ppermute x4, waiting for transfers between devices, narrow_sum_swaps(): recv = lax.ppermute(give, 'narrow', [(i, i ^ bit) for i in range(size)])  14.3 us
  transfers between devices with their start and end apart: 61, of which 16 were waited for; matrix products, arithmetic and copies ran while one was open for 11% of the time, Pallas kernels for 37%

profile of v2, /device:TPU:0, one launch (start us, length us, event | category | flops | bytes accessed | tf_op | source)
XLA Modules:
  0.0 520.7 jit_solution(12988060858448099660)
XLA Ops:
  14.5 14.3 %forward_attention0.2 = (bf16[512,2304]{1,0:T(8,128)(2,1)}, f32[16,512]{1,0:T(8,128)S(1)}, bf16[512,768]{1,0:T(8,128)(2,1)S(1)}, bf16[512,768]{1,0:T(8,128)(2,1)...) custom-call(s32[1]{0:T(128)} %select_n.508.refs_0_, bf16[2,512,768]{2,1,0:T(8,128)(2,1)} %refs_1_.5, ...), custom_call_target="tpu_custom_call" | custom-call | flops 14000000000 | bytes 16000000 | tf_op jit(solution)/shard_map/forward_attention0/pallas_call | solution.py:110
  32.1 3.1 collective-permute-start
  35.1 2.6 collective-permute-start.1
  41.0 17.5 %forward_ff0.2 = (bf16[512,3072]{1,0:T(8,128)(2,1)}, bf16[512,3072]{1,0:T(8,128)(2,1)}, bf16[512,768]{1,0:T(8,128)(2,1)}, bf16[528,768]{1,0:T(8,128)(2,1)}, f32[...) custom-call(s32[1]{0:T(128)} %select_n.508.refs_0_, ...), custom_call_target="tpu_custom_call" | custom-call | flops 17999998976 | bytes 20000000 | tf_op jit(solution)/shard_map/forward_ff0/pallas_call | solution.py:110
  63.7 3.1 route.1
  77.7 14.2 %forward_attention0.3 = (bf16[512,2304]{1,0:T(8,128)(2,1)}, f32[16,512]{1,0:T(8,128)S(1)}, bf16[512,768]{1,0:T(8,128)(2,1)S(1)}, bf16[512,768]{1,0:T(8,128)(2,1)...) custom-call(s32[1]{0:T(128)} %bitcast.6.refs_0_, bf16[2,512,768]{2,1,0:T(8,128)(2,1)} %refs_1_.5, ...), custom_call_target="tpu_custom_call" | custom-call | flops 14000000000 | bytes 16000000 | tf_op jit(solution)/shard_map/forward_attention0/pallas_call | solution.py:110
  96.6 17.2 %forward_ff0.3 = (bf16[512,3072]{1,0:T(8,128)(2,1)}, bf16[512,3072]{1,0:T(8,128)(2,1)}, bf16[512,768]{1,0:T(8,128)(2,1)}, bf16[528,768]{1,0:T(8,128)(2,1)}, f32[...) custom-call(s32[1]{0:T(128)} %bitcast.6.refs_0_, ...), custom_call_target="tpu_custom_call" | custom-call | flops 17999998976 | bytes 20000000 | tf_op jit(solution)/shard_map/forward_ff0/pallas_call | solution.py:110
  118.7 14.3 %forward_attention1.1 = (bf16[512,2304]{1,0:T(8,128)(2,1)}, f32[16,512]{1,0:T(8,128)S(1)}, bf16[512,768]{1,0:T(8,128)(2,1)S(1)}, bf16[512,768]{1,0:T(8,128)(2,1)...) custom-call(s32[1]{0:T(128)} %constant.240.clone.1.refs_0_, ...), custom_call_target="tpu_custom_call" | custom-call | flops 14000000000 | bytes 16000000 | tf_op jit(solution)/shard_map/forward_attention1/pallas_call | solution.py:110
  135.2 17.1 %forward_ff1.1 = (bf16[512,3072]{1,0:T(8,128)(2,1)}, bf16[512,3072]{1,0:T(8,128)(2,1)}, bf16[512,768]{1,0:T(8,128)(2,1)}, bf16[528,768]{1,0:T(8,128)(2,1)}, f32[...) custom-call(s32[1]{0:T(128)} %constant.240.clone.1.refs_0_, ...), custom_call_target="tpu_custom_call" | custom-call | flops 17999998976 | bytes 20000000 | tf_op jit(solution)/shard_map/forward_ff1/pallas_call | solution.py:110
  153.1 13.4 %backward_ff1.1 = (bf16[512,768]{1,0:T(8,128)(2,1)S(1)}, bf16[512,3072]{1,0:T(8,128)(2,1)}, bf16[512,768]{1,0:T(8,128)(2,1)}, f32[512,768]{1,0:T(8,128)}, f32[8,3072]{1,0:T(8,128)S(1)}) custom-call(bf16[512,768]{1,0:T(8,128)(2,1)} %bitcast_select_fusion.1.refs_19_.refs_0_, bf16[512,128]{1,0:T(8,128)(2,1)S(1)} %get-tuple-element.185.refs_1_, ...), custom_call_target="tpu_custom_call" | custom-call | flops 16000000000 | bytes 22000000 | tf_op jit(solution)/shard_map/backward_ff1/pallas_call | solution.py:110
  166.5 8.7 %weight_grad_rows.2 = (bf16[4,192,1536]{2,1,0:T(8,128)(2,1)}, bf16[4,192,1536]{2,1,0:T(8,128)(2,1)}) custom-call(s32[1]{0:T(128)} %bitcast.18.half_ref, bf16[512,3072]{1,0:T(8,128)(2,1)} %get-tuple-element.195.refs_0_, bf16[512,768]{1,0:T(8,128)(2,1)S(1)} %get-tuple-element.196.refs_1_), custom_call_target="tpu_custom_call" | custom-call | flops 1000000 | bytes 100000 | tf_op jit(solution)/shard_map/weight_grad_rows/pallas_call | solution.py:865
  176.0 3.0 weight_grad_cols.7
  179.4 7.2 %weight_grad_cols.6 = (bf16[4,192,1536]{2,1,0:T(8,128)(2,1)}, bf16[4,192,1536]{2,1,0:T(8,128)(2,1)}) custom-call(s32[1]{0:T(128)} %bitcast.18.half_ref, bf16[512,768]{1,0:T(8,128)(2,1)S(1)} %copy-done.7, bf16[512,3072]{1,0:T(8,128)(2,1)} %get-tuple-element.193.refs_1_), custom_call_target="tpu_custom_call" | custom-call | flops 1000000 | bytes 100000 | tf_op jit(solution)/shard_map/weight_grad_cols/pallas_call | solution.py:805
  186.7 15.2 %backward_attention1.1 = (bf16[512,2304]{1,0:T(8,128)(2,1)}, bf16[512,768]{1,0:T(8,128)(2,1)S(1)}, f32[8,3072]{1,0:T(8,128)S(1)}) custom-call(s32[1]{0:T(128)} %constant.240.clone.1.refs_0_, s32[1,512]{1,0:T(1,128)S(1)} %slice_convert_fusion.refs_2_.refs_4_.refs_1_, f32[16,512]{1,0:T(8,128)S(1)} %get-tuple-element.182.refs_2_, ...), custom_call_target="tpu_custom_call" | custom-call | flops 20000000000 | bytes 16000000 | tf_op jit(solution)/shard_map/backward_attention1/pallas_call | solution.py:110
  205.2 2.3 add_convert_fusion.2
  210.9 2.3 add_convert_fusion.3
  214.6 7.4 %weight_grad_cols.8 = (bf16[4,192,1152]{2,1,0:T(8,128)(2,1)}, bf16[4,192,1152]{2,1,0:T(8,128)(2,1)}) custom-call(s32[1]{0:T(128)} %bitcast.18.half_ref, bf16[512,768]{1,0:T(8,128)(2,1)S(1)} %slice.121.refs_0_, bf16[512,2304]{1,0:T(8,128)(2,1)} %get-tuple-element.200.refs_1_, bf16[4,96,1536]{2,1,0:T(8,128)(2,1)S(1)} %constant_dynamic-slice_fusion.29.refs_2_, ...), custom_call_target="tpu_custom_call" | custom-call | flops 1000000 | bytes 100000 | tf_op jit(solution)/shard_map/weight_grad_cols/pallas_call | solution.py:805
  230.2 2.3 bitcast_select_fusion.refs_0_
  236.3 9.0 %collective-permute-done.18 = bf16[512,768]{1,0:T(8,128)(2,1)} collective-permute-done((bf16[512,768]{1,0:T(8,128)(2,1)}, bf16[512,768]{1,0:T(8,128)(2,1)}, u32[]{:S(2)}, u32[]{:S(2)}) %collective-permute-start.18) | collective-permute-done | bytes 786464 | tf_op jit(solution)/shard_map/ppermute | solution.py:1303
  245.3 14.0 %backward_ff0.2 = (bf16[512,768]{1,0:T(8,128)(2,1)}, bf16[512,3072]{1,0:T(8,128)(2,1)}, bf16[512,768]{1,0:T(8,128)(2,1)}, f32[512,768]{1,0:T(8,128)}, f32[8,3072]{1,0:T(8,128)S(1)}) custom-call(bf16[512,768]{1,0:T(8,128)(2,1)} %bitcast_select_fusion.refs_0_, bf16[512,128]{1,0:T(8,128)(2,1)S(1)} %copy-done.56, f32[512,128]{1,0:T(8,128)S(1)} %copy-done.50, ...), custom_call_target="tpu_custom_call" | custom-call | flops 16000000000 | bytes 22000000 | tf_op jit(solution)/shard_map/backward_ff0/pallas_call | solution.py:110
  259.9 2.3 broadcast_select_fusion.4
  262.3 2.3 broadcast_select_fusion.1.refs_15_
  264.5 3.3 collective-permute-start.20
  270.5 2.6 collective-permute-start.26
  277.9 13.8 %backward_ff0.3 = (bf16[512,768]{1,0:T(8,128)(2,1)}, bf16[512,3072]{1,0:T(8,128)(2,1)}, bf16[512,768]{1,0:T(8,128)(2,1)}, f32[512,768]{1,0:T(8,128)}, f32[8,3072]{1,0:T(8,128)S(1)}) custom-call(bf16[512,768]{1,0:T(8,128)(2,1)} %broadcast_select_fusion.4, bf16[512,128]{1,0:T(8,128)(2,1)S(1)} %copy-done.54, f32[512,128]{1,0:T(8,128)S(1)} %copy-done.46, ...), custom_call_target="tpu_custom_call" | custom-call | flops 16000000000 | bytes 22000000 | tf_op jit(solution)/shard_map/backward_ff0/pallas_call | solution.py:110
  293.5 3.3 broadcast_select_fusion.3
  299.6 5.1 collective-permute-done.28
  307.3 10.9 %weight_grad_rows.3 = (bf16[4,192,1536]{2,1,0:T(8,128)(2,1)}, bf16[4,192,1536]{2,1,0:T(8,128)(2,1)}) custom-call(s32[1]{0:T(128)} %bitcast.18.half_ref, bf16[512,3072]{1,0:T(8,128)(2,1)} %get-tuple-element.249.refs_0_, bf16[512,3072]{1,0:T(8,128)(2,1)} %get-tuple-element.250.refs_1_, bf16[512,768]{1,0:T(8,128)(2,1)S(1)} %copy-done.5, ...), custom_call_target="tpu_custom_call" | custom-call | flops 1000000 | bytes 100000 | tf_op jit(solution)/shard_map/weight_grad_rows/pallas_call | solution.py:865
  318.2 4.6 weight_grad_cols.10
  325.1 9.9 %weight_grad_cols.9 = (bf16[4,192,1536]{2,1,0:T(8,128)(2,1)}, bf16[4,192,1536]{2,1,0:T(8,128)(2,1)}) custom-call(s32[1]{0:T(128)} %bitcast.18.half_ref, bf16[512,768]{1,0:T(8,128)(2,1)S(1)} %copy-done.3, bf16[512,768]{1,0:T(8,128)(2,1)} %get-tuple-element.169.refs_1_, bf16[512,3072]{1,0:T(8,128)(2,1)} %get-tuple-element.241.refs_2_, ...), custom_call_target="tpu_custom_call" | custom-call | flops 1000000 | bytes 100000 | tf_op jit(solution)/shard_map/weight_grad_cols/pallas_call | solution.py:805
  337.4 2.9 collective-permute-done.35
  343.4 2.3 add_convert_fusion
  347.4 2.3 add_convert_fusion.1
  353.4 15.4 %backward_attention0.2 = (bf16[512,2304]{1,0:T(8,128)(2,1)}, bf16[512,768]{1,0:T(8,128)(2,1)S(1)}, f32[8,3072]{1,0:T(8,128)S(1)}) custom-call(s32[1]{0:T(128)} %bitcast.6.refs_0_, s32[2,512]{1,0:T(2,128)S(1)} %copy-done.35, f32[16,512]{1,0:T(8,128)S(1)} %copy-done.58, bf16[2,768,2304]{2,1,0:T(8,128)(2,1)} %refs_3_.11, bf16[2,768,768]{2,1,0:T(8,128)(2,1)} %refs_4_.21, ...), custom_call_target="tpu_custom_call" | custom-call | flops 20000000000 | bytes 16000000 | tf_op jit(solution)/shard_map/backward_attention0/pallas_call | solution.py:110
  368.9 9.7 %collective-permute-done.37 = bf16[4,96,1536]{2,1,0:T(8,128)(2,1)} collective-permute-done((bf16[4,96,1536]{2,1,0:T(8,128)(2,1)S(1)}, bf16[4,96,1536]{2,1,0:T(8,128)(2,1)}, u32[]{:S(2)}, u32[]{:S(2)}) %collective-permute-start.37) | collective-permute-done | bytes 1179680 | tf_op jit(solution)/shard_map/ppermute | solution.py:887
  381.4 5.0 collective-permute-done.38
  390.3 16.2 %backward_attention0.3 = (bf16[512,2304]{1,0:T(8,128)(2,1)}, bf16[512,768]{1,0:T(8,128)(2,1)}, f32[8,3072]{1,0:T(8,128)S(1)}) custom-call(s32[1]{0:T(128)} %select_n.508.refs_0_, s32[2,512]{1,0:T(2,128)S(1)} %copy-done.35, f32[16,512]{1,0:T(8,128)S(1)} %copy-done.60, bf16[2,768,2304]{2,1,0:T(8,128)(2,1)} %refs_3_.11, bf16[2,768,768]{2,1,0:T(8,128)(2,1)} %refs_4_.21, ...), custom_call_target="tpu_custom_call" | custom-call | flops 20000000000 | bytes 16000000 | tf_op jit(solution)/shard_map/backward_attention0/pallas_call | solution.py:110
  410.6 9.8 %weight_grad_cols.11 = (bf16[4,192,1152]{2,1,0:T(8,128)(2,1)}, bf16[4,192,1152]{2,1,0:T(8,128)(2,1)}) custom-call(s32[1]{0:T(128)} %bitcast.18.half_ref, bf16[512,768]{1,0:T(8,128)(2,1)S(1)} %get-tuple-element.335.refs_0_, bf16[512,768]{1,0:T(8,128)(2,1)S(1)} %get-tuple-element.334.refs_1_, bf16[512,2304]{1,0:T(8,128)(2,1)} %get-tuple-element.265.refs_2_, ...), custom_call_target="tpu_custom_call" | custom-call | flops 1000000 | bytes 100000 | tf_op jit(solution)/shard_map/weight_grad_cols/pallas_call | solution.py:805
  437.2 16.4 %collective-permute-done.55 = bf16[1,48,3456]{2,1,0:T(8,128)(2,1)S(1)} collective-permute-done((bf16[1,48,3456]{2,1,0:T(8,128)(2,1)S(1)}, bf16[1,48,3456]{2,1,0:T(8,128)(2,1)S(1)}, u32[]{:S(2)}, u32[]{:S(2)}) %collective-permute-start.55) | collective-permute-done | bytes 331808 | tf_op jit(solution)/shard_map/ppermute | solution.py:887
  457.4 3.1 collective-permute-done.43
  460.6 3.6 collective-permute-done.46
  466.1 5.7 %collective-permute-done.47 = bf16[2,1,48,1280]{3,2,1,0:T(8,128)(2,1)S(1)} collective-permute-done((bf16[2,1,48,1280]{3,2,1,0:T(8,128)(2,1)S(1)}, bf16[2,1,48,1280]{3,2,1,0:T(8,128)(2,1)S(1)}, u32[]{:S(2)}, u32[]{:S(2)}) %collective-permute-start.47) | collective-permute-done | bytes 245792 | tf_op jit(solution)/shard_map/ppermute | solution.py:955
  473.5 5.6 %collective-permute-done.48 = bf16[1,1,48,1280]{3,2,1,0:T(8,128)(2,1)S(1)} collective-permute-done((bf16[1,1,48,1280]{3,2,1,0:T(8,128)(2,1)S(1)}, bf16[1,1,48,1280]{3,2,1,0:T(8,128)(2,1)S(1)}, u32[]{:S(2)}, u32[]{:S(2)}) %collective-permute-start.48) | collective-permute-done | bytes 122912 | tf_op jit(solution)/shard_map/ppermute | solution.py:955
  480.4 4.4 collective-permute-done.49
  486.2 4.9 collective-permute-done.50
  495.7 4.3 place_ff1.1
  500.0 4.2 all-gather.3.cloned.1.call-done
  504.1 4.3 place_ff0.1
  (439 shorter events, 130.7 us)
Async XLA Ops:
  7.2 382.2 %reduce-scatter.3.cloned.1.call-start = ((), (), s32[]{:S(2)}) async-start(), calls=%async_computation.2 | async-start | bytes 614400 | tf_op jit(solution)/shard_map/reduce_scatter | solution.py:974
  32.1 30.2 %collective-permute-start = (s32[1]{0:T(128)}, s32[1]{0:T(128)}, u32[]{:S(2)}, u32[]{:S(2)}) collective-permute-start(s32[1]{0:T(128)} %bitcast.2.refs_0_), channel_id=1, source_target_pairs={{0,1},{1,2},{2,3},{3,0},{4,5},{5,6},{6,7},{7,4},{8,9},{9,10},{10,1... | collective-permute-start | bytes 20 | tf_op jit(solution)/shard_map/ppermute | solution.py:1284
  35.1 28.6 %collective-permute-start.1 = (s32[1]{0:T(128)}, s32[1]{0:T(128)}, u32[]{:S(2)}, u32[]{:S(2)}) collective-permute-start(s32[1]{0:T(128)} %bitcast.2.refs_0_), channel_id=1, source_target_pairs={{0,2},{1,3},{2,0},{3,1},{4,6},{5,7},{6,4},{7,5},{8,10},{9,11},{10,... | collective-permute-start | bytes 20 | tf_op jit(solution)/shard_map/ppermute | solution.py:1284
  37.7 26.0 %collective-permute-start.2 = (s32[1]{0:T(128)}, s32[1]{0:T(128)}, u32[]{:S(2)}, u32[]{:S(2)}) collective-permute-start(s32[1]{0:T(128)} %bitcast.2.refs_0_), channel_id=1, source_target_pairs={{0,3},{1,0},{2,1},{3,2},{4,7},{5,4},{6,5},{7,6},{8,11},{9,8},{10,9... | collective-permute-start | bytes 20 | tf_op jit(solution)/shard_map/ppermute | solution.py:1284
  40.0 35.6 %collective-permute-start.3 = (bf16[512,768]{1,0:T(8,128)(2,1)}, bf16[512,768]{1,0:T(8,128)(2,1)}, u32[]{:S(2)}, u32[]{:S(2)}) collective-permute-start(bf16[512,768]{1,0:T(8,128)(2,1)} %dynamic-slice_bitcast_fusion.2.refs_19_), channel_id=1, source_target_pairs={{0,1},{1,0},{2,3},{3,2},{4,5},{5,4},{6,7},{7,6},{8,9},{9,8},{10,11... | collective-permute-start | bytes 2359304 | tf_op jit(solution)/shard_map/ppermute | solution.py:1303
  40.7 34.9 %collective-permute-start.4 = (bf16[512,768]{1,0:T(8,128)(2,1)}, bf16[512,768]{1,0:T(8,128)(2,1)}, u32[]{:S(2)}, u32[]{:S(2)}) collective-permute-start(bf16[512,768]{1,0:T(8,128)(2,1)} %dynamic-slice_bitcast_fusion.2.refs_19_), channel_id=1, source_target_pairs={{0,4},{1,2},{2,1},{3,7},{4,0},{5,6},{6,5},{7,3},{8,12},{9,10},{10,... | collective-permute-start | bytes 2359304 | tf_op jit(solution)/shard_map/ppermute | solution.py:1304
  62.3 30.5 %collective-permute-start.5 = (bf16[528,768]{1,0:T(8,128)(2,1)S(1)}, bf16[528,768]{1,0:T(8,128)(2,1)}, u32[]{:S(2)}, u32[]{:S(2)}) collective-permute-start(bf16[528,768]{1,0:T(8,128)(2,1)S(1)} %copy-done.74), channel_id=1, source_target_pairs={{0,1},{1,0},{2,3},{3,2},{4,5},{5,4},{6,7},{7,6},{8,9},{9,8},{10,11... | collective-permute-start | bytes 2433032 | tf_op jit(solution)/shard_map/ppermute | solution.py:1303
  63.7 29.1 %collective-permute-start.6 = (bf16[528,768]{1,0:T(8,128)(2,1)S(1)}, bf16[528,768]{1,0:T(8,128)(2,1)}, u32[]{:S(2)}, u32[]{:S(2)}) collective-permute-start(bf16[528,768]{1,0:T(8,128)(2,1)S(1)} %copy-done.74), channel_id=1, source_target_pairs={{0,4},{1,2},{2,1},{3,7},{4,0},{5,6},{6,5},{7,3},{8,12},{9,10},{10,... | collective-permute-start | bytes 2433032 | tf_op jit(solution)/shard_map/ppermute | solution.py:1304
  94.4 21.7 %collective-permute-start.7 = (bf16[528,768]{1,0:T(8,128)(2,1)S(1)}, bf16[528,768]{1,0:T(8,128)(2,1)S(1)}, u32[]{:S(2)}, u32[]{:S(2)}) collective-permute-start(bf16[528,768]{1,0:T(8,128)(2,1)S(1)} %broadcast_select_fusion.2.refs_19_), channel_id=1, source_target_pairs={{0,1},{1,0},{2,3},{3,2},{4,5},{5,4},{6,7},{7,6},{8,9},{9,8},{10,11... | collective-permute-start | bytes 2433032 | tf_op jit(solution)/shard_map/ppermute | solution.py:1303
  96.6 19.5 %collective-permute-start.8 = (bf16[528,768]{1,0:T(8,128)(2,1)S(1)}, bf16[528,768]{1,0:T(8,128)(2,1)S(1)}, u32[]{:S(2)}, u32[]{:S(2)}) collective-permute-start(bf16[528,768]{1,0:T(8,128)(2,1)S(1)} %broadcast_select_fusion.2.refs_19_), channel_id=1, source_target_pairs={{0,4},{1,2},{2,1},{3,7},{4,0},{5,6},{6,5},{7,3},{8,12},{9,10},{10,... | collective-permute-start | bytes 2433032 | tf_op jit(solution)/shard_map/ppermute | solution.py:1304
  113.9 19.0 %collective-permute-start.10 = (bf16[512,768]{1,0:T(8,128)(2,1)S(1)}, bf16[512,768]{1,0:T(8,128)(2,1)S(1)}, u32[]{:S(2)}, u32[]{:S(2)}) collective-permute-start(bf16[512,768]{1,0:T(8,128)(2,1)S(1)} %copy-done.83), channel_id=1, source_target_pairs={{0,4},{1,2},{2,1},{3,7},{4,0},{5,6},{6,5},{7,3},{8,12},{9,10},{10,... | collective-permute-start | bytes 2359304 | tf_op jit(solution)/shard_map/ppermute | solution.py:1304
  114.5 19.5 %collective-permute-start.9 = (bf16[512,768]{1,0:T(8,128)(2,1)S(1)}, bf16[512,768]{1,0:T(8,128)(2,1)S(1)}, u32[]{:S(2)}, u32[]{:S(2)}) collective-permute-start(bf16[512,768]{1,0:T(8,128)(2,1)S(1)} %copy-done.83), channel_id=1, source_target_pairs={{0,1},{1,0},{2,3},{3,2},{4,5},{5,4},{6,7},{7,6},{8,9},{9,8},{10,11... | collective-permute-start | bytes 2359304 | tf_op jit(solution)/shard_map/ppermute | solution.py:1303
  175.3 29.9 %collective-permute-start.16 = (bf16[4,192,1536]{2,1,0:T(8,128)(2,1)}, bf16[4,192,1536]{2,1,0:T(8,128)(2,1)}, u32[]{:S(2)}, u32[]{:S(2)}) collective-permute-start(bf16[4,192,1536]{2,1,0:T(8,128)(2,1)} %get-tuple-element.197.refs_10_), channel_id=1, source_target_pairs={{0,4},{4,0},{8,12},{12,8},{16,20},{20,16},{24,28},{28,24},{1,5},{5... | collective-permute-start | bytes 7077896 | tf_op jit(solution)/shard_map/ppermute | solution.py:887
  178.9 25.3 %collective-permute-start.17 = (bf16[4,192,384]{2,1,0:T(8,128)(2,1)S(1)}, bf16[4,192,384]{2,1,0:T(8,128)(2,1)S(1)}, u32[]{:S(2)}, u32[]{:S(2)}) collective-permute-start(bf16[4,192,384]{2,1,0:T(8,128)(2,1)S(1)} %get-tuple-element.198.refs_11_), channel_id=1, source_target_pairs={{0,4},{4,0},{8,12},{12,8},{16,20},{20,16},{24,28},{28,24},{1,5},{5... | collective-permute-start | bytes 1769480 | tf_op jit(solution)/shard_map/ppermute | solution.py:887
  186.6 23.3 %collective-permute-start.15 = (bf16[4,192,1536]{2,1,0:T(8,128)(2,1)}, bf16[4,192,1536]{2,1,0:T(8,128)(2,1)}, u32[]{:S(2)}, u32[]{:S(2)}) collective-permute-start(bf16[4,192,1536]{2,1,0:T(8,128)(2,1)} %get-tuple-element.194.refs_9_), channel_id=1, source_target_pairs={{0,4},{4,0},{8,12},{12,8},{16,20},{20,16},{24,28},{28,24},{1,5},{5... | collective-permute-start | bytes 7077896 | tf_op jit(solution)/shard_map/ppermute | solution.py:887
  202.6 20.0 %collective-permute-start.13 = (bf16[512,768]{1,0:T(8,128)(2,1)S(1)}, bf16[512,768]{1,0:T(8,128)(2,1)S(1)}, u32[]{:S(2)}, u32[]{:S(2)}) collective-permute-start(bf16[512,768]{1,0:T(8,128)(2,1)S(1)} %get-tuple-element.199), channel_id=1, source_target_pairs={{0,1},{1,0},{2,3},{3,2},{4,5},{5,4},{6,7},{7,6},{8,9},{9,8},{10,11... | collective-permute-start | bytes 2359304 | tf_op jit(solution)/shard_map/ppermute | solution.py:1303
  204.1 18.5 %collective-permute-start.14 = (bf16[512,768]{1,0:T(8,128)(2,1)S(1)}, bf16[512,768]{1,0:T(8,128)(2,1)S(1)}, u32[]{:S(2)}, u32[]{:S(2)}) collective-permute-start(bf16[512,768]{1,0:T(8,128)(2,1)S(1)} %get-tuple-element.199), channel_id=1, source_target_pairs={{0,4},{1,2},{2,1},{3,7},{4,0},{5,6},{6,5},{7,3},{8,12},{9,10},{10,... | collective-permute-start | bytes 2359304 | tf_op jit(solution)/shard_map/ppermute | solution.py:1304
  224.5 20.8 %collective-permute-start.18 = (bf16[512,768]{1,0:T(8,128)(2,1)}, bf16[512,768]{1,0:T(8,128)(2,1)}, u32[]{:S(2)}, u32[]{:S(2)}) collective-permute-start(bf16[512,768]{1,0:T(8,128)(2,1)} %broadcast_select_fusion.5.refs_12_), channel_id=1, source_target_pairs={{0,1},{1,0},{2,3},{3,2},{4,5},{5,4},{6,7},{7,6},{8,9},{9,8},{10,11... | collective-permute-start | bytes 2359304 | tf_op jit(solution)/shard_map/ppermute | solution.py:1303
  225.9 36.4 %collective-permute-start.11 = (bf16[528,768]{1,0:T(8,128)(2,1)}, bf16[528,768]{1,0:T(8,128)(2,1)}, u32[]{:S(2)}, u32[]{:S(2)}) collective-permute-start(bf16[528,768]{1,0:T(8,128)(2,1)} %get-tuple-element.181.refs_11_), channel_id=1, source_target_pairs={{0,1},{1,0},{2,3},{3,2},{4,5},{5,4},{6,7},{7,6},{8,9},{9,8},{10,11... | collective-permute-start | bytes 2433032 | tf_op jit(solution)/shard_map/ppermute | solution.py:1303
  226.6 35.6 %collective-permute-start.12 = (bf16[528,768]{1,0:T(8,128)(2,1)}, bf16[528,768]{1,0:T(8,128)(2,1)}, u32[]{:S(2)}, u32[]{:S(2)}) collective-permute-start(bf16[528,768]{1,0:T(8,128)(2,1)} %get-tuple-element.181.refs_11_), channel_id=1, source_target_pairs={{0,4},{1,2},{2,1},{3,7},{4,0},{5,6},{6,5},{7,3},{8,12},{9,10},{10,... | collective-permute-start | bytes 2433032 | tf_op jit(solution)/shard_map/ppermute | solution.py:1304
  233.3 39.9 %collective-permute-start.25 = (bf16[4,96,1920]{2,1,0:T(8,128)(2,1)S(1)}, bf16[4,96,1920]{2,1,0:T(8,128)(2,1)}, u32[]{:S(2)}, u32[]{:S(2)}) collective-permute-start(bf16[4,96,1920]{2,1,0:T(8,128)(2,1)S(1)} %copy-done.68), channel_id=1, source_target_pairs={{0,16},{4,20},{8,24},{12,28},{16,0},{20,4},{24,8},{28,12},{1,17},{... | collective-permute-start | bytes 4423688 | tf_op jit(solution)/shard_map/ppermute | solution.py:887
  234.8 33.3 %collective-permute-start.24 = (bf16[4,96,1536]{2,1,0:T(8,128)(2,1)S(1)}, bf16[4,96,1536]{2,1,0:T(8,128)(2,1)}, u32[]{:S(2)}, u32[]{:S(2)}) collective-permute-start(bf16[4,96,1536]{2,1,0:T(8,128)(2,1)S(1)} %constant_dynamic-slice_fusion.29.refs_2_), channel_id=1, source_target_pairs={{0,8},{4,12},{8,0},{12,4},{16,24},{20,28},{24,16},{28,20},{1,9},{5... | collective-permute-start | bytes 3538952 | tf_op jit(solution)/shard_map/ppermute | solution.py:887
  245.2 14.1 %collective-permute-start.19 = (bf16[512,768]{1,0:T(8,128)(2,1)}, bf16[512,768]{1,0:T(8,128)(2,1)S(1)}, u32[]{:S(2)}, u32[]{:S(2)}) collective-permute-start(bf16[512,768]{1,0:T(8,128)(2,1)} %broadcast_select_fusion.5.refs_12_), channel_id=1, source_target_pairs={{0,4},{1,2},{2,1},{3,7},{4,0},{5,6},{6,5},{7,3},{8,12},{9,10},{10,... | collective-permute-start | bytes 2359304 | tf_op jit(solution)/shard_map/ppermute | solution.py:1304
  259.3 16.2 %collective-permute-start.22 = (bf16[4,192,1152]{2,1,0:T(8,128)(2,1)}, bf16[4,192,1152]{2,1,0:T(8,128)(2,1)S(1)}, u32[]{:S(2)}, u32[]{:S(2)}) collective-permute-start(bf16[4,192,1152]{2,1,0:T(8,128)(2,1)} %get-tuple-element.204.refs_11_), channel_id=1, source_target_pairs={{0,4},{4,0},{8,12},{12,8},{16,20},{20,16},{24,28},{28,24},{1,5},{5... | collective-permute-start | bytes 5308424 | tf_op jit(solution)/shard_map/ppermute | solution.py:887
  264.5 28.9 %collective-permute-start.20 = (bf16[528,768]{1,0:T(8,128)(2,1)}, bf16[528,768]{1,0:T(8,128)(2,1)}, u32[]{:S(2)}, u32[]{:S(2)}) collective-permute-start(bf16[528,768]{1,0:T(8,128)(2,1)} %broadcast_select_fusion.1.refs_15_), channel_id=1, source_target_pairs={{0,1},{1,0},{2,3},{3,2},{4,5},{5,4},{6,7},{7,6},{8,9},{9,8},{10,11... | collective-permute-start | bytes 2433032 | tf_op jit(solution)/shard_map/ppermute | solution.py:1303
  267.8 25.7 %collective-permute-start.21 = (bf16[528,768]{1,0:T(8,128)(2,1)}, bf16[528,768]{1,0:T(8,128)(2,1)}, u32[]{:S(2)}, u32[]{:S(2)}) collective-permute-start(bf16[528,768]{1,0:T(8,128)(2,1)} %broadcast_select_fusion.1.refs_15_), channel_id=1, source_target_pairs={{0,4},{1,2},{2,1},{3,7},{4,0},{5,6},{6,5},{7,3},{8,12},{9,10},{10,... | collective-permute-start | bytes 2433032 | tf_op jit(solution)/shard_map/ppermute | solution.py:1304
  270.5 21.2 %collective-permute-start.26 = (bf16[4,48,1536]{2,1,0:T(8,128)(2,1)}, bf16[4,48,1536]{2,1,0:T(8,128)(2,1)}, u32[]{:S(2)}, u32[]{:S(2)}) collective-permute-start(bf16[4,48,1536]{2,1,0:T(8,128)(2,1)} %constant_dynamic-slice_fusion.23.refs_13_), channel_id=1, source_target_pairs={{0,16},{4,20},{8,24},{12,28},{16,0},{20,4},{24,8},{28,12},{1,17},{... | collective-permute-start | bytes 1769480 | tf_op jit(solution)/shard_map/ppermute | solution.py:887
  275.1 22.9 %collective-permute-start.27 = (bf16[4,48,1920]{2,1,0:T(8,128)(2,1)S(1)}, bf16[4,48,1920]{2,1,0:T(8,128)(2,1)S(1)}, u32[]{:S(2)}, u32[]{:S(2)}) collective-permute-start(bf16[4,48,1920]{2,1,0:T(8,128)(2,1)S(1)} %constant_dynamic-slice_fusion.20.refs_14_), channel_id=1, source_target_pairs={{0,8},{4,12},{8,0},{12,4},{16,24},{20,28},{24,16},{28,20},{1,9},{5... | collective-permute-start | bytes 2211848 | tf_op jit(solution)/shard_map/ppermute | solution.py:887
  277.1 22.3 %collective-permute-start.29 = (bf16[4,96,640]{2,1,0:T(8,128)(2,1)S(1)}, bf16[4,96,640]{2,1,0:T(8,128)(2,1)S(1)}, u32[]{:S(2)}, u32[]{:S(2)}) collective-permute-start(bf16[4,96,640]{2,1,0:T(8,128)(2,1)S(1)} %pad_maximum_fusion.8.refs_12_), channel_id=1, source_target_pairs={{0,16},{4,20},{8,24},{12,28},{16,0},{20,4},{24,8},{28,12},{1,17},{... | collective-permute-start | bytes 1474568 | tf_op jit(solution)/shard_map/ppermute | solution.py:887
  291.7 12.9 %collective-permute-start.28 = (bf16[4,96,640]{2,1,0:T(8,128)(2,1)S(1)}, bf16[4,96,640]{2,1,0:T(8,128)(2,1)S(1)}, u32[]{:S(2)}, u32[]{:S(2)}) collective-permute-start(bf16[4,96,640]{2,1,0:T(8,128)(2,1)S(1)} %constant_dynamic-slice_fusion.26.refs_11_), channel_id=1, source_target_pairs={{0,8},{4,12},{8,0},{12,4},{16,24},{20,28},{24,16},{28,20},{1,9},{5... | collective-permute-start | bytes 1474568 | tf_op jit(solution)/shard_map/ppermute | solution.py:887
  304.8 30.1 %collective-permute-start.33 = (bf16[4,48,640]{2,1,0:T(8,128)(2,1)S(1)}, bf16[4,48,640]{2,1,0:T(8,128)(2,1)S(1)}, u32[]{:S(2)}, u32[]{:S(2)}) collective-permute-start(bf16[4,48,640]{2,1,0:T(8,128)(2,1)S(1)} %constant_dynamic-slice_fusion.19.refs_5_), channel_id=1, source_target_pairs={{0,16},{4,20},{8,24},{12,28},{16,0},{20,4},{24,8},{28,12},{1,17},{... | collective-permute-start | bytes 737288 | tf_op jit(solution)/shard_map/ppermute | solution.py:887
  305.9 29.1 %collective-permute-start.34 = (bf16[4,48,640]{2,1,0:T(8,128)(2,1)S(1)}, bf16[4,48,640]{2,1,0:T(8,128)(2,1)S(1)}, u32[]{:S(2)}, u32[]{:S(2)}) collective-permute-start(bf16[4,48,640]{2,1,0:T(8,128)(2,1)S(1)} %constant_dynamic-slice_fusion.17.refs_6_), channel_id=1, source_target_pairs={{0,8},{4,12},{8,0},{12,4},{16,24},{20,28},{24,16},{28,20},{1,9},{5... | collective-permute-start | bytes 737288 | tf_op jit(solution)/shard_map/ppermute | solution.py:887
  318.2 25.2 %collective-permute-start.31 = (bf16[4,192,1536]{2,1,0:T(8,128)(2,1)}, bf16[4,192,1536]{2,1,0:T(8,128)(2,1)}, u32[]{:S(2)}, u32[]{:S(2)}) collective-permute-start(bf16[4,192,1536]{2,1,0:T(8,128)(2,1)} %get-tuple-element.254), channel_id=1, source_target_pairs={{0,4},{4,0},{8,12},{12,8},{16,20},{20,16},{24,28},{28,24},{1,5},{5... | collective-permute-start | bytes 7077896 | tf_op jit(solution)/shard_map/ppermute | solution.py:887
  322.8 13.2 %collective-permute-start.32 = (bf16[4,192,384]{2,1,0:T(8,128)(2,1)S(1)}, bf16[4,192,384]{2,1,0:T(8,128)(2,1)}, u32[]{:S(2)}, u32[]{:S(2)}) collective-permute-start(bf16[4,192,384]{2,1,0:T(8,128)(2,1)S(1)} %get-tuple-element.256), channel_id=1, source_target_pairs={{0,4},{4,0},{8,12},{12,8},{16,20},{20,16},{24,28},{28,24},{1,5},{5... | collective-permute-start | bytes 1769480 | tf_op jit(solution)/shard_map/ppermute | solution.py:887
  323.3 17.0 %collective-permute-start.35 = (bf16[2,1,48,3456]{3,2,1,0:T(8,128)(2,1)S(1)}, bf16[2,1,48,3456]{3,2,1,0:T(8,128)(2,1)}, u32[]{:S(2)}, u32[]{:S(2)}) collective-permute-start(bf16[2,1,48,3456]{3,2,1,0:T(8,128)(2,1)S(1)} %constant_dynamic-slice_fusion.13), channel_id=1, source_target_pairs={{0,1},{1,0},{2,3},{3,2},{4,5},{5,4},{6,7},{7,6},{8,9},{9,8},{10,11... | collective-permute-start | bytes 1990664 | tf_op jit(solution)/shard_map/ppermute | solution.py:955
  336.0 130.2 %reduce-scatter.5.cloned.1.call-start = ((), (), s32[]{:S(2)}) async-start(), calls=%async_computation.3 | async-start | bytes 1658880 | tf_op jit(solution)/shard_map/reduce_scatter | solution.py:974
  341.7 27.1 %collective-permute-start.36 = (bf16[1,1,48,3456]{3,2,1,0:T(8,128)(2,1)S(1)}, bf16[1,1,48,3456]{3,2,1,0:T(8,128)(2,1)S(1)}, u32[]{:S(2)}, u32[]{:S(2)}) collective-permute-start(bf16[1,1,48,3456]{3,2,1,0:T(8,128)(2,1)S(1)} %constant_dynamic-slice_fusion.12), channel_id=1, source_target_pairs={{0,2},{1,3},{2,0},{3,1},{4,6},{5,7},{6,4},{7,5},{8,10},{9,11},{10,... | collective-permute-start | bytes 995336 | tf_op jit(solution)/shard_map/ppermute | solution.py:955
  351.0 35.4 %collective-permute-start.38 = (bf16[4,96,1920]{2,1,0:T(8,128)(2,1)}, bf16[4,96,1920]{2,1,0:T(8,128)(2,1)S(1)}, u32[]{:S(2)}, u32[]{:S(2)}) collective-permute-start(bf16[4,96,1920]{2,1,0:T(8,128)(2,1)} %pad_maximum_fusion.2.refs_10_), channel_id=1, source_target_pairs={{0,16},{4,20},{8,24},{12,28},{16,0},{20,4},{24,8},{28,12},{1,17},{... | collective-permute-start | bytes 4423688 | tf_op jit(solution)/shard_map/ppermute | solution.py:887
  352.0 26.6 %collective-permute-start.37 = (bf16[4,96,1536]{2,1,0:T(8,128)(2,1)S(1)}, bf16[4,96,1536]{2,1,0:T(8,128)(2,1)}, u32[]{:S(2)}, u32[]{:S(2)}) collective-permute-start(bf16[4,96,1536]{2,1,0:T(8,128)(2,1)S(1)} %constant_dynamic-slice_fusion.16.refs_9_), channel_id=1, source_target_pairs={{0,8},{4,12},{8,0},{12,4},{16,24},{20,28},{24,16},{28,20},{1,9},{5... | collective-permute-start | bytes 3538952 | tf_op jit(solution)/shard_map/ppermute | solution.py:887
  380.4 26.2 %collective-permute-start.39 = (bf16[4,48,1536]{2,1,0:T(8,128)(2,1)S(1)}, bf16[4,48,1536]{2,1,0:T(8,128)(2,1)}, u32[]{:S(2)}, u32[]{:S(2)}) collective-permute-start(bf16[4,48,1536]{2,1,0:T(8,128)(2,1)S(1)} %constant_dynamic-slice_fusion.11.refs_12_), channel_id=1, source_target_pairs={{0,16},{4,20},{8,24},{12,28},{16,0},{20,4},{24,8},{28,12},{1,17},{... | collective-permute-start | bytes 1769480 | tf_op jit(solution)/shard_map/ppermute | solution.py:887
  388.0 19.9 %collective-permute-start.40 = (bf16[4,48,1920]{2,1,0:T(8,128)(2,1)S(1)}, bf16[4,48,1920]{2,1,0:T(8,128)(2,1)}, u32[]{:S(2)}, u32[]{:S(2)}) collective-permute-start(bf16[4,48,1920]{2,1,0:T(8,128)(2,1)S(1)} %constant_dynamic-slice_fusion.8.refs_13_), channel_id=1, source_target_pairs={{0,8},{4,12},{8,0},{12,4},{16,24},{20,28},{24,16},{28,20},{1,9},{5... | collective-permute-start | bytes 2211848 | tf_op jit(solution)/shard_map/ppermute | solution.py:887
  432.6 71.5 %all-gather.3.cloned.1.call-start = ((), (), s32[]{:S(2)}) async-start(), calls=%async_computation.4 | async-start | bytes 2985984 | tf_op jit(solution)/shard_map/all_gather | solution.py:1434
  433.0 20.7 %collective-permute-start.42 = (bf16[4,96,640]{2,1,0:T(8,128)(2,1)S(1)}, bf16[4,96,640]{2,1,0:T(8,128)(2,1)S(1)}, u32[]{:S(2)}, u32[]{:S(2)}) collective-permute-start(bf16[4,96,640]{2,1,0:T(8,128)(2,1)S(1)} %constant_dynamic-slice_fusion.7), channel_id=1, source_target_pairs={{0,8},{4,12},{8,0},{12,4},{16,24},{20,28},{24,16},{28,20},{1,9},{5... | collective-permute-start | bytes 1474568 | tf_op jit(solution)/shard_map/ppermute | solution.py:887
  433.7 21.2 %collective-permute-start.45 = (bf16[4,96,640]{2,1,0:T(8,128)(2,1)}, bf16[4,96,640]{2,1,0:T(8,128)(2,1)S(1)}, u32[]{:S(2)}, u32[]{:S(2)}) collective-permute-start(bf16[4,96,640]{2,1,0:T(8,128)(2,1)} %pad_maximum_fusion.10), channel_id=1, source_target_pairs={{0,16},{4,20},{8,24},{12,28},{16,0},{20,4},{24,8},{28,12},{1,17},{... | collective-permute-start | bytes 1474568 | tf_op jit(solution)/shard_map/ppermute | solution.py:887
  434.8 18.9 %collective-permute-start.55 = (bf16[1,48,3456]{2,1,0:T(8,128)(2,1)S(1)}, bf16[1,48,3456]{2,1,0:T(8,128)(2,1)S(1)}, u32[]{:S(2)}, u32[]{:S(2)}) collective-permute-start(bf16[1,48,3456]{2,1,0:T(8,128)(2,1)S(1)} %bitcast.148), channel_id=1, source_target_pairs={{0,16},{4,20},{8,24},{12,28},{16,0},{20,4},{24,8},{28,12},{1,17},{... | collective-permute-start | bytes 995336 | tf_op jit(solution)/shard_map/ppermute | solution.py:887
  435.8 30.2 %collective-permute-start.53 = (bf16[2,48,1280]{2,1,0:T(8,128)(2,1)S(1)}, bf16[2,48,1280]{2,1,0:T(8,128)(2,1)S(1)}, u32[]{:S(2)}, u32[]{:S(2)}) collective-permute-start(bf16[2,48,1280]{2,1,0:T(8,128)(2,1)S(1)} %maximum_bitcast_fusion.2), channel_id=1, source_target_pairs={{0,8},{4,12},{8,0},{12,4},{16,24},{20,28},{24,16},{28,20},{1,9},{5... | collective-permute-start | bytes 737288 | tf_op jit(solution)/shard_map/ppermute | solution.py:887
  456.6 23.6 %collective-permute-start.56 = (bf16[2,48,3456]{2,1,0:T(8,128)(2,1)S(1)}, bf16[2,48,3456]{2,1,0:T(8,128)(2,1)S(1)}, u32[]{:S(2)}, u32[]{:S(2)}) collective-permute-start(bf16[2,48,3456]{2,1,0:T(8,128)(2,1)S(1)} %maximum_bitcast_fusion), channel_id=1, source_target_pairs={{0,8},{4,12},{8,0},{12,4},{16,24},{20,28},{24,16},{28,20},{1,9},{5... | collective-permute-start | bytes 1990664 | tf_op jit(solution)/shard_map/ppermute | solution.py:887
  473.4 17.9 %collective-permute-start.54 = (bf16[4,48,1280]{2,1,0:T(8,128)(2,1)S(1)}, bf16[4,48,1280]{2,1,0:T(8,128)(2,1)S(1)}, u32[]{:S(2)}, u32[]{:S(2)}) collective-permute-start(bf16[4,48,1280]{2,1,0:T(8,128)(2,1)S(1)} %bitcast.158), channel_id=1, source_target_pairs={{0,4},{4,0},{8,12},{12,8},{16,20},{20,16},{24,28},{28,24},{1,5},{5... | collective-permute-start | bytes 1474568 | tf_op jit(solution)/shard_map/ppermute | solution.py:887
  (119 other events, 780.9 us)
Sparse Core Ops, SparseCore 0:
  336.1 31.0 reduce-scatter.2
  432.8 30.4 reduce-scatter.4
  473.6 30.4 all-gather.2

commit v3 on v2

--- a/solution.py
+++ b/solution.py
@@ -943,19 +943,25 @@
         return jnp.concatenate(mine, -1)
 
 
-def narrow_sum_swaps(mine, ons=(None, None)):
+def narrow_parts(mine):
+    return mine.reshape((2,) * (mine.shape[0].bit_length() - 1) + mine.shape[1:])
+
+
+def narrow_level(cur, level, on=None):
     size = lax.axis_size("narrow")
-    place = lax.axis_index("narrow")
-    cur = mine.reshape((2,) * (size.bit_length() - 1) + mine.shape[1:])
     depth = size.bit_length() - 1
-    for level in range(depth):
-        bit = 1 << level
-        axis = depth - 1 - level
-        keep, give = halves(cur, (place // bit) % 2, axis)
-        recv = lax.ppermute(give, "narrow", [(i, i ^ bit) for i in range(size)])
-        if level < len(ons) and ons[level] is not None:
-            recv = tie(recv, ons[level])
-        cur = add_low(keep, recv)
+    bit = 1 << level
+    keep, give = halves(cur, (lax.axis_index("narrow") // bit) % 2, depth - 1 - level)
+    recv = lax.ppermute(give, "narrow", [(i, i ^ bit) for i in range(size)])
+    if on is not None:
+        recv = tie(recv, on)
+    return add_low(keep, recv)
+
+
+def narrow_sum_swaps(mine, ons=()):
+    cur = narrow_parts(mine)
+    for level in range(lax.axis_size("narrow").bit_length() - 1):
+        cur = narrow_level(cur, level, ons[level] if level < len(ons) else None)
     return cur.reshape(mine.shape[1:])
 
 
@@ -1402,19 +1408,15 @@
     halves0 = weight_grads(ff_jobs([a1, b1], [a2, b2], [a3, b3]), (mine_ff1, *flying))
     ff0 = ff_halving(core_sum(halves0))
     flying = ff0.step()
-    mine_at1 = at1.finish(halves0[-1][0])
     far_h = back_two(sent_h, pair_h, tie(pair_h2, a3[2]))
     b4 = backward_attention(
-        0, ib, segments, b1, b3[2], b3[3], weights, (*flying, mine_at1, far_h)
-    )
-    sum_at1 = narrow_sum(mine_at1)
-    sum_ff1 = narrow_sum_swaps(mine_ff1, (halves0[1][0], b4[1]))
+        0, ib, segments, b1, b3[2], b3[3], weights, (*flying, far_h)
+    )
     flying = ff0.step(b4[1])
-    a4 = backward_attention(
-        0, ia, segments, a1, a3[2], a3[3], weights, (b4[1], sum_at1, sum_ff1, *flying)
-    )
+    sum_at1 = narrow_sum(at1.finish(b4[1]))
+    a4 = backward_attention(0, ia, segments, a1, a3[2], a3[3], weights, (b4[1], *flying))
     mine_ff0 = ff0.finish(a4[1])
-    sum_ff0 = narrow_sum(mine_ff0)
+    sum_ff1 = narrow_sum_swaps(mine_ff1, (b4[1], a4[1]))
     half0 = weight_grads(
         (
             (
@@ -1423,16 +1425,21 @@
                 [a4[0], b4[0]],
             ),
         ),
-        (mine_ff0,),
-    )
+        (mine_ff0, sum_ff1),
+    )
+    part_ff0 = narrow_level(narrow_parts(mine_ff0), 0, half0[0][0])
+    got_ff1 = tie(swap(tie(sum_ff1, mine_ff0), wide_bits()[-1]), half0[0][0])
+    half0 = [(tie(half0[0][0], (part_ff0, got_ff1)), half0[0][1])]
+    all_ff1 = wide_gather_swaps(sum_ff1, got_ff1)
     small0 = small_pack([a2[6], b2[6]], [a3[4], b3[4], a4[2], b4[2]], narrow)
+    for level in range(1, narrow.bit_length() - 1):
+        part_ff0 = narrow_level(part_ff0, level, small0)
+    sum_ff0 = part_ff0.reshape(mine_ff0.shape[1:])
     at0 = attn_halving(core_sum(half0)[0], small0)
     flying = at0.step()
-    all_ff1 = wide_gather_swaps(tie(sum_ff1, flying[0]))
-    got = swap(tie(sum_at1, flying), wide_bits()[-1])
-    all_at1 = wide_gather_swaps(sum_at1, got)
-    all_ff0 = lax.all_gather(tie(sum_ff0, got), "wide", axis=0, tiled=False)
-    all_at0 = wide_gather_swaps(narrow_sum_swaps(at0.finish(), (sum_ff0,)))
+    all_ff0 = lax.all_gather(sum_ff0, "wide", axis=0, tiled=False)
+    all_at1 = wide_gather_swaps(tie(sum_at1, flying))
+    all_at0 = wide_gather_swaps(narrow_sum_swaps(at0.finish(), (None, all_ff0)))
 
     deep = ff_in.shape[2]
     unit = width // narrow

time: 526 us -> 529 us (level)
  waiting for transfers between devices: 81.7 us -> 68.8 us
  starting transfers between devices: 56.9 us -> 63.9 us
    ppermute x35, waiting for transfers between devices: 52.6 us -> 46.5 us  [swap(): return lax.ppermute(value, 'wide', [(i, i ^ bit) for i in range(size)])]
    ppermute x35, starting transfers between devices: 29.3 us -> 35.4 us  [swap(): return lax.ppermute(value, 'wide', [(i, i ^ bit) for i in range(size)])]
    ppermute x4 -> x6, waiting for transfers between devices: 14.3 us -> 11.7 us  [narrow_level(): recv = lax.ppermute(give, 'narrow', [(i, i ^ bit) for i in range(size)])]
    unnamed x215 -> x221, local copies, waits for them, and re-layouts: 23.3 us -> 21.9 us
    convert_element_type x27 -> x30, other arithmetic: 24.6 us -> 25.7 us  [add_low(): return (left.astype(F32) + right.astype(F32)).astype(BF16)]
  transfers between devices with their start and end apart: 61 -> 62, of which waited for: 16 -> 15; matrix products, arithmetic and copies ran while one was open for 11% -> 14% of each run, Pallas kernels for 37% -> 38%
where the time goes in v3:
time: 529 us; the launch traced here: 524 us
  Pallas kernels  264 us (50%)
  waiting for transfers between devices  68.8 us (13%)
  starting transfers between devices  63.9 us (12%)
  other arithmetic  62.3 us (12%)
  local copies, waits for them, and re-layouts  39.1 us (7%)
  between operations  25.5 us (5%)
    pallas_call x12, Pallas kernels, call(): pl.pallas_call(body, out_shape=outs, in_specs=list(in_specs) + [ANY] * ex...  182 us
    ppermute x35, waiting for transfers between devices, swap(): return lax.ppermute(value, 'wide', [(i, i ^ bit) for i in range(size)])  46.5 us
    pallas_call x6, Pallas kernels, weight_grad_cols(): pl.pallas_call(partial(grad_cols_kernel, rows=rows, steps=steps), out_sha...  41.5 us
    ppermute x35, starting transfers between devices, swap(): return lax.ppermute(value, 'wide', [(i, i ^ bit) for i in range(size)])  35.4 us
    convert_element_type x30, other arithmetic, add_low(): return (left.astype(F32) + right.astype(F32)).astype(BF16)  25.7 us
    unnamed x221, local copies, waits for them, and re-layouts  21.9 us
    pallas_call x2, Pallas kernels, weight_grad_rows(): pl.pallas_call(partial(grad_rows_kernel, rows=rows, narrow=narrow), out_s...  19.8 us
    ppermute x8, starting transfers between devices, shift(): lax.ppermute(value, 'narrow', inner)  12.7 us
  transfers between devices with their start and end apart: 62, of which 15 were waited for; matrix products, arithmetic and copies ran while one was open for 14% of the time, Pallas kernels for 38%

profile of v3, /device:TPU:0, one launch (start us, length us, event | category | flops | bytes accessed | tf_op | source)
XLA Modules:
  0.0 523.8 jit_solution(9172913542222714212)
XLA Ops:
  15.4 14.2 %forward_attention0.2 = (bf16[512,2304]{1,0:T(8,128)(2,1)}, f32[16,512]{1,0:T(8,128)S(1)}, bf16[512,768]{1,0:T(8,128)(2,1)S(1)}, bf16[512,768]{1,0:T(8,128)(2,1)...) custom-call(s32[1]{0:T(128)} %select_n.520.refs_0_, bf16[2,512,768]{2,1,0:T(8,128)(2,1)} %refs_1_.5, ...), custom_call_target="tpu_custom_call" | custom-call | flops 14000000000 | bytes 16000000 | tf_op jit(solution)/shard_map/forward_attention0/pallas_call | solution.py:110
  32.7 3.0 collective-permute-start
  35.7 2.6 collective-permute-start.1
  42.8 17.4 %forward_ff0.2 = (bf16[512,3072]{1,0:T(8,128)(2,1)}, bf16[512,3072]{1,0:T(8,128)(2,1)}, bf16[512,768]{1,0:T(8,128)(2,1)}, bf16[528,768]{1,0:T(8,128)(2,1)}, f32[...) custom-call(s32[1]{0:T(128)} %select_n.520.refs_0_, ...), custom_call_target="tpu_custom_call" | custom-call | flops 17999998976 | bytes 20000000 | tf_op jit(solution)/shard_map/forward_ff0/pallas_call | solution.py:110
  64.5 3.2 route.1
  78.5 14.2 %forward_attention0.3 = (bf16[512,2304]{1,0:T(8,128)(2,1)}, f32[16,512]{1,0:T(8,128)S(1)}, bf16[512,768]{1,0:T(8,128)(2,1)S(1)}, bf16[512,768]{1,0:T(8,128)(2,1)...) custom-call(s32[1]{0:T(128)} %bitcast.6.refs_0_, bf16[2,512,768]{2,1,0:T(8,128)(2,1)} %refs_1_.5, ...), custom_call_target="tpu_custom_call" | custom-call | flops 14000000000 | bytes 16000000 | tf_op jit(solution)/shard_map/forward_attention0/pallas_call | solution.py:110
  97.4 17.2 %forward_ff0.3 = (bf16[512,3072]{1,0:T(8,128)(2,1)}, bf16[512,3072]{1,0:T(8,128)(2,1)}, bf16[512,768]{1,0:T(8,128)(2,1)}, bf16[528,768]{1,0:T(8,128)(2,1)}, f32[...) custom-call(s32[1]{0:T(128)} %bitcast.6.refs_0_, ...), custom_call_target="tpu_custom_call" | custom-call | flops 17999998976 | bytes 20000000 | tf_op jit(solution)/shard_map/forward_ff0/pallas_call | solution.py:110
  119.2 14.3 %forward_attention1.1 = (bf16[512,2304]{1,0:T(8,128)(2,1)}, f32[16,512]{1,0:T(8,128)S(1)}, bf16[512,768]{1,0:T(8,128)(2,1)S(1)}, bf16[512,768]{1,0:T(8,128)(2,1)...) custom-call(s32[1]{0:T(128)} %constant.248.clone.1.refs_0_, ...), custom_call_target="tpu_custom_call" | custom-call | flops 14000000000 | bytes 16000000 | tf_op jit(solution)/shard_map/forward_attention1/pallas_call | solution.py:110
  136.0 17.1 %forward_ff1.1 = (bf16[512,3072]{1,0:T(8,128)(2,1)}, bf16[512,3072]{1,0:T(8,128)(2,1)}, bf16[512,768]{1,0:T(8,128)(2,1)}, bf16[528,768]{1,0:T(8,128)(2,1)}, f32[...) custom-call(s32[1]{0:T(128)} %constant.248.clone.1.refs_0_, ...), custom_call_target="tpu_custom_call" | custom-call | flops 17999998976 | bytes 20000000 | tf_op jit(solution)/shard_map/forward_ff1/pallas_call | solution.py:110
  153.9 13.4 %backward_ff1.1 = (bf16[512,768]{1,0:T(8,128)(2,1)S(1)}, bf16[512,3072]{1,0:T(8,128)(2,1)}, bf16[512,768]{1,0:T(8,128)(2,1)}, f32[512,768]{1,0:T(8,128)}, f32[8,3072]{1,0:T(8,128)S(1)}) custom-call(bf16[512,768]{1,0:T(8,128)(2,1)} %bitcast_select_fusion.1.refs_19_.refs_0_, bf16[512,128]{1,0:T(8,128)(2,1)S(1)} %get-tuple-element.188.refs_1_, ...), custom_call_target="tpu_custom_call" | custom-call | flops 16000000000 | bytes 22000000 | tf_op jit(solution)/shard_map/backward_ff1/pallas_call | solution.py:110
  167.3 8.8 %weight_grad_rows.2 = (bf16[4,192,1536]{2,1,0:T(8,128)(2,1)}, bf16[4,192,1536]{2,1,0:T(8,128)(2,1)}) custom-call(s32[1]{0:T(128)} %bitcast.18.half_ref, bf16[512,3072]{1,0:T(8,128)(2,1)} %get-tuple-element.198.refs_0_, bf16[512,768]{1,0:T(8,128)(2,1)S(1)} %get-tuple-element.199.refs_1_), custom_call_target="tpu_custom_call" | custom-call | flops 1000000 | bytes 100000 | tf_op jit(solution)/shard_map/weight_grad_rows/pallas_call | solution.py:865
  176.9 3.0 weight_grad_cols.7
  180.3 7.1 %weight_grad_cols.6 = (bf16[4,192,1536]{2,1,0:T(8,128)(2,1)}, bf16[4,192,1536]{2,1,0:T(8,128)(2,1)}) custom-call(s32[1]{0:T(128)} %bitcast.18.half_ref, bf16[512,768]{1,0:T(8,128)(2,1)S(1)} %copy-done.7, bf16[512,3072]{1,0:T(8,128)(2,1)} %get-tuple-element.196.refs_1_), custom_call_target="tpu_custom_call" | custom-call | flops 1000000 | bytes 100000 | tf_op jit(solution)/shard_map/weight_grad_cols/pallas_call | solution.py:805
  187.5 15.2 %backward_attention1.1 = (bf16[512,2304]{1,0:T(8,128)(2,1)}, bf16[512,768]{1,0:T(8,128)(2,1)S(1)}, f32[8,3072]{1,0:T(8,128)S(1)}) custom-call(s32[1]{0:T(128)} %constant.248.clone.1.refs_0_, s32[1,512]{1,0:T(1,128)S(1)} %slice_convert_fusion.refs_2_.refs_4_.refs_1_, f32[16,512]{1,0:T(8,128)S(1)} %get-tuple-element.185.refs_2_, ...), custom_call_target="tpu_custom_call" | custom-call | flops 20000000000 | bytes 16000000 | tf_op jit(solution)/shard_map/backward_attention1/pallas_call | solution.py:110
  206.1 2.3 add_convert_fusion.2
  211.8 2.3 add_convert_fusion.3
  215.5 7.5 %weight_grad_cols.8 = (bf16[4,192,1152]{2,1,0:T(8,128)(2,1)}, bf16[4,192,1152]{2,1,0:T(8,128)(2,1)}) custom-call(s32[1]{0:T(128)} %bitcast.18.half_ref, bf16[512,768]{1,0:T(8,128)(2,1)S(1)} %slice.121.refs_0_, bf16[512,2304]{1,0:T(8,128)(2,1)} %get-tuple-element.203.refs_1_, bf16[4,96,1536]{2,1,0:T(8,128)(2,1)S(1)} %constant_dynamic-slice_fusion.31.refs_2_, ...), custom_call_target="tpu_custom_call" | custom-call | flops 1000000 | bytes 100000 | tf_op jit(solution)/shard_map/weight_grad_cols/pallas_call | solution.py:805
  231.0 2.3 bitcast_select_fusion.refs_0_
  237.1 9.0 %collective-permute-done.18 = bf16[512,768]{1,0:T(8,128)(2,1)} collective-permute-done((bf16[512,768]{1,0:T(8,128)(2,1)}, bf16[512,768]{1,0:T(8,128)(2,1)}, u32[]{:S(2)}, u32[]{:S(2)}) %collective-permute-start.18) | collective-permute-done | bytes 786464 | tf_op jit(solution)/shard_map/ppermute | solution.py:1309
  246.1 14.0 %backward_ff0.2 = (bf16[512,768]{1,0:T(8,128)(2,1)}, bf16[512,3072]{1,0:T(8,128)(2,1)}, bf16[512,768]{1,0:T(8,128)(2,1)}, f32[512,768]{1,0:T(8,128)}, f32[8,3072]{1,0:T(8,128)S(1)}) custom-call(bf16[512,768]{1,0:T(8,128)(2,1)} %bitcast_select_fusion.refs_0_, bf16[512,128]{1,0:T(8,128)(2,1)S(1)} %copy-done.54, f32[512,128]{1,0:T(8,128)S(1)} %copy-done.48, ...), custom_call_target="tpu_custom_call" | custom-call | flops 16000000000 | bytes 22000000 | tf_op jit(solution)/shard_map/backward_ff0/pallas_call | solution.py:110
  260.7 2.3 broadcast_select_fusion.4
  263.0 2.3 broadcast_select_fusion.1.refs_15_
  265.3 3.3 collective-permute-start.20
  270.1 2.4 collective-permute-start.26
  278.8 13.9 %backward_ff0.3 = (bf16[512,768]{1,0:T(8,128)(2,1)}, bf16[512,3072]{1,0:T(8,128)(2,1)}, bf16[512,768]{1,0:T(8,128)(2,1)}, f32[512,768]{1,0:T(8,128)}, f32[8,3072]{1,0:T(8,128)S(1)}) custom-call(bf16[512,768]{1,0:T(8,128)(2,1)} %broadcast_select_fusion.4, bf16[512,128]{1,0:T(8,128)(2,1)S(1)} %copy-done.52, f32[512,128]{1,0:T(8,128)S(1)} %copy-done.44, ...), custom_call_target="tpu_custom_call" | custom-call | flops 16000000000 | bytes 22000000 | tf_op jit(solution)/shard_map/backward_ff0/pallas_call | solution.py:110
  293.7 2.7 broadcast_select_fusion.3
  300.3 5.0 collective-permute-done.28
  305.5 11.1 %weight_grad_rows.3 = (bf16[4,192,1536]{2,1,0:T(8,128)(2,1)}, bf16[4,192,1536]{2,1,0:T(8,128)(2,1)}) custom-call(s32[1]{0:T(128)} %bitcast.18.half_ref, bf16[512,3072]{1,0:T(8,128)(2,1)} %get-tuple-element.252.refs_0_, bf16[512,3072]{1,0:T(8,128)(2,1)} %get-tuple-element.253.refs_1_, bf16[512,768]{1,0:T(8,128)(2,1)S(1)} %copy-done.5, ...), custom_call_target="tpu_custom_call" | custom-call | flops 1000000 | bytes 100000 | tf_op jit(solution)/shard_map/weight_grad_rows/pallas_call | solution.py:865
  317.9 10.1 %weight_grad_cols.9 = (bf16[4,192,1536]{2,1,0:T(8,128)(2,1)}, bf16[4,192,1536]{2,1,0:T(8,128)(2,1)}) custom-call(s32[1]{0:T(128)} %bitcast.18.half_ref, bf16[512,768]{1,0:T(8,128)(2,1)S(1)} %copy-done.2, bf16[512,768]{1,0:T(8,128)(2,1)} %get-tuple-element.172.refs_1_, bf16[512,3072]{1,0:T(8,128)(2,1)} %get-tuple-element.244.refs_2_, ...), custom_call_target="tpu_custom_call" | custom-call | flops 1000000 | bytes 100000 | tf_op jit(solution)/shard_map/weight_grad_cols/pallas_call | solution.py:805
  328.6 4.2 weight_grad_cols.10
  335.0 2.2 collective-permute-start.37
  342.5 2.3 add_convert_fusion.1
  349.3 15.2 %backward_attention0.2 = (bf16[512,2304]{1,0:T(8,128)(2,1)}, bf16[512,768]{1,0:T(8,128)(2,1)S(1)}, f32[8,3072]{1,0:T(8,128)S(1)}) custom-call(s32[1]{0:T(128)} %bitcast.6.refs_0_, s32[2,512]{1,0:T(2,128)S(1)} %copy-done.33, f32[16,512]{1,0:T(8,128)S(1)} %copy-done.56, bf16[2,768,2304]{2,1,0:T(8,128)(2,1)} %refs_3_.11, bf16[2,768,768]{2,1,0:T(8,128)(2,1)} %refs_4_.21, ...), custom_call_target="tpu_custom_call" | custom-call | flops 20000000000 | bytes 16000000 | tf_op jit(solution)/shard_map/backward_attention0/pallas_call | solution.py:110
  370.5 4.7 collective-permute-done.33
  378.9 3.9 collective-permute-done.34
  386.5 16.3 %backward_attention0.3 = (bf16[512,2304]{1,0:T(8,128)(2,1)}, bf16[512,768]{1,0:T(8,128)(2,1)}, f32[8,3072]{1,0:T(8,128)S(1)}) custom-call(s32[1]{0:T(128)} %select_n.520.refs_0_, s32[2,512]{1,0:T(2,128)S(1)} %copy-done.33, f32[16,512]{1,0:T(8,128)S(1)} %copy-done.58, bf16[2,768,2304]{2,1,0:T(8,128)(2,1)} %refs_3_.11, bf16[2,768,768]{2,1,0:T(8,128)(2,1)} %refs_4_.21, ...), custom_call_target="tpu_custom_call" | custom-call | flops 20000000000 | bytes 16000000 | tf_op jit(solution)/shard_map/backward_attention0/pallas_call | solution.py:110
  413.1 9.6 %weight_grad_cols.11 = (bf16[4,192,1152]{2,1,0:T(8,128)(2,1)}, bf16[4,192,1152]{2,1,0:T(8,128)(2,1)}) custom-call(s32[1]{0:T(128)} %bitcast.18.half_ref, bf16[512,768]{1,0:T(8,128)(2,1)S(1)} %get-tuple-element.381.refs_0_, bf16[512,768]{1,0:T(8,128)(2,1)S(1)} %get-tuple-element.380.refs_1_, bf16[512,2304]{1,0:T(8,128)(2,1)} %get-tuple-element.264.refs_2_, ...), custom_call_target="tpu_custom_call" | custom-call | flops 1000000 | bytes 100000 | tf_op jit(solution)/shard_map/weight_grad_cols/pallas_call | solution.py:805
  423.9 5.4 %collective-permute-done.39 = bf16[2,1,48,3456]{3,2,1,0:T(8,128)(2,1)S(1)} collective-permute-done((bf16[2,1,48,3456]{3,2,1,0:T(8,128)(2,1)S(1)}, bf16[2,1,48,3456]{3,2,1,0:T(8,128)(2,1)S(1)}, u32[]{:S(2)}, u32[]{:S(2)}) %collective-permute-start.39) | collective-permute-done | bytes 663584 | tf_op jit(solution)/shard_map/ppermute | solution.py:955
  431.6 8.5 %collective-permute-done.58 = bf16[2,48,3456]{2,1,0:T(8,128)(2,1)S(1)} collective-permute-done((bf16[2,48,3456]{2,1,0:T(8,128)(2,1)S(1)}, bf16[2,48,3456]{2,1,0:T(8,128)(2,1)S(1)}, u32[]{:S(2)}, u32[]{:S(2)}) %collective-permute-start.58) | collective-permute-done | bytes 663584 | tf_op jit(solution)/shard_map/ppermute | solution.py:887
  441.4 6.2 %collective-permute-done.49 = bf16[1,1,48,3456]{3,2,1,0:T(8,128)(2,1)S(1)} collective-permute-done((bf16[1,1,48,3456]{3,2,1,0:T(8,128)(2,1)S(1)}, bf16[1,1,48,3456]{3,2,1,0:T(8,128)(2,1)S(1)}, u32[]{:S(2)}, u32[]{:S(2)}) %collective-permute-start.49) | collective-permute-done | bytes 331808 | tf_op jit(solution)/shard_map/ppermute | solution.py:955
  454.4 11.3 %collective-permute-done.42 = bf16[4,96,640]{2,1,0:T(8,128)(2,1)} collective-permute-done((bf16[4,96,640]{2,1,0:T(8,128)(2,1)}, bf16[4,96,640]{2,1,0:T(8,128)(2,1)}, u32[]{:S(2)}, u32[]{:S(2)}) %collective-permute-start.42) | collective-permute-done | bytes 491552 | tf_op jit(solution)/shard_map/ppermute | solution.py:887
  473.2 4.3 collective-permute-done.46
  479.5 4.3 place_ff1.1
  485.3 3.7 collective-permute-done.55
  492.0 3.2 collective-permute-start.56
  495.3 4.8 collective-permute-start.51
  500.3 4.0 collective-permute-done.51
  506.1 4.4 place_ff0.1
  (452 shorter events, 138.7 us)
Async XLA Ops:
  8.0 475.8 %reduce-scatter.2.cloned.1.call-start = ((), (), s32[]{:S(2)}) async-start(), calls=%async_computation.1 | async-start | bytes 614400 | tf_op jit(solution)/shard_map/reduce_scatter | solution.py:980
  32.7 30.4 %collective-permute-start = (s32[1]{0:T(128)}, s32[1]{0:T(128)}, u32[]{:S(2)}, u32[]{:S(2)}) collective-permute-start(s32[1]{0:T(128)} %bitcast.2.refs_0_), channel_id=1, source_target_pairs={{0,1},{1,2},{2,3},{3,0},{4,5},{5,6},{6,7},{7,4},{8,9},{9,10},{10,1... | collective-permute-start | bytes 20 | tf_op jit(solution)/shard_map/ppermute | solution.py:1290
  35.7 28.7 %collective-permute-start.1 = (s32[1]{0:T(128)}, s32[1]{0:T(128)}, u32[]{:S(2)}, u32[]{:S(2)}) collective-permute-start(s32[1]{0:T(128)} %bitcast.2.refs_0_), channel_id=1, source_target_pairs={{0,2},{1,3},{2,0},{3,1},{4,6},{5,7},{6,4},{7,5},{8,10},{9,11},{10,... | collective-permute-start | bytes 20 | tf_op jit(solution)/shard_map/ppermute | solution.py:1290
  38.3 26.2 %collective-permute-start.2 = (s32[1]{0:T(128)}, s32[1]{0:T(128)}, u32[]{:S(2)}, u32[]{:S(2)}) collective-permute-start(s32[1]{0:T(128)} %bitcast.2.refs_0_), channel_id=1, source_target_pairs={{0,3},{1,0},{2,1},{3,2},{4,7},{5,4},{6,5},{7,6},{8,11},{9,8},{10,9... | collective-permute-start | bytes 20 | tf_op jit(solution)/shard_map/ppermute | solution.py:1290
  41.7 34.7 %collective-permute-start.3 = (bf16[512,768]{1,0:T(8,128)(2,1)S(1)}, bf16[512,768]{1,0:T(8,128)(2,1)}, u32[]{:S(2)}, u32[]{:S(2)}) collective-permute-start(bf16[512,768]{1,0:T(8,128)(2,1)S(1)} %get-tuple-element.169.refs_19_), channel_id=1, source_target_pairs={{0,1},{1,0},{2,3},{3,2},{4,5},{5,4},{6,7},{7,6},{8,9},{9,8},{10,11... | collective-permute-start | bytes 2359304 | tf_op jit(solution)/shard_map/ppermute | solution.py:1309
  42.5 33.9 %collective-permute-start.4 = (bf16[512,768]{1,0:T(8,128)(2,1)S(1)}, bf16[512,768]{1,0:T(8,128)(2,1)}, u32[]{:S(2)}, u32[]{:S(2)}) collective-permute-start(bf16[512,768]{1,0:T(8,128)(2,1)S(1)} %get-tuple-element.169.refs_19_), channel_id=1, source_target_pairs={{0,4},{1,2},{2,1},{3,7},{4,0},{5,6},{6,5},{7,3},{8,12},{9,10},{10,... | collective-permute-start | bytes 2359304 | tf_op jit(solution)/shard_map/ppermute | solution.py:1310
  63.1 30.5 %collective-permute-start.5 = (bf16[528,768]{1,0:T(8,128)(2,1)}, bf16[528,768]{1,0:T(8,128)(2,1)}, u32[]{:S(2)}, u32[]{:S(2)}) collective-permute-start(bf16[528,768]{1,0:T(8,128)(2,1)} %get-tuple-element.168.refs_9_), channel_id=1, source_target_pairs={{0,1},{1,0},{2,3},{3,2},{4,5},{5,4},{6,7},{7,6},{8,9},{9,8},{10,11... | collective-permute-start | bytes 2433032 | tf_op jit(solution)/shard_map/ppermute | solution.py:1309
  64.5 29.1 %collective-permute-start.6 = (bf16[528,768]{1,0:T(8,128)(2,1)}, bf16[528,768]{1,0:T(8,128)(2,1)}, u32[]{:S(2)}, u32[]{:S(2)}) collective-permute-start(bf16[528,768]{1,0:T(8,128)(2,1)} %get-tuple-element.168.refs_9_), channel_id=1, source_target_pairs={{0,4},{1,2},{2,1},{3,7},{4,0},{5,6},{6,5},{7,3},{8,12},{9,10},{10,... | collective-permute-start | bytes 2433032 | tf_op jit(solution)/shard_map/ppermute | solution.py:1310
  95.2 21.6 %collective-permute-start.7 = (bf16[528,768]{1,0:T(8,128)(2,1)S(1)}, bf16[528,768]{1,0:T(8,128)(2,1)S(1)}, u32[]{:S(2)}, u32[]{:S(2)}) collective-permute-start(bf16[528,768]{1,0:T(8,128)(2,1)S(1)} %broadcast_select_fusion.2.refs_19_), channel_id=1, source_target_pairs={{0,1},{1,0},{2,3},{3,2},{4,5},{5,4},{6,7},{7,6},{8,9},{9,8},{10,11... | collective-permute-start | bytes 2433032 | tf_op jit(solution)/shard_map/ppermute | solution.py:1309
  97.4 19.5 %collective-permute-start.8 = (bf16[528,768]{1,0:T(8,128)(2,1)S(1)}, bf16[528,768]{1,0:T(8,128)(2,1)S(1)}, u32[]{:S(2)}, u32[]{:S(2)}) collective-permute-start(bf16[528,768]{1,0:T(8,128)(2,1)S(1)} %broadcast_select_fusion.2.refs_19_), channel_id=1, source_target_pairs={{0,4},{1,2},{2,1},{3,7},{4,0},{5,6},{6,5},{7,3},{8,12},{9,10},{10,... | collective-permute-start | bytes 2433032 | tf_op jit(solution)/shard_map/ppermute | solution.py:1310
  114.7 18.9 %collective-permute-start.10 = (bf16[512,768]{1,0:T(8,128)(2,1)S(1)}, bf16[512,768]{1,0:T(8,128)(2,1)S(1)}, u32[]{:S(2)}, u32[]{:S(2)}) collective-permute-start(bf16[512,768]{1,0:T(8,128)(2,1)S(1)} %copy-done.87), channel_id=1, source_target_pairs={{0,4},{1,2},{2,1},{3,7},{4,0},{5,6},{6,5},{7,3},{8,12},{9,10},{10,... | collective-permute-start | bytes 2359304 | tf_op jit(solution)/shard_map/ppermute | solution.py:1310
  115.2 19.5 %collective-permute-start.9 = (bf16[512,768]{1,0:T(8,128)(2,1)S(1)}, bf16[512,768]{1,0:T(8,128)(2,1)S(1)}, u32[]{:S(2)}, u32[]{:S(2)}) collective-permute-start(bf16[512,768]{1,0:T(8,128)(2,1)S(1)} %copy-done.87), channel_id=1, source_target_pairs={{0,1},{1,0},{2,3},{3,2},{4,5},{5,4},{6,7},{7,6},{8,9},{9,8},{10,11... | collective-permute-start | bytes 2359304 | tf_op jit(solution)/shard_map/ppermute | solution.py:1309
  176.1 30.0 %collective-permute-start.16 = (bf16[4,192,1536]{2,1,0:T(8,128)(2,1)}, bf16[4,192,1536]{2,1,0:T(8,128)(2,1)}, u32[]{:S(2)}, u32[]{:S(2)}) collective-permute-start(bf16[4,192,1536]{2,1,0:T(8,128)(2,1)} %get-tuple-element.200.refs_10_), channel_id=1, source_target_pairs={{0,4},{4,0},{8,12},{12,8},{16,20},{20,16},{24,28},{28,24},{1,5},{5... | collective-permute-start | bytes 7077896 | tf_op jit(solution)/shard_map/ppermute | solution.py:887
  179.8 25.3 %collective-permute-start.17 = (bf16[4,192,384]{2,1,0:T(8,128)(2,1)S(1)}, bf16[4,192,384]{2,1,0:T(8,128)(2,1)S(1)}, u32[]{:S(2)}, u32[]{:S(2)}) collective-permute-start(bf16[4,192,384]{2,1,0:T(8,128)(2,1)S(1)} %get-tuple-element.201.refs_11_), channel_id=1, source_target_pairs={{0,4},{4,0},{8,12},{12,8},{16,20},{20,16},{24,28},{28,24},{1,5},{5... | collective-permute-start | bytes 1769480 | tf_op jit(solution)/shard_map/ppermute | solution.py:887
  187.5 23.3 %collective-permute-start.15 = (bf16[4,192,1536]{2,1,0:T(8,128)(2,1)}, bf16[4,192,1536]{2,1,0:T(8,128)(2,1)}, u32[]{:S(2)}, u32[]{:S(2)}) collective-permute-start(bf16[4,192,1536]{2,1,0:T(8,128)(2,1)} %get-tuple-element.197.refs_9_), channel_id=1, source_target_pairs={{0,4},{4,0},{8,12},{12,8},{16,20},{20,16},{24,28},{28,24},{1,5},{5... | collective-permute-start | bytes 7077896 | tf_op jit(solution)/shard_map/ppermute | solution.py:887
  203.5 20.0 %collective-permute-start.13 = (bf16[512,768]{1,0:T(8,128)(2,1)S(1)}, bf16[512,768]{1,0:T(8,128)(2,1)S(1)}, u32[]{:S(2)}, u32[]{:S(2)}) collective-permute-start(bf16[512,768]{1,0:T(8,128)(2,1)S(1)} %get-tuple-element.202), channel_id=1, source_target_pairs={{0,1},{1,0},{2,3},{3,2},{4,5},{5,4},{6,7},{7,6},{8,9},{9,8},{10,11... | collective-permute-start | bytes 2359304 | tf_op jit(solution)/shard_map/ppermute | solution.py:1309
  205.0 18.5 %collective-permute-start.14 = (bf16[512,768]{1,0:T(8,128)(2,1)S(1)}, bf16[512,768]{1,0:T(8,128)(2,1)S(1)}, u32[]{:S(2)}, u32[]{:S(2)}) collective-permute-start(bf16[512,768]{1,0:T(8,128)(2,1)S(1)} %get-tuple-element.202), channel_id=1, source_target_pairs={{0,4},{1,2},{2,1},{3,7},{4,0},{5,6},{6,5},{7,3},{8,12},{9,10},{10,... | collective-permute-start | bytes 2359304 | tf_op jit(solution)/shard_map/ppermute | solution.py:1310
  225.3 20.7 %collective-permute-start.18 = (bf16[512,768]{1,0:T(8,128)(2,1)}, bf16[512,768]{1,0:T(8,128)(2,1)}, u32[]{:S(2)}, u32[]{:S(2)}) collective-permute-start(bf16[512,768]{1,0:T(8,128)(2,1)} %broadcast_select_fusion.5.refs_12_), channel_id=1, source_target_pairs={{0,1},{1,0},{2,3},{3,2},{4,5},{5,4},{6,7},{7,6},{8,9},{9,8},{10,11... | collective-permute-start | bytes 2359304 | tf_op jit(solution)/shard_map/ppermute | solution.py:1309
  226.7 36.3 %collective-permute-start.11 = (bf16[528,768]{1,0:T(8,128)(2,1)}, bf16[528,768]{1,0:T(8,128)(2,1)}, u32[]{:S(2)}, u32[]{:S(2)}) collective-permute-start(bf16[528,768]{1,0:T(8,128)(2,1)} %get-tuple-element.184.refs_11_), channel_id=1, source_target_pairs={{0,1},{1,0},{2,3},{3,2},{4,5},{5,4},{6,7},{7,6},{8,9},{9,8},{10,11... | collective-permute-start | bytes 2433032 | tf_op jit(solution)/shard_map/ppermute | solution.py:1309
  227.4 35.6 %collective-permute-start.12 = (bf16[528,768]{1,0:T(8,128)(2,1)}, bf16[528,768]{1,0:T(8,128)(2,1)}, u32[]{:S(2)}, u32[]{:S(2)}) collective-permute-start(bf16[528,768]{1,0:T(8,128)(2,1)} %get-tuple-element.184.refs_11_), channel_id=1, source_target_pairs={{0,4},{1,2},{2,1},{3,7},{4,0},{5,6},{6,5},{7,3},{8,12},{9,10},{10,... | collective-permute-start | bytes 2433032 | tf_op jit(solution)/shard_map/ppermute | solution.py:1310
  234.1 38.4 %collective-permute-start.25 = (bf16[4,96,1920]{2,1,0:T(8,128)(2,1)S(1)}, bf16[4,96,1920]{2,1,0:T(8,128)(2,1)}, u32[]{:S(2)}, u32[]{:S(2)}) collective-permute-start(bf16[4,96,1920]{2,1,0:T(8,128)(2,1)S(1)} %copy-done.68), channel_id=1, source_target_pairs={{0,16},{4,20},{8,24},{12,28},{16,0},{20,4},{24,8},{28,12},{1,17},{... | collective-permute-start | bytes 4423688 | tf_op jit(solution)/shard_map/ppermute | solution.py:887
  235.6 33.3 %collective-permute-start.24 = (bf16[4,96,1536]{2,1,0:T(8,128)(2,1)S(1)}, bf16[4,96,1536]{2,1,0:T(8,128)(2,1)S(1)}, u32[]{:S(2)}, u32[]{:S(2)}) collective-permute-start(bf16[4,96,1536]{2,1,0:T(8,128)(2,1)S(1)} %constant_dynamic-slice_fusion.31.refs_2_), channel_id=1, source_target_pairs={{0,8},{4,12},{8,0},{12,4},{16,24},{20,28},{24,16},{28,20},{1,9},{5... | collective-permute-start | bytes 3538952 | tf_op jit(solution)/shard_map/ppermute | solution.py:887
  246.0 14.1 %collective-permute-start.19 = (bf16[512,768]{1,0:T(8,128)(2,1)}, bf16[512,768]{1,0:T(8,128)(2,1)S(1)}, u32[]{:S(2)}, u32[]{:S(2)}) collective-permute-start(bf16[512,768]{1,0:T(8,128)(2,1)} %broadcast_select_fusion.5.refs_12_), channel_id=1, source_target_pairs={{0,4},{1,2},{2,1},{3,7},{4,0},{5,6},{6,5},{7,3},{8,12},{9,10},{10,... | collective-permute-start | bytes 2359304 | tf_op jit(solution)/shard_map/ppermute | solution.py:1310
  260.1 15.8 %collective-permute-start.22 = (bf16[4,192,1152]{2,1,0:T(8,128)(2,1)}, bf16[4,192,1152]{2,1,0:T(8,128)(2,1)S(1)}, u32[]{:S(2)}, u32[]{:S(2)}) collective-permute-start(bf16[4,192,1152]{2,1,0:T(8,128)(2,1)} %get-tuple-element.207.refs_11_), channel_id=1, source_target_pairs={{0,4},{4,0},{8,12},{12,8},{16,20},{20,16},{24,28},{28,24},{1,5},{5... | collective-permute-start | bytes 5308424 | tf_op jit(solution)/shard_map/ppermute | solution.py:887
  265.3 27.3 %collective-permute-start.20 = (bf16[528,768]{1,0:T(8,128)(2,1)}, bf16[528,768]{1,0:T(8,128)(2,1)S(1)}, u32[]{:S(2)}, u32[]{:S(2)}) collective-permute-start(bf16[528,768]{1,0:T(8,128)(2,1)} %broadcast_select_fusion.1.refs_15_), channel_id=1, source_target_pairs={{0,1},{1,0},{2,3},{3,2},{4,5},{5,4},{6,7},{7,6},{8,9},{9,8},{10,11... | collective-permute-start | bytes 2433032 | tf_op jit(solution)/shard_map/ppermute | solution.py:1309
  268.7 25.0 %collective-permute-start.21 = (bf16[528,768]{1,0:T(8,128)(2,1)}, bf16[528,768]{1,0:T(8,128)(2,1)}, u32[]{:S(2)}, u32[]{:S(2)}) collective-permute-start(bf16[528,768]{1,0:T(8,128)(2,1)} %broadcast_select_fusion.1.refs_15_), channel_id=1, source_target_pairs={{0,4},{1,2},{2,1},{3,7},{4,0},{5,6},{6,5},{7,3},{8,12},{9,10},{10,... | collective-permute-start | bytes 2433032 | tf_op jit(solution)/shard_map/ppermute | solution.py:1310
  270.1 26.3 %collective-permute-start.26 = (bf16[4,48,1536]{2,1,0:T(8,128)(2,1)}, bf16[4,48,1536]{2,1,0:T(8,128)(2,1)}, u32[]{:S(2)}, u32[]{:S(2)}) collective-permute-start(bf16[4,48,1536]{2,1,0:T(8,128)(2,1)} %constant_dynamic-slice_fusion.25.refs_13_), channel_id=1, source_target_pairs={{0,16},{4,20},{8,24},{12,28},{16,0},{20,4},{24,8},{28,12},{1,17},{... | collective-permute-start | bytes 1769480 | tf_op jit(solution)/shard_map/ppermute | solution.py:887
  275.3 22.3 %collective-permute-start.27 = (bf16[4,48,1920]{2,1,0:T(8,128)(2,1)}, bf16[4,48,1920]{2,1,0:T(8,128)(2,1)S(1)}, u32[]{:S(2)}, u32[]{:S(2)}) collective-permute-start(bf16[4,48,1920]{2,1,0:T(8,128)(2,1)} %constant_dynamic-slice_fusion.22.refs_14_), channel_id=1, source_target_pairs={{0,8},{4,12},{8,0},{12,4},{16,24},{20,28},{24,16},{28,20},{1,9},{5... | collective-permute-start | bytes 2211848 | tf_op jit(solution)/shard_map/ppermute | solution.py:887
  278.2 20.8 %collective-permute-start.29 = (bf16[4,96,640]{2,1,0:T(8,128)(2,1)}, bf16[4,96,640]{2,1,0:T(8,128)(2,1)}, u32[]{:S(2)}, u32[]{:S(2)}) collective-permute-start(bf16[4,96,640]{2,1,0:T(8,128)(2,1)} %pad_maximum_fusion.8.refs_12_), channel_id=1, source_target_pairs={{0,16},{4,20},{8,24},{12,28},{16,0},{20,4},{24,8},{28,12},{1,17},{... | collective-permute-start | bytes 1474568 | tf_op jit(solution)/shard_map/ppermute | solution.py:887
  292.7 12.6 %collective-permute-start.28 = (bf16[4,96,640]{2,1,0:T(8,128)(2,1)S(1)}, bf16[4,96,640]{2,1,0:T(8,128)(2,1)S(1)}, u32[]{:S(2)}, u32[]{:S(2)}) collective-permute-start(bf16[4,96,640]{2,1,0:T(8,128)(2,1)S(1)} %constant_dynamic-slice_fusion.28.refs_11_), channel_id=1, source_target_pairs={{0,8},{4,12},{8,0},{12,4},{16,24},{20,28},{24,16},{28,20},{1,9},{5... | collective-permute-start | bytes 1474568 | tf_op jit(solution)/shard_map/ppermute | solution.py:887
  316.6 23.6 %collective-permute-start.31 = (bf16[4,192,1536]{2,1,0:T(8,128)(2,1)}, bf16[4,192,1536]{2,1,0:T(8,128)(2,1)S(1)}, u32[]{:S(2)}, u32[]{:S(2)}) collective-permute-start(bf16[4,192,1536]{2,1,0:T(8,128)(2,1)} %get-tuple-element.257), channel_id=1, source_target_pairs={{0,4},{4,0},{8,12},{12,8},{16,20},{20,16},{24,28},{28,24},{1,5},{5... | collective-permute-start | bytes 7077896 | tf_op jit(solution)/shard_map/ppermute | solution.py:887
  328.0 13.0 %collective-permute-start.30 = (bf16[4,192,1536]{2,1,0:T(8,128)(2,1)}, bf16[4,192,1536]{2,1,0:T(8,128)(2,1)}, u32[]{:S(2)}, u32[]{:S(2)}) collective-permute-start(bf16[4,192,1536]{2,1,0:T(8,128)(2,1)} %get-tuple-element.251), channel_id=1, source_target_pairs={{0,4},{4,0},{8,12},{12,8},{16,20},{20,16},{24,28},{28,24},{1,5},{5... | collective-permute-start | bytes 7077896 | tf_op jit(solution)/shard_map/ppermute | solution.py:887
  335.0 29.6 %collective-permute-start.37 = (bf16[2,1,48,3456]{3,2,1,0:T(8,128)(2,1)S(1)}, bf16[2,1,48,3456]{3,2,1,0:T(8,128)(2,1)S(1)}, u32[]{:S(2)}, u32[]{:S(2)}) collective-permute-start(bf16[2,1,48,3456]{3,2,1,0:T(8,128)(2,1)S(1)} %constant_dynamic-slice_fusion.11), channel_id=1, source_target_pairs={{0,1},{1,0},{2,3},{3,2},{4,5},{5,4},{6,7},{7,6},{8,9},{9,8},{10,11... | collective-permute-start | bytes 1990664 | tf_op jit(solution)/shard_map/ppermute | solution.py:955
  337.2 30.3 %collective-permute-start.53 = (bf16[4,48,640]{2,1,0:T(8,128)(2,1)S(1)}, bf16[4,48,640]{2,1,0:T(8,128)(2,1)}, u32[]{:S(2)}, u32[]{:S(2)}) collective-permute-start(bf16[4,48,640]{2,1,0:T(8,128)(2,1)S(1)} %constant_dynamic-slice_fusion.21.refs_5_), channel_id=1, source_target_pairs={{0,16},{4,20},{8,24},{12,28},{16,0},{20,4},{24,8},{28,12},{1,17},{... | collective-permute-start | bytes 737288 | tf_op jit(solution)/shard_map/ppermute | solution.py:887
  338.9 28.5 %collective-permute-start.54 = (bf16[4,48,640]{2,1,0:T(8,128)(2,1)S(1)}, bf16[4,48,640]{2,1,0:T(8,128)(2,1)}, u32[]{:S(2)}, u32[]{:S(2)}) collective-permute-start(bf16[4,48,640]{2,1,0:T(8,128)(2,1)S(1)} %constant_dynamic-slice_fusion.19.refs_6_), channel_id=1, source_target_pairs={{0,8},{4,12},{8,0},{12,4},{16,24},{20,28},{24,16},{28,20},{1,9},{5... | collective-permute-start | bytes 737288 | tf_op jit(solution)/shard_map/ppermute | solution.py:887
  347.3 35.5 %collective-permute-start.34 = (bf16[4,96,1920]{2,1,0:T(8,128)(2,1)}, bf16[4,96,1920]{2,1,0:T(8,128)(2,1)}, u32[]{:S(2)}, u32[]{:S(2)}) collective-permute-start(bf16[4,96,1920]{2,1,0:T(8,128)(2,1)} %pad_maximum_fusion.2.refs_10_), channel_id=1, source_target_pairs={{0,16},{4,20},{8,24},{12,28},{16,0},{20,4},{24,8},{28,12},{1,17},{... | collective-permute-start | bytes 4423688 | tf_op jit(solution)/shard_map/ppermute | solution.py:887
  347.6 27.5 %collective-permute-start.33 = (bf16[4,96,1536]{2,1,0:T(8,128)(2,1)}, bf16[4,96,1536]{2,1,0:T(8,128)(2,1)}, u32[]{:S(2)}, u32[]{:S(2)}) collective-permute-start(bf16[4,96,1536]{2,1,0:T(8,128)(2,1)} %constant_dynamic-slice_fusion.18.refs_9_), channel_id=1, source_target_pairs={{0,8},{4,12},{8,0},{12,4},{16,24},{20,28},{24,16},{28,20},{1,9},{5... | collective-permute-start | bytes 3538952 | tf_op jit(solution)/shard_map/ppermute | solution.py:887
  365.5 37.9 %collective-permute-start.38 = (bf16[1,1,48,3456]{3,2,1,0:T(8,128)(2,1)}, bf16[1,1,48,3456]{3,2,1,0:T(8,128)(2,1)}, u32[]{:S(2)}, u32[]{:S(2)}) collective-permute-start(bf16[1,1,48,3456]{3,2,1,0:T(8,128)(2,1)} %constant_dynamic-slice_fusion.10), channel_id=1, source_target_pairs={{0,2},{1,3},{2,0},{3,1},{4,6},{5,7},{6,4},{7,5},{8,10},{9,11},{10,... | collective-permute-start | bytes 995336 | tf_op jit(solution)/shard_map/ppermute | solution.py:955
  370.4 119.6 %all-gather.3.cloned.1.call-start = ((), (), s32[]{:S(2)}) async-start(), calls=%async_computation.2 | async-start | bytes 2985984 | tf_op jit(solution)/shard_map/all_gather | solution.py:1440
  377.1 32.2 %collective-permute-start.35 = (bf16[4,48,1536]{2,1,0:T(8,128)(2,1)S(1)}, bf16[4,48,1536]{2,1,0:T(8,128)(2,1)}, u32[]{:S(2)}, u32[]{:S(2)}) collective-permute-start(bf16[4,48,1536]{2,1,0:T(8,128)(2,1)S(1)} %constant_dynamic-slice_fusion.15.refs_10_), channel_id=1, source_target_pairs={{0,16},{4,20},{8,24},{12,28},{16,0},{20,4},{24,8},{28,12},{1,17},{... | collective-permute-start | bytes 1769480 | tf_op jit(solution)/shard_map/ppermute | solution.py:887
  384.7 25.9 %collective-permute-start.36 = (bf16[4,48,1920]{2,1,0:T(8,128)(2,1)S(1)}, bf16[4,48,1920]{2,1,0:T(8,128)(2,1)}, u32[]{:S(2)}, u32[]{:S(2)}) collective-permute-start(bf16[4,48,1920]{2,1,0:T(8,128)(2,1)S(1)} %constant_dynamic-slice_fusion.12.refs_11_), channel_id=1, source_target_pairs={{0,8},{4,12},{8,0},{12,4},{16,24},{20,28},{24,16},{28,20},{1,9},{5... | collective-permute-start | bytes 2211848 | tf_op jit(solution)/shard_map/ppermute | solution.py:887
  412.5 16.8 %collective-permute-start.39 = (bf16[2,1,48,3456]{3,2,1,0:T(8,128)(2,1)S(1)}, bf16[2,1,48,3456]{3,2,1,0:T(8,128)(2,1)S(1)}, u32[]{:S(2)}, u32[]{:S(2)}) collective-permute-start(bf16[2,1,48,3456]{3,2,1,0:T(8,128)(2,1)S(1)} %constant_dynamic-slice_fusion.9), channel_id=1, source_target_pairs={{0,1},{1,0},{2,3},{3,2},{4,5},{5,4},{6,7},{7,6},{8,9},{9,8},{10,11... | collective-permute-start | bytes 1990664 | tf_op jit(solution)/shard_map/ppermute | solution.py:955
  422.9 17.1 %collective-permute-start.58 = (bf16[2,48,3456]{2,1,0:T(8,128)(2,1)S(1)}, bf16[2,48,3456]{2,1,0:T(8,128)(2,1)S(1)}, u32[]{:S(2)}, u32[]{:S(2)}) collective-permute-start(bf16[2,48,3456]{2,1,0:T(8,128)(2,1)S(1)} %maximum_bitcast_fusion), channel_id=1, source_target_pairs={{0,8},{4,12},{8,0},{12,4},{16,24},{20,28},{24,16},{28,20},{1,9},{5... | collective-permute-start | bytes 1990664 | tf_op jit(solution)/shard_map/ppermute | solution.py:887
  429.5 18.1 %collective-permute-start.41 = (bf16[4,192,1152]{2,1,0:T(8,128)(2,1)S(1)}, bf16[4,192,1152]{2,1,0:T(8,128)(2,1)S(1)}, u32[]{:S(2)}, u32[]{:S(2)}) collective-permute-start(bf16[4,192,1152]{2,1,0:T(8,128)(2,1)S(1)} %copy-done.107), channel_id=1, source_target_pairs={{0,4},{4,0},{8,12},{12,8},{16,20},{20,16},{24,28},{28,24},{1,5},{5... | collective-permute-start | bytes 5308424 | tf_op jit(solution)/shard_map/ppermute | solution.py:887
  429.6 18.0 %collective-permute-start.49 = (bf16[1,1,48,3456]{3,2,1,0:T(8,128)(2,1)S(1)}, bf16[1,1,48,3456]{3,2,1,0:T(8,128)(2,1)S(1)}, u32[]{:S(2)}, u32[]{:S(2)}) collective-permute-start(bf16[1,1,48,3456]{3,2,1,0:T(8,128)(2,1)S(1)} %constant_dynamic-slice_fusion), channel_id=1, source_target_pairs={{0,2},{1,3},{2,0},{3,1},{4,6},{5,7},{6,4},{7,5},{8,10},{9,11},{10,... | collective-permute-start | bytes 995336 | tf_op jit(solution)/shard_map/ppermute | solution.py:955
  441.4 29.0 %collective-permute-start.59 = (bf16[4,48,3456]{2,1,0:T(8,128)(2,1)}, bf16[4,48,3456]{2,1,0:T(8,128)(2,1)}, u32[]{:S(2)}, u32[]{:S(2)}) collective-permute-start(bf16[4,48,3456]{2,1,0:T(8,128)(2,1)} %bitcast.68), channel_id=1, source_target_pairs={{0,4},{4,0},{8,12},{12,8},{16,20},{20,16},{24,28},{28,24},{1,5},{5... | collective-permute-start | bytes 3981320 | tf_op jit(solution)/shard_map/ppermute | solution.py:887
  449.1 16.6 %collective-permute-start.42 = (bf16[4,96,640]{2,1,0:T(8,128)(2,1)}, bf16[4,96,640]{2,1,0:T(8,128)(2,1)}, u32[]{:S(2)}, u32[]{:S(2)}) collective-permute-start(bf16[4,96,640]{2,1,0:T(8,128)(2,1)} %constant_dynamic-slice_fusion.8), channel_id=1, source_target_pairs={{0,8},{4,12},{8,0},{12,4},{16,24},{20,28},{24,16},{28,20},{1,9},{5... | collective-permute-start | bytes 1474568 | tf_op jit(solution)/shard_map/ppermute | solution.py:887
  451.2 17.7 %collective-permute-start.45 = (bf16[4,96,640]{2,1,0:T(8,128)(2,1)S(1)}, bf16[4,96,640]{2,1,0:T(8,128)(2,1)S(1)}, u32[]{:S(2)}, u32[]{:S(2)}) collective-permute-start(bf16[4,96,640]{2,1,0:T(8,128)(2,1)S(1)} %pad_maximum_fusion.9), channel_id=1, source_target_pairs={{0,16},{4,20},{8,24},{12,28},{16,0},{20,4},{24,8},{28,12},{1,17},{... | collective-permute-start | bytes 1474568 | tf_op jit(solution)/shard_map/ppermute | solution.py:887
  (123 other events, 723.9 us)
Sparse Core Ops, SparseCore 0:
  370.5 20.4 reduce-scatter.1
Sparse Core Ops, SparseCore 1:
  451.0 32.9 all-gather.2

commit v4 on v3

--- a/solution.py
+++ b/solution.py
@@ -965,11 +965,13 @@
     return cur.reshape(mine.shape[1:])
 
 
-def wide_gather_swaps(mine, got=None):
+def wide_gather_swaps(mine, got=None, on=None):
     place = lax.axis_index("wide")
     cur = mine[None]
     for number, bit in enumerate(wide_bits()[::-1]):
         other = got[None] if number == 0 and got is not None else swap(cur, bit)
+        if number > 0 and on is not None:
+            other = tie(other, on)
         upper = (place // bit) % 2 == 1
         cur = jnp.stack([jnp.where(upper, other, cur), jnp.where(upper, cur, other)])
         cur = cur.reshape((-1,) + mine.shape)
@@ -1415,7 +1417,7 @@
     flying = ff0.step(b4[1])
     sum_at1 = narrow_sum(at1.finish(b4[1]))
     a4 = backward_attention(0, ia, segments, a1, a3[2], a3[3], weights, (b4[1], *flying))
-    mine_ff0 = ff0.finish(a4[1])
+    mine_ff0 = ff0.finish((a4[1], sum_at1))
     sum_ff1 = narrow_sum_swaps(mine_ff1, (b4[1], a4[1]))
     half0 = weight_grads(
         (
@@ -1429,14 +1431,15 @@
     )
     part_ff0 = narrow_level(narrow_parts(mine_ff0), 0, half0[0][0])
     got_ff1 = tie(swap(tie(sum_ff1, mine_ff0), wide_bits()[-1]), half0[0][0])
-    half0 = [(tie(half0[0][0], (part_ff0, got_ff1)), half0[0][1])]
-    all_ff1 = wide_gather_swaps(sum_ff1, got_ff1)
-    small0 = small_pack([a2[6], b2[6]], [a3[4], b3[4], a4[2], b4[2]], narrow)
-    for level in range(1, narrow.bit_length() - 1):
-        part_ff0 = narrow_level(part_ff0, level, small0)
-    sum_ff0 = part_ff0.reshape(mine_ff0.shape[1:])
+    half0 = [(tie(half0[0][0], part_ff0), half0[0][1])]
+    last_sums = tie(a4[2], half0[0][0])
+    small0 = small_pack([a2[6], b2[6]], [a3[4], b3[4], last_sums, b4[2]], narrow)
     at0 = attn_halving(core_sum(half0)[0], small0)
     flying = at0.step()
+    for level in range(1, narrow.bit_length() - 1):
+        part_ff0 = narrow_level(part_ff0, level, flying)
+    sum_ff0 = part_ff0.reshape(mine_ff0.shape[1:])
+    all_ff1 = wide_gather_swaps(sum_ff1, got_ff1, flying)
     all_ff0 = lax.all_gather(sum_ff0, "wide", axis=0, tiled=False)
     all_at1 = wide_gather_swaps(tie(sum_at1, flying))
     all_at0 = wide_gather_swaps(narrow_sum_swaps(at0.finish(), (None, all_ff0)))

time: 529 us -> 520 us (0.983)
  waiting for transfers between devices: 68.8 us -> 60 us
    ppermute x35, waiting for transfers between devices: 46.5 us -> 38.1 us  [swap(): return lax.ppermute(value, 'wide', [(i, i ^ bit) for i in range(size)])]
    ppermute x35, starting transfers between devices: 35.4 us -> 28.6 us  [swap(): return lax.ppermute(value, 'wide', [(i, i ^ bit) for i in range(size)])]
    unnamed x221 -> x229, local copies, waits for them, and re-layouts: 21.9 us -> 22.6 us
  transfers between devices with their start and end apart: 62 -> 62, of which waited for: 15 -> 16; matrix products, arithmetic and copies ran while one was open for 14% -> 15% of each run, Pallas kernels for 38% -> 38%
where the time goes in v4:
time: 520 us; the launch traced here: 513 us
  Pallas kernels  264 us (51%)
  other arithmetic  64.1 us (12%)
  waiting for transfers between devices  60 us (12%)
  starting transfers between devices  59.6 us (11%)
  local copies, waits for them, and re-layouts  41.5 us (8%)
  between operations  24.1 us (5%)
    pallas_call x12, Pallas kernels, call(): pl.pallas_call(body, out_shape=outs, in_specs=list(in_specs) + [ANY] * ex...  182 us
    pallas_call x6, Pallas kernels, weight_grad_cols(): pl.pallas_call(partial(grad_cols_kernel, rows=rows, steps=steps), out_sha...  41.8 us
    ppermute x35, waiting for transfers between devices, swap(): return lax.ppermute(value, 'wide', [(i, i ^ bit) for i in range(size)])  38.1 us
    ppermute x35, starting transfers between devices, swap(): return lax.ppermute(value, 'wide', [(i, i ^ bit) for i in range(size)])  28.6 us
    convert_element_type x30, other arithmetic, add_low(): return (left.astype(F32) + right.astype(F32)).astype(BF16)  27.3 us
    unnamed x229, local copies, waits for them, and re-layouts  22.6 us
    pallas_call x2, Pallas kernels, weight_grad_rows(): pl.pallas_call(partial(grad_rows_kernel, rows=rows, narrow=narrow), out_s...  19.8 us
    ppermute x8, starting transfers between devices, shift(): lax.ppermute(value, 'narrow', inner)  12.7 us
  transfers between devices with their start and end apart: 62, of which 16 were waited for; matrix products, arithmetic and copies ran while one was open for 15% of the time, Pallas kernels for 38%

profile of v4, /device:TPU:0, one launch (start us, length us, event | category | flops | bytes accessed | tf_op | source)
XLA Modules:
  0.0 513.4 jit_solution(5190182996826939671)
XLA Ops:
  14.5 14.2 %forward_attention0.2 = (bf16[512,2304]{1,0:T(8,128)(2,1)}, f32[16,512]{1,0:T(8,128)S(1)}, bf16[512,768]{1,0:T(8,128)(2,1)S(1)}, bf16[512,768]{1,0:T(8,128)(2,1)...) custom-call(s32[1]{0:T(128)} %select_n.520.refs_0_, bf16[2,512,768]{2,1,0:T(8,128)(2,1)} %refs_1_.5, ...), custom_call_target="tpu_custom_call" | custom-call | flops 14000000000 | bytes 16000000 | tf_op jit(solution)/shard_map/forward_attention0/pallas_call | solution.py:110
  31.8 3.0 collective-permute-start
  34.8 2.6 collective-permute-start.1
  42.0 17.4 %forward_ff0.2 = (bf16[512,3072]{1,0:T(8,128)(2,1)}, bf16[512,3072]{1,0:T(8,128)(2,1)}, bf16[512,768]{1,0:T(8,128)(2,1)}, bf16[528,768]{1,0:T(8,128)(2,1)}, f32[...) custom-call(s32[1]{0:T(128)} %select_n.520.refs_0_, ...), custom_call_target="tpu_custom_call" | custom-call | flops 17999998976 | bytes 20000000 | tf_op jit(solution)/shard_map/forward_ff0/pallas_call | solution.py:110
  63.6 3.1 route.1
  77.6 14.2 %forward_attention0.3 = (bf16[512,2304]{1,0:T(8,128)(2,1)}, f32[16,512]{1,0:T(8,128)S(1)}, bf16[512,768]{1,0:T(8,128)(2,1)S(1)}, bf16[512,768]{1,0:T(8,128)(2,1)...) custom-call(s32[1]{0:T(128)} %bitcast.6.refs_0_, bf16[2,512,768]{2,1,0:T(8,128)(2,1)} %refs_1_.5, ...), custom_call_target="tpu_custom_call" | custom-call | flops 14000000000 | bytes 16000000 | tf_op jit(solution)/shard_map/forward_attention0/pallas_call | solution.py:110
  94.3 2.1 collective-permute-start.7
  96.5 17.2 %forward_ff0.3 = (bf16[512,3072]{1,0:T(8,128)(2,1)}, bf16[512,3072]{1,0:T(8,128)(2,1)}, bf16[512,768]{1,0:T(8,128)(2,1)}, bf16[528,768]{1,0:T(8,128)(2,1)}, f32[...) custom-call(s32[1]{0:T(128)} %bitcast.6.refs_0_, ...), custom_call_target="tpu_custom_call" | custom-call | flops 17999998976 | bytes 20000000 | tf_op jit(solution)/shard_map/forward_ff0/pallas_call | solution.py:110
  118.3 14.3 %forward_attention1.1 = (bf16[512,2304]{1,0:T(8,128)(2,1)}, f32[16,512]{1,0:T(8,128)S(1)}, bf16[512,768]{1,0:T(8,128)(2,1)S(1)}, bf16[512,768]{1,0:T(8,128)(2,1)...) custom-call(s32[1]{0:T(128)} %constant.248.clone.1.refs_0_, ...), custom_call_target="tpu_custom_call" | custom-call | flops 14000000000 | bytes 16000000 | tf_op jit(solution)/shard_map/forward_attention1/pallas_call | solution.py:110
  135.0 17.1 %forward_ff1.1 = (bf16[512,3072]{1,0:T(8,128)(2,1)}, bf16[512,3072]{1,0:T(8,128)(2,1)}, bf16[512,768]{1,0:T(8,128)(2,1)}, bf16[528,768]{1,0:T(8,128)(2,1)}, f32[...) custom-call(s32[1]{0:T(128)} %constant.248.clone.1.refs_0_, ...), custom_call_target="tpu_custom_call" | custom-call | flops 17999998976 | bytes 20000000 | tf_op jit(solution)/shard_map/forward_ff1/pallas_call | solution.py:110
  152.9 13.4 %backward_ff1.1 = (bf16[512,768]{1,0:T(8,128)(2,1)S(1)}, bf16[512,3072]{1,0:T(8,128)(2,1)}, bf16[512,768]{1,0:T(8,128)(2,1)}, f32[512,768]{1,0:T(8,128)}, f32[8,3072]{1,0:T(8,128)S(1)}) custom-call(bf16[512,768]{1,0:T(8,128)(2,1)} %bitcast_select_fusion.1.refs_19_.refs_0_, bf16[512,128]{1,0:T(8,128)(2,1)S(1)} %get-tuple-element.191.refs_1_, ...), custom_call_target="tpu_custom_call" | custom-call | flops 16000000000 | bytes 22000000 | tf_op jit(solution)/shard_map/backward_ff1/pallas_call | solution.py:110
  166.4 8.8 %weight_grad_rows.2 = (bf16[4,192,1536]{2,1,0:T(8,128)(2,1)}, bf16[4,192,1536]{2,1,0:T(8,128)(2,1)}) custom-call(s32[1]{0:T(128)} %bitcast.18.half_ref, bf16[512,3072]{1,0:T(8,128)(2,1)} %get-tuple-element.201.refs_0_, bf16[512,768]{1,0:T(8,128)(2,1)S(1)} %get-tuple-element.202.refs_1_), custom_call_target="tpu_custom_call" | custom-call | flops 1000000 | bytes 100000 | tf_op jit(solution)/shard_map/weight_grad_rows/pallas_call | solution.py:865
  175.9 3.0 weight_grad_cols.7
  179.3 7.2 %weight_grad_cols.6 = (bf16[4,192,1536]{2,1,0:T(8,128)(2,1)}, bf16[4,192,1536]{2,1,0:T(8,128)(2,1)}) custom-call(s32[1]{0:T(128)} %bitcast.18.half_ref, bf16[512,768]{1,0:T(8,128)(2,1)S(1)} %copy-done.7, bf16[512,3072]{1,0:T(8,128)(2,1)} %get-tuple-element.199.refs_1_), custom_call_target="tpu_custom_call" | custom-call | flops 1000000 | bytes 100000 | tf_op jit(solution)/shard_map/weight_grad_cols/pallas_call | solution.py:805
  186.6 15.2 %backward_attention1.1 = (bf16[512,2304]{1,0:T(8,128)(2,1)}, bf16[512,768]{1,0:T(8,128)(2,1)S(1)}, f32[8,3072]{1,0:T(8,128)S(1)}) custom-call(s32[1]{0:T(128)} %constant.248.clone.1.refs_0_, s32[1,512]{1,0:T(1,128)S(1)} %slice_convert_fusion.refs_2_.refs_4_.refs_1_, f32[16,512]{1,0:T(8,128)S(1)} %get-tuple-element.188.refs_2_, ...), custom_call_target="tpu_custom_call" | custom-call | flops 20000000000 | bytes 16000000 | tf_op jit(solution)/shard_map/backward_attention1/pallas_call | solution.py:110
  205.1 2.3 add_convert_fusion.2
  210.8 2.3 add_convert_fusion.3
  214.5 7.5 %weight_grad_cols.8 = (bf16[4,192,1152]{2,1,0:T(8,128)(2,1)}, bf16[4,192,1152]{2,1,0:T(8,128)(2,1)}) custom-call(s32[1]{0:T(128)} %bitcast.18.half_ref, bf16[512,768]{1,0:T(8,128)(2,1)S(1)} %slice.121.refs_0_, bf16[512,2304]{1,0:T(8,128)(2,1)} %get-tuple-element.206.refs_1_, bf16[4,96,1536]{2,1,0:T(8,128)(2,1)S(1)} %constant_dynamic-slice_fusion.31.refs_2_, ...), custom_call_target="tpu_custom_call" | custom-call | flops 1000000 | bytes 100000 | tf_op jit(solution)/shard_map/weight_grad_cols/pallas_call | solution.py:805
  230.0 2.3 bitcast_select_fusion.refs_0_
  236.1 9.0 %collective-permute-done.18 = bf16[512,768]{1,0:T(8,128)(2,1)} collective-permute-done((bf16[512,768]{1,0:T(8,128)(2,1)}, bf16[512,768]{1,0:T(8,128)(2,1)}, u32[]{:S(2)}, u32[]{:S(2)}) %collective-permute-start.18) | collective-permute-done | bytes 786464 | tf_op jit(solution)/shard_map/ppermute | solution.py:1311
  245.1 14.0 %backward_ff0.2 = (bf16[512,768]{1,0:T(8,128)(2,1)}, bf16[512,3072]{1,0:T(8,128)(2,1)}, bf16[512,768]{1,0:T(8,128)(2,1)}, f32[512,768]{1,0:T(8,128)}, f32[8,3072]{1,0:T(8,128)S(1)}) custom-call(bf16[512,768]{1,0:T(8,128)(2,1)} %bitcast_select_fusion.refs_0_, bf16[512,128]{1,0:T(8,128)(2,1)S(1)} %copy-done.54, f32[512,128]{1,0:T(8,128)S(1)} %copy-done.48, ...), custom_call_target="tpu_custom_call" | custom-call | flops 16000000000 | bytes 22000000 | tf_op jit(solution)/shard_map/backward_ff0/pallas_call | solution.py:110
  259.7 2.3 broadcast_select_fusion.4
  262.0 2.4 broadcast_select_fusion.1.refs_15_
  264.4 3.3 collective-permute-start.20
  277.1 13.8 %backward_ff0.3 = (bf16[512,768]{1,0:T(8,128)(2,1)}, bf16[512,3072]{1,0:T(8,128)(2,1)}, bf16[512,768]{1,0:T(8,128)(2,1)}, f32[512,768]{1,0:T(8,128)}, f32[8,3072]{1,0:T(8,128)S(1)}) custom-call(bf16[512,768]{1,0:T(8,128)(2,1)} %broadcast_select_fusion.4, bf16[512,128]{1,0:T(8,128)(2,1)S(1)} %copy-done.52, f32[512,128]{1,0:T(8,128)S(1)} %copy-done.44, ...), custom_call_target="tpu_custom_call" | custom-call | flops 16000000000 | bytes 22000000 | tf_op jit(solution)/shard_map/backward_ff0/pallas_call | solution.py:110
  292.8 2.7 broadcast_select_fusion.3
  298.3 5.4 %collective-permute-done.28 = bf16[4,96,640]{2,1,0:T(8,128)(2,1)S(1)} collective-permute-done((bf16[4,96,640]{2,1,0:T(8,128)(2,1)S(1)}, bf16[4,96,640]{2,1,0:T(8,128)(2,1)S(1)}, u32[]{:S(2)}, u32[]{:S(2)}) %collective-permute-start.28) | collective-permute-done | bytes 491552 | tf_op jit(solution)/shard_map/ppermute | solution.py:887
  303.9 11.1 %weight_grad_rows.3 = (bf16[4,192,1536]{2,1,0:T(8,128)(2,1)}, bf16[4,192,1536]{2,1,0:T(8,128)(2,1)}) custom-call(s32[1]{0:T(128)} %bitcast.18.half_ref, bf16[512,3072]{1,0:T(8,128)(2,1)} %get-tuple-element.255.refs_0_, bf16[512,3072]{1,0:T(8,128)(2,1)} %get-tuple-element.256.refs_1_, bf16[512,768]{1,0:T(8,128)(2,1)S(1)} %copy-done.5, ...), custom_call_target="tpu_custom_call" | custom-call | flops 1000000 | bytes 100000 | tf_op jit(solution)/shard_map/weight_grad_rows/pallas_call | solution.py:865
  316.1 10.1 %weight_grad_cols.9 = (bf16[4,192,1536]{2,1,0:T(8,128)(2,1)}, bf16[4,192,1536]{2,1,0:T(8,128)(2,1)}) custom-call(s32[1]{0:T(128)} %bitcast.18.half_ref, bf16[512,768]{1,0:T(8,128)(2,1)S(1)} %copy-done.2, bf16[512,768]{1,0:T(8,128)(2,1)} %get-tuple-element.175.refs_1_, bf16[512,3072]{1,0:T(8,128)(2,1)} %get-tuple-element.247.refs_2_, ...), custom_call_target="tpu_custom_call" | custom-call | flops 1000000 | bytes 100000 | tf_op jit(solution)/shard_map/weight_grad_cols/pallas_call | solution.py:805
  327.6 4.3 weight_grad_cols.10
  340.0 2.3 add_convert_fusion.1
  345.7 15.2 %backward_attention0.2 = (bf16[512,2304]{1,0:T(8,128)(2,1)}, bf16[512,768]{1,0:T(8,128)(2,1)S(1)}, f32[8,3072]{1,0:T(8,128)S(1)}) custom-call(s32[1]{0:T(128)} %bitcast.6.refs_0_, s32[2,512]{1,0:T(2,128)S(1)} %copy-done.33, f32[16,512]{1,0:T(8,128)S(1)} %copy-done.56, bf16[2,768,2304]{2,1,0:T(8,128)(2,1)} %refs_3_.11, bf16[2,768,768]{2,1,0:T(8,128)(2,1)} %refs_4_.21, ...), custom_call_target="tpu_custom_call" | custom-call | flops 20000000000 | bytes 16000000 | tf_op jit(solution)/shard_map/backward_attention0/pallas_call | solution.py:110
  366.5 6.1 %collective-permute-done.33 = bf16[4,96,1536]{2,1,0:T(8,128)(2,1)} collective-permute-done((bf16[4,96,1536]{2,1,0:T(8,128)(2,1)}, bf16[4,96,1536]{2,1,0:T(8,128)(2,1)}, u32[]{:S(2)}, u32[]{:S(2)}) %collective-permute-start.33) | collective-permute-done | bytes 1179680 | tf_op jit(solution)/shard_map/ppermute | solution.py:887
  376.3 3.9 collective-permute-done.34
  383.1 16.3 %backward_attention0.3 = (bf16[512,2304]{1,0:T(8,128)(2,1)}, bf16[512,768]{1,0:T(8,128)(2,1)}, f32[8,3072]{1,0:T(8,128)S(1)}) custom-call(s32[1]{0:T(128)} %select_n.520.refs_0_, s32[2,512]{1,0:T(2,128)S(1)} %copy-done.33, f32[16,512]{1,0:T(8,128)S(1)} %copy-done.58, bf16[2,768,2304]{2,1,0:T(8,128)(2,1)} %refs_3_.11, bf16[2,768,768]{2,1,0:T(8,128)(2,1)} %refs_4_.21, ...), custom_call_target="tpu_custom_call" | custom-call | flops 20000000000 | bytes 16000000 | tf_op jit(solution)/shard_map/backward_attention0/pallas_call | solution.py:110
  410.1 9.8 %weight_grad_cols.11 = (bf16[4,192,1152]{2,1,0:T(8,128)(2,1)}, bf16[4,192,1152]{2,1,0:T(8,128)(2,1)}) custom-call(s32[1]{0:T(128)} %bitcast.18.half_ref, bf16[512,768]{1,0:T(8,128)(2,1)S(1)} %get-tuple-element.387.refs_0_, bf16[512,768]{1,0:T(8,128)(2,1)S(1)} %get-tuple-element.386.refs_1_, bf16[512,2304]{1,0:T(8,128)(2,1)} %get-tuple-element.267.refs_2_, ...), custom_call_target="tpu_custom_call" | custom-call | flops 1000000 | bytes 100000 | tf_op jit(solution)/shard_map/weight_grad_cols/pallas_call | solution.py:805
  422.2 2.2 small_pack.3
  435.4 3.8 collective-permute-done.58
  439.1 4.7 collective-permute-done.50
  447.5 2.3 collective-permute-done.54
  455.8 5.9 %collective-permute-done.44 = bf16[4,48,640]{2,1,0:T(8,128)(2,1)S(1)} collective-permute-done((bf16[4,48,640]{2,1,0:T(8,128)(2,1)S(1)}, bf16[4,48,640]{2,1,0:T(8,128)(2,1)S(1)}, u32[]{:S(2)}, u32[]{:S(2)}) %collective-permute-start.44) | collective-permute-done | bytes 245792 | tf_op jit(solution)/shard_map/ppermute | solution.py:887
  465.3 2.7 collective-permute-done.55
  470.3 2.6 collective-permute-start.49
  473.0 4.6 collective-permute-done.49
  480.7 2.2 collective-permute-done.51
  486.0 4.0 collective-permute-done.52
  492.0 4.3 place_ff1.1
  496.3 4.3 place_ff0.1
  (460 shorter events, 146.9 us)
Async XLA Ops:
  7.2 392.8 %reduce-scatter.2.cloned.1.call-start = ((), (), s32[]{:S(2)}) async-start(), calls=%async_computation.1 | async-start | bytes 614400 | tf_op jit(solution)/shard_map/reduce_scatter | solution.py:982
  31.8 30.4 %collective-permute-start = (s32[1]{0:T(128)}, s32[1]{0:T(128)}, u32[]{:S(2)}, u32[]{:S(2)}) collective-permute-start(s32[1]{0:T(128)} %bitcast.2.refs_0_), channel_id=1, source_target_pairs={{0,1},{1,2},{2,3},{3,0},{4,5},{5,6},{6,7},{7,4},{8,9},{9,10},{10,1... | collective-permute-start | bytes 20 | tf_op jit(solution)/shard_map/ppermute | solution.py:1292
  34.8 28.7 %collective-permute-start.1 = (s32[1]{0:T(128)}, s32[1]{0:T(128)}, u32[]{:S(2)}, u32[]{:S(2)}) collective-permute-start(s32[1]{0:T(128)} %bitcast.2.refs_0_), channel_id=1, source_target_pairs={{0,2},{1,3},{2,0},{3,1},{4,6},{5,7},{6,4},{7,5},{8,10},{9,11},{10,... | collective-permute-start | bytes 20 | tf_op jit(solution)/shard_map/ppermute | solution.py:1292
  37.4 26.2 %collective-permute-start.2 = (s32[1]{0:T(128)}, s32[1]{0:T(128)}, u32[]{:S(2)}, u32[]{:S(2)}) collective-permute-start(s32[1]{0:T(128)} %bitcast.2.refs_0_), channel_id=1, source_target_pairs={{0,3},{1,0},{2,1},{3,2},{4,7},{5,4},{6,5},{7,6},{8,11},{9,8},{10,9... | collective-permute-start | bytes 20 | tf_op jit(solution)/shard_map/ppermute | solution.py:1292
  40.9 34.6 %collective-permute-start.3 = (bf16[512,768]{1,0:T(8,128)(2,1)S(1)}, bf16[512,768]{1,0:T(8,128)(2,1)}, u32[]{:S(2)}, u32[]{:S(2)}) collective-permute-start(bf16[512,768]{1,0:T(8,128)(2,1)S(1)} %get-tuple-element.172.refs_19_), channel_id=1, source_target_pairs={{0,1},{1,0},{2,3},{3,2},{4,5},{5,4},{6,7},{7,6},{8,9},{9,8},{10,11... | collective-permute-start | bytes 2359304 | tf_op jit(solution)/shard_map/ppermute | solution.py:1311
  41.6 33.9 %collective-permute-start.4 = (bf16[512,768]{1,0:T(8,128)(2,1)S(1)}, bf16[512,768]{1,0:T(8,128)(2,1)}, u32[]{:S(2)}, u32[]{:S(2)}) collective-permute-start(bf16[512,768]{1,0:T(8,128)(2,1)S(1)} %get-tuple-element.172.refs_19_), channel_id=1, source_target_pairs={{0,4},{1,2},{2,1},{3,7},{4,0},{5,6},{6,5},{7,3},{8,12},{9,10},{10,... | collective-permute-start | bytes 2359304 | tf_op jit(solution)/shard_map/ppermute | solution.py:1312
  62.2 30.5 %collective-permute-start.5 = (bf16[528,768]{1,0:T(8,128)(2,1)}, bf16[528,768]{1,0:T(8,128)(2,1)}, u32[]{:S(2)}, u32[]{:S(2)}) collective-permute-start(bf16[528,768]{1,0:T(8,128)(2,1)} %get-tuple-element.171.refs_9_), channel_id=1, source_target_pairs={{0,1},{1,0},{2,3},{3,2},{4,5},{5,4},{6,7},{7,6},{8,9},{9,8},{10,11... | collective-permute-start | bytes 2433032 | tf_op jit(solution)/shard_map/ppermute | solution.py:1311
  63.6 29.1 %collective-permute-start.6 = (bf16[528,768]{1,0:T(8,128)(2,1)}, bf16[528,768]{1,0:T(8,128)(2,1)}, u32[]{:S(2)}, u32[]{:S(2)}) collective-permute-start(bf16[528,768]{1,0:T(8,128)(2,1)} %get-tuple-element.171.refs_9_), channel_id=1, source_target_pairs={{0,4},{1,2},{2,1},{3,7},{4,0},{5,6},{6,5},{7,3},{8,12},{9,10},{10,... | collective-permute-start | bytes 2433032 | tf_op jit(solution)/shard_map/ppermute | solution.py:1312
  94.3 21.6 %collective-permute-start.7 = (bf16[528,768]{1,0:T(8,128)(2,1)S(1)}, bf16[528,768]{1,0:T(8,128)(2,1)S(1)}, u32[]{:S(2)}, u32[]{:S(2)}) collective-permute-start(bf16[528,768]{1,0:T(8,128)(2,1)S(1)} %broadcast_select_fusion.2.refs_19_), channel_id=1, source_target_pairs={{0,1},{1,0},{2,3},{3,2},{4,5},{5,4},{6,7},{7,6},{8,9},{9,8},{10,11... | collective-permute-start | bytes 2433032 | tf_op jit(solution)/shard_map/ppermute | solution.py:1311
  96.5 19.5 %collective-permute-start.8 = (bf16[528,768]{1,0:T(8,128)(2,1)S(1)}, bf16[528,768]{1,0:T(8,128)(2,1)S(1)}, u32[]{:S(2)}, u32[]{:S(2)}) collective-permute-start(bf16[528,768]{1,0:T(8,128)(2,1)S(1)} %broadcast_select_fusion.2.refs_19_), channel_id=1, source_target_pairs={{0,4},{1,2},{2,1},{3,7},{4,0},{5,6},{6,5},{7,3},{8,12},{9,10},{10,... | collective-permute-start | bytes 2433032 | tf_op jit(solution)/shard_map/ppermute | solution.py:1312
  113.8 18.9 %collective-permute-start.10 = (bf16[512,768]{1,0:T(8,128)(2,1)S(1)}, bf16[512,768]{1,0:T(8,128)(2,1)S(1)}, u32[]{:S(2)}, u32[]{:S(2)}) collective-permute-start(bf16[512,768]{1,0:T(8,128)(2,1)S(1)} %copy-done.84), channel_id=1, source_target_pairs={{0,4},{1,2},{2,1},{3,7},{4,0},{5,6},{6,5},{7,3},{8,12},{9,10},{10,... | collective-permute-start | bytes 2359304 | tf_op jit(solution)/shard_map/ppermute | solution.py:1312
  114.3 19.5 %collective-permute-start.9 = (bf16[512,768]{1,0:T(8,128)(2,1)S(1)}, bf16[512,768]{1,0:T(8,128)(2,1)S(1)}, u32[]{:S(2)}, u32[]{:S(2)}) collective-permute-start(bf16[512,768]{1,0:T(8,128)(2,1)S(1)} %copy-done.84), channel_id=1, source_target_pairs={{0,1},{1,0},{2,3},{3,2},{4,5},{5,4},{6,7},{7,6},{8,9},{9,8},{10,11... | collective-permute-start | bytes 2359304 | tf_op jit(solution)/shard_map/ppermute | solution.py:1311
  175.1 30.0 %collective-permute-start.16 = (bf16[4,192,1536]{2,1,0:T(8,128)(2,1)}, bf16[4,192,1536]{2,1,0:T(8,128)(2,1)}, u32[]{:S(2)}, u32[]{:S(2)}) collective-permute-start(bf16[4,192,1536]{2,1,0:T(8,128)(2,1)} %get-tuple-element.203.refs_10_), channel_id=1, source_target_pairs={{0,4},{4,0},{8,12},{12,8},{16,20},{20,16},{24,28},{28,24},{1,5},{5... | collective-permute-start | bytes 7077896 | tf_op jit(solution)/shard_map/ppermute | solution.py:887
  178.8 25.3 %collective-permute-start.17 = (bf16[4,192,384]{2,1,0:T(8,128)(2,1)S(1)}, bf16[4,192,384]{2,1,0:T(8,128)(2,1)S(1)}, u32[]{:S(2)}, u32[]{:S(2)}) collective-permute-start(bf16[4,192,384]{2,1,0:T(8,128)(2,1)S(1)} %get-tuple-element.204.refs_11_), channel_id=1, source_target_pairs={{0,4},{4,0},{8,12},{12,8},{16,20},{20,16},{24,28},{28,24},{1,5},{5... | collective-permute-start | bytes 1769480 | tf_op jit(solution)/shard_map/ppermute | solution.py:887
  186.5 23.3 %collective-permute-start.15 = (bf16[4,192,1536]{2,1,0:T(8,128)(2,1)}, bf16[4,192,1536]{2,1,0:T(8,128)(2,1)}, u32[]{:S(2)}, u32[]{:S(2)}) collective-permute-start(bf16[4,192,1536]{2,1,0:T(8,128)(2,1)} %get-tuple-element.200.refs_9_), channel_id=1, source_target_pairs={{0,4},{4,0},{8,12},{12,8},{16,20},{20,16},{24,28},{28,24},{1,5},{5... | collective-permute-start | bytes 7077896 | tf_op jit(solution)/shard_map/ppermute | solution.py:887
  202.5 20.0 %collective-permute-start.13 = (bf16[512,768]{1,0:T(8,128)(2,1)S(1)}, bf16[512,768]{1,0:T(8,128)(2,1)S(1)}, u32[]{:S(2)}, u32[]{:S(2)}) collective-permute-start(bf16[512,768]{1,0:T(8,128)(2,1)S(1)} %get-tuple-element.205), channel_id=1, source_target_pairs={{0,1},{1,0},{2,3},{3,2},{4,5},{5,4},{6,7},{7,6},{8,9},{9,8},{10,11... | collective-permute-start | bytes 2359304 | tf_op jit(solution)/shard_map/ppermute | solution.py:1311
  204.0 18.5 %collective-permute-start.14 = (bf16[512,768]{1,0:T(8,128)(2,1)S(1)}, bf16[512,768]{1,0:T(8,128)(2,1)S(1)}, u32[]{:S(2)}, u32[]{:S(2)}) collective-permute-start(bf16[512,768]{1,0:T(8,128)(2,1)S(1)} %get-tuple-element.205), channel_id=1, source_target_pairs={{0,4},{1,2},{2,1},{3,7},{4,0},{5,6},{6,5},{7,3},{8,12},{9,10},{10,... | collective-permute-start | bytes 2359304 | tf_op jit(solution)/shard_map/ppermute | solution.py:1312
  224.3 20.7 %collective-permute-start.18 = (bf16[512,768]{1,0:T(8,128)(2,1)}, bf16[512,768]{1,0:T(8,128)(2,1)}, u32[]{:S(2)}, u32[]{:S(2)}) collective-permute-start(bf16[512,768]{1,0:T(8,128)(2,1)} %broadcast_select_fusion.5.refs_12_), channel_id=1, source_target_pairs={{0,1},{1,0},{2,3},{3,2},{4,5},{5,4},{6,7},{7,6},{8,9},{9,8},{10,11... | collective-permute-start | bytes 2359304 | tf_op jit(solution)/shard_map/ppermute | solution.py:1311
  225.7 36.3 %collective-permute-start.11 = (bf16[528,768]{1,0:T(8,128)(2,1)}, bf16[528,768]{1,0:T(8,128)(2,1)}, u32[]{:S(2)}, u32[]{:S(2)}) collective-permute-start(bf16[528,768]{1,0:T(8,128)(2,1)} %get-tuple-element.187.refs_11_), channel_id=1, source_target_pairs={{0,1},{1,0},{2,3},{3,2},{4,5},{5,4},{6,7},{7,6},{8,9},{9,8},{10,11... | collective-permute-start | bytes 2433032 | tf_op jit(solution)/shard_map/ppermute | solution.py:1311
  226.4 35.6 %collective-permute-start.12 = (bf16[528,768]{1,0:T(8,128)(2,1)}, bf16[528,768]{1,0:T(8,128)(2,1)}, u32[]{:S(2)}, u32[]{:S(2)}) collective-permute-start(bf16[528,768]{1,0:T(8,128)(2,1)} %get-tuple-element.187.refs_11_), channel_id=1, source_target_pairs={{0,4},{1,2},{2,1},{3,7},{4,0},{5,6},{6,5},{7,3},{8,12},{9,10},{10,... | collective-permute-start | bytes 2433032 | tf_op jit(solution)/shard_map/ppermute | solution.py:1312
  233.0 36.9 %collective-permute-start.25 = (bf16[4,96,1920]{2,1,0:T(8,128)(2,1)S(1)}, bf16[4,96,1920]{2,1,0:T(8,128)(2,1)}, u32[]{:S(2)}, u32[]{:S(2)}) collective-permute-start(bf16[4,96,1920]{2,1,0:T(8,128)(2,1)S(1)} %copy-done.68), channel_id=1, source_target_pairs={{0,16},{4,20},{8,24},{12,28},{16,0},{20,4},{24,8},{28,12},{1,17},{... | collective-permute-start | bytes 4423688 | tf_op jit(solution)/shard_map/ppermute | solution.py:887
  234.6 34.5 %collective-permute-start.24 = (bf16[4,96,1536]{2,1,0:T(8,128)(2,1)S(1)}, bf16[4,96,1536]{2,1,0:T(8,128)(2,1)S(1)}, u32[]{:S(2)}, u32[]{:S(2)}) collective-permute-start(bf16[4,96,1536]{2,1,0:T(8,128)(2,1)S(1)} %constant_dynamic-slice_fusion.31.refs_2_), channel_id=1, source_target_pairs={{0,8},{4,12},{8,0},{12,4},{16,24},{20,28},{24,16},{28,20},{1,9},{5... | collective-permute-start | bytes 3538952 | tf_op jit(solution)/shard_map/ppermute | solution.py:887
  245.0 14.1 %collective-permute-start.19 = (bf16[512,768]{1,0:T(8,128)(2,1)}, bf16[512,768]{1,0:T(8,128)(2,1)S(1)}, u32[]{:S(2)}, u32[]{:S(2)}) collective-permute-start(bf16[512,768]{1,0:T(8,128)(2,1)} %broadcast_select_fusion.5.refs_12_), channel_id=1, source_target_pairs={{0,4},{1,2},{2,1},{3,7},{4,0},{5,6},{6,5},{7,3},{8,12},{9,10},{10,... | collective-permute-start | bytes 2359304 | tf_op jit(solution)/shard_map/ppermute | solution.py:1312
  259.1 15.1 %collective-permute-start.22 = (bf16[4,192,1152]{2,1,0:T(8,128)(2,1)}, bf16[4,192,1152]{2,1,0:T(8,128)(2,1)S(1)}, u32[]{:S(2)}, u32[]{:S(2)}) collective-permute-start(bf16[4,192,1152]{2,1,0:T(8,128)(2,1)} %get-tuple-element.210.refs_11_), channel_id=1, source_target_pairs={{0,4},{4,0},{8,12},{12,8},{16,20},{20,16},{24,28},{28,24},{1,5},{5... | collective-permute-start | bytes 5308424 | tf_op jit(solution)/shard_map/ppermute | solution.py:887
  264.4 28.3 %collective-permute-start.20 = (bf16[528,768]{1,0:T(8,128)(2,1)}, bf16[528,768]{1,0:T(8,128)(2,1)S(1)}, u32[]{:S(2)}, u32[]{:S(2)}) collective-permute-start(bf16[528,768]{1,0:T(8,128)(2,1)} %broadcast_select_fusion.1.refs_15_), channel_id=1, source_target_pairs={{0,1},{1,0},{2,3},{3,2},{4,5},{5,4},{6,7},{7,6},{8,9},{9,8},{10,11... | collective-permute-start | bytes 2433032 | tf_op jit(solution)/shard_map/ppermute | solution.py:1311
  267.7 25.0 %collective-permute-start.21 = (bf16[528,768]{1,0:T(8,128)(2,1)}, bf16[528,768]{1,0:T(8,128)(2,1)}, u32[]{:S(2)}, u32[]{:S(2)}) collective-permute-start(bf16[528,768]{1,0:T(8,128)(2,1)} %broadcast_select_fusion.1.refs_15_), channel_id=1, source_target_pairs={{0,4},{1,2},{2,1},{3,7},{4,0},{5,6},{6,5},{7,3},{8,12},{9,10},{10,... | collective-permute-start | bytes 2433032 | tf_op jit(solution)/shard_map/ppermute | solution.py:1312
  269.5 21.5 %collective-permute-start.26 = (bf16[4,48,1536]{2,1,0:T(8,128)(2,1)S(1)}, bf16[4,48,1536]{2,1,0:T(8,128)(2,1)S(1)}, u32[]{:S(2)}, u32[]{:S(2)}) collective-permute-start(bf16[4,48,1536]{2,1,0:T(8,128)(2,1)S(1)} %constant_dynamic-slice_fusion.25.refs_13_), channel_id=1, source_target_pairs={{0,16},{4,20},{8,24},{12,28},{16,0},{20,4},{24,8},{28,12},{1,17},{... | collective-permute-start | bytes 1769480 | tf_op jit(solution)/shard_map/ppermute | solution.py:887
  272.7 22.9 %collective-permute-start.27 = (bf16[4,48,1920]{2,1,0:T(8,128)(2,1)}, bf16[4,48,1920]{2,1,0:T(8,128)(2,1)S(1)}, u32[]{:S(2)}, u32[]{:S(2)}) collective-permute-start(bf16[4,48,1920]{2,1,0:T(8,128)(2,1)} %constant_dynamic-slice_fusion.22.refs_14_), channel_id=1, source_target_pairs={{0,8},{4,12},{8,0},{12,4},{16,24},{20,28},{24,16},{28,20},{1,9},{5... | collective-permute-start | bytes 2211848 | tf_op jit(solution)/shard_map/ppermute | solution.py:887
  276.6 20.4 %collective-permute-start.29 = (bf16[4,96,640]{2,1,0:T(8,128)(2,1)}, bf16[4,96,640]{2,1,0:T(8,128)(2,1)}, u32[]{:S(2)}, u32[]{:S(2)}) collective-permute-start(bf16[4,96,640]{2,1,0:T(8,128)(2,1)} %pad_maximum_fusion.8.refs_12_), channel_id=1, source_target_pairs={{0,16},{4,20},{8,24},{12,28},{16,0},{20,4},{24,8},{28,12},{1,17},{... | collective-permute-start | bytes 1474568 | tf_op jit(solution)/shard_map/ppermute | solution.py:887
  291.0 12.6 %collective-permute-start.28 = (bf16[4,96,640]{2,1,0:T(8,128)(2,1)S(1)}, bf16[4,96,640]{2,1,0:T(8,128)(2,1)S(1)}, u32[]{:S(2)}, u32[]{:S(2)}) collective-permute-start(bf16[4,96,640]{2,1,0:T(8,128)(2,1)S(1)} %constant_dynamic-slice_fusion.28.refs_11_), channel_id=1, source_target_pairs={{0,8},{4,12},{8,0},{12,4},{16,24},{20,28},{24,16},{28,20},{1,9},{5... | collective-permute-start | bytes 1474568 | tf_op jit(solution)/shard_map/ppermute | solution.py:887
  314.9 22.7 %collective-permute-start.31 = (bf16[4,192,1536]{2,1,0:T(8,128)(2,1)}, bf16[4,192,1536]{2,1,0:T(8,128)(2,1)S(1)}, u32[]{:S(2)}, u32[]{:S(2)}) collective-permute-start(bf16[4,192,1536]{2,1,0:T(8,128)(2,1)} %get-tuple-element.260), channel_id=1, source_target_pairs={{0,4},{4,0},{8,12},{12,8},{16,20},{20,16},{24,28},{28,24},{1,5},{5... | collective-permute-start | bytes 7077896 | tf_op jit(solution)/shard_map/ppermute | solution.py:887
  332.2 28.7 %collective-permute-start.39 = (bf16[2,1,48,3456]{3,2,1,0:T(8,128)(2,1)S(1)}, bf16[2,1,48,3456]{3,2,1,0:T(8,128)(2,1)S(1)}, u32[]{:S(2)}, u32[]{:S(2)}) collective-permute-start(bf16[2,1,48,3456]{3,2,1,0:T(8,128)(2,1)S(1)} %constant_dynamic-slice_fusion.11), channel_id=1, source_target_pairs={{0,1},{1,0},{2,3},{3,2},{4,5},{5,4},{6,7},{7,6},{8,9},{9,8},{10,11... | collective-permute-start | bytes 1990664 | tf_op jit(solution)/shard_map/ppermute | solution.py:955
  333.5 30.0 %collective-permute-start.36 = (bf16[4,48,640]{2,1,0:T(8,128)(2,1)S(1)}, bf16[4,48,640]{2,1,0:T(8,128)(2,1)}, u32[]{:S(2)}, u32[]{:S(2)}) collective-permute-start(bf16[4,48,640]{2,1,0:T(8,128)(2,1)S(1)} %constant_dynamic-slice_fusion.21.refs_5_), channel_id=1, source_target_pairs={{0,16},{4,20},{8,24},{12,28},{16,0},{20,4},{24,8},{28,12},{1,17},{... | collective-permute-start | bytes 737288 | tf_op jit(solution)/shard_map/ppermute | solution.py:887
  335.0 28.5 %collective-permute-start.37 = (bf16[4,48,640]{2,1,0:T(8,128)(2,1)S(1)}, bf16[4,48,640]{2,1,0:T(8,128)(2,1)}, u32[]{:S(2)}, u32[]{:S(2)}) collective-permute-start(bf16[4,48,640]{2,1,0:T(8,128)(2,1)S(1)} %constant_dynamic-slice_fusion.19.refs_6_), channel_id=1, source_target_pairs={{0,8},{4,12},{8,0},{12,4},{16,24},{20,28},{24,16},{28,20},{1,9},{5... | collective-permute-start | bytes 737288 | tf_op jit(solution)/shard_map/ppermute | solution.py:887
  344.7 35.5 %collective-permute-start.34 = (bf16[4,96,1920]{2,1,0:T(8,128)(2,1)}, bf16[4,96,1920]{2,1,0:T(8,128)(2,1)}, u32[]{:S(2)}, u32[]{:S(2)}) collective-permute-start(bf16[4,96,1920]{2,1,0:T(8,128)(2,1)} %pad_maximum_fusion.2.refs_10_), channel_id=1, source_target_pairs={{0,16},{4,20},{8,24},{12,28},{16,0},{20,4},{24,8},{28,12},{1,17},{... | collective-permute-start | bytes 4423688 | tf_op jit(solution)/shard_map/ppermute | solution.py:887
  345.0 27.5 %collective-permute-start.33 = (bf16[4,96,1536]{2,1,0:T(8,128)(2,1)}, bf16[4,96,1536]{2,1,0:T(8,128)(2,1)}, u32[]{:S(2)}, u32[]{:S(2)}) collective-permute-start(bf16[4,96,1536]{2,1,0:T(8,128)(2,1)} %constant_dynamic-slice_fusion.18.refs_9_), channel_id=1, source_target_pairs={{0,8},{4,12},{8,0},{12,4},{16,24},{20,28},{24,16},{28,20},{1,9},{5... | collective-permute-start | bytes 3538952 | tf_op jit(solution)/shard_map/ppermute | solution.py:887
  361.8 38.2 %collective-permute-start.40 = (bf16[1,1,48,3456]{3,2,1,0:T(8,128)(2,1)}, bf16[1,1,48,3456]{3,2,1,0:T(8,128)(2,1)}, u32[]{:S(2)}, u32[]{:S(2)}) collective-permute-start(bf16[1,1,48,3456]{3,2,1,0:T(8,128)(2,1)} %constant_dynamic-slice_fusion.10), channel_id=1, source_target_pairs={{0,2},{1,3},{2,0},{3,1},{4,6},{5,7},{6,4},{7,5},{8,10},{9,11},{10,... | collective-permute-start | bytes 995336 | tf_op jit(solution)/shard_map/ppermute | solution.py:955
  366.4 111.2 %all-gather.3.cloned.1.call-start = ((), (), s32[]{:S(2)}) async-start(), calls=%async_computation.2 | async-start | bytes 2985984 | tf_op jit(solution)/shard_map/all_gather | solution.py:1443
  374.6 25.5 %collective-permute-start.35 = (bf16[4,48,1536]{2,1,0:T(8,128)(2,1)S(1)}, bf16[4,48,1536]{2,1,0:T(8,128)(2,1)}, u32[]{:S(2)}, u32[]{:S(2)}) collective-permute-start(bf16[4,48,1536]{2,1,0:T(8,128)(2,1)S(1)} %constant_dynamic-slice_fusion.15.refs_10_), channel_id=1, source_target_pairs={{0,16},{4,20},{8,24},{12,28},{16,0},{20,4},{24,8},{28,12},{1,17},{... | collective-permute-start | bytes 1769480 | tf_op jit(solution)/shard_map/ppermute | solution.py:887
  382.1 19.5 %collective-permute-start.38 = (bf16[4,48,1920]{2,1,0:T(8,128)(2,1)S(1)}, bf16[4,48,1920]{2,1,0:T(8,128)(2,1)}, u32[]{:S(2)}, u32[]{:S(2)}) collective-permute-start(bf16[4,48,1920]{2,1,0:T(8,128)(2,1)S(1)} %constant_dynamic-slice_fusion.12.refs_11_), channel_id=1, source_target_pairs={{0,8},{4,12},{8,0},{12,4},{16,24},{20,28},{24,16},{28,20},{1,9},{5... | collective-permute-start | bytes 2211848 | tf_op jit(solution)/shard_map/ppermute | solution.py:887
  403.3 16.5 %collective-permute-start.41 = (bf16[2,1,48,3456]{3,2,1,0:T(8,128)(2,1)S(1)}, bf16[2,1,48,3456]{3,2,1,0:T(8,128)(2,1)S(1)}, u32[]{:S(2)}, u32[]{:S(2)}) collective-permute-start(bf16[2,1,48,3456]{3,2,1,0:T(8,128)(2,1)S(1)} %constant_dynamic-slice_fusion.9), channel_id=1, source_target_pairs={{0,1},{1,0},{2,3},{3,2},{4,5},{5,4},{6,7},{7,6},{8,9},{9,8},{10,11... | collective-permute-start | bytes 1990664 | tf_op jit(solution)/shard_map/ppermute | solution.py:955
  405.4 14.4 %collective-permute-start.57 = (bf16[48,3456]{1,0:T(8,128)(2,1)S(1)}, bf16[48,3456]{1,0:T(8,128)(2,1)S(1)}, u32[]{:S(2)}, u32[]{:S(2)}) collective-permute-start(bf16[48,3456]{1,0:T(8,128)(2,1)S(1)} %fusion.refs_5_), channel_id=1, source_target_pairs={{0,16},{4,20},{8,24},{12,28},{16,0},{20,4},{24,8},{28,12},{1,17},{... | collective-permute-start | bytes 995336 | tf_op jit(solution)/shard_map/ppermute | solution.py:887
  421.1 18.0 %collective-permute-start.58 = (bf16[2,48,3456]{2,1,0:T(8,128)(2,1)}, bf16[2,48,3456]{2,1,0:T(8,128)(2,1)}, u32[]{:S(2)}, u32[]{:S(2)}) collective-permute-start(bf16[2,48,3456]{2,1,0:T(8,128)(2,1)} %maximum_bitcast_fusion), channel_id=1, source_target_pairs={{0,8},{4,12},{8,0},{12,4},{16,24},{20,28},{24,16},{28,20},{1,9},{5... | collective-permute-start | bytes 1990664 | tf_op jit(solution)/shard_map/ppermute | solution.py:887
  425.7 18.1 %collective-permute-start.50 = (bf16[1,1,48,3456]{3,2,1,0:T(8,128)(2,1)S(1)}, bf16[1,1,48,3456]{3,2,1,0:T(8,128)(2,1)S(1)}, u32[]{:S(2)}, u32[]{:S(2)}) collective-permute-start(bf16[1,1,48,3456]{3,2,1,0:T(8,128)(2,1)S(1)} %constant_dynamic-slice_fusion), channel_id=1, source_target_pairs={{0,2},{1,3},{2,0},{3,1},{4,6},{5,7},{6,4},{7,5},{8,10},{9,11},{10,... | collective-permute-start | bytes 995336 | tf_op jit(solution)/shard_map/ppermute | solution.py:955
  431.4 18.4 %collective-permute-start.43 = (bf16[4,96,640]{2,1,0:T(8,128)(2,1)}, bf16[4,96,640]{2,1,0:T(8,128)(2,1)}, u32[]{:S(2)}, u32[]{:S(2)}) collective-permute-start(bf16[4,96,640]{2,1,0:T(8,128)(2,1)} %constant_dynamic-slice_fusion.8), channel_id=1, source_target_pairs={{0,8},{4,12},{8,0},{12,4},{16,24},{20,28},{24,16},{28,20},{1,9},{5... | collective-permute-start | bytes 1474568 | tf_op jit(solution)/shard_map/ppermute | solution.py:887
  434.0 18.4 %collective-permute-start.46 = (bf16[4,96,640]{2,1,0:T(8,128)(2,1)}, bf16[4,96,640]{2,1,0:T(8,128)(2,1)}, u32[]{:S(2)}, u32[]{:S(2)}) collective-permute-start(bf16[4,96,640]{2,1,0:T(8,128)(2,1)} %pad_maximum_fusion.10), channel_id=1, source_target_pairs={{0,16},{4,20},{8,24},{12,28},{16,0},{20,4},{24,8},{28,12},{1,17},{... | collective-permute-start | bytes 1474568 | tf_op jit(solution)/shard_map/ppermute | solution.py:887
  447.4 33.3 %collective-permute-start.59 = (bf16[4,48,3456]{2,1,0:T(8,128)(2,1)S(1)}, bf16[4,48,3456]{2,1,0:T(8,128)(2,1)}, u32[]{:S(2)}, u32[]{:S(2)}) collective-permute-start(bf16[4,48,3456]{2,1,0:T(8,128)(2,1)S(1)} %bitcast.143), channel_id=1, source_target_pairs={{0,4},{4,0},{8,12},{12,8},{16,20},{20,16},{24,28},{28,24},{1,5},{5... | collective-permute-start | bytes 3981320 | tf_op jit(solution)/shard_map/ppermute | solution.py:887
  454.7 13.3 %collective-permute-start.55 = (bf16[2,48,1280]{2,1,0:T(8,128)(2,1)S(1)}, bf16[2,48,1280]{2,1,0:T(8,128)(2,1)S(1)}, u32[]{:S(2)}, u32[]{:S(2)}) collective-permute-start(bf16[2,48,1280]{2,1,0:T(8,128)(2,1)S(1)} %maximum_bitcast_fusion.2), channel_id=1, source_target_pairs={{0,8},{4,12},{8,0},{12,4},{16,24},{20,28},{24,16},{28,20},{1,9},{5... | collective-permute-start | bytes 737288 | tf_op jit(solution)/shard_map/ppermute | solution.py:887
  (127 other events, 743.8 us)
Sparse Core Ops, SparseCore 0:
  366.6 20.7 reduce-scatter.1
  444.8 32.4 all-gather.2

commit v5 on v4

--- a/solution.py
+++ b/solution.py
@@ -1442,13 +1442,14 @@
     all_ff1 = wide_gather_swaps(sum_ff1, got_ff1, flying)
     all_ff0 = lax.all_gather(sum_ff0, "wide", axis=0, tiled=False)
     all_at1 = wide_gather_swaps(tie(sum_at1, flying))
-    all_at0 = wide_gather_swaps(narrow_sum_swaps(at0.finish(), (None, all_ff0)))
+    sum_at0 = narrow_sum_swaps(at0.finish(), (None, all_ff0))
 
     deep = ff_in.shape[2]
     unit = width // narrow
     shapes = [full(2, unit, deep), full(2, deep // narrow, width), full(2, unit, width)]
     attn_shape = full(2, unit, 3 * width)
     placed = place_ff(1, all_ff1, True, shapes)
+    all_at0 = wide_gather_swaps(sum_at0, None, placed[2])
     d_attn_in, small1 = place_attn(1, all_at1, attn_shape)
     placed = place_ff(0, all_ff0, False, shapes, placed)
     d_attn_in, small0 = place_attn(0, all_at0, attn_shape, (d_attn_in,), (placed[2],))

time: 520 us -> 517 us (level)
    unnamed x229 -> x231, local copies, waits for them, and re-layouts: 22.6 us -> 23.6 us
where the time goes in v5:
time: 517 us; the launch traced here: 510 us
  Pallas kernels  264 us (51%)
  other arithmetic  64.1 us (12%)
  starting transfers between devices  60.5 us (12%)
  waiting for transfers between devices  55.2 us (11%)
  local copies, waits for them, and re-layouts  42.5 us (8%)
  between operations  24.1 us (5%)
    pallas_call x12, Pallas kernels, call(): pl.pallas_call(body, out_shape=outs, in_specs=list(in_specs) + [ANY] * ex...  182 us
    pallas_call x6, Pallas kernels, weight_grad_cols(): pl.pallas_call(partial(grad_cols_kernel, rows=rows, steps=steps), out_sha...  41.7 us
    ppermute x35, waiting for transfers between devices, swap(): return lax.ppermute(value, 'wide', [(i, i ^ bit) for i in range(size)])  34.4 us
    ppermute x35, starting transfers between devices, swap(): return lax.ppermute(value, 'wide', [(i, i ^ bit) for i in range(size)])  30.3 us
    convert_element_type x30, other arithmetic, add_low(): return (left.astype(F32) + right.astype(F32)).astype(BF16)  27.2 us
    unnamed x231, local copies, waits for them, and re-layouts  23.6 us
    pallas_call x2, Pallas kernels, weight_grad_rows(): pl.pallas_call(partial(grad_rows_kernel, rows=rows, narrow=narrow), out_s...  19.8 us
    ppermute x8, starting transfers between devices, shift(): lax.ppermute(value, 'narrow', inner)  12.7 us
  transfers between devices with their start and end apart: 62, of which 16 were waited for; matrix products, arithmetic and copies ran while one was open for 15% of the time, Pallas kernels for 38%

profile of v5, /device:TPU:0, one launch (start us, length us, event | category | flops | bytes accessed | tf_op | source)
XLA Modules:
  0.0 510.4 jit_solution(4956354145917984657)
XLA Ops:
  14.5 14.2 %forward_attention0.2 = (bf16[512,2304]{1,0:T(8,128)(2,1)}, f32[16,512]{1,0:T(8,128)S(1)}, bf16[512,768]{1,0:T(8,128)(2,1)S(1)}, bf16[512,768]{1,0:T(8,128)(2,1)...) custom-call(s32[1]{0:T(128)} %select_n.520.refs_0_, bf16[2,512,768]{2,1,0:T(8,128)(2,1)} %refs_1_.5, ...), custom_call_target="tpu_custom_call" | custom-call | flops 14000000000 | bytes 16000000 | tf_op jit(solution)/shard_map/forward_attention0/pallas_call | solution.py:110
  31.8 3.0 collective-permute-start
  34.8 2.6 collective-permute-start.1
  41.9 17.4 %forward_ff0.2 = (bf16[512,3072]{1,0:T(8,128)(2,1)}, bf16[512,3072]{1,0:T(8,128)(2,1)}, bf16[512,768]{1,0:T(8,128)(2,1)}, bf16[528,768]{1,0:T(8,128)(2,1)}, f32[...) custom-call(s32[1]{0:T(128)} %select_n.520.refs_0_, ...), custom_call_target="tpu_custom_call" | custom-call | flops 17999998976 | bytes 20000000 | tf_op jit(solution)/shard_map/forward_ff0/pallas_call | solution.py:110
  63.6 3.2 route.1
  77.6 14.2 %forward_attention0.3 = (bf16[512,2304]{1,0:T(8,128)(2,1)}, f32[16,512]{1,0:T(8,128)S(1)}, bf16[512,768]{1,0:T(8,128)(2,1)S(1)}, bf16[512,768]{1,0:T(8,128)(2,1)...) custom-call(s32[1]{0:T(128)} %bitcast.6.refs_0_, bf16[2,512,768]{2,1,0:T(8,128)(2,1)} %refs_1_.5, ...), custom_call_target="tpu_custom_call" | custom-call | flops 14000000000 | bytes 16000000 | tf_op jit(solution)/shard_map/forward_attention0/pallas_call | solution.py:110
  94.4 2.1 collective-permute-start.7
  96.6 17.2 %forward_ff0.3 = (bf16[512,3072]{1,0:T(8,128)(2,1)}, bf16[512,3072]{1,0:T(8,128)(2,1)}, bf16[512,768]{1,0:T(8,128)(2,1)}, bf16[528,768]{1,0:T(8,128)(2,1)}, f32[...) custom-call(s32[1]{0:T(128)} %bitcast.6.refs_0_, ...), custom_call_target="tpu_custom_call" | custom-call | flops 17999998976 | bytes 20000000 | tf_op jit(solution)/shard_map/forward_ff0/pallas_call | solution.py:110
  118.4 14.3 %forward_attention1.1 = (bf16[512,2304]{1,0:T(8,128)(2,1)}, f32[16,512]{1,0:T(8,128)S(1)}, bf16[512,768]{1,0:T(8,128)(2,1)S(1)}, bf16[512,768]{1,0:T(8,128)(2,1)...) custom-call(s32[1]{0:T(128)} %constant.248.clone.1.refs_0_, ...), custom_call_target="tpu_custom_call" | custom-call | flops 14000000000 | bytes 16000000 | tf_op jit(solution)/shard_map/forward_attention1/pallas_call | solution.py:110
  135.1 17.1 %forward_ff1.1 = (bf16[512,3072]{1,0:T(8,128)(2,1)}, bf16[512,3072]{1,0:T(8,128)(2,1)}, bf16[512,768]{1,0:T(8,128)(2,1)}, bf16[528,768]{1,0:T(8,128)(2,1)}, f32[...) custom-call(s32[1]{0:T(128)} %constant.248.clone.1.refs_0_, ...), custom_call_target="tpu_custom_call" | custom-call | flops 17999998976 | bytes 20000000 | tf_op jit(solution)/shard_map/forward_ff1/pallas_call | solution.py:110
  153.0 13.4 %backward_ff1.1 = (bf16[512,768]{1,0:T(8,128)(2,1)S(1)}, bf16[512,3072]{1,0:T(8,128)(2,1)}, bf16[512,768]{1,0:T(8,128)(2,1)}, f32[512,768]{1,0:T(8,128)}, f32[8,3072]{1,0:T(8,128)S(1)}) custom-call(bf16[512,768]{1,0:T(8,128)(2,1)} %bitcast_select_fusion.1.refs_19_.refs_0_, bf16[512,128]{1,0:T(8,128)(2,1)S(1)} %get-tuple-element.193.refs_1_, ...), custom_call_target="tpu_custom_call" | custom-call | flops 16000000000 | bytes 22000000 | tf_op jit(solution)/shard_map/backward_ff1/pallas_call | solution.py:110
  166.5 8.7 %weight_grad_rows.2 = (bf16[4,192,1536]{2,1,0:T(8,128)(2,1)}, bf16[4,192,1536]{2,1,0:T(8,128)(2,1)}) custom-call(s32[1]{0:T(128)} %bitcast.18.half_ref, bf16[512,3072]{1,0:T(8,128)(2,1)} %get-tuple-element.203.refs_0_, bf16[512,768]{1,0:T(8,128)(2,1)S(1)} %get-tuple-element.204.refs_1_), custom_call_target="tpu_custom_call" | custom-call | flops 1000000 | bytes 100000 | tf_op jit(solution)/shard_map/weight_grad_rows/pallas_call | solution.py:865
  176.0 3.0 weight_grad_cols.7
  179.4 7.1 %weight_grad_cols.6 = (bf16[4,192,1536]{2,1,0:T(8,128)(2,1)}, bf16[4,192,1536]{2,1,0:T(8,128)(2,1)}) custom-call(s32[1]{0:T(128)} %bitcast.18.half_ref, bf16[512,768]{1,0:T(8,128)(2,1)S(1)} %copy-done.7, bf16[512,3072]{1,0:T(8,128)(2,1)} %get-tuple-element.201.refs_1_), custom_call_target="tpu_custom_call" | custom-call | flops 1000000 | bytes 100000 | tf_op jit(solution)/shard_map/weight_grad_cols/pallas_call | solution.py:805
  186.6 15.2 %backward_attention1.1 = (bf16[512,2304]{1,0:T(8,128)(2,1)}, bf16[512,768]{1,0:T(8,128)(2,1)S(1)}, f32[8,3072]{1,0:T(8,128)S(1)}) custom-call(s32[1]{0:T(128)} %constant.248.clone.1.refs_0_, s32[1,512]{1,0:T(1,128)S(1)} %slice_convert_fusion.refs_2_.refs_4_.refs_1_, f32[16,512]{1,0:T(8,128)S(1)} %get-tuple-element.190.refs_2_, ...), custom_call_target="tpu_custom_call" | custom-call | flops 20000000000 | bytes 16000000 | tf_op jit(solution)/shard_map/backward_attention1/pallas_call | solution.py:110
  205.2 2.3 add_convert_fusion.2
  210.9 2.3 add_convert_fusion.3
  214.6 7.4 %weight_grad_cols.8 = (bf16[4,192,1152]{2,1,0:T(8,128)(2,1)}, bf16[4,192,1152]{2,1,0:T(8,128)(2,1)}) custom-call(s32[1]{0:T(128)} %bitcast.18.half_ref, bf16[512,768]{1,0:T(8,128)(2,1)S(1)} %slice.121.refs_0_, bf16[512,2304]{1,0:T(8,128)(2,1)} %get-tuple-element.208.refs_1_, bf16[4,96,1536]{2,1,0:T(8,128)(2,1)S(1)} %constant_dynamic-slice_fusion.31.refs_2_, ...), custom_call_target="tpu_custom_call" | custom-call | flops 1000000 | bytes 100000 | tf_op jit(solution)/shard_map/weight_grad_cols/pallas_call | solution.py:805
  230.1 2.3 bitcast_select_fusion.refs_0_
  236.2 9.0 %collective-permute-done.18 = bf16[512,768]{1,0:T(8,128)(2,1)} collective-permute-done((bf16[512,768]{1,0:T(8,128)(2,1)}, bf16[512,768]{1,0:T(8,128)(2,1)}, u32[]{:S(2)}, u32[]{:S(2)}) %collective-permute-start.18) | collective-permute-done | bytes 786464 | tf_op jit(solution)/shard_map/ppermute | solution.py:1311
  245.2 14.0 %backward_ff0.2 = (bf16[512,768]{1,0:T(8,128)(2,1)}, bf16[512,3072]{1,0:T(8,128)(2,1)}, bf16[512,768]{1,0:T(8,128)(2,1)}, f32[512,768]{1,0:T(8,128)}, f32[8,3072]{1,0:T(8,128)S(1)}) custom-call(bf16[512,768]{1,0:T(8,128)(2,1)} %bitcast_select_fusion.refs_0_, bf16[512,128]{1,0:T(8,128)(2,1)S(1)} %copy-done.54, f32[512,128]{1,0:T(8,128)S(1)} %copy-done.48, ...), custom_call_target="tpu_custom_call" | custom-call | flops 16000000000 | bytes 22000000 | tf_op jit(solution)/shard_map/backward_ff0/pallas_call | solution.py:110
  259.8 2.3 broadcast_select_fusion.4
  262.1 2.3 broadcast_select_fusion.1.refs_15_
  264.5 3.3 collective-permute-start.20
  268.4 2.7 collective-permute-start.26
  278.3 13.8 %backward_ff0.3 = (bf16[512,768]{1,0:T(8,128)(2,1)}, bf16[512,3072]{1,0:T(8,128)(2,1)}, bf16[512,768]{1,0:T(8,128)(2,1)}, f32[512,768]{1,0:T(8,128)}, f32[8,3072]{1,0:T(8,128)S(1)}) custom-call(bf16[512,768]{1,0:T(8,128)(2,1)} %broadcast_select_fusion.4, bf16[512,128]{1,0:T(8,128)(2,1)S(1)} %copy-done.52, f32[512,128]{1,0:T(8,128)S(1)} %copy-done.44, ...), custom_call_target="tpu_custom_call" | custom-call | flops 16000000000 | bytes 22000000 | tf_op jit(solution)/shard_map/backward_ff0/pallas_call | solution.py:110
  293.0 2.7 broadcast_select_fusion.3
  298.6 6.3 %collective-permute-done.28 = bf16[4,96,640]{2,1,0:T(8,128)(2,1)S(1)} collective-permute-done((bf16[4,96,640]{2,1,0:T(8,128)(2,1)S(1)}, bf16[4,96,640]{2,1,0:T(8,128)(2,1)S(1)}, u32[]{:S(2)}, u32[]{:S(2)}) %collective-permute-start.28) | collective-permute-done | bytes 491552 | tf_op jit(solution)/shard_map/ppermute | solution.py:887
  305.0 11.1 %weight_grad_rows.3 = (bf16[4,192,1536]{2,1,0:T(8,128)(2,1)}, bf16[4,192,1536]{2,1,0:T(8,128)(2,1)}) custom-call(s32[1]{0:T(128)} %bitcast.18.half_ref, bf16[512,3072]{1,0:T(8,128)(2,1)} %get-tuple-element.257.refs_0_, bf16[512,3072]{1,0:T(8,128)(2,1)} %get-tuple-element.258.refs_1_, bf16[512,768]{1,0:T(8,128)(2,1)S(1)} %copy-done.5, ...), custom_call_target="tpu_custom_call" | custom-call | flops 1000000 | bytes 100000 | tf_op jit(solution)/shard_map/weight_grad_rows/pallas_call | solution.py:865
  317.3 10.1 %weight_grad_cols.9 = (bf16[4,192,1536]{2,1,0:T(8,128)(2,1)}, bf16[4,192,1536]{2,1,0:T(8,128)(2,1)}) custom-call(s32[1]{0:T(128)} %bitcast.18.half_ref, bf16[512,768]{1,0:T(8,128)(2,1)S(1)} %copy-done.2, bf16[512,768]{1,0:T(8,128)(2,1)} %get-tuple-element.177.refs_1_, bf16[512,3072]{1,0:T(8,128)(2,1)} %get-tuple-element.249.refs_2_, ...), custom_call_target="tpu_custom_call" | custom-call | flops 1000000 | bytes 100000 | tf_op jit(solution)/shard_map/weight_grad_cols/pallas_call | solution.py:805
  328.8 4.3 weight_grad_cols.10
  340.1 2.3 add_convert_fusion.1
  346.7 15.2 %backward_attention0.2 = (bf16[512,2304]{1,0:T(8,128)(2,1)}, bf16[512,768]{1,0:T(8,128)(2,1)S(1)}, f32[8,3072]{1,0:T(8,128)S(1)}) custom-call(s32[1]{0:T(128)} %bitcast.6.refs_0_, s32[2,512]{1,0:T(2,128)S(1)} %copy-done.33, f32[16,512]{1,0:T(8,128)S(1)} %copy-done.56, bf16[2,768,2304]{2,1,0:T(8,128)(2,1)} %refs_3_.11, bf16[2,768,768]{2,1,0:T(8,128)(2,1)} %refs_4_.21, ...), custom_call_target="tpu_custom_call" | custom-call | flops 20000000000 | bytes 16000000 | tf_op jit(solution)/shard_map/backward_attention0/pallas_call | solution.py:110
  367.8 5.1 collective-permute-done.33
  376.5 3.9 collective-permute-done.34
  383.8 16.3 %backward_attention0.3 = (bf16[512,2304]{1,0:T(8,128)(2,1)}, bf16[512,768]{1,0:T(8,128)(2,1)}, f32[8,3072]{1,0:T(8,128)S(1)}) custom-call(s32[1]{0:T(128)} %select_n.520.refs_0_, s32[2,512]{1,0:T(2,128)S(1)} %copy-done.33, f32[16,512]{1,0:T(8,128)S(1)} %copy-done.58, bf16[2,768,2304]{2,1,0:T(8,128)(2,1)} %refs_3_.11, bf16[2,768,768]{2,1,0:T(8,128)(2,1)} %refs_4_.21, ...), custom_call_target="tpu_custom_call" | custom-call | flops 20000000000 | bytes 16000000 | tf_op jit(solution)/shard_map/backward_attention0/pallas_call | solution.py:110
  410.7 9.8 %weight_grad_cols.11 = (bf16[4,192,1152]{2,1,0:T(8,128)(2,1)}, bf16[4,192,1152]{2,1,0:T(8,128)(2,1)}) custom-call(s32[1]{0:T(128)} %bitcast.18.half_ref, bf16[512,768]{1,0:T(8,128)(2,1)S(1)} %get-tuple-element.391.refs_0_, bf16[512,768]{1,0:T(8,128)(2,1)S(1)} %get-tuple-element.390.refs_1_, bf16[512,2304]{1,0:T(8,128)(2,1)} %get-tuple-element.269.refs_2_, ...), custom_call_target="tpu_custom_call" | custom-call | flops 1000000 | bytes 100000 | tf_op jit(solution)/shard_map/weight_grad_cols/pallas_call | solution.py:805
  422.7 2.2 small_pack.3
  436.1 3.7 collective-permute-done.54
  439.8 4.5 collective-permute-done.50
  448.0 2.4 collective-permute-done.57
  456.5 5.8 %collective-permute-done.44 = bf16[4,48,640]{2,1,0:T(8,128)(2,1)S(1)} collective-permute-done((bf16[4,48,640]{2,1,0:T(8,128)(2,1)S(1)}, bf16[4,48,640]{2,1,0:T(8,128)(2,1)S(1)}, u32[]{:S(2)}, u32[]{:S(2)}) %collective-permute-start.44) | collective-permute-done | bytes 245792 | tf_op jit(solution)/shard_map/ppermute | solution.py:887
  466.0 2.7 collective-permute-done.58
  471.0 2.6 collective-permute-start.49
  474.8 3.4 collective-permute-done.49
  481.3 2.3 collective-permute-done.51
  487.0 4.3 place_ff1.1
  493.5 4.3 place_ff0.1
  (462 shorter events, 146.6 us)
Async XLA Ops:
  7.2 393.5 %reduce-scatter.2.cloned.1.call-start = ((), (), s32[]{:S(2)}) async-start(), calls=%async_computation.1 | async-start | bytes 614400 | tf_op jit(solution)/shard_map/reduce_scatter | solution.py:982
  31.8 30.4 %collective-permute-start = (s32[1]{0:T(128)}, s32[1]{0:T(128)}, u32[]{:S(2)}, u32[]{:S(2)}) collective-permute-start(s32[1]{0:T(128)} %bitcast.2.refs_0_), channel_id=1, source_target_pairs={{0,1},{1,2},{2,3},{3,0},{4,5},{5,6},{6,7},{7,4},{8,9},{9,10},{10,1... | collective-permute-start | bytes 20 | tf_op jit(solution)/shard_map/ppermute | solution.py:1292
  34.8 28.7 %collective-permute-start.1 = (s32[1]{0:T(128)}, s32[1]{0:T(128)}, u32[]{:S(2)}, u32[]{:S(2)}) collective-permute-start(s32[1]{0:T(128)} %bitcast.2.refs_0_), channel_id=1, source_target_pairs={{0,2},{1,3},{2,0},{3,1},{4,6},{5,7},{6,4},{7,5},{8,10},{9,11},{10,... | collective-permute-start | bytes 20 | tf_op jit(solution)/shard_map/ppermute | solution.py:1292
  37.4 26.2 %collective-permute-start.2 = (s32[1]{0:T(128)}, s32[1]{0:T(128)}, u32[]{:S(2)}, u32[]{:S(2)}) collective-permute-start(s32[1]{0:T(128)} %bitcast.2.refs_0_), channel_id=1, source_target_pairs={{0,3},{1,0},{2,1},{3,2},{4,7},{5,4},{6,5},{7,6},{8,11},{9,8},{10,9... | collective-permute-start | bytes 20 | tf_op jit(solution)/shard_map/ppermute | solution.py:1292
  40.9 34.7 %collective-permute-start.3 = (bf16[512,768]{1,0:T(8,128)(2,1)S(1)}, bf16[512,768]{1,0:T(8,128)(2,1)}, u32[]{:S(2)}, u32[]{:S(2)}) collective-permute-start(bf16[512,768]{1,0:T(8,128)(2,1)S(1)} %get-tuple-element.174.refs_19_), channel_id=1, source_target_pairs={{0,1},{1,0},{2,3},{3,2},{4,5},{5,4},{6,7},{7,6},{8,9},{9,8},{10,11... | collective-permute-start | bytes 2359304 | tf_op jit(solution)/shard_map/ppermute | solution.py:1311
  41.6 33.9 %collective-permute-start.4 = (bf16[512,768]{1,0:T(8,128)(2,1)S(1)}, bf16[512,768]{1,0:T(8,128)(2,1)}, u32[]{:S(2)}, u32[]{:S(2)}) collective-permute-start(bf16[512,768]{1,0:T(8,128)(2,1)S(1)} %get-tuple-element.174.refs_19_), channel_id=1, source_target_pairs={{0,4},{1,2},{2,1},{3,7},{4,0},{5,6},{6,5},{7,3},{8,12},{9,10},{10,... | collective-permute-start | bytes 2359304 | tf_op jit(solution)/shard_map/ppermute | solution.py:1312
  62.2 30.5 %collective-permute-start.5 = (bf16[528,768]{1,0:T(8,128)(2,1)}, bf16[528,768]{1,0:T(8,128)(2,1)}, u32[]{:S(2)}, u32[]{:S(2)}) collective-permute-start(bf16[528,768]{1,0:T(8,128)(2,1)} %get-tuple-element.173.refs_9_), channel_id=1, source_target_pairs={{0,1},{1,0},{2,3},{3,2},{4,5},{5,4},{6,7},{7,6},{8,9},{9,8},{10,11... | collective-permute-start | bytes 2433032 | tf_op jit(solution)/shard_map/ppermute | solution.py:1311
  63.6 29.2 %collective-permute-start.6 = (bf16[528,768]{1,0:T(8,128)(2,1)}, bf16[528,768]{1,0:T(8,128)(2,1)}, u32[]{:S(2)}, u32[]{:S(2)}) collective-permute-start(bf16[528,768]{1,0:T(8,128)(2,1)} %get-tuple-element.173.refs_9_), channel_id=1, source_target_pairs={{0,4},{1,2},{2,1},{3,7},{4,0},{5,6},{6,5},{7,3},{8,12},{9,10},{10,... | collective-permute-start | bytes 2433032 | tf_op jit(solution)/shard_map/ppermute | solution.py:1312
  94.4 21.6 %collective-permute-start.7 = (bf16[528,768]{1,0:T(8,128)(2,1)S(1)}, bf16[528,768]{1,0:T(8,128)(2,1)S(1)}, u32[]{:S(2)}, u32[]{:S(2)}) collective-permute-start(bf16[528,768]{1,0:T(8,128)(2,1)S(1)} %broadcast_select_fusion.2.refs_19_), channel_id=1, source_target_pairs={{0,1},{1,0},{2,3},{3,2},{4,5},{5,4},{6,7},{7,6},{8,9},{9,8},{10,11... | collective-permute-start | bytes 2433032 | tf_op jit(solution)/shard_map/ppermute | solution.py:1311
  96.5 19.5 %collective-permute-start.8 = (bf16[528,768]{1,0:T(8,128)(2,1)S(1)}, bf16[528,768]{1,0:T(8,128)(2,1)S(1)}, u32[]{:S(2)}, u32[]{:S(2)}) collective-permute-start(bf16[528,768]{1,0:T(8,128)(2,1)S(1)} %broadcast_select_fusion.2.refs_19_), channel_id=1, source_target_pairs={{0,4},{1,2},{2,1},{3,7},{4,0},{5,6},{6,5},{7,3},{8,12},{9,10},{10,... | collective-permute-start | bytes 2433032 | tf_op jit(solution)/shard_map/ppermute | solution.py:1312
  113.8 18.9 %collective-permute-start.10 = (bf16[512,768]{1,0:T(8,128)(2,1)S(1)}, bf16[512,768]{1,0:T(8,128)(2,1)S(1)}, u32[]{:S(2)}, u32[]{:S(2)}) collective-permute-start(bf16[512,768]{1,0:T(8,128)(2,1)S(1)} %copy-done.84), channel_id=1, source_target_pairs={{0,4},{1,2},{2,1},{3,7},{4,0},{5,6},{6,5},{7,3},{8,12},{9,10},{10,... | collective-permute-start | bytes 2359304 | tf_op jit(solution)/shard_map/ppermute | solution.py:1312
  114.4 19.5 %collective-permute-start.9 = (bf16[512,768]{1,0:T(8,128)(2,1)S(1)}, bf16[512,768]{1,0:T(8,128)(2,1)S(1)}, u32[]{:S(2)}, u32[]{:S(2)}) collective-permute-start(bf16[512,768]{1,0:T(8,128)(2,1)S(1)} %copy-done.84), channel_id=1, source_target_pairs={{0,1},{1,0},{2,3},{3,2},{4,5},{5,4},{6,7},{7,6},{8,9},{9,8},{10,11... | collective-permute-start | bytes 2359304 | tf_op jit(solution)/shard_map/ppermute | solution.py:1311
  175.2 30.0 %collective-permute-start.16 = (bf16[4,192,1536]{2,1,0:T(8,128)(2,1)}, bf16[4,192,1536]{2,1,0:T(8,128)(2,1)}, u32[]{:S(2)}, u32[]{:S(2)}) collective-permute-start(bf16[4,192,1536]{2,1,0:T(8,128)(2,1)} %get-tuple-element.205.refs_10_), channel_id=1, source_target_pairs={{0,4},{4,0},{8,12},{12,8},{16,20},{20,16},{24,28},{28,24},{1,5},{5... | collective-permute-start | bytes 7077896 | tf_op jit(solution)/shard_map/ppermute | solution.py:887
  178.9 25.3 %collective-permute-start.17 = (bf16[4,192,384]{2,1,0:T(8,128)(2,1)S(1)}, bf16[4,192,384]{2,1,0:T(8,128)(2,1)S(1)}, u32[]{:S(2)}, u32[]{:S(2)}) collective-permute-start(bf16[4,192,384]{2,1,0:T(8,128)(2,1)S(1)} %get-tuple-element.206.refs_11_), channel_id=1, source_target_pairs={{0,4},{4,0},{8,12},{12,8},{16,20},{20,16},{24,28},{28,24},{1,5},{5... | collective-permute-start | bytes 1769480 | tf_op jit(solution)/shard_map/ppermute | solution.py:887
  186.5 23.4 %collective-permute-start.15 = (bf16[4,192,1536]{2,1,0:T(8,128)(2,1)}, bf16[4,192,1536]{2,1,0:T(8,128)(2,1)}, u32[]{:S(2)}, u32[]{:S(2)}) collective-permute-start(bf16[4,192,1536]{2,1,0:T(8,128)(2,1)} %get-tuple-element.202.refs_9_), channel_id=1, source_target_pairs={{0,4},{4,0},{8,12},{12,8},{16,20},{20,16},{24,28},{28,24},{1,5},{5... | collective-permute-start | bytes 7077896 | tf_op jit(solution)/shard_map/ppermute | solution.py:887
  202.6 20.0 %collective-permute-start.13 = (bf16[512,768]{1,0:T(8,128)(2,1)S(1)}, bf16[512,768]{1,0:T(8,128)(2,1)S(1)}, u32[]{:S(2)}, u32[]{:S(2)}) collective-permute-start(bf16[512,768]{1,0:T(8,128)(2,1)S(1)} %get-tuple-element.207), channel_id=1, source_target_pairs={{0,1},{1,0},{2,3},{3,2},{4,5},{5,4},{6,7},{7,6},{8,9},{9,8},{10,11... | collective-permute-start | bytes 2359304 | tf_op jit(solution)/shard_map/ppermute | solution.py:1311
  204.1 18.5 %collective-permute-start.14 = (bf16[512,768]{1,0:T(8,128)(2,1)S(1)}, bf16[512,768]{1,0:T(8,128)(2,1)S(1)}, u32[]{:S(2)}, u32[]{:S(2)}) collective-permute-start(bf16[512,768]{1,0:T(8,128)(2,1)S(1)} %get-tuple-element.207), channel_id=1, source_target_pairs={{0,4},{1,2},{2,1},{3,7},{4,0},{5,6},{6,5},{7,3},{8,12},{9,10},{10,... | collective-permute-start | bytes 2359304 | tf_op jit(solution)/shard_map/ppermute | solution.py:1312
  224.4 20.7 %collective-permute-start.18 = (bf16[512,768]{1,0:T(8,128)(2,1)}, bf16[512,768]{1,0:T(8,128)(2,1)}, u32[]{:S(2)}, u32[]{:S(2)}) collective-permute-start(bf16[512,768]{1,0:T(8,128)(2,1)} %broadcast_select_fusion.5.refs_12_), channel_id=1, source_target_pairs={{0,1},{1,0},{2,3},{3,2},{4,5},{5,4},{6,7},{7,6},{8,9},{9,8},{10,11... | collective-permute-start | bytes 2359304 | tf_op jit(solution)/shard_map/ppermute | solution.py:1311
  225.8 36.3 %collective-permute-start.11 = (bf16[528,768]{1,0:T(8,128)(2,1)}, bf16[528,768]{1,0:T(8,128)(2,1)}, u32[]{:S(2)}, u32[]{:S(2)}) collective-permute-start(bf16[528,768]{1,0:T(8,128)(2,1)} %get-tuple-element.189.refs_11_), channel_id=1, source_target_pairs={{0,1},{1,0},{2,3},{3,2},{4,5},{5,4},{6,7},{7,6},{8,9},{9,8},{10,11... | collective-permute-start | bytes 2433032 | tf_op jit(solution)/shard_map/ppermute | solution.py:1311
  226.5 35.6 %collective-permute-start.12 = (bf16[528,768]{1,0:T(8,128)(2,1)}, bf16[528,768]{1,0:T(8,128)(2,1)}, u32[]{:S(2)}, u32[]{:S(2)}) collective-permute-start(bf16[528,768]{1,0:T(8,128)(2,1)} %get-tuple-element.189.refs_11_), channel_id=1, source_target_pairs={{0,4},{1,2},{2,1},{3,7},{4,0},{5,6},{6,5},{7,3},{8,12},{9,10},{10,... | collective-permute-start | bytes 2433032 | tf_op jit(solution)/shard_map/ppermute | solution.py:1312
  233.1 38.0 %collective-permute-start.25 = (bf16[4,96,1920]{2,1,0:T(8,128)(2,1)S(1)}, bf16[4,96,1920]{2,1,0:T(8,128)(2,1)}, u32[]{:S(2)}, u32[]{:S(2)}) collective-permute-start(bf16[4,96,1920]{2,1,0:T(8,128)(2,1)S(1)} %copy-done.68), channel_id=1, source_target_pairs={{0,16},{4,20},{8,24},{12,28},{16,0},{20,4},{24,8},{28,12},{1,17},{... | collective-permute-start | bytes 4423688 | tf_op jit(solution)/shard_map/ppermute | solution.py:887
  234.7 33.4 %collective-permute-start.24 = (bf16[4,96,1536]{2,1,0:T(8,128)(2,1)S(1)}, bf16[4,96,1536]{2,1,0:T(8,128)(2,1)S(1)}, u32[]{:S(2)}, u32[]{:S(2)}) collective-permute-start(bf16[4,96,1536]{2,1,0:T(8,128)(2,1)S(1)} %constant_dynamic-slice_fusion.31.refs_2_), channel_id=1, source_target_pairs={{0,8},{4,12},{8,0},{12,4},{16,24},{20,28},{24,16},{28,20},{1,9},{5... | collective-permute-start | bytes 3538952 | tf_op jit(solution)/shard_map/ppermute | solution.py:887
  245.1 14.1 %collective-permute-start.19 = (bf16[512,768]{1,0:T(8,128)(2,1)}, bf16[512,768]{1,0:T(8,128)(2,1)S(1)}, u32[]{:S(2)}, u32[]{:S(2)}) collective-permute-start(bf16[512,768]{1,0:T(8,128)(2,1)} %broadcast_select_fusion.5.refs_12_), channel_id=1, source_target_pairs={{0,4},{1,2},{2,1},{3,7},{4,0},{5,6},{6,5},{7,3},{8,12},{9,10},{10,... | collective-permute-start | bytes 2359304 | tf_op jit(solution)/shard_map/ppermute | solution.py:1312
  259.2 16.2 %collective-permute-start.22 = (bf16[4,192,1152]{2,1,0:T(8,128)(2,1)}, bf16[4,192,1152]{2,1,0:T(8,128)(2,1)S(1)}, u32[]{:S(2)}, u32[]{:S(2)}) collective-permute-start(bf16[4,192,1152]{2,1,0:T(8,128)(2,1)} %get-tuple-element.212.refs_11_), channel_id=1, source_target_pairs={{0,4},{4,0},{8,12},{12,8},{16,20},{20,16},{24,28},{28,24},{1,5},{5... | collective-permute-start | bytes 5308424 | tf_op jit(solution)/shard_map/ppermute | solution.py:887
  264.5 27.8 %collective-permute-start.20 = (bf16[528,768]{1,0:T(8,128)(2,1)}, bf16[528,768]{1,0:T(8,128)(2,1)S(1)}, u32[]{:S(2)}, u32[]{:S(2)}) collective-permute-start(bf16[528,768]{1,0:T(8,128)(2,1)} %broadcast_select_fusion.1.refs_15_), channel_id=1, source_target_pairs={{0,1},{1,0},{2,3},{3,2},{4,5},{5,4},{6,7},{7,6},{8,9},{9,8},{10,11... | collective-permute-start | bytes 2433032 | tf_op jit(solution)/shard_map/ppermute | solution.py:1311
  267.8 25.2 %collective-permute-start.21 = (bf16[528,768]{1,0:T(8,128)(2,1)}, bf16[528,768]{1,0:T(8,128)(2,1)}, u32[]{:S(2)}, u32[]{:S(2)}) collective-permute-start(bf16[528,768]{1,0:T(8,128)(2,1)} %broadcast_select_fusion.1.refs_15_), channel_id=1, source_target_pairs={{0,4},{1,2},{2,1},{3,7},{4,0},{5,6},{6,5},{7,3},{8,12},{9,10},{10,... | collective-permute-start | bytes 2433032 | tf_op jit(solution)/shard_map/ppermute | solution.py:1312
  268.4 23.8 %collective-permute-start.26 = (bf16[4,48,1536]{2,1,0:T(8,128)(2,1)S(1)}, bf16[4,48,1536]{2,1,0:T(8,128)(2,1)S(1)}, u32[]{:S(2)}, u32[]{:S(2)}) collective-permute-start(bf16[4,48,1536]{2,1,0:T(8,128)(2,1)S(1)} %constant_dynamic-slice_fusion.25.refs_13_), channel_id=1, source_target_pairs={{0,16},{4,20},{8,24},{12,28},{16,0},{20,4},{24,8},{28,12},{1,17},{... | collective-permute-start | bytes 1769480 | tf_op jit(solution)/shard_map/ppermute | solution.py:887
  273.9 22.0 %collective-permute-start.27 = (bf16[4,48,1920]{2,1,0:T(8,128)(2,1)}, bf16[4,48,1920]{2,1,0:T(8,128)(2,1)S(1)}, u32[]{:S(2)}, u32[]{:S(2)}) collective-permute-start(bf16[4,48,1920]{2,1,0:T(8,128)(2,1)} %constant_dynamic-slice_fusion.22.refs_14_), channel_id=1, source_target_pairs={{0,8},{4,12},{8,0},{12,4},{16,24},{20,28},{24,16},{28,20},{1,9},{5... | collective-permute-start | bytes 2211848 | tf_op jit(solution)/shard_map/ppermute | solution.py:887
  277.8 19.5 %collective-permute-start.29 = (bf16[4,96,640]{2,1,0:T(8,128)(2,1)}, bf16[4,96,640]{2,1,0:T(8,128)(2,1)}, u32[]{:S(2)}, u32[]{:S(2)}) collective-permute-start(bf16[4,96,640]{2,1,0:T(8,128)(2,1)} %pad_maximum_fusion.8.refs_12_), channel_id=1, source_target_pairs={{0,16},{4,20},{8,24},{12,28},{16,0},{20,4},{24,8},{28,12},{1,17},{... | collective-permute-start | bytes 1474568 | tf_op jit(solution)/shard_map/ppermute | solution.py:887
  316.1 21.6 %collective-permute-start.31 = (bf16[4,192,1536]{2,1,0:T(8,128)(2,1)}, bf16[4,192,1536]{2,1,0:T(8,128)(2,1)S(1)}, u32[]{:S(2)}, u32[]{:S(2)}) collective-permute-start(bf16[4,192,1536]{2,1,0:T(8,128)(2,1)} %get-tuple-element.262), channel_id=1, source_target_pairs={{0,4},{4,0},{8,12},{12,8},{16,20},{20,16},{24,28},{28,24},{1,5},{5... | collective-permute-start | bytes 7077896 | tf_op jit(solution)/shard_map/ppermute | solution.py:887
  333.4 28.5 %collective-permute-start.39 = (bf16[2,1,48,3456]{3,2,1,0:T(8,128)(2,1)S(1)}, bf16[2,1,48,3456]{3,2,1,0:T(8,128)(2,1)S(1)}, u32[]{:S(2)}, u32[]{:S(2)}) collective-permute-start(bf16[2,1,48,3456]{3,2,1,0:T(8,128)(2,1)S(1)} %constant_dynamic-slice_fusion.11), channel_id=1, source_target_pairs={{0,1},{1,0},{2,3},{3,2},{4,5},{5,4},{6,7},{7,6},{8,9},{9,8},{10,11... | collective-permute-start | bytes 1990664 | tf_op jit(solution)/shard_map/ppermute | solution.py:955
  334.5 30.2 %collective-permute-start.36 = (bf16[4,48,640]{2,1,0:T(8,128)(2,1)S(1)}, bf16[4,48,640]{2,1,0:T(8,128)(2,1)}, u32[]{:S(2)}, u32[]{:S(2)}) collective-permute-start(bf16[4,48,640]{2,1,0:T(8,128)(2,1)S(1)} %constant_dynamic-slice_fusion.21.refs_5_), channel_id=1, source_target_pairs={{0,16},{4,20},{8,24},{12,28},{16,0},{20,4},{24,8},{28,12},{1,17},{... | collective-permute-start | bytes 737288 | tf_op jit(solution)/shard_map/ppermute | solution.py:887
  336.2 28.5 %collective-permute-start.37 = (bf16[4,48,640]{2,1,0:T(8,128)(2,1)S(1)}, bf16[4,48,640]{2,1,0:T(8,128)(2,1)}, u32[]{:S(2)}, u32[]{:S(2)}) collective-permute-start(bf16[4,48,640]{2,1,0:T(8,128)(2,1)S(1)} %constant_dynamic-slice_fusion.19.refs_6_), channel_id=1, source_target_pairs={{0,8},{4,12},{8,0},{12,4},{16,24},{20,28},{24,16},{28,20},{1,9},{5... | collective-permute-start | bytes 737288 | tf_op jit(solution)/shard_map/ppermute | solution.py:887
  344.8 35.5 %collective-permute-start.34 = (bf16[4,96,1920]{2,1,0:T(8,128)(2,1)}, bf16[4,96,1920]{2,1,0:T(8,128)(2,1)}, u32[]{:S(2)}, u32[]{:S(2)}) collective-permute-start(bf16[4,96,1920]{2,1,0:T(8,128)(2,1)} %pad_maximum_fusion.2.refs_10_), channel_id=1, source_target_pairs={{0,16},{4,20},{8,24},{12,28},{16,0},{20,4},{24,8},{28,12},{1,17},{... | collective-permute-start | bytes 4423688 | tf_op jit(solution)/shard_map/ppermute | solution.py:887
  345.2 27.7 %collective-permute-start.33 = (bf16[4,96,1536]{2,1,0:T(8,128)(2,1)}, bf16[4,96,1536]{2,1,0:T(8,128)(2,1)}, u32[]{:S(2)}, u32[]{:S(2)}) collective-permute-start(bf16[4,96,1536]{2,1,0:T(8,128)(2,1)} %constant_dynamic-slice_fusion.18.refs_9_), channel_id=1, source_target_pairs={{0,8},{4,12},{8,0},{12,4},{16,24},{20,28},{24,16},{28,20},{1,9},{5... | collective-permute-start | bytes 3538952 | tf_op jit(solution)/shard_map/ppermute | solution.py:887
  362.8 37.9 %collective-permute-start.40 = (bf16[1,1,48,3456]{3,2,1,0:T(8,128)(2,1)}, bf16[1,1,48,3456]{3,2,1,0:T(8,128)(2,1)}, u32[]{:S(2)}, u32[]{:S(2)}) collective-permute-start(bf16[1,1,48,3456]{3,2,1,0:T(8,128)(2,1)} %constant_dynamic-slice_fusion.10), channel_id=1, source_target_pairs={{0,2},{1,3},{2,0},{3,1},{4,6},{5,7},{6,4},{7,5},{8,10},{9,11},{10,... | collective-permute-start | bytes 995336 | tf_op jit(solution)/shard_map/ppermute | solution.py:955
  367.7 110.5 %all-gather.3.cloned.1.call-start = ((), (), s32[]{:S(2)}) async-start(), calls=%async_computation.2 | async-start | bytes 2985984 | tf_op jit(solution)/shard_map/all_gather | solution.py:1443
  374.8 25.9 %collective-permute-start.35 = (bf16[4,48,1536]{2,1,0:T(8,128)(2,1)S(1)}, bf16[4,48,1536]{2,1,0:T(8,128)(2,1)}, u32[]{:S(2)}, u32[]{:S(2)}) collective-permute-start(bf16[4,48,1536]{2,1,0:T(8,128)(2,1)S(1)} %constant_dynamic-slice_fusion.15.refs_10_), channel_id=1, source_target_pairs={{0,16},{4,20},{8,24},{12,28},{16,0},{20,4},{24,8},{28,12},{1,17},{... | collective-permute-start | bytes 1769480 | tf_op jit(solution)/shard_map/ppermute | solution.py:887
  382.2 20.0 %collective-permute-start.38 = (bf16[4,48,1920]{2,1,0:T(8,128)(2,1)S(1)}, bf16[4,48,1920]{2,1,0:T(8,128)(2,1)}, u32[]{:S(2)}, u32[]{:S(2)}) collective-permute-start(bf16[4,48,1920]{2,1,0:T(8,128)(2,1)S(1)} %constant_dynamic-slice_fusion.12.refs_11_), channel_id=1, source_target_pairs={{0,8},{4,12},{8,0},{12,4},{16,24},{20,28},{24,16},{28,20},{1,9},{5... | collective-permute-start | bytes 2211848 | tf_op jit(solution)/shard_map/ppermute | solution.py:887
  404.0 16.5 %collective-permute-start.41 = (bf16[2,1,48,3456]{3,2,1,0:T(8,128)(2,1)S(1)}, bf16[2,1,48,3456]{3,2,1,0:T(8,128)(2,1)S(1)}, u32[]{:S(2)}, u32[]{:S(2)}) collective-permute-start(bf16[2,1,48,3456]{3,2,1,0:T(8,128)(2,1)S(1)} %constant_dynamic-slice_fusion.9), channel_id=1, source_target_pairs={{0,1},{1,0},{2,3},{3,2},{4,5},{5,4},{6,7},{7,6},{8,9},{9,8},{10,11... | collective-permute-start | bytes 1990664 | tf_op jit(solution)/shard_map/ppermute | solution.py:955
  406.1 14.4 %collective-permute-start.53 = (bf16[48,3456]{1,0:T(8,128)(2,1)S(1)}, bf16[48,3456]{1,0:T(8,128)(2,1)S(1)}, u32[]{:S(2)}, u32[]{:S(2)}) collective-permute-start(bf16[48,3456]{1,0:T(8,128)(2,1)S(1)} %fusion.refs_5_), channel_id=1, source_target_pairs={{0,16},{4,20},{8,24},{12,28},{16,0},{20,4},{24,8},{28,12},{1,17},{... | collective-permute-start | bytes 995336 | tf_op jit(solution)/shard_map/ppermute | solution.py:887
  421.8 18.0 %collective-permute-start.54 = (bf16[2,48,3456]{2,1,0:T(8,128)(2,1)}, bf16[2,48,3456]{2,1,0:T(8,128)(2,1)}, u32[]{:S(2)}, u32[]{:S(2)}) collective-permute-start(bf16[2,48,3456]{2,1,0:T(8,128)(2,1)} %maximum_bitcast_fusion), channel_id=1, source_target_pairs={{0,8},{4,12},{8,0},{12,4},{16,24},{20,28},{24,16},{28,20},{1,9},{5... | collective-permute-start | bytes 1990664 | tf_op jit(solution)/shard_map/ppermute | solution.py:887
  426.3 18.1 %collective-permute-start.50 = (bf16[1,1,48,3456]{3,2,1,0:T(8,128)(2,1)S(1)}, bf16[1,1,48,3456]{3,2,1,0:T(8,128)(2,1)S(1)}, u32[]{:S(2)}, u32[]{:S(2)}) collective-permute-start(bf16[1,1,48,3456]{3,2,1,0:T(8,128)(2,1)S(1)} %constant_dynamic-slice_fusion), channel_id=1, source_target_pairs={{0,2},{1,3},{2,0},{3,1},{4,6},{5,7},{6,4},{7,5},{8,10},{9,11},{10,... | collective-permute-start | bytes 995336 | tf_op jit(solution)/shard_map/ppermute | solution.py:955
  432.0 18.5 %collective-permute-start.43 = (bf16[4,96,640]{2,1,0:T(8,128)(2,1)}, bf16[4,96,640]{2,1,0:T(8,128)(2,1)}, u32[]{:S(2)}, u32[]{:S(2)}) collective-permute-start(bf16[4,96,640]{2,1,0:T(8,128)(2,1)} %constant_dynamic-slice_fusion.8), channel_id=1, source_target_pairs={{0,8},{4,12},{8,0},{12,4},{16,24},{20,28},{24,16},{28,20},{1,9},{5... | collective-permute-start | bytes 1474568 | tf_op jit(solution)/shard_map/ppermute | solution.py:887
  434.7 18.4 %collective-permute-start.46 = (bf16[4,96,640]{2,1,0:T(8,128)(2,1)}, bf16[4,96,640]{2,1,0:T(8,128)(2,1)}, u32[]{:S(2)}, u32[]{:S(2)}) collective-permute-start(bf16[4,96,640]{2,1,0:T(8,128)(2,1)} %pad_maximum_fusion.10), channel_id=1, source_target_pairs={{0,16},{4,20},{8,24},{12,28},{16,0},{20,4},{24,8},{28,12},{1,17},{... | collective-permute-start | bytes 1474568 | tf_op jit(solution)/shard_map/ppermute | solution.py:887
  448.0 25.8 %collective-permute-start.55 = (bf16[4,48,3456]{2,1,0:T(8,128)(2,1)S(1)}, bf16[4,48,3456]{2,1,0:T(8,128)(2,1)S(1)}, u32[]{:S(2)}, u32[]{:S(2)}) collective-permute-start(bf16[4,48,3456]{2,1,0:T(8,128)(2,1)S(1)} %bitcast.143), channel_id=1, source_target_pairs={{0,4},{4,0},{8,12},{12,8},{16,20},{20,16},{24,28},{28,24},{1,5},{5... | collective-permute-start | bytes 3981320 | tf_op jit(solution)/shard_map/ppermute | solution.py:887
  455.3 13.4 %collective-permute-start.58 = (bf16[2,48,1280]{2,1,0:T(8,128)(2,1)S(1)}, bf16[2,48,1280]{2,1,0:T(8,128)(2,1)S(1)}, u32[]{:S(2)}, u32[]{:S(2)}) collective-permute-start(bf16[2,48,1280]{2,1,0:T(8,128)(2,1)S(1)} %maximum_bitcast_fusion.2), channel_id=1, source_target_pairs={{0,8},{4,12},{8,0},{12,4},{16,24},{20,28},{24,16},{28,20},{1,9},{5... | collective-permute-start | bytes 737288 | tf_op jit(solution)/shard_map/ppermute | solution.py:887
  473.6 17.9 %collective-permute-start.59 = (bf16[4,48,1280]{2,1,0:T(8,128)(2,1)S(1)}, bf16[4,48,1280]{2,1,0:T(8,128)(2,1)S(1)}, u32[]{:S(2)}, u32[]{:S(2)}) collective-permute-start(bf16[4,48,1280]{2,1,0:T(8,128)(2,1)S(1)} %bitcast.146), channel_id=1, source_target_pairs={{0,4},{4,0},{8,12},{12,8},{16,20},{20,16},{24,28},{28,24},{1,5},{5... | collective-permute-start | bytes 1474568 | tf_op jit(solution)/shard_map/ppermute | solution.py:887
  (128 other events, 747.5 us)
Sparse Core Ops, SparseCore 0:
  367.8 20.0 reduce-scatter.1
  445.3 32.6 all-gather.2
